TPU v7x, 512 devices: a whole 4x4x16 slice. The times are simulated.
512 devices in a mesh: pair: 2 (over core), latent: 32 (over x, z_lo), tok: 8 (over y, z_hi).
Axes of the slice: x: 4, y: 4, z: 16 (z_hi: 2, z_lo: 8; z = z_hi * 8 + z_lo), core: 2. Of those that a mesh axis runs over, the one named last changes fastest.
Arguments:
- activations: bfloat16 [2, 512, 3584], P('pair', 'tok'), may hold values from -6 to 6
- enc_weight: bfloat16 [2, 3584, 65536], P('pair', None, ('latent', 'tok')), may hold values from -0.0625 to 0.0625
- enc_bias: float32 [65536], P(('latent', 'tok')), may hold values from -3 to 3
- thresholds: int32 [65536], P(('latent', 'tok')), may hold values from 1 to 4
- dec_weight: bfloat16 [2, 65536, 3584], P('pair', 'latent', 'tok'), may hold values from -0.0234375 to 0.0234375
- dec_bias: float32 [2, 3584], P('pair', 'tok'), may hold values from -3 to 3
Outputs:
- recon: bfloat16 [2, 512, 3584], P('pair', 'latent', 'tok')
- token_loss: float32 [512], P('latent')
- scaling: float32 [2, 65536], P('pair', ('latent', 'tok'))
All inputs are finite; a program needn't handle non-finite values.
Results may differ from a plain program's by a relative error of at most 0.017.
Values may be sent and summed in bfloat16 or wider, within the bound.
No kernel may reach another device: no remote copies, remote signals or barrier semaphores. Data moves between devices by JAX's collectives and lax.ppermute only.
A program may use at most 64 MiB of HBM per device.

v0:
```python
import jax
import jax.numpy as jnp
from jax import lax
from jax.sharding import PartitionSpec as P

D = 3584


smooth_width = 0.1
penalty = 0.0001
tiny_term = 1e-06


def body(activations, enc_weight, enc_bias, thresholds, dec_weight, dec_bias):
    gathered = lax.all_gather(activations[0], "tok", axis=0, tiled=True)
    partial_value = jnp.dot(gathered, enc_weight[0], preferred_element_type=jnp.float32)
    thresh_level = thresholds.astype(jnp.float32) * 0.25
    shifted = lax.psum(partial_value, "pair") + enc_bias
    local_feats = (shifted * jax.nn.sigmoid((shifted - thresh_level) / smooth_width)).astype(
        jnp.bfloat16
    )
    block_feats = lax.all_gather(local_feats, "tok", axis=1, tiled=True)
    tok_index = lax.axis_index("tok")
    lat_index = lax.axis_index("latent")
    dec_block = dec_weight[0]
    slice_width = dec_block.shape[1]
    own_count = enc_weight.shape[2]
    tokens_all = block_feats.shape[0]
    row_count = tokens_all // lax.axis_size("latent")
    act_slice = lax.dynamic_slice_in_dim(gathered, tok_index * slice_width, slice_width, 1)
    inner_prod = lax.dot_general(
        block_feats, act_slice, (((0,), (0,)), ((), ())), preferred_element_type=jnp.float32
    )
    dec_wide = dec_block.astype(jnp.float32)
    num_part = jnp.sum(inner_prod * dec_wide, axis=1)
    nsq_part = jnp.sum(dec_wide * dec_wide, axis=1)
    num_all, nsq_all = lax.psum((num_part, nsq_part), "tok")
    norm_vals = jnp.sqrt(nsq_all)
    own_cols = lax.dynamic_slice_in_dim(block_feats, tok_index * own_count, own_count, 1).astype(
        jnp.float32
    )
    mean_sq = jnp.mean(own_cols * own_cols, axis=0)
    num_own = lax.dynamic_slice_in_dim(num_all, tok_index * own_count, own_count, 0) / tokens_all
    nsq_own = lax.dynamic_slice_in_dim(nsq_all, tok_index * own_count, own_count, 0)
    scaling = num_own / (nsq_own * mean_sq + tiny_term)
    recon_part = lax.psum_scatter(
        jnp.dot(block_feats, dec_block, preferred_element_type=jnp.float32),
        "latent",
        scatter_dimension=0,
        tiled=True,
    )
    recon_vals = recon_part + dec_bias[0]
    act_own = lax.dynamic_slice_in_dim(act_slice, lat_index * row_count, row_count, 0).astype(
        jnp.float32
    )
    residue = act_own - recon_vals
    sq_error = jnp.sum(residue * residue, axis=1)
    sparse = jnp.sum(block_feats.astype(jnp.float32) * norm_vals, axis=1)
    sparse_term = penalty * sparse / lax.axis_size("tok")
    own_terms = lax.dynamic_slice_in_dim(
        sparse_term, lat_index * row_count, row_count, 0
    ) + sq_error / (2.0 * D)
    loss_terms = lax.dynamic_update_slice_in_dim(sparse_term, own_terms, lat_index * row_count, 0)
    summed = lax.psum(loss_terms, ("pair", "latent", "tok"))
    token_loss = lax.dynamic_slice_in_dim(summed, lat_index * row_count, row_count, 0)
    return (recon_vals.astype(jnp.bfloat16)[None], token_loss, scaling[None])


def solution(mesh):
    return jax.shard_map(
        body,
        mesh=mesh,
        in_specs=(
            P("pair", "tok", None),
            P("pair", None, ("latent", "tok")),
            P(("latent", "tok")),
            P(("latent", "tok")),
            P("pair", "latent", "tok"),
            P("pair", "tok"),
        ),
        out_specs=(P("pair", "latent", "tok"), P("latent"), P("pair", ("latent", "tok"))),
        check_vma=False,
    )
```

profile of v0, /device:TPU:1, one launch (start us, length us, event | category | flops | bytes accessed | tf_op | source)
XLA Modules:
  0.0 686.3 jit_solution(3793005959864992193)
XLA Ops:
  7.2 0.0 copy-start
  7.2 0.0 all-gather.6.cloned.1.call-start
  7.2 0.7 all-gather.6.cloned.1.call-update
  7.9 0.0 copy-start.3
  7.9 0.0 copy-start.2
  7.9 0.0 all-reduce.3.cloned.1.call-start
  8.0 168.3 %all-gather.6.cloned.1.call-done = bf16[1,512,3584]{2,1,0:T(8,128)(2,1)} async-done(((bf16[1,64,3584]{2,1,0:T(8,128)(2,1)}), bf16[1,512,3584]{2,1,0:T(8,128)(2,1)}) %all-gather.6.cloned.1.call-update) | async-done | bytes 3670032 | tf_op jit(solution)/shard_map/all_gather | solution.py:15
  176.3 0.0 copy-done
  176.3 3.9 fusion.2
  180.3 0.0 all-reduce.3.cloned.1.call-update
  180.3 0.0 all-gather.4.cloned.1.call-start
  180.3 0.0 copy-done.3
  180.4 35.7 %all-reduce.3.cloned.1.call-done = f32[512,256]{1,0:T(8,128)} async-done(((f32[512,256]{1,0:T(8,128)}), f32[512,256]{1,0:T(8,128)}) %all-reduce.3.cloned.1.call-update) | async-done | bytes 524304 | tf_op jit(solution)/shard_map/psum | solution.py:18
  216.1 1.9 multiply_convert_fusion
  218.0 0.0 all-gather.4.cloned.1.call-update
  218.0 0.0 reduce-scatter.2.cloned.1.call-start
  218.1 118.3 %all-gather.4.cloned.1.call-done = bf16[512,2048]{1,0:T(8,128)(2,1)} async-done(((bf16[512,256]{1,0:T(8,128)(2,1)}), bf16[512,2048]{1,0:T(8,128)(2,1)}) %all-gather.4.cloned.1.call-update) | async-done | bytes 2097168 | tf_op jit(solution)/shard_map/all_gather | solution.py:22
  336.4 4.4 fusion.4
  340.8 0.0 reduce-scatter.2.cloned.1.call-update
  340.8 1.9 fusion
  342.7 3.7 fusion.1
  346.4 0.0 copy-start.1
  346.4 58.9 %all-reduce = (f32[2048]{0:T(1024)S(1)}, f32[2048]{0:T(1024)S(1)}) all-reduce(f32[2048]{0:T(1024)S(1)} %fusion, f32[2048]{0:T(1024)S(1)} %fusion.1), channel_id=1, replica_groups=mesh['pair'=2,'latent'=32,'tok'=8] {'tok'}, use_global_device_ids=true, to_apply=%region_3.0 | all-reduce | flops 4096 | bytes 32768 | tf_op jit(solution)/shard_map/psum | solution.py:37
  405.2 1.0 multiply_reduce_fusion.1
  406.3 0.6 add_divide_fusion
  406.9 2.1 multiply_reduce_fusion
  409.0 144.2 %reduce-scatter.2.cloned.1.call-done = f32[16,448]{1,0:T(8,128)} async-done(((f32[512,448]{1,0:T(8,128)}), f32[16,448]{1,0:T(8,128)}) %reduce-scatter.2.cloned.1.call-update) | async-done | bytes 28688 | tf_op jit(solution)/shard_map/reduce_scatter | solution.py:46
  553.3 0.0 copy-done.1
  553.3 1.5 fusion.10
  554.8 0.2 add_dynamic-update-slice_fusion
  554.9 124.3 %psum.30 = f32[512]{0:T(512)S(1)} all-reduce(f32[512]{0:T(512)S(1)} %add_dynamic-update-slice_fusion), channel_id=1, replica_groups=mesh['pair'=2,'latent'=32,'tok'=8] {'pair','latent','tok'}, use_global_device_ids=true, to_apply=%region_6.0 | all-reduce | flops 512 | bytes 4096 | tf_op jit(solution)/shard_map/psum | solution.py:64
  679.2 0.6 dynamic_slice.23
  (4 shorter events, 0.0 us)
Async XLA Ops:
  7.2 169.2 %copy-start = (bf16[1,3584,256]{2,1,0:T(8,128)(2,1)S(1)}, bf16[1,3584,256]{2,1,0:T(8,128)(2,1)}, u32[]{:S(2)}) copy-start(bf16[1,3584,256]{2,1,0:T(8,128)(2,1)} %param.7) | copy-start | bytes 5505028
  7.2 169.1 %all-gather.6.cloned.1.call-start = ((), (), s32[]{:S(2)}) async-start(), calls=%async_computation.4 | async-start | bytes 4128768 | tf_op jit(solution)/shard_map/all_gather | solution.py:15
  7.9 172.4 %copy-start.3 = (s32[256]{0:T(256)S(1)}, s32[256]{0:T(256)}, u32[]{:S(2)}) copy-start(s32[256]{0:T(256)} %param.9) | copy-start | bytes 3076
  7.9 208.2 %copy-start.2 = (f32[256]{0:T(256)S(1)}, f32[256]{0:T(256)}, u32[]{:S(2)}) copy-start(f32[256]{0:T(256)} %param.8) | copy-start | bytes 3076
  7.9 208.2 %all-reduce.3.cloned.1.call-start = ((), (), s32[]{:S(2)}) async-start(), calls=%async_computation.1 | async-start | bytes 1048576 | tf_op jit(solution)/shard_map/psum | solution.py:18
  180.3 156.1 %all-gather.4.cloned.1.call-start = ((), (), s32[]{:S(2)}) async-start(), calls=%async_computation.2 | async-start | bytes 2359296 | tf_op jit(solution)/shard_map/all_gather | solution.py:22
  218.0 335.2 %reduce-scatter.2.cloned.1.call-start = ((), (), s32[]{:S(2)}) async-start(), calls=%async_computation.3 | async-start | bytes 1081344 | tf_op jit(solution)/shard_map/reduce_scatter | solution.py:46
  346.4 206.9 %copy-start.1 = (f32[1,448]{1,0:T(1,128)S(1)}, f32[1,448]{1,0:T(1,128)}, u32[]{:S(2)}) copy-start(f32[1,448]{1,0:T(1,128)} %param.11) | copy-start | bytes 5380
Sparse Core Ops, SparseCore 0:
  11.2 165.0 all-gather.5
  180.4 35.6 all-reduce.2
  219.6 116.7 all-gather.3
  340.9 212.3 reduce-scatter.1
where the time goes:
time: 687 us; the launch traced here: 686 us
  waiting for transfers between devices  467 us (68%)
  blocking collectives  183 us (27%)
  between operations  13.8 us (2%)
  matrix products  12 us (2%)
  other arithmetic  9.24 us (1%)
    all_gather x1, waiting for transfers between devices, body(): gathered = lax.all_gather(activations[0], 'tok', axis=0, tiled=True)  168 us
    reduce_scatter x1, waiting for transfers between devices, body(): lax.psum_scatter(jnp.dot(block_feats, dec_block, preferred_element_type=j...  144 us
    psum x1, blocking collectives, body(): summed = lax.psum(loss_terms, ('pair', 'latent', 'tok'))  124 us
    all_gather x1, waiting for transfers between devices, body(): block_feats = lax.all_gather(local_feats, 'tok', axis=1, tiled=True)  118 us
    psum x1, blocking collectives, body(): num_all, nsq_all = lax.psum((num_part, nsq_part), 'tok')  58.9 us
    psum x1, waiting for transfers between devices, body(): shifted = lax.psum(partial_value, 'pair') + enc_bias  35.7 us
  transfers between devices with their start and end apart: 4, of which 4 were waited for; matrix products, arithmetic and copies ran while one was open for 1% of the time, Pallas kernels for 0%

commit v1 on v0

v1 whole, which is shorter than its diff:
```python
import jax
import jax.numpy as jnp
from jax import lax
from jax.sharding import Mesh, PartitionSpec as P

D = 3584
smooth_width = 0.1
penalty = 0.0001
tiny_term = 1e-06
LAT = ("x", "zl")
TOK = ("y", "zh")
BF = jnp.bfloat16
F32 = jnp.float32


def shift(value, axis, step):
    size = lax.axis_size(axis)
    return lax.ppermute(value, axis, [(i, (i + step) % size) for i in range(size)])


def ring_blocks(block):
    half = block.shape[0] // 2
    prev = shift(block, "y", 1)
    succ = shift(block, "y", -1)
    far_top = shift(prev[:half], "y", 1)
    far_low = shift(succ[half:], "y", -1)
    return [block, prev, succ, jnp.concatenate([far_top, far_low], axis=0)]


def body(activations, enc_weight, enc_bias, thresholds, dec_weight, dec_bias):
    y_at = lax.axis_index("y")
    zh_at = lax.axis_index("zh")
    tok_at = y_at * 2 + zh_at
    lat_at = lax.axis_index(LAT)
    act = activations[0]
    enc = enc_weight[0]
    dec = dec_weight[0]
    count = act.shape[0]
    own = enc.shape[1]
    width = dec.shape[1]
    places = [y_at, (y_at + 3) % 4, (y_at + 1) % 4, (y_at + 2) % 4]

    other_act = shift(act, "zh", 1)
    near = jnp.concatenate(ring_blocks(act), axis=0)
    far = jnp.concatenate(ring_blocks(other_act), axis=0)

    dec_wide = dec.astype(F32)
    nsq_part = jnp.sum(dec_wide * dec_wide, axis=1)
    nsq_own = jnp.sum(
        lax.all_to_all(nsq_part.reshape(8, own), TOK, 0, 0, tiled=True), axis=0
    )
    norm_own = jnp.sqrt(nsq_own)

    pre_near = jnp.dot(near, enc, preferred_element_type=F32)
    pre_far = jnp.dot(far, enc, preferred_element_type=F32)

    def in_order(from_near, from_far):
        cols = from_near.shape[1]
        out = jnp.zeros((8 * count, cols), from_near.dtype)
        for part, half_at in ((from_near, zh_at), (from_far, 1 - zh_at)):
            for k, place in enumerate(places):
                out = lax.dynamic_update_slice(
                    out, part[k * count : (k + 1) * count], ((place * 2 + half_at) * count, 0)
                )
        return out

    partial_value = in_order(pre_near, pre_far)
    thresh_level = thresholds.astype(F32) * 0.25
    pre = partial_value + shift(partial_value, "pair", 1) + enc_bias
    feats = (pre * jax.nn.sigmoid((pre - thresh_level) / smooth_width)).astype(BF)
    feats_wide = feats.astype(F32)
    mean_sq = jnp.mean(feats_wide * feats_wide, axis=0)
    sparse_part = jnp.sum(feats_wide * norm_own, axis=1)

    act_slice = in_order(
        lax.dynamic_slice_in_dim(near, tok_at * width, width, 1),
        lax.dynamic_slice_in_dim(far, tok_at * width, width, 1),
    )

    other_feats = shift(feats, "zh", 1)
    blocks_near = ring_blocks(feats)
    blocks_far = ring_blocks(other_feats)
    block_feats = jnp.zeros((8 * count, 8 * own), BF)
    for blocks, half_at in ((blocks_near, zh_at), (blocks_far, 1 - zh_at)):
        for place, blk in zip(places, blocks):
            block_feats = lax.dynamic_update_slice(
                block_feats, blk, (0, (place * 2 + half_at) * own)
            )

    recon_part = jnp.dot(block_feats, dec, preferred_element_type=F32).astype(BF)
    sparse_hi = sparse_part.astype(BF)
    sparse_lo = (sparse_part - sparse_hi.astype(F32)).astype(BF)
    payload = jnp.concatenate(
        [
            recon_part,
            sparse_hi[:, None],
            sparse_lo[:, None],
            jnp.zeros((8 * count, 62), BF),
        ],
        axis=1,
    )
    arrived = lax.all_to_all(payload, LAT, 0, 0, tiled=True)

    inner_prod = lax.dot_general(
        act_slice, dec, (((1,), (1,)), ((), ())), preferred_element_type=F32
    )
    num_part = jnp.sum(inner_prod * block_feats.astype(F32), axis=0)

    row_count = 8 * count // lax.axis_size(LAT)
    total = jnp.sum(arrived.reshape(32, row_count, 512).astype(F32), axis=0)
    recon_vals = total[:, :width] + dec_bias[0]
    sparse = total[:, width] + total[:, width + 1]
    act_own = lax.dynamic_slice_in_dim(act_slice, lat_at * row_count, row_count, 0)
    residue = act_own.astype(F32) - recon_vals
    own_terms = jnp.sum(residue * residue, axis=1) / (2.0 * D) + penalty * sparse

    last = jnp.concatenate(
        [
            jnp.broadcast_to(num_part.reshape(1, 8, own), (2, 8, own)),
            jnp.broadcast_to(own_terms, (2, 8, row_count)),
        ],
        axis=2,
    ).reshape(16, own + row_count)
    got = lax.all_to_all(last, ("pair",) + TOK, 0, 0, tiled=True)
    token_loss = jnp.sum(got[:, own:], axis=0)
    mine = lax.dynamic_slice_in_dim(got, lax.axis_index("pair") * 8, 8, 0)[:, :own]
    num_own = jnp.sum(mine, axis=0) / (8 * count)
    scaling = num_own / (nsq_own * mean_sq + tiny_term)
    return (recon_vals.astype(BF)[None], token_loss, scaling[None])


def solution(mesh):
    fine = Mesh(mesh.devices.reshape(2, 4, 8, 4, 2), ("pair", "x", "zl", "y", "zh"))
    return jax.shard_map(
        body,
        mesh=fine,
        in_specs=(
            P("pair", TOK, None),
            P("pair", None, LAT + TOK),
            P(LAT + TOK),
            P(LAT + TOK),
            P("pair", LAT, TOK),
            P("pair", TOK),
        ),
        out_specs=(P("pair", LAT, TOK), P(LAT), P("pair", LAT + TOK)),
        check_vma=False,
    )
```

time: 687 us -> 247 us (0.36)
  waiting for transfers between devices: 467 us -> 60.4 us
  blocking collectives: 183 us -> 0 us
  starting transfers between devices: 0.16 us -> 149 us
  local copies, waits for them, and re-layouts: 0.61 us -> 20.6 us
  between operations: 13.8 us -> 1.28 us
    all_gather x2 -> x0, waiting for transfers between devices: 287 us -> none  [the longest x1 168 us: body(): gathered = lax.all_gather(activations[0], 'tok', axis=0, tiled=True)]
    psum x2 -> x0, blocking collectives: 183 us -> none  [the longest x1 124 us: body(): summed = lax.psum(loss_terms, ('pair', 'latent', 'tok'))]
    reduce_scatter x1 -> x0, waiting for transfers between devices: 144 us -> none  [body(): lax.psum_scatter(jnp.dot(block_feats, dec_block, preferred_element_type=j...]
    ppermute x0 -> x19, starting transfers between devices: none -> 77.8 us  [shift(): lax.ppermute(value, axis, [(i, (i + step) % size) for i in range(size)])]
    all_to_all x0 -> x3, starting transfers between devices: none -> 71.1 us  [the longest x1 48.7 us: body(): arrived = lax.all_to_all(payload, LAT, 0, 0, tiled=True)]
    all_to_all x0 -> x3, waiting for transfers between devices: none -> 45.4 us  [the longest x1 17.5 us: body(): arrived = lax.all_to_all(payload, LAT, 0, 0, tiled=True)]
    psum x1 -> x0, waiting for transfers between devices: 35.7 us -> none  [body(): shifted = lax.psum(partial_value, 'pair') + enc_bias]
    ppermute x0 -> x19, waiting for transfers between devices: none -> 15 us  [shift(): lax.ppermute(value, axis, [(i, (i + step) % size) for i in range(size)])]
  transfers between devices with their start and end apart: 4 -> 22, of which waited for: 4 -> 9; matrix products, arithmetic and copies ran while one was open for 1% -> 10% of each run, Pallas kernels for 0% -> 0%
where the time goes in v1:
time: 247 us; the launch traced here: 246 us
  starting transfers between devices  149 us (60%)
  waiting for transfers between devices  60.4 us (24%)
  local copies, waits for them, and re-layouts  20.6 us (8%)
  matrix products  8.92 us (4%)
  other arithmetic  6.01 us (2%)
    ppermute x19, starting transfers between devices, shift(): lax.ppermute(value, axis, [(i, (i + step) % size) for i in range(size)])  77.8 us
    all_to_all x1, starting transfers between devices, body(): arrived = lax.all_to_all(payload, LAT, 0, 0, tiled=True)  48.7 us
    all_to_all x1, waiting for transfers between devices, body(): arrived = lax.all_to_all(payload, LAT, 0, 0, tiled=True)  17.5 us
    all_to_all x1, starting transfers between devices, body(): lax.all_to_all(nsq_part.reshape(8, own), TOK, 0, 0, tiled=True)  15.4 us
    ppermute x19, waiting for transfers between devices, shift(): lax.ppermute(value, axis, [(i, (i + step) % size) for i in range(size)])  15 us
    all_to_all x1, waiting for transfers between devices, body(): got = lax.all_to_all(last, ('pair',) + TOK, 0, 0, tiled=True)  14.2 us
    all_to_all x1, waiting for transfers between devices, body(): lax.all_to_all(nsq_part.reshape(8, own), TOK, 0, 0, tiled=True)  13.6 us
    dynamic_update_slice x16, local copies, waits for them, and re-layouts, in_order(): lax.dynamic_update_slice(out, part[k * count:(k + 1) * count], ((place *...  8.04 us
  transfers between devices with their start and end apart: 22, of which 9 were waited for; matrix products, arithmetic and copies ran while one was open for 10% of the time, Pallas kernels for 0%

profile of v1, /device:TPU:1, one launch (start us, length us, event | category | flops | bytes accessed | tf_op | source)
XLA Modules:
  0.0 246.2 jit_solution(3442081144251816006)
XLA Ops:
  0.6 4.2 %collective-permute-start = (bf16[64,3584]{1,0:T(8,128)(2,1)}, bf16[64,3584]{1,0:T(8,128)(2,1)S(1)}, u32[]{:S(2)}, u32[]{:S(2)}) collective-permute-start(bf16[64,3584]{1,0:T(8,128)(2,1)} %bitcast.34), channel_id=1, source_target_pairs={{0,2},{2,4},{4,6},{6,0},{1,3},{3,5},{5,7},{7,1},{8,10},{10,12},{12... | collective-permute-start | bytes 1376264 | tf_op jit(solution)/shard_map/ppermute | solution.py:18
  4.8 3.4 %collective-permute-start.1 = (bf16[64,3584]{1,0:T(8,128)(2,1)}, bf16[64,3584]{1,0:T(8,128)(2,1)S(1)}, u32[]{:S(2)}, u32[]{:S(2)}) collective-permute-start(bf16[64,3584]{1,0:T(8,128)(2,1)} %bitcast.35), channel_id=1, source_target_pairs={{0,6},{2,0},{4,2},{6,4},{1,7},{3,1},{5,3},{7,5},{8,14},{10,8},{12,... | collective-permute-start | bytes 1376264 | tf_op jit(solution)/shard_map/ppermute | solution.py:18
  8.2 15.4 %collective-permute-start.4 = (bf16[64,3584]{1,0:T(8,128)(2,1)}, bf16[64,3584]{1,0:T(8,128)(2,1)S(1)}, u32[]{:S(2)}, u32[]{:S(2)}) collective-permute-start(bf16[64,3584]{1,0:T(8,128)(2,1)} %bitcast.36), channel_id=1, source_target_pairs={{0,1},{1,0},{2,3},{3,2},{4,5},{5,4},{6,7},{7,6},{8,9},{9,8},{10,11... | collective-permute-start | bytes 1376264 | tf_op jit(solution)/shard_map/ppermute | solution.py:18
  23.6 1.8 constant_dynamic-update-slice_fusion.4
  25.5 1.9 collective-permute-start.2
  27.4 4.6 %collective-permute-start.3 = (bf16[32,3584]{1,0:T(8,128)(2,1)S(1)}, bf16[32,3584]{1,0:T(8,128)(2,1)S(1)}, u32[]{:S(2)}, u32[]{:S(2)}) collective-permute-start(bf16[32,3584]{1,0:T(8,128)(2,1)S(1)} %slice.117), channel_id=1, source_target_pairs={{0,6},{2,0},{4,2},{6,4},{1,7},{3,1},{5,3},{7,5},{8,14},{10,8},{12,... | collective-permute-start | bytes 688136 | tf_op jit(solution)/shard_map/ppermute | solution.py:18
  32.0 4.8 %collective-permute-done.4 = bf16[64,3584]{1,0:T(8,128)(2,1)S(1)} collective-permute-done((bf16[64,3584]{1,0:T(8,128)(2,1)}, bf16[64,3584]{1,0:T(8,128)(2,1)S(1)}, u32[]{:S(2)}, u32[]{:S(2)}) %collective-permute-start.4) | collective-permute-done | bytes 458784 | tf_op jit(solution)/shard_map/ppermute | solution.py:18
  36.9 2.0 collective-permute-start.5
  38.9 4.5 %collective-permute-start.6 = (bf16[64,3584]{1,0:T(8,128)(2,1)S(1)}, bf16[64,3584]{1,0:T(8,128)(2,1)S(1)}, u32[]{:S(2)}, u32[]{:S(2)}) collective-permute-start(bf16[64,3584]{1,0:T(8,128)(2,1)S(1)} %collective-permute-done.4), channel_id=1, source_target_pairs={{0,6},{2,0},{4,2},{6,4},{1,7},{3,1},{5,3},{7,5},{8,14},{10,8},{12,... | collective-permute-start | bytes 1376264 | tf_op jit(solution)/shard_map/ppermute | solution.py:18
  46.5 2.1 fusion.6
  49.0 1.9 collective-permute-start.7
  51.0 4.6 %collective-permute-start.8 = (bf16[32,3584]{1,0:T(8,128)(2,1)S(1)}, bf16[32,3584]{1,0:T(8,128)(2,1)S(1)}, u32[]{:S(2)}, u32[]{:S(2)}) collective-permute-start(bf16[32,3584]{1,0:T(8,128)(2,1)S(1)} %slice.123), channel_id=1, source_target_pairs={{0,6},{2,0},{4,2},{6,4},{1,7},{3,1},{5,3},{7,5},{8,14},{10,8},{12,... | collective-permute-start | bytes 688136 | tf_op jit(solution)/shard_map/ppermute | solution.py:18
  57.0 1.5 collective-permute-done.8
  59.8 6.9 %collective-permute-start.9 = (f32[512,256]{1,0:T(8,128)S(1)}, f32[512,256]{1,0:T(8,128)S(1)}, u32[]{:S(2)}, u32[]{:S(2)}) collective-permute-start(f32[512,256]{1,0:T(8,128)S(1)} %slice_dynamic-update-slice_fusion), channel_id=1, source_target_pairs={{0,256},{256,0},{1,257},{257,1},{2,258},{258,2},{3,259},{259,3},{4... | collective-permute-start | bytes 1572872 | tf_op jit(solution)/shard_map/ppermute | solution.py:18
  67.8 15.4 %all-to-all-start = ((f32[8,1,256]{2,1,0:T(1,128)}), f32[8,1,256]{2,1,0:T(1,128)S(1)}, u32[]{:S(2)}, u32[]{:S(2)}) async-start(f32[8,1,256]{2,1,0:T(1,128)} %bitcast.4), calls=%async_computation | async-start | bytes 16384 | tf_op jit(solution)/shard_map/all_to_all | solution.py:50
  83.3 13.6 %all-to-all-done = f32[8,1,256]{2,1,0:T(1,128)S(1)} async-done(((f32[8,1,256]{2,1,0:T(1,128)}), f32[8,1,256]{2,1,0:T(1,128)S(1)}, u32[]{:S(2)}, u32[]{:S(2)}) %all-to-all-start) | async-done | bytes 8224 | tf_op jit(solution)/shard_map/all_to_all | solution.py:50
  98.7 2.2 collective-permute-start.10
  100.9 4.3 %collective-permute-start.11 = (bf16[512,256]{1,0:T(8,128)(2,1)S(1)}, bf16[512,256]{1,0:T(8,128)(2,1)S(1)}, u32[]{:S(2)}, u32[]{:S(2)}) collective-permute-start(bf16[512,256]{1,0:T(8,128)(2,1)S(1)} %get-tuple-element.6), channel_id=1, source_target_pairs={{0,6},{2,0},{4,2},{6,4},{1,7},{3,1},{5,3},{7,5},{8,14},{10,8},{12,... | collective-permute-start | bytes 786440 | tf_op jit(solution)/shard_map/ppermute | solution.py:18
  105.2 2.5 %collective-permute-start.14 = (bf16[512,256]{1,0:T(8,128)(2,1)S(1)}, bf16[512,256]{1,0:T(8,128)(2,1)S(1)}, u32[]{:S(2)}, u32[]{:S(2)}) collective-permute-start(bf16[512,256]{1,0:T(8,128)(2,1)S(1)} %get-tuple-element.6), channel_id=1, source_target_pairs={{0,1},{1,0},{2,3},{3,2},{4,5},{5,4},{6,7},{7,6},{8,9},{9,8},{10,11... | collective-permute-start | bytes 786440 | tf_op jit(solution)/shard_map/ppermute | solution.py:18
  108.5 1.9 collective-permute-start.12
  110.5 4.6 %collective-permute-start.13 = (bf16[256,256]{1,0:T(8,128)(2,1)S(1)}, bf16[256,256]{1,0:T(8,128)(2,1)S(1)}, u32[]{:S(2)}, u32[]{:S(2)}) collective-permute-start(bf16[256,256]{1,0:T(8,128)(2,1)S(1)} %slice.129), channel_id=1, source_target_pairs={{0,6},{2,0},{4,2},{6,4},{1,7},{3,1},{5,3},{7,5},{8,14},{10,8},{12,... | collective-permute-start | bytes 393224 | tf_op jit(solution)/shard_map/ppermute | solution.py:18
  115.1 6.6 %collective-permute-done.14 = bf16[512,256]{1,0:T(8,128)(2,1)S(1)} collective-permute-done((bf16[512,256]{1,0:T(8,128)(2,1)S(1)}, bf16[512,256]{1,0:T(8,128)(2,1)S(1)}, u32[]{:S(2)}, u32[]{:S(2)}) %collective-permute-start.14) | collective-permute-done | bytes 262176 | tf_op jit(solution)/shard_map/ppermute | solution.py:18
  121.6 1.9 collective-permute-start.15
  123.6 4.6 %collective-permute-start.16 = (bf16[512,256]{1,0:T(8,128)(2,1)S(1)}, bf16[512,256]{1,0:T(8,128)(2,1)S(1)}, u32[]{:S(2)}, u32[]{:S(2)}) collective-permute-start(bf16[512,256]{1,0:T(8,128)(2,1)S(1)} %collective-permute-done.14), channel_id=1, source_target_pairs={{0,6},{2,0},{4,2},{6,4},{1,7},{3,1},{5,3},{7,5},{8,14},{10,8},{12,... | collective-permute-start | bytes 786440 | tf_op jit(solution)/shard_map/ppermute | solution.py:18
  131.2 1.9 collective-permute-start.17
  133.1 4.6 %collective-permute-start.18 = (bf16[256,256]{1,0:T(8,128)(2,1)S(1)}, bf16[256,256]{1,0:T(8,128)(2,1)S(1)}, u32[]{:S(2)}, u32[]{:S(2)}) collective-permute-start(bf16[256,256]{1,0:T(8,128)(2,1)S(1)} %slice.131), channel_id=1, source_target_pairs={{0,6},{2,0},{4,2},{6,4},{1,7},{3,1},{5,3},{7,5},{8,14},{10,8},{12,... | collective-permute-start | bytes 393224 | tf_op jit(solution)/shard_map/ppermute | solution.py:18
  140.4 2.7 %fusion.10 = bf16[512,448]{0,1:T(8,128)(2,1)S(1)} fusion(bf16[512,2048]{1,0:T(8,128)(2,1)} %maximum_dynamic-update-slice_fusion.1, bf16[1,2048,448]{1,2,0:T(8,128)(2,1)S(1)} %copy-done.4), kind=kOutput, calls=%fused_computation.10 | convolution fusion | flops 939753472 | bytes 4390912 | tf_op jit(solution)/shard_map/dot_general | solution.py:90
  144.3 48.7 %all-to-all-start.1 = ((bf16[32,16,512]{2,1,0:T(8,128)(2,1)}), bf16[32,16,512]{2,1,0:T(8,128)(2,1)S(1)}, u32[]{:S(2)}, u32[]{:S(2)}) async-start(bf16[32,16,512]{2,1,0:T(8,128)(2,1)} %maximum_maximum_fusion), calls=%async_computation.1 | async-start | bytes 1048576 | tf_op jit(solution)/shard_map/all_to_all | solution.py:102
  201.1 3.4 %multiply_reduce_fusion = f32[2048]{0:T(1024)S(1)} fusion(bf16[512,2048]{1,0:T(8,128)(2,1)} %maximum_dynamic-update-slice_fusion.1, bf16[512,448]{1,0:T(8,128)(2,1)S(1)} %dynamic-slice_dynamic-update-slice_fusion, bf16[1,2048,448]{1,2,0:T(8,128)(2,1)} %param.10), kind=kOutput, calls=%fused_computation | convolution fusion | flops 942667776 | bytes 4399104 | tf_op jit(solution)/shard_map/dot_general | solution.py:104
  204.5 17.5 %all-to-all-done.1 = bf16[32,16,512]{2,1,0:T(8,128)(2,1)S(1)} async-done(((bf16[32,16,512]{2,1,0:T(8,128)(2,1)}), bf16[32,16,512]{2,1,0:T(8,128)(2,1)S(1)}, u32[]{:S(2)}, u32[]{:S(2)}) %all-to-all-start.1) | async-done | bytes 524320 | tf_op jit(solution)/shard_map/all_to_all | solution.py:102
  223.8 7.0 %all-to-all-start.2 = ((f32[16,1,272]{2,1,0:T(1,128)}), f32[16,1,272]{2,1,0:T(1,128)S(1)}, u32[]{:S(2)}, u32[]{:S(2)}) async-start(f32[16,1,272]{2,1,0:T(1,128)} %all_to_all.21), calls=%async_computation.2 | async-start | bytes 49152 | tf_op jit(solution)/shard_map/all_to_all | solution.py:124
  230.8 14.2 %all-to-all-done.2 = f32[16,1,272]{2,1,0:T(1,128)S(1)} async-done(((f32[16,1,272]{2,1,0:T(1,128)}), f32[16,1,272]{2,1,0:T(1,128)S(1)}, u32[]{:S(2)}, u32[]{:S(2)}) %all-to-all-start.2) | async-done | bytes 17440 | tf_op jit(solution)/shard_map/all_to_all | solution.py:124
  (106 shorter events, 27.5 us)
Async XLA Ops:
  0.6 45.8 %copy-start = (bf16[1,3584,256]{2,1,0:T(8,128)(2,1)S(1)}, bf16[1,3584,256]{2,1,0:T(8,128)(2,1)}, u32[]{:S(2)}) copy-start(bf16[1,3584,256]{2,1,0:T(8,128)(2,1)} %param.7) | copy-start | bytes 5505028
  0.6 24.8 %collective-permute-start = (bf16[64,3584]{1,0:T(8,128)(2,1)}, bf16[64,3584]{1,0:T(8,128)(2,1)S(1)}, u32[]{:S(2)}, u32[]{:S(2)}) collective-permute-start(bf16[64,3584]{1,0:T(8,128)(2,1)} %bitcast.34), channel_id=1, source_target_pairs={{0,2},{2,4},{4,6},{6,0},{1,3},{3,5},{5,7},{7,1},{8,10},{10,12},{12... | collective-permute-start | bytes 1376264 | tf_op jit(solution)/shard_map/ppermute | solution.py:18
  4.8 22.6 %collective-permute-start.1 = (bf16[64,3584]{1,0:T(8,128)(2,1)}, bf16[64,3584]{1,0:T(8,128)(2,1)S(1)}, u32[]{:S(2)}, u32[]{:S(2)}) collective-permute-start(bf16[64,3584]{1,0:T(8,128)(2,1)} %bitcast.35), channel_id=1, source_target_pairs={{0,6},{2,0},{4,2},{6,4},{1,7},{3,1},{5,3},{7,5},{8,14},{10,8},{12,... | collective-permute-start | bytes 1376264 | tf_op jit(solution)/shard_map/ppermute | solution.py:18
  8.2 28.7 %collective-permute-start.4 = (bf16[64,3584]{1,0:T(8,128)(2,1)}, bf16[64,3584]{1,0:T(8,128)(2,1)S(1)}, u32[]{:S(2)}, u32[]{:S(2)}) collective-permute-start(bf16[64,3584]{1,0:T(8,128)(2,1)} %bitcast.36), channel_id=1, source_target_pairs={{0,1},{1,0},{2,3},{3,2},{4,5},{5,4},{6,7},{7,6},{8,9},{9,8},{10,11... | collective-permute-start | bytes 1376264 | tf_op jit(solution)/shard_map/ppermute | solution.py:18
  25.5 19.5 %collective-permute-start.2 = (bf16[32,3584]{1,0:T(8,128)(2,1)S(1)}, bf16[32,3584]{1,0:T(8,128)(2,1)S(1)}, u32[]{:S(2)}, u32[]{:S(2)}) collective-permute-start(bf16[32,3584]{1,0:T(8,128)(2,1)S(1)} %slice.116), channel_id=1, source_target_pairs={{0,2},{2,4},{4,6},{6,0},{1,3},{3,5},{5,7},{7,1},{8,10},{10,12},{12... | collective-permute-start | bytes 688136 | tf_op jit(solution)/shard_map/ppermute | solution.py:18
  27.4 18.3 %collective-permute-start.3 = (bf16[32,3584]{1,0:T(8,128)(2,1)S(1)}, bf16[32,3584]{1,0:T(8,128)(2,1)S(1)}, u32[]{:S(2)}, u32[]{:S(2)}) collective-permute-start(bf16[32,3584]{1,0:T(8,128)(2,1)S(1)} %slice.117), channel_id=1, source_target_pairs={{0,6},{2,0},{4,2},{6,4},{1,7},{3,1},{5,3},{7,5},{8,14},{10,8},{12,... | collective-permute-start | bytes 688136 | tf_op jit(solution)/shard_map/ppermute | solution.py:18
  36.9 12.1 %collective-permute-start.5 = (bf16[64,3584]{1,0:T(8,128)(2,1)S(1)}, bf16[64,3584]{1,0:T(8,128)(2,1)S(1)}, u32[]{:S(2)}, u32[]{:S(2)}) collective-permute-start(bf16[64,3584]{1,0:T(8,128)(2,1)S(1)} %collective-permute-done.4), channel_id=1, source_target_pairs={{0,2},{2,4},{4,6},{6,0},{1,3},{3,5},{5,7},{7,1},{8,10},{10,12},{12... | collective-permute-start | bytes 1376264 | tf_op jit(solution)/shard_map/ppermute | solution.py:18
  38.9 12.0 %collective-permute-start.6 = (bf16[64,3584]{1,0:T(8,128)(2,1)S(1)}, bf16[64,3584]{1,0:T(8,128)(2,1)S(1)}, u32[]{:S(2)}, u32[]{:S(2)}) collective-permute-start(bf16[64,3584]{1,0:T(8,128)(2,1)S(1)} %collective-permute-done.4), channel_id=1, source_target_pairs={{0,6},{2,0},{4,2},{6,4},{1,7},{3,1},{5,3},{7,5},{8,14},{10,8},{12,... | collective-permute-start | bytes 1376264 | tf_op jit(solution)/shard_map/ppermute | solution.py:18
  49.0 8.0 %collective-permute-start.7 = (bf16[32,3584]{1,0:T(8,128)(2,1)S(1)}, bf16[32,3584]{1,0:T(8,128)(2,1)S(1)}, u32[]{:S(2)}, u32[]{:S(2)}) collective-permute-start(bf16[32,3584]{1,0:T(8,128)(2,1)S(1)} %slice.122), channel_id=1, source_target_pairs={{0,2},{2,4},{4,6},{6,0},{1,3},{3,5},{5,7},{7,1},{8,10},{10,12},{12... | collective-permute-start | bytes 688136 | tf_op jit(solution)/shard_map/ppermute | solution.py:18
  51.0 7.5 %collective-permute-start.8 = (bf16[32,3584]{1,0:T(8,128)(2,1)S(1)}, bf16[32,3584]{1,0:T(8,128)(2,1)S(1)}, u32[]{:S(2)}, u32[]{:S(2)}) collective-permute-start(bf16[32,3584]{1,0:T(8,128)(2,1)S(1)} %slice.123), channel_id=1, source_target_pairs={{0,6},{2,0},{4,2},{6,4},{1,7},{3,1},{5,3},{7,5},{8,14},{10,8},{12,... | collective-permute-start | bytes 688136 | tf_op jit(solution)/shard_map/ppermute | solution.py:18
  58.5 1.2 copy-start.1
  58.5 8.2 %copy-start.3 = (bf16[1,2048,448]{1,2,0:T(8,128)(2,1)S(1)}, bf16[1,2048,448]{1,2,0:T(8,128)(2,1)}, u32[]{:S(2)}) copy-start(bf16[1,2048,448]{1,2,0:T(8,128)(2,1)} %param.10) | copy-start | bytes 5505028
  59.8 23.4 %copy-start.6 = (s32[256]{0:T(256)S(1)}, s32[256]{0:T(256)}, u32[]{:S(2)}) copy-start(s32[256]{0:T(256)} %param.9) | copy-start | bytes 3076
  59.8 37.4 %copy-start.7 = (f32[256]{0:T(256)S(1)}, f32[256]{0:T(256)}, u32[]{:S(2)}) copy-start(f32[256]{0:T(256)} %param.8) | copy-start | bytes 3076
  59.8 37.1 %collective-permute-start.9 = (f32[512,256]{1,0:T(8,128)S(1)}, f32[512,256]{1,0:T(8,128)S(1)}, u32[]{:S(2)}, u32[]{:S(2)}) collective-permute-start(f32[512,256]{1,0:T(8,128)S(1)} %slice_dynamic-update-slice_fusion), channel_id=1, source_target_pairs={{0,256},{256,0},{1,257},{257,1},{2,258},{258,2},{3,259},{259,3},{4... | collective-permute-start | bytes 1572872 | tf_op jit(solution)/shard_map/ppermute | solution.py:18
  67.8 29.1 %all-to-all-start = ((f32[8,1,256]{2,1,0:T(1,128)}), f32[8,1,256]{2,1,0:T(1,128)S(1)}, u32[]{:S(2)}, u32[]{:S(2)}) async-start(f32[8,1,256]{2,1,0:T(1,128)} %bitcast.4), calls=%async_computation | async-start | bytes 16384 | tf_op jit(solution)/shard_map/all_to_all | solution.py:50
  97.4 1.3 copy-start.2
  98.7 9.8 %collective-permute-start.10 = (bf16[512,256]{1,0:T(8,128)(2,1)S(1)}, bf16[512,256]{1,0:T(8,128)(2,1)S(1)}, u32[]{:S(2)}, u32[]{:S(2)}) collective-permute-start(bf16[512,256]{1,0:T(8,128)(2,1)S(1)} %get-tuple-element.6), channel_id=1, source_target_pairs={{0,2},{2,4},{4,6},{6,0},{1,3},{3,5},{5,7},{7,1},{8,10},{10,12},{12... | collective-permute-start | bytes 786440 | tf_op jit(solution)/shard_map/ppermute | solution.py:18
  100.9 9.5 %collective-permute-start.11 = (bf16[512,256]{1,0:T(8,128)(2,1)S(1)}, bf16[512,256]{1,0:T(8,128)(2,1)S(1)}, u32[]{:S(2)}, u32[]{:S(2)}) collective-permute-start(bf16[512,256]{1,0:T(8,128)(2,1)S(1)} %get-tuple-element.6), channel_id=1, source_target_pairs={{0,6},{2,0},{4,2},{6,4},{1,7},{3,1},{5,3},{7,5},{8,14},{10,8},{12,... | collective-permute-start | bytes 786440 | tf_op jit(solution)/shard_map/ppermute | solution.py:18
  105.2 16.4 %collective-permute-start.14 = (bf16[512,256]{1,0:T(8,128)(2,1)S(1)}, bf16[512,256]{1,0:T(8,128)(2,1)S(1)}, u32[]{:S(2)}, u32[]{:S(2)}) collective-permute-start(bf16[512,256]{1,0:T(8,128)(2,1)S(1)} %get-tuple-element.6), channel_id=1, source_target_pairs={{0,1},{1,0},{2,3},{3,2},{4,5},{5,4},{6,7},{7,6},{8,9},{9,8},{10,11... | collective-permute-start | bytes 786440 | tf_op jit(solution)/shard_map/ppermute | solution.py:18
  108.5 21.1 %collective-permute-start.12 = (bf16[256,256]{1,0:T(8,128)(2,1)S(1)}, bf16[256,256]{1,0:T(8,128)(2,1)S(1)}, u32[]{:S(2)}, u32[]{:S(2)}) collective-permute-start(bf16[256,256]{1,0:T(8,128)(2,1)S(1)} %slice.128), channel_id=1, source_target_pairs={{0,2},{2,4},{4,6},{6,0},{1,3},{3,5},{5,7},{7,1},{8,10},{10,12},{12... | collective-permute-start | bytes 393224 | tf_op jit(solution)/shard_map/ppermute | solution.py:18
  110.5 19.1 %collective-permute-start.13 = (bf16[256,256]{1,0:T(8,128)(2,1)S(1)}, bf16[256,256]{1,0:T(8,128)(2,1)S(1)}, u32[]{:S(2)}, u32[]{:S(2)}) collective-permute-start(bf16[256,256]{1,0:T(8,128)(2,1)S(1)} %slice.129), channel_id=1, source_target_pairs={{0,6},{2,0},{4,2},{6,4},{1,7},{3,1},{5,3},{7,5},{8,14},{10,8},{12,... | collective-permute-start | bytes 393224 | tf_op jit(solution)/shard_map/ppermute | solution.py:18
  121.6 9.5 %collective-permute-start.15 = (bf16[512,256]{1,0:T(8,128)(2,1)S(1)}, bf16[512,256]{1,0:T(8,128)(2,1)S(1)}, u32[]{:S(2)}, u32[]{:S(2)}) collective-permute-start(bf16[512,256]{1,0:T(8,128)(2,1)S(1)} %collective-permute-done.14), channel_id=1, source_target_pairs={{0,2},{2,4},{4,6},{6,0},{1,3},{3,5},{5,7},{7,1},{8,10},{10,12},{12... | collective-permute-start | bytes 786440 | tf_op jit(solution)/shard_map/ppermute | solution.py:18
  123.6 9.5 %collective-permute-start.16 = (bf16[512,256]{1,0:T(8,128)(2,1)S(1)}, bf16[512,256]{1,0:T(8,128)(2,1)S(1)}, u32[]{:S(2)}, u32[]{:S(2)}) collective-permute-start(bf16[512,256]{1,0:T(8,128)(2,1)S(1)} %collective-permute-done.14), channel_id=1, source_target_pairs={{0,6},{2,0},{4,2},{6,4},{1,7},{3,1},{5,3},{7,5},{8,14},{10,8},{12,... | collective-permute-start | bytes 786440 | tf_op jit(solution)/shard_map/ppermute | solution.py:18
  128.9 11.5 %copy-start.4 = (bf16[1,2048,448]{1,2,0:T(8,128)(2,1)S(1)}, bf16[1,2048,448]{1,2,0:T(8,128)(2,1)}, u32[]{:S(2)}) copy-start(bf16[1,2048,448]{1,2,0:T(8,128)(2,1)} %param.10) | copy-start | bytes 5505028
  131.2 8.1 %collective-permute-start.17 = (bf16[256,256]{1,0:T(8,128)(2,1)S(1)}, bf16[256,256]{1,0:T(8,128)(2,1)S(1)}, u32[]{:S(2)}, u32[]{:S(2)}) collective-permute-start(bf16[256,256]{1,0:T(8,128)(2,1)S(1)} %slice.130), channel_id=1, source_target_pairs={{0,2},{2,4},{4,6},{6,0},{1,3},{3,5},{5,7},{7,1},{8,10},{10,12},{12... | collective-permute-start | bytes 393224 | tf_op jit(solution)/shard_map/ppermute | solution.py:18
  133.1 6.5 %collective-permute-start.18 = (bf16[256,256]{1,0:T(8,128)(2,1)S(1)}, bf16[256,256]{1,0:T(8,128)(2,1)S(1)}, u32[]{:S(2)}, u32[]{:S(2)}) collective-permute-start(bf16[256,256]{1,0:T(8,128)(2,1)S(1)} %slice.131), channel_id=1, source_target_pairs={{0,6},{2,0},{4,2},{6,4},{1,7},{3,1},{5,3},{7,5},{8,14},{10,8},{12,... | collective-permute-start | bytes 393224 | tf_op jit(solution)/shard_map/ppermute | solution.py:18
  144.3 77.8 %all-to-all-start.1 = ((bf16[32,16,512]{2,1,0:T(8,128)(2,1)}), bf16[32,16,512]{2,1,0:T(8,128)(2,1)S(1)}, u32[]{:S(2)}, u32[]{:S(2)}) async-start(bf16[32,16,512]{2,1,0:T(8,128)(2,1)} %maximum_maximum_fusion), calls=%async_computation.1 | async-start | bytes 1048576 | tf_op jit(solution)/shard_map/all_to_all | solution.py:102
  201.1 21.3 %copy-start.5 = (f32[1,448]{1,0:T(1,128)S(1)}, f32[1,448]{1,0:T(1,128)}, u32[]{:S(2)}) copy-start(f32[1,448]{1,0:T(1,128)} %param.11) | copy-start | bytes 5380
  223.8 21.2 %all-to-all-start.2 = ((f32[16,1,272]{2,1,0:T(1,128)}), f32[16,1,272]{2,1,0:T(1,128)S(1)}, u32[]{:S(2)}, u32[]{:S(2)}) async-start(f32[16,1,272]{2,1,0:T(1,128)} %all_to_all.21), calls=%async_computation.2 | async-start | bytes 49152 | tf_op jit(solution)/shard_map/all_to_all | solution.py:124

commit v2 on v1

v2 whole, which is shorter than its diff:
```python
import jax
import jax.numpy as jnp
from jax import lax
from jax.experimental import pallas as pl
from jax.experimental.pallas import tpu as pltpu
from jax.sharding import Mesh, PartitionSpec as P

D = 3584
smooth_width = 0.1
penalty = 0.0001
tiny_term = 1e-06
LAT = ("x", "zl")
TOK = ("y", "zh")
BF = jnp.bfloat16
F32 = jnp.float32
VMEM = pl.BlockSpec(memory_space=pltpu.VMEM)
SMEM = pl.BlockSpec(memory_space=pltpu.SMEM)
NT = (((1,), (1,)), ((), ()))


def swap(value, axis):
    return lax.ppermute(value, axis, [(0, 1), (1, 0)])


def gather(value, axes):
    size = lax.axis_size(axes)
    copies = jnp.broadcast_to(value[None], (size,) + value.shape)
    return lax.all_to_all(copies, axes, 0, 0, tiled=False)


def encode(at_ref, a_ref, enc_ref, keep_ref, send_ref, cols_ref, v_ref):
    pair_at, tok_at = at_ref[0], at_ref[2]
    v_ref[...] = jnp.dot(a_ref[...], enc_ref[...], preferred_element_type=F32)
    keep_ref[...] = v_ref[pl.ds(pl.multiple_of(pair_at * 128, 128), 128), :]
    send_ref[...] = v_ref[pl.ds(pl.multiple_of((1 - pair_at) * 128, 128), 128), :]
    base = (tok_at // 2) * 896 + (tok_at % 2) * 384
    window = a_ref[:, pl.ds(pl.multiple_of(base, 128), 512)]
    cols_ref[...] = jnp.where(tok_at % 2 == 1, window[:, 64:512], window[:, 0:448])


def near_kernel(at_ref, b0, b1, b2, b3, enc_ref, keep_ref, send_ref, cols_ref, a_ref, v_ref):
    y_at = at_ref[3]
    for ref, step in ((b0, 0), (b1, 3), (b2, 1), (b3, 2)):
        row = pl.multiple_of(((y_at + step) % 4) * 64, 64)
        a_ref[pl.ds(row, 64), :] = ref[...]
    encode(at_ref, a_ref, enc_ref, keep_ref, send_ref, cols_ref, v_ref)


def far_kernel(at_ref, a_ref, enc_ref, keep_ref, send_ref, cols_ref, v_ref):
    encode(at_ref, a_ref, enc_ref, keep_ref, send_ref, cols_ref, v_ref)


def decode_kernel(
    at_ref, g1, g2, p1, p2, dec_ref, out_ref, f_ref, nsq_ref, wide_ref, norm_ref
):
    pair_at, zh_at = at_ref[0], at_ref[1]

    nsq = jnp.zeros((8, 256), F32)
    for y in range(4):
        rows = g1[y, 384:400, :].astype(F32)
        nsq = nsq + (rows[0:8] + rows[8:16])
    nsq_ref[...] = nsq
    norm = jnp.sqrt(nsq) * 0.125
    high = norm.astype(BF).astype(F32)
    wide_ref[...] = jnp.zeros_like(wide_ref)
    for k in range(8):
        wide_ref[0:1, k * 256 : (k + 1) * 256] = high[k : k + 1]
        wide_ref[1:2, k * 256 : (k + 1) * 256] = (norm - high)[k : k + 1]
    norm_ref[...] = wide_ref[...].astype(BF)

    def place(half, own, oth):
        near = pl.multiple_of(half * 256 + zh_at * 128, 128)
        far = pl.multiple_of(half * 256 + (1 - zh_at) * 128, 128)
        for y in range(4):
            mine = pl.multiple_of((2 * y + zh_at) * 256, 256)
            theirs = pl.multiple_of((2 * y + 1 - zh_at) * 256, 256)
            f_ref[pl.ds(near, 128), pl.ds(mine, 256)] = own[y, 0:128, :]
            f_ref[pl.ds(far, 128), pl.ds(theirs, 256)] = own[y, 128:256, :]
            f_ref[pl.ds(far, 128), pl.ds(mine, 256)] = own[y, 256:384, :]
            f_ref[pl.ds(near, 128), pl.ds(theirs, 256)] = oth[y]

    place(pair_at, g1, g2)
    place(1 - pair_at, p1, p2)
    for half in range(2):
        feats = f_ref[half * 256 : (half + 1) * 256, :]
        value = lax.dot_general(feats, dec_ref[...], NT, preferred_element_type=F32)
        sparse = lax.dot_general(feats, norm_ref[...], NT, preferred_element_type=F32)
        value, sparse = value.astype(BF), sparse.astype(BF)
        for zh in range(2):
            for yy in range(2):
                src = (zh * 2 + yy) * 64
                dst = ((half * 2 + yy) * 2 + zh) * 64
                out_ref[dst : dst + 64, 0:448] = value[src : src + 64, :]
                out_ref[dst : dst + 64, 448:512] = sparse[src : src + 64, :]


def numer_kernel(at_ref, f_ref, near_ref, far_ref, dec_ref, num_ref, msq_ref, a_ref):
    zh_at, tok_at = at_ref[1], at_ref[2]
    for half in range(2):
        near = pl.multiple_of(half * 256 + zh_at * 128, 128)
        far = pl.multiple_of(half * 256 + (1 - zh_at) * 128, 128)
        a_ref[pl.ds(near, 128), :] = near_ref[half * 128 : (half + 1) * 128, :]
        a_ref[pl.ds(far, 128), :] = far_ref[half * 128 : (half + 1) * 128, :]
    for k in range(8):
        cols = slice(k * 256, (k + 1) * 256)
        inner = jnp.dot(a_ref[...], dec_ref[:, cols], preferred_element_type=F32)
        num_ref[k : k + 1, :] = jnp.sum(
            inner * f_ref[:, cols].astype(F32), axis=0, keepdims=True
        )
    own = f_ref[:, pl.ds(pl.multiple_of(tok_at * 256, 256), 256)].astype(F32)
    msq_ref[...] = jnp.sum(own * own, axis=0, keepdims=True)


def call(kernel, name, flops, outs, count, scratch):
    return pl.pallas_call(
        kernel,
        out_shape=tuple(jax.ShapeDtypeStruct(shape, kind) for shape, kind in outs),
        in_specs=[SMEM] + [VMEM] * count,
        out_specs=(VMEM,) * len(outs),
        scratch_shapes=[pltpu.VMEM(shape, kind) for shape, kind in scratch],
        compiler_params=pltpu.CompilerParams(vmem_limit_bytes=40 << 20),
        cost_estimate=pl.CostEstimate(
            flops=flops, bytes_accessed=6 << 20, transcendentals=0
        ),
        name=name,
    )


def body(activations, enc_weight, enc_bias, thresholds, dec_weight, dec_bias):
    pair_at = lax.axis_index("pair")
    x_at = lax.axis_index("x")
    zh_at = lax.axis_index("zh")
    tok_at = lax.axis_index(TOK)
    lat_at = lax.axis_index(LAT)
    act = activations[0]
    enc = enc_weight[0]
    dec = dec_weight[0]
    dec_t = dec.T
    own, width = enc.shape[1], dec.shape[1]
    tokens = 8 * act.shape[0]
    rows = tokens // lax.axis_size(LAT)
    at = jnp.stack([pair_at, zh_at, tok_at, lax.axis_index("y")]).astype(jnp.int32)

    quarter = swap(lax.dynamic_slice_in_dim(act, x_at * 16, 16, 0), "zh")
    blocks = [act] + [
        lax.ppermute(act, "y", [(i, (i + k) % 4) for i in range(4)]) for k in (1, 3, 2)
    ]
    quarter, blocks[1], blocks[2] = lax.optimization_barrier((quarter, blocks[1], blocks[2]))
    far = gather(quarter, ("y", "x")).reshape(256, D)

    dec_wide = dec.astype(F32)
    nsq_part = jnp.sum(dec_wide * dec_wide, axis=1).reshape(8, own)

    def split(value):
        high = value.astype(BF)
        return [high, (value - high.astype(F32)).astype(BF)]

    thresh_level = thresholds.astype(F32) * 0.25

    def features(keep, send):
        pre = keep + swap(send, "pair") + enc_bias
        return (pre * jax.nn.sigmoid((pre - thresh_level) / smooth_width)).astype(BF)

    enc_outs = [((128, own), F32), ((128, own), F32), ((256, width), BF)]
    enc_flops = 2 * 256 * D * own
    half_value = ((256, own), F32)
    keep, send, near_cols = call(
        near_kernel, "near", enc_flops, enc_outs, 5, [((256, D), BF), half_value]
    )(at, *blocks, enc)
    feats_near = features(keep, send)
    over = swap(jnp.concatenate([feats_near] + split(nsq_part), axis=0), "zh")
    over_near = over[:128]
    nsq_both = nsq_part + over[128:136].astype(F32) + over[136:144].astype(F32)

    keep, send, far_cols = call(far_kernel, "far", enc_flops, enc_outs, 2, [half_value])(
        at, far, enc
    )
    feats_far = features(keep, send)
    over_far = swap(feats_far, "zh")
    g1 = gather(
        jnp.concatenate([feats_near, over_near, feats_far] + split(nsq_both), axis=0), "y"
    )
    g2 = gather(over_far, "y")
    p1 = swap(g1, "pair")
    p2 = swap(g2, "pair")

    payload, block_feats, nsq_all = call(
        decode_kernel,
        "decode",
        2 * tokens * 8 * own * 512,
        [((tokens, 512), BF), ((tokens, 8 * own), BF), ((8, own), F32)],
        5,
        [((64, 8 * own), F32), ((64, 8 * own), BF)],
    )(at, g1, g2, p1, p2, dec_t)
    nsq_own = lax.dynamic_index_in_dim(nsq_all, tok_at, 0, keepdims=False)
    arrived = lax.all_to_all(payload, LAT, 0, 0, tiled=True)

    num_part, sum_sq = call(
        numer_kernel,
        "numer",
        2 * tokens * 8 * own * width,
        [((8, own), F32), ((1, own), F32)],
        4,
        [((tokens, width), BF)],
    )(at, block_feats, near_cols, far_cols, dec_t)
    mean_sq = sum_sq[0] / tokens

    total = jnp.sum(arrived.reshape(32, rows, 512).astype(F32), axis=0)
    recon_vals = total[:, :width] + dec_bias[0]
    sparse = total[:, width] + total[:, width + 1]
    own_row = (lat_at // 8) * 64 + (lat_at % 4) * rows
    act_own = jnp.where(
        (lat_at // 4) % 2 == zh_at,
        lax.dynamic_slice_in_dim(near_cols, own_row, rows, 0),
        lax.dynamic_slice_in_dim(far_cols, own_row, rows, 0),
    )
    residue = act_own.astype(F32) - recon_vals
    own_terms = jnp.sum(residue * residue, axis=1) / (2.0 * D) + penalty * sparse

    last = jnp.concatenate(
        [
            jnp.broadcast_to(num_part.reshape(1, 8, own), (2, 8, own)),
            jnp.broadcast_to(own_terms, (2, 8, rows)),
        ],
        axis=2,
    ).reshape(16, own + rows)
    got = lax.all_to_all(last, ("pair",) + TOK, 0, 0, tiled=True)
    token_loss = jnp.sum(got[:, own:], axis=0)
    mine = lax.dynamic_slice_in_dim(got, pair_at * 8, 8, 0)[:, :own]
    num_own = jnp.sum(mine, axis=0) / tokens
    scaling = num_own / (nsq_own * mean_sq + tiny_term)
    return (recon_vals.astype(BF)[None], token_loss, scaling[None])


def solution(mesh):
    fine = Mesh(mesh.devices.reshape(2, 4, 8, 4, 2), ("pair", "x", "zl", "y", "zh"))
    return jax.shard_map(
        body,
        mesh=fine,
        in_specs=(
            P("pair", TOK, None),
            P("pair", None, LAT + TOK),
            P(LAT + TOK),
            P(LAT + TOK),
            P("pair", LAT, TOK),
            P("pair", TOK),
        ),
        out_specs=(P("pair", LAT, TOK), P(LAT), P("pair", LAT + TOK)),
        check_vma=False,
    )
```

time: 247 us -> 217 us (0.88)
  starting transfers between devices: 149 us -> 93.3 us
  blocking collectives: 0 us -> 23 us
  waiting for transfers between devices: 60.4 us -> 77.8 us
  local copies, waits for them, and re-layouts: 20.6 us -> 9 us
  Pallas kernels: 0 us -> 9.32 us
  matrix products: 8.92 us -> 0 us
  other arithmetic: 6.01 us -> 2.76 us
    all_to_all x1, starting transfers between devices: 48.7 us -> 15 us  [body(): arrived = lax.all_to_all(payload, LAT, 0, 0, tiled=True)]
    all_to_all x0 -> x2, blocking collectives: none -> 23 us  [gather(): return lax.all_to_all(copies, axes, 0, 0, tiled=False)]
    ppermute x19 -> x10, waiting for transfers between devices: 15 us -> 37.7 us  [the longest x3 25.5 us: body(): lax.ppermute(act, 'y', [(i, (i + k) % 4) for i in range(4)])]
    ppermute x19 -> x10, starting transfers between devices: 77.8 us -> 62.8 us  [the longest x7 50.6 us: swap(): return lax.ppermute(value, axis, [(0, 1), (1, 0)])]
    all_to_all x1, waiting for transfers between devices: 13.6 us -> 0.01 us  [gather(): return lax.all_to_all(copies, axes, 0, 0, tiled=False)]
    dynamic_update_slice x21 -> x0, local copies, waits for them, and re-layouts: 11.8 us -> none  [the longest x16 8.04 us: in_order(): lax.dynamic_update_slice(out, part[k * count:(k + 1) * count], ((place *...]
    pallas_call x0 -> x4, Pallas kernels: none -> 9.32 us  [the longest x1 3.47 us: body(): call(decode_kernel, 'decode', 2 * tokens * 8 * own * 512, [((tokens, 512)...]
    dot_general x4 -> x0, matrix products: 8.92 us -> none  [the longest x1 3.41 us: body(): lax.dot_general(act_slice, dec, (((1,), (1,)), ((), ())), preferred_eleme...]
  transfers between devices with their start and end apart: 22 -> 13, of which waited for: 9 -> 8; matrix products, arithmetic and copies ran while one was open for 10% -> 1% of each run, Pallas kernels for 0% -> 3%
where the time goes in v2:
time: 217 us; the launch traced here: 216 us
  starting transfers between devices  93.3 us (43%)
  waiting for transfers between devices  77.8 us (36%)
  blocking collectives  23 us (11%)
  Pallas kernels  9.32 us (4%)
  local copies, waits for them, and re-layouts  9 us (4%)
  other arithmetic  2.76 us (1%)
    ppermute x7, starting transfers between devices, swap(): return lax.ppermute(value, axis, [(0, 1), (1, 0)])  50.6 us
    all_to_all x1, waiting for transfers between devices, body(): arrived = lax.all_to_all(payload, LAT, 0, 0, tiled=True)  25.9 us
    ppermute x3, waiting for transfers between devices, body(): lax.ppermute(act, 'y', [(i, (i + k) % 4) for i in range(4)])  25.5 us
    all_to_all x2, blocking collectives, gather(): return lax.all_to_all(copies, axes, 0, 0, tiled=False)  23 us
    all_to_all x1, starting transfers between devices, body(): arrived = lax.all_to_all(payload, LAT, 0, 0, tiled=True)  15 us
    all_to_all x1, waiting for transfers between devices, body(): got = lax.all_to_all(last, ('pair',) + TOK, 0, 0, tiled=True)  14.2 us
    ppermute x7, waiting for transfers between devices, swap(): return lax.ppermute(value, axis, [(0, 1), (1, 0)])  12.2 us
    ppermute x3, starting transfers between devices, body(): lax.ppermute(act, 'y', [(i, (i + k) % 4) for i in range(4)])  12.1 us
  transfers between devices with their start and end apart: 13, of which 8 were waited for; matrix products, arithmetic and copies ran while one was open for 1% of the time, Pallas kernels for 3%

profile of v2, /device:TPU:1, one launch (start us, length us, event | category | flops | bytes accessed | tf_op | source)
XLA Modules:
  0.0 216.1 jit_solution(12976696236912845377)
XLA Ops:
  0.6 5.5 %collective-permute-start.2 = (bf16[64,3584]{1,0:T(8,128)(2,1)}, bf16[64,3584]{1,0:T(8,128)(2,1)S(1)}, u32[]{:S(2)}, u32[]{:S(2)}) collective-permute-start(bf16[64,3584]{1,0:T(8,128)(2,1)} %bitcast.28), channel_id=1, source_target_pairs={{0,6},{2,0},{4,2},{6,4},{1,7},{3,1},{5,3},{7,5},{8,14},{10,8},{12,... | collective-permute-start | bytes 1376264 | tf_op jit(solution)/shard_map/ppermute | solution.py:146
  6.1 1.9 collective-permute-start.1
  9.0 15.4 %collective-permute-start = (bf16[16,3584]{1,0:T(8,128)(2,1)S(1)}, bf16[16,3584]{1,0:T(8,128)(2,1)S(1)}, u32[]{:S(2)}, u32[]{:S(2)}) collective-permute-start(bf16[16,3584]{1,0:T(8,128)(2,1)S(1)} %dynamic-slice_bitcast_fusion), channel_id=1, source_target_pairs={{0,1},{1,0},{2,3},{3,2},{4,5},{5,4},{6,7},{7,6},{8,9},{9,8},{10,11... | collective-permute-start | bytes 344072 | tf_op jit(solution)/shard_map/ppermute | solution.py:22
  24.4 2.5 %collective-permute-done = bf16[16,3584]{1,0:T(8,128)(2,1)S(1)} collective-permute-done((bf16[16,3584]{1,0:T(8,128)(2,1)S(1)}, bf16[16,3584]{1,0:T(8,128)(2,1)S(1)}, u32[]{:S(2)}, u32[]{:S(2)}) %collective-permute-start) | collective-permute-done | bytes 114720 | tf_op jit(solution)/shard_map/ppermute | solution.py:22
  26.9 1.4 broadcast_in_dim.12
  28.3 6.7 %all-to-all-start = ((bf16[16,16,3584]{2,1,0:T(8,128)(2,1)}), bf16[16,16,3584]{2,1,0:T(8,128)(2,1)}, u32[]{:S(2)}, u32[]{:S(2)}) async-start(bf16[16,16,3584]{2,1,0:T(8,128)(2,1)} %broadcast_in_dim.12), calls=%async_computation | async-start | bytes 3670016 | tf_op jit(solution)/shard_map/all_to_all | solution.py:28
  35.0 4.7 %collective-permute-start.3 = (bf16[64,3584]{1,0:T(8,128)(2,1)S(1)}, bf16[64,3584]{1,0:T(8,128)(2,1)}, u32[]{:S(2)}, u32[]{:S(2)}) collective-permute-start(bf16[64,3584]{1,0:T(8,128)(2,1)S(1)} %bitcast.30), channel_id=1, source_target_pairs={{0,4},{2,6},{4,0},{6,2},{1,5},{3,7},{5,1},{7,3},{8,12},{10,14},{12... | collective-permute-start | bytes 1376264 | tf_op jit(solution)/shard_map/ppermute | solution.py:146
  40.2 25.5 %collective-permute-done.3.b3 = bf16[64,3584]{1,0:T(8,128)(2,1)} collective-permute-done((bf16[64,3584]{1,0:T(8,128)(2,1)S(1)}, bf16[64,3584]{1,0:T(8,128)(2,1)}, u32[]{:S(2)}, u32[]{:S(2)}) %collective-permute-start.3) | collective-permute-done | bytes 458784 | tf_op jit(solution)/shard_map/ppermute | solution.py:146
  65.7 1.5 copy-done.1
  67.2 1.8 near.1
  69.1 5.5 %collective-permute-start.4 = (f32[128,256]{1,0:T(8,128)S(1)}, f32[128,256]{1,0:T(8,128)S(1)}, u32[]{:S(2)}, u32[]{:S(2)}) collective-permute-start(f32[128,256]{1,0:T(8,128)S(1)} %get-tuple-element.20), channel_id=1, source_target_pairs={{0,256},{256,0},{1,257},{257,1},{2,258},{258,2},{3,259},{259,3},{4... | collective-permute-start | bytes 393224 | tf_op jit(solution)/shard_map/ppermute | solution.py:22
  74.6 0.9 collective-permute-done.4
  75.6 12.1 %collective-permute-start.5 = (bf16[144,256]{1,0:T(8,128)(2,1)S(1)}, bf16[144,256]{1,0:T(8,128)(2,1)S(1)}, u32[]{:S(2)}, u32[]{:S(2)}) collective-permute-start(bf16[144,256]{1,0:T(8,128)(2,1)S(1)} %pad_maximum_fusion), channel_id=1, source_target_pairs={{0,1},{1,0},{2,3},{3,2},{4,5},{5,4},{6,7},{7,6},{8,9},{9,8},{10,11... | collective-permute-start | bytes 221192 | tf_op jit(solution)/shard_map/ppermute | solution.py:22
  87.8 1.5 copy-done.2
  89.2 2.2 %far.1 = (f32[128,256]{1,0:T(8,128)S(1)}, f32[128,256]{1,0:T(8,128)S(1)}, bf16[256,448]{1,0:T(8,128)(2,1)S(1)}) custom-call(s32[4]{0:T(128)S(1)} %pad_add_fusion.at_ref, bf16[256,3584]{1,0:T(8,128)(2,1)} %bitcast.8.a_ref, bf16[3584,256]{1,0:T(8,128)(2,1)S(1)} %bitcast.27), custom_call_target="tpu_custom_call" | custom-call | flops 469762048 | bytes 6291456 | tf_op jit(solution)/shard_map/far/pallas_call | solution.py:175
  91.4 2.6 %collective-permute-start.6 = (f32[128,256]{1,0:T(8,128)S(1)}, f32[128,256]{1,0:T(8,128)S(1)}, u32[]{:S(2)}, u32[]{:S(2)}) collective-permute-start(f32[128,256]{1,0:T(8,128)S(1)} %get-tuple-element.23), channel_id=1, source_target_pairs={{0,256},{256,0},{1,257},{257,1},{2,258},{258,2},{3,259},{259,3},{4... | collective-permute-start | bytes 393224 | tf_op jit(solution)/shard_map/ppermute | solution.py:22
  94.0 0.9 collective-permute-done.6
  95.1 15.0 %all_to_all.36.g1 = bf16[4,400,256]{2,1,0:T(8,128)(2,1)S(1)} all-to-all(bf16[4,400,256]{2,1,0:T(8,128)(2,1)S(1)} %broadcast_in_dim.13), channel_id=1, replica_groups=mesh['pair'=2,'x'=4,'zl'=8,'y'=4,'zh'=2] {'y'}, dimensions={0} | all-to-all | bytes 1638400 | tf_op jit(solution)/shard_map/all_to_all | solution.py:28
  110.1 3.4 %collective-permute-start.8 = (bf16[4,400,256]{2,1,0:T(8,128)(2,1)S(1)}, bf16[4,400,256]{2,1,0:T(8,128)(2,1)S(1)}, u32[]{:S(2)}, u32[]{:S(2)}) collective-permute-start(bf16[4,400,256]{2,1,0:T(8,128)(2,1)S(1)} %all_to_all.36.g1), channel_id=1, source_target_pairs={{0,256},{256,0},{1,257},{257,1},{2,258},{258,2},{3,259},{259,3},{4... | collective-permute-start | bytes 2457608 | tf_op jit(solution)/shard_map/ppermute | solution.py:22
  113.5 7.6 %collective-permute-start.7 = (bf16[128,256]{1,0:T(8,128)(2,1)S(1)}, bf16[128,256]{1,0:T(8,128)(2,1)S(1)}, u32[]{:S(2)}, u32[]{:S(2)}) collective-permute-start(bf16[128,256]{1,0:T(8,128)(2,1)S(1)} %get-tuple-element.32), channel_id=1, source_target_pairs={{0,1},{1,0},{2,3},{3,2},{4,5},{5,4},{6,7},{7,6},{8,9},{9,8},{10,11... | collective-permute-start | bytes 196616 | tf_op jit(solution)/shard_map/ppermute | solution.py:22
  121.1 6.7 %collective-permute-done.7 = bf16[128,256]{1,0:T(8,128)(2,1)S(1)} collective-permute-done((bf16[128,256]{1,0:T(8,128)(2,1)S(1)}, bf16[128,256]{1,0:T(8,128)(2,1)S(1)}, u32[]{:S(2)}, u32[]{:S(2)}) %collective-permute-start.7) | collective-permute-done | bytes 65568 | tf_op jit(solution)/shard_map/ppermute | solution.py:22
  127.9 7.9 %all_to_all.37.g2 = bf16[4,128,256]{2,1,0:T(8,128)(2,1)S(1)} all-to-all(bf16[4,128,256]{2,1,0:T(8,128)(2,1)S(1)} %broadcast_in_dim.14), channel_id=1, replica_groups=mesh['pair'=2,'x'=4,'zl'=8,'y'=4,'zh'=2] {'y'}, dimensions={0} | all-to-all | bytes 524288 | tf_op jit(solution)/shard_map/all_to_all | solution.py:28
  135.8 4.0 %collective-permute-start.9 = (bf16[4,128,256]{2,1,0:T(8,128)(2,1)S(1)}, bf16[4,128,256]{2,1,0:T(8,128)(2,1)S(1)}, u32[]{:S(2)}, u32[]{:S(2)}) collective-permute-start(bf16[4,128,256]{2,1,0:T(8,128)(2,1)S(1)} %all_to_all.37.g2), channel_id=1, source_target_pairs={{0,256},{256,0},{1,257},{257,1},{2,258},{258,2},{3,259},{259,3},{4... | collective-permute-start | bytes 786440 | tf_op jit(solution)/shard_map/ppermute | solution.py:22
  139.9 1.1 collective-permute-done.9.p2
  141.0 3.5 %decode.1 = (bf16[512,512]{1,0:T(8,128)(2,1)}, bf16[512,2048]{1,0:T(8,128)(2,1)S(1)}, f32[8,256]{1,0:T(8,128)S(1)}) custom-call(s32[4]{0:T(128)S(1)} %pad_add_fusion.at_ref, bf16[4,400,256]{2,1,0:T(8,128)(2,1)S(1)} %all_to_all.36.g1, bf16[4,128,256]{2,1,0:T(8,128)(2,1)S(1)} %all_to_all.37.g2, bf16[4,400,256]{2,1,0:T(8,128)(2,1)S(1)} %collective-permute-done.8.p1, ...), custom_call_target="tpu_custom_call" | custom-call | flops 1073741824 | bytes 6291456 | tf_op jit(solution)/shard_map/decode/pallas_call | solution.py:187
  144.5 1.3 copy-done.3
  145.8 15.0 %all-to-all-start.3 = ((bf16[32,16,512]{2,1,0:T(8,128)(2,1)}), bf16[32,16,512]{2,1,0:T(8,128)(2,1)S(1)}, u32[]{:S(2)}, u32[]{:S(2)}) async-start(bf16[32,16,512]{2,1,0:T(8,128)(2,1)} %bitcast.10), calls=%async_computation.3 | async-start | bytes 1048576 | tf_op jit(solution)/shard_map/all_to_all | solution.py:196
  160.9 1.6 copy-done.4
  162.5 1.9 numer.1
  164.4 25.9 %all-to-all-done.3 = bf16[32,16,512]{2,1,0:T(8,128)(2,1)S(1)} async-done(((bf16[32,16,512]{2,1,0:T(8,128)(2,1)}), bf16[32,16,512]{2,1,0:T(8,128)(2,1)S(1)}, u32[]{:S(2)}, u32[]{:S(2)}) %all-to-all-start.3) | async-done | bytes 524320 | tf_op jit(solution)/shard_map/all_to_all | solution.py:196
  191.9 8.8 %all-to-all-start.4 = ((f32[16,1,272]{2,1,0:T(1,128)}), f32[16,1,272]{2,1,0:T(1,128)S(1)}, u32[]{:S(2)}, u32[]{:S(2)}) async-start(f32[16,1,272]{2,1,0:T(1,128)} %all_to_all.28), calls=%async_computation.4 | async-start | bytes 49152 | tf_op jit(solution)/shard_map/all_to_all | solution.py:227
  200.7 14.2 %all-to-all-done.4 = f32[16,1,272]{2,1,0:T(1,128)S(1)} async-done(((f32[16,1,272]{2,1,0:T(1,128)}), f32[16,1,272]{2,1,0:T(1,128)S(1)}, u32[]{:S(2)}, u32[]{:S(2)}) %all-to-all-start.4) | async-done | bytes 17440 | tf_op jit(solution)/shard_map/all_to_all | solution.py:227
  (48 shorter events, 4.5 us)
Async XLA Ops:
  0.6 26.2 %collective-permute-start.2 = (bf16[64,3584]{1,0:T(8,128)(2,1)}, bf16[64,3584]{1,0:T(8,128)(2,1)S(1)}, u32[]{:S(2)}, u32[]{:S(2)}) collective-permute-start(bf16[64,3584]{1,0:T(8,128)(2,1)} %bitcast.28), channel_id=1, source_target_pairs={{0,6},{2,0},{4,2},{6,4},{1,7},{3,1},{5,3},{7,5},{8,14},{10,8},{12,... | collective-permute-start | bytes 1376264 | tf_op jit(solution)/shard_map/ppermute | solution.py:146
  6.1 20.8 %collective-permute-start.1 = (bf16[64,3584]{1,0:T(8,128)(2,1)}, bf16[64,3584]{1,0:T(8,128)(2,1)S(1)}, u32[]{:S(2)}, u32[]{:S(2)}) collective-permute-start(bf16[64,3584]{1,0:T(8,128)(2,1)} %bitcast.29), channel_id=1, source_target_pairs={{0,2},{2,4},{4,6},{6,0},{1,3},{3,5},{5,7},{7,1},{8,10},{10,12},{12... | collective-permute-start | bytes 1376264 | tf_op jit(solution)/shard_map/ppermute | solution.py:146
  9.0 17.9 %collective-permute-start = (bf16[16,3584]{1,0:T(8,128)(2,1)S(1)}, bf16[16,3584]{1,0:T(8,128)(2,1)S(1)}, u32[]{:S(2)}, u32[]{:S(2)}) collective-permute-start(bf16[16,3584]{1,0:T(8,128)(2,1)S(1)} %dynamic-slice_bitcast_fusion), channel_id=1, source_target_pairs={{0,1},{1,0},{2,3},{3,2},{4,5},{5,4},{6,7},{7,6},{8,9},{9,8},{10,11... | collective-permute-start | bytes 344072 | tf_op jit(solution)/shard_map/ppermute | solution.py:22
  28.3 6.7 %copy-start.5 = (bf16[1,64,3584]{2,1,0:T(8,128)(2,1)S(1)}, bf16[1,64,3584]{2,1,0:T(8,128)(2,1)}, u32[]{:S(2)}) copy-start(bf16[1,64,3584]{2,1,0:T(8,128)(2,1)} %param.6) | copy-start | bytes 1376260
  28.3 11.5 %copy-start = (bf16[1,2048,448]{1,2,0:T(8,128)(2,1)S(1)}, bf16[1,2048,448]{1,2,0:T(8,128)(2,1)}, u32[]{:S(2)}) copy-start(bf16[1,2048,448]{1,2,0:T(8,128)(2,1)} %param.10) | copy-start | bytes 5505028
  28.3 59.4 %all-to-all-start = ((bf16[16,16,3584]{2,1,0:T(8,128)(2,1)}), bf16[16,16,3584]{2,1,0:T(8,128)(2,1)}, u32[]{:S(2)}, u32[]{:S(2)}) async-start(bf16[16,16,3584]{2,1,0:T(8,128)(2,1)} %broadcast_in_dim.12), calls=%async_computation | async-start | bytes 3670016 | tf_op jit(solution)/shard_map/all_to_all | solution.py:28
  35.0 30.7 %collective-permute-start.3 = (bf16[64,3584]{1,0:T(8,128)(2,1)S(1)}, bf16[64,3584]{1,0:T(8,128)(2,1)}, u32[]{:S(2)}, u32[]{:S(2)}) collective-permute-start(bf16[64,3584]{1,0:T(8,128)(2,1)S(1)} %bitcast.30), channel_id=1, source_target_pairs={{0,4},{2,6},{4,0},{6,2},{1,5},{3,7},{5,1},{7,3},{8,12},{10,14},{12... | collective-permute-start | bytes 1376264 | tf_op jit(solution)/shard_map/ppermute | solution.py:146
  65.7 1.5 copy-start.1
  67.2 7.3 %copy-start.8 = (s32[256]{0:T(256)S(1)}, s32[256]{0:T(256)}, u32[]{:S(2)}) copy-start(s32[256]{0:T(256)} %param.9) | copy-start | bytes 3076
  67.2 8.3 %copy-start.6 = (f32[256]{0:T(256)S(1)}, f32[256]{0:T(256)}, u32[]{:S(2)}) copy-start(f32[256]{0:T(256)} %param.8) | copy-start | bytes 3076
  69.1 6.5 %collective-permute-start.4 = (f32[128,256]{1,0:T(8,128)S(1)}, f32[128,256]{1,0:T(8,128)S(1)}, u32[]{:S(2)}, u32[]{:S(2)}) collective-permute-start(f32[128,256]{1,0:T(8,128)S(1)} %get-tuple-element.20), channel_id=1, source_target_pairs={{0,256},{256,0},{1,257},{257,1},{2,258},{258,2},{3,259},{259,3},{4... | collective-permute-start | bytes 393224 | tf_op jit(solution)/shard_map/ppermute | solution.py:22
  75.6 18.4 %collective-permute-start.5 = (bf16[144,256]{1,0:T(8,128)(2,1)S(1)}, bf16[144,256]{1,0:T(8,128)(2,1)S(1)}, u32[]{:S(2)}, u32[]{:S(2)}) collective-permute-start(bf16[144,256]{1,0:T(8,128)(2,1)S(1)} %pad_maximum_fusion), channel_id=1, source_target_pairs={{0,1},{1,0},{2,3},{3,2},{4,5},{5,4},{6,7},{7,6},{8,9},{9,8},{10,11... | collective-permute-start | bytes 221192 | tf_op jit(solution)/shard_map/ppermute | solution.py:22
  87.7 1.5 copy-start.2
  91.4 3.5 %collective-permute-start.6 = (f32[128,256]{1,0:T(8,128)S(1)}, f32[128,256]{1,0:T(8,128)S(1)}, u32[]{:S(2)}, u32[]{:S(2)}) collective-permute-start(f32[128,256]{1,0:T(8,128)S(1)} %get-tuple-element.23), channel_id=1, source_target_pairs={{0,256},{256,0},{1,257},{257,1},{2,258},{258,2},{3,259},{259,3},{4... | collective-permute-start | bytes 393224 | tf_op jit(solution)/shard_map/ppermute | solution.py:22
  110.1 30.9 %collective-permute-start.8 = (bf16[4,400,256]{2,1,0:T(8,128)(2,1)S(1)}, bf16[4,400,256]{2,1,0:T(8,128)(2,1)S(1)}, u32[]{:S(2)}, u32[]{:S(2)}) collective-permute-start(bf16[4,400,256]{2,1,0:T(8,128)(2,1)S(1)} %all_to_all.36.g1), channel_id=1, source_target_pairs={{0,256},{256,0},{1,257},{257,1},{2,258},{258,2},{3,259},{259,3},{4... | collective-permute-start | bytes 2457608 | tf_op jit(solution)/shard_map/ppermute | solution.py:22
  113.5 14.3 %collective-permute-start.7 = (bf16[128,256]{1,0:T(8,128)(2,1)S(1)}, bf16[128,256]{1,0:T(8,128)(2,1)S(1)}, u32[]{:S(2)}, u32[]{:S(2)}) collective-permute-start(bf16[128,256]{1,0:T(8,128)(2,1)S(1)} %get-tuple-element.32), channel_id=1, source_target_pairs={{0,1},{1,0},{2,3},{3,2},{4,5},{5,4},{6,7},{7,6},{8,9},{9,8},{10,11... | collective-permute-start | bytes 196616 | tf_op jit(solution)/shard_map/ppermute | solution.py:22
  135.8 5.2 %collective-permute-start.9 = (bf16[4,128,256]{2,1,0:T(8,128)(2,1)S(1)}, bf16[4,128,256]{2,1,0:T(8,128)(2,1)S(1)}, u32[]{:S(2)}, u32[]{:S(2)}) collective-permute-start(bf16[4,128,256]{2,1,0:T(8,128)(2,1)S(1)} %all_to_all.37.g2), channel_id=1, source_target_pairs={{0,256},{256,0},{1,257},{257,1},{2,258},{258,2},{3,259},{259,3},{4... | collective-permute-start | bytes 786440 | tf_op jit(solution)/shard_map/ppermute | solution.py:22
  144.5 1.3 copy-start.3
  145.8 44.4 %all-to-all-start.3 = ((bf16[32,16,512]{2,1,0:T(8,128)(2,1)}), bf16[32,16,512]{2,1,0:T(8,128)(2,1)S(1)}, u32[]{:S(2)}, u32[]{:S(2)}) async-start(bf16[32,16,512]{2,1,0:T(8,128)(2,1)} %bitcast.10), calls=%async_computation.3 | async-start | bytes 1048576 | tf_op jit(solution)/shard_map/all_to_all | solution.py:196
  160.9 1.6 copy-start.4
  162.5 28.0 %copy-start.7 = (f32[1,448]{1,0:T(1,128)S(1)}, f32[1,448]{1,0:T(1,128)}, u32[]{:S(2)}) copy-start(f32[1,448]{1,0:T(1,128)} %param.11) | copy-start | bytes 5380
  191.9 23.0 %all-to-all-start.4 = ((f32[16,1,272]{2,1,0:T(1,128)}), f32[16,1,272]{2,1,0:T(1,128)S(1)}, u32[]{:S(2)}, u32[]{:S(2)}) async-start(f32[16,1,272]{2,1,0:T(1,128)} %all_to_all.28), calls=%async_computation.4 | async-start | bytes 49152 | tf_op jit(solution)/shard_map/all_to_all | solution.py:227

commit v3 on v2

--- a/solution.py
+++ b/solution.py
@@ -28,7 +28,7 @@
     return lax.all_to_all(copies, axes, 0, 0, tiled=False)
 
 
-def encode(at_ref, a_ref, enc_ref, keep_ref, send_ref, cols_ref, v_ref):
+def encode_kernel(at_ref, a_ref, enc_ref, keep_ref, send_ref, cols_ref, v_ref):
     pair_at, tok_at = at_ref[0], at_ref[2]
     v_ref[...] = jnp.dot(a_ref[...], enc_ref[...], preferred_element_type=F32)
     keep_ref[...] = v_ref[pl.ds(pl.multiple_of(pair_at * 128, 128), 128), :]
@@ -36,18 +36,6 @@
     base = (tok_at // 2) * 896 + (tok_at % 2) * 384
     window = a_ref[:, pl.ds(pl.multiple_of(base, 128), 512)]
     cols_ref[...] = jnp.where(tok_at % 2 == 1, window[:, 64:512], window[:, 0:448])
-
-
-def near_kernel(at_ref, b0, b1, b2, b3, enc_ref, keep_ref, send_ref, cols_ref, a_ref, v_ref):
-    y_at = at_ref[3]
-    for ref, step in ((b0, 0), (b1, 3), (b2, 1), (b3, 2)):
-        row = pl.multiple_of(((y_at + step) % 4) * 64, 64)
-        a_ref[pl.ds(row, 64), :] = ref[...]
-    encode(at_ref, a_ref, enc_ref, keep_ref, send_ref, cols_ref, v_ref)
-
-
-def far_kernel(at_ref, a_ref, enc_ref, keep_ref, send_ref, cols_ref, v_ref):
-    encode(at_ref, a_ref, enc_ref, keep_ref, send_ref, cols_ref, v_ref)
 
 
 def decode_kernel(
@@ -139,13 +127,10 @@
     own, width = enc.shape[1], dec.shape[1]
     tokens = 8 * act.shape[0]
     rows = tokens // lax.axis_size(LAT)
-    at = jnp.stack([pair_at, zh_at, tok_at, lax.axis_index("y")]).astype(jnp.int32)
+    at = jnp.stack([pair_at, zh_at, tok_at]).astype(jnp.int32)
 
     quarter = swap(lax.dynamic_slice_in_dim(act, x_at * 16, 16, 0), "zh")
-    blocks = [act] + [
-        lax.ppermute(act, "y", [(i, (i + k) % 4) for i in range(4)]) for k in (1, 3, 2)
-    ]
-    quarter, blocks[1], blocks[2] = lax.optimization_barrier((quarter, blocks[1], blocks[2]))
+    near = gather(act, "y").reshape(256, D)
     far = gather(quarter, ("y", "x")).reshape(256, D)
 
     dec_wide = dec.astype(F32)
@@ -164,24 +149,22 @@
     enc_outs = [((128, own), F32), ((128, own), F32), ((256, width), BF)]
     enc_flops = 2 * 256 * D * own
     half_value = ((256, own), F32)
-    keep, send, near_cols = call(
-        near_kernel, "near", enc_flops, enc_outs, 5, [((256, D), BF), half_value]
-    )(at, *blocks, enc)
+    encode = call(encode_kernel, "encode", enc_flops, enc_outs, 2, [half_value])
+    keep, send, near_cols = encode(at, near, enc)
     feats_near = features(keep, send)
     over = swap(jnp.concatenate([feats_near] + split(nsq_part), axis=0), "zh")
     over_near = over[:128]
     nsq_both = nsq_part + over[128:136].astype(F32) + over[136:144].astype(F32)
 
-    keep, send, far_cols = call(far_kernel, "far", enc_flops, enc_outs, 2, [half_value])(
-        at, far, enc
-    )
+    keep, send, far_cols = encode(at, far, enc)
     feats_far = features(keep, send)
     over_far = swap(feats_far, "zh")
     g1 = gather(
         jnp.concatenate([feats_near, over_near, feats_far] + split(nsq_both), axis=0), "y"
     )
+    p1 = swap(g1, "pair")
+    over_far, g1 = lax.optimization_barrier((over_far, g1))
     g2 = gather(over_far, "y")
-    p1 = swap(g1, "pair")
     p2 = swap(g2, "pair")
 
     payload, block_feats, nsq_all = call(

time: 217 us -> 197 us (0.908)
  waiting for transfers between devices: 77.8 us -> 48.1 us
  starting transfers between devices: 93.3 us -> 99 us
  local copies, waits for them, and re-layouts: 9 us -> 14.2 us
    ppermute x3 -> x0, waiting for transfers between devices: 25.5 us -> none  [body(): lax.ppermute(act, 'y', [(i, (i + k) % 4) for i in range(4)])]
    ppermute x3 -> x0, starting transfers between devices: 12.1 us -> none  [body(): lax.ppermute(act, 'y', [(i, (i + k) % 4) for i in range(4)])]
    ppermute x7, starting transfers between devices: 50.6 us -> 61.8 us  [swap(): return lax.ppermute(value, axis, [(0, 1), (1, 0)])]
    all_to_all x1 -> x2, starting transfers between devices: 6.68 us -> 13.7 us  [gather(): return lax.all_to_all(copies, axes, 0, 0, tiled=False)]
    ppermute x7, waiting for transfers between devices: 12.2 us -> 7.93 us  [swap(): return lax.ppermute(value, axis, [(0, 1), (1, 0)])]
    all_to_all x1, starting transfers between devices: 15 us -> 12.2 us  [body(): arrived = lax.all_to_all(payload, LAT, 0, 0, tiled=True)]
    unnamed x21 -> x23, local copies, waits for them, and re-layouts: 5.95 us -> 8.68 us
    all_to_all x1, starting transfers between devices: 8.8 us -> 11.4 us  [body(): got = lax.all_to_all(last, ('pair',) + TOK, 0, 0, tiled=True)]
  transfers between devices with their start and end apart: 13 -> 11, of which waited for: 8 -> 7; matrix products, arithmetic and copies ran while one was open for 1% -> 1% of each run, Pallas kernels for 3% -> 3%
where the time goes in v3:
time: 197 us; the launch traced here: 196 us
  starting transfers between devices  99 us (50%)
  waiting for transfers between devices  48.1 us (24%)
  blocking collectives  22.6 us (11%)
  local copies, waits for them, and re-layouts  14.2 us (7%)
  Pallas kernels  8.57 us (4%)
  other arithmetic  2.76 us (1%)
    ppermute x7, starting transfers between devices, swap(): return lax.ppermute(value, axis, [(0, 1), (1, 0)])  61.8 us
    all_to_all x1, waiting for transfers between devices, body(): arrived = lax.all_to_all(payload, LAT, 0, 0, tiled=True)  25.9 us
    all_to_all x2, blocking collectives, gather(): return lax.all_to_all(copies, axes, 0, 0, tiled=False)  22.6 us
    all_to_all x1, waiting for transfers between devices, body(): got = lax.all_to_all(last, ('pair',) + TOK, 0, 0, tiled=True)  14.2 us
    all_to_all x2, starting transfers between devices, gather(): return lax.all_to_all(copies, axes, 0, 0, tiled=False)  13.7 us
    all_to_all x1, starting transfers between devices, body(): arrived = lax.all_to_all(payload, LAT, 0, 0, tiled=True)  12.2 us
    all_to_all x1, starting transfers between devices, body(): got = lax.all_to_all(last, ('pair',) + TOK, 0, 0, tiled=True)  11.4 us
    unnamed x23, local copies, waits for them, and re-layouts  8.68 us
  transfers between devices with their start and end apart: 11, of which 7 were waited for; matrix products, arithmetic and copies ran while one was open for 1% of the time, Pallas kernels for 3%

profile of v3, /device:TPU:1, one launch (start us, length us, event | category | flops | bytes accessed | tf_op | source)
XLA Modules:
  0.0 196.2 jit_solution(4379073129456925632)
XLA Ops:
  0.6 2.4 %broadcast_in_dim.18 = bf16[4,64,3584]{2,1,0:T(8,128)(2,1)} broadcast(bf16[64,3584]{1,0:T(8,128)(2,1)} %bitcast.29), dimensions={1,2} | broadcast | bytes 2293760 | tf_op jit(solution)/shard_map/broadcast_in_dim | solution.py:27
  3.1 5.0 %all-to-all-start.1 = ((bf16[4,64,3584]{2,1,0:T(8,128)(2,1)}), bf16[4,64,3584]{2,1,0:T(8,128)(2,1)S(1)}, u32[]{:S(2)}, u32[]{:S(2)}) async-start(bf16[4,64,3584]{2,1,0:T(8,128)(2,1)} %broadcast_in_dim.18), calls=%async_computation.1 | async-start | bytes 3670016 | tf_op jit(solution)/shard_map/all_to_all | solution.py:28
  9.0 15.4 %collective-permute-start = (bf16[16,3584]{1,0:T(8,128)(2,1)S(1)}, bf16[16,3584]{1,0:T(8,128)(2,1)S(1)}, u32[]{:S(2)}, u32[]{:S(2)}) collective-permute-start(bf16[16,3584]{1,0:T(8,128)(2,1)S(1)} %dynamic-slice_bitcast_fusion), channel_id=1, source_target_pairs={{0,1},{1,0},{2,3},{3,2},{4,5},{5,4},{6,7},{7,6},{8,9},{9,8},{10,11... | collective-permute-start | bytes 344072 | tf_op jit(solution)/shard_map/ppermute | solution.py:22
  24.4 2.5 %collective-permute-done = bf16[16,3584]{1,0:T(8,128)(2,1)S(1)} collective-permute-done((bf16[16,3584]{1,0:T(8,128)(2,1)S(1)}, bf16[16,3584]{1,0:T(8,128)(2,1)S(1)}, u32[]{:S(2)}, u32[]{:S(2)}) %collective-permute-start) | collective-permute-done | bytes 114720 | tf_op jit(solution)/shard_map/ppermute | solution.py:22
  26.9 1.2 copy-done.1
  28.1 1.4 broadcast_in_dim.16
  29.6 8.7 %all-to-all-start = ((bf16[16,16,3584]{2,1,0:T(8,128)(2,1)}), bf16[16,16,3584]{2,1,0:T(8,128)(2,1)}, u32[]{:S(2)}, u32[]{:S(2)}) async-start(bf16[16,16,3584]{2,1,0:T(8,128)(2,1)} %broadcast_in_dim.16), calls=%async_computation | async-start | bytes 3670016 | tf_op jit(solution)/shard_map/all_to_all | solution.py:28
  38.8 1.5 copy-done.2
  40.3 1.5 copy-done.3
  41.8 1.2 encode.3
  43.0 7.3 %collective-permute-start.3 = (f32[128,256]{1,0:T(8,128)S(1)}, f32[128,256]{1,0:T(8,128)S(1)}, u32[]{:S(2)}, u32[]{:S(2)}) collective-permute-start(f32[128,256]{1,0:T(8,128)S(1)} %get-tuple-element.19), channel_id=1, source_target_pairs={{0,256},{256,0},{1,257},{257,1},{2,258},{258,2},{3,259},{259,3},{4... | collective-permute-start | bytes 393224 | tf_op jit(solution)/shard_map/ppermute | solution.py:22
  50.3 0.9 collective-permute-done.3
  51.3 12.8 %collective-permute-start.4 = (bf16[144,256]{1,0:T(8,128)(2,1)S(1)}, bf16[144,256]{1,0:T(8,128)(2,1)S(1)}, u32[]{:S(2)}, u32[]{:S(2)}) collective-permute-start(bf16[144,256]{1,0:T(8,128)(2,1)S(1)} %pad_maximum_fusion), channel_id=1, source_target_pairs={{0,1},{1,0},{2,3},{3,2},{4,5},{5,4},{6,7},{7,6},{8,9},{9,8},{10,11... | collective-permute-start | bytes 221192 | tf_op jit(solution)/shard_map/ppermute | solution.py:22
  64.1 1.5 copy-done.4
  65.6 2.2 %encode.2 = (f32[128,256]{1,0:T(8,128)S(1)}, f32[128,256]{1,0:T(8,128)S(1)}, bf16[256,448]{1,0:T(8,128)(2,1)S(1)}) custom-call(s32[3]{0:T(128)S(1)} %pad_add_fusion.at_ref, bf16[256,3584]{1,0:T(8,128)(2,1)} %bitcast.4.a_ref, bf16[3584,256]{1,0:T(8,128)(2,1)S(1)} %bitcast.28), custom_call_target="tpu_custom_call" | custom-call | flops 469762048 | bytes 6291456 | tf_op jit(solution)/shard_map/encode/pallas_call | solution.py:159
  67.8 4.8 %collective-permute-start.1 = (f32[128,256]{1,0:T(8,128)S(1)}, f32[128,256]{1,0:T(8,128)S(1)}, u32[]{:S(2)}, u32[]{:S(2)}) collective-permute-start(f32[128,256]{1,0:T(8,128)S(1)} %get-tuple-element.17), channel_id=1, source_target_pairs={{0,256},{256,0},{1,257},{257,1},{2,258},{258,2},{3,259},{259,3},{4... | collective-permute-start | bytes 393224 | tf_op jit(solution)/shard_map/ppermute | solution.py:22
  72.6 0.9 collective-permute-done.1
  73.7 14.6 %all_to_all.41.g1 = bf16[4,400,256]{2,1,0:T(8,128)(2,1)S(1)} all-to-all(bf16[4,400,256]{2,1,0:T(8,128)(2,1)S(1)} %broadcast_in_dim.19), channel_id=1, replica_groups=mesh['pair'=2,'x'=4,'zl'=8,'y'=4,'zh'=2] {'y'}, dimensions={0} | all-to-all | bytes 1638400 | tf_op jit(solution)/shard_map/all_to_all | solution.py:28
  88.3 3.3 %collective-permute-start.5 = (bf16[4,400,256]{2,1,0:T(8,128)(2,1)S(1)}, bf16[4,400,256]{2,1,0:T(8,128)(2,1)S(1)}, u32[]{:S(2)}, u32[]{:S(2)}) collective-permute-start(bf16[4,400,256]{2,1,0:T(8,128)(2,1)S(1)} %all_to_all.41.g1), channel_id=1, source_target_pairs={{0,256},{256,0},{1,257},{257,1},{2,258},{258,2},{3,259},{259,3},{4... | collective-permute-start | bytes 2457608 | tf_op jit(solution)/shard_map/ppermute | solution.py:22
  91.6 14.4 %collective-permute-start.2 = (bf16[128,256]{1,0:T(8,128)(2,1)S(1)}, bf16[128,256]{1,0:T(8,128)(2,1)S(1)}, u32[]{:S(2)}, u32[]{:S(2)}) collective-permute-start(bf16[128,256]{1,0:T(8,128)(2,1)S(1)} %get-tuple-element.30), channel_id=1, source_target_pairs={{0,1},{1,0},{2,3},{3,2},{4,5},{5,4},{6,7},{7,6},{8,9},{9,8},{10,11... | collective-permute-start | bytes 196616 | tf_op jit(solution)/shard_map/ppermute | solution.py:22
  105.9 2.4 %collective-permute-done.2 = bf16[128,256]{1,0:T(8,128)(2,1)S(1)} collective-permute-done((bf16[128,256]{1,0:T(8,128)(2,1)S(1)}, bf16[128,256]{1,0:T(8,128)(2,1)S(1)}, u32[]{:S(2)}, u32[]{:S(2)}) %collective-permute-start.2) | collective-permute-done | bytes 65568 | tf_op jit(solution)/shard_map/ppermute | solution.py:22
  108.4 8.0 %all_to_all.42.g2 = bf16[4,128,256]{2,1,0:T(8,128)(2,1)S(1)} all-to-all(bf16[4,128,256]{2,1,0:T(8,128)(2,1)S(1)} %broadcast_in_dim.20), channel_id=1, replica_groups=mesh['pair'=2,'x'=4,'zl'=8,'y'=4,'zh'=2] {'y'}, dimensions={0} | all-to-all | bytes 524288 | tf_op jit(solution)/shard_map/all_to_all | solution.py:28
  116.4 3.9 %collective-permute-start.6 = (bf16[4,128,256]{2,1,0:T(8,128)(2,1)S(1)}, bf16[4,128,256]{2,1,0:T(8,128)(2,1)S(1)}, u32[]{:S(2)}, u32[]{:S(2)}) collective-permute-start(bf16[4,128,256]{2,1,0:T(8,128)(2,1)S(1)} %all_to_all.42.g2), channel_id=1, source_target_pairs={{0,256},{256,0},{1,257},{257,1},{2,258},{258,2},{3,259},{259,3},{4... | collective-permute-start | bytes 786440 | tf_op jit(solution)/shard_map/ppermute | solution.py:22
  120.3 1.1 collective-permute-done.6.p2
  121.4 3.4 %decode.1 = (bf16[512,512]{1,0:T(8,128)(2,1)}, bf16[512,2048]{1,0:T(8,128)(2,1)S(1)}, f32[8,256]{1,0:T(8,128)S(1)}) custom-call(s32[3]{0:T(128)S(1)} %pad_add_fusion.at_ref, bf16[4,400,256]{2,1,0:T(8,128)(2,1)S(1)} %all_to_all.41.g1, bf16[4,128,256]{2,1,0:T(8,128)(2,1)S(1)} %all_to_all.42.g2, bf16[4,400,256]{2,1,0:T(8,128)(2,1)S(1)} %collective-permute-done.5.p1, ...), custom_call_target="tpu_custom_call" | custom-call | flops 1073741824 | bytes 6291456 | tf_op jit(solution)/shard_map/decode/pallas_call | solution.py:170
  124.9 1.3 copy-done.5
  126.2 12.2 %all-to-all-start.4 = ((bf16[32,16,512]{2,1,0:T(8,128)(2,1)}), bf16[32,16,512]{2,1,0:T(8,128)(2,1)S(1)}, u32[]{:S(2)}, u32[]{:S(2)}) async-start(bf16[32,16,512]{2,1,0:T(8,128)(2,1)} %bitcast.10), calls=%async_computation.4 | async-start | bytes 1048576 | tf_op jit(solution)/shard_map/all_to_all | solution.py:179
  138.4 1.6 copy-done.6
  140.0 1.8 numer.1
  141.8 25.9 %all-to-all-done.4 = bf16[32,16,512]{2,1,0:T(8,128)(2,1)S(1)} async-done(((bf16[32,16,512]{2,1,0:T(8,128)(2,1)}), bf16[32,16,512]{2,1,0:T(8,128)(2,1)S(1)}, u32[]{:S(2)}, u32[]{:S(2)}) %all-to-all-start.4) | async-done | bytes 524320 | tf_op jit(solution)/shard_map/all_to_all | solution.py:179
  169.4 11.4 %all-to-all-start.5 = ((f32[16,1,272]{2,1,0:T(1,128)}), f32[16,1,272]{2,1,0:T(1,128)S(1)}, u32[]{:S(2)}, u32[]{:S(2)}) async-start(f32[16,1,272]{2,1,0:T(1,128)} %all_to_all.32), calls=%async_computation.5 | async-start | bytes 49152 | tf_op jit(solution)/shard_map/all_to_all | solution.py:210
  180.8 14.2 %all-to-all-done.5 = f32[16,1,272]{2,1,0:T(1,128)S(1)} async-done(((f32[16,1,272]{2,1,0:T(1,128)}), f32[16,1,272]{2,1,0:T(1,128)S(1)}, u32[]{:S(2)}, u32[]{:S(2)}) %all-to-all-start.5) | async-done | bytes 17440 | tf_op jit(solution)/shard_map/all_to_all | solution.py:210
  (47 shorter events, 4.4 us)
Async XLA Ops:
  3.1 23.8 %all-to-all-start.1 = ((bf16[4,64,3584]{2,1,0:T(8,128)(2,1)}), bf16[4,64,3584]{2,1,0:T(8,128)(2,1)S(1)}, u32[]{:S(2)}, u32[]{:S(2)}) async-start(bf16[4,64,3584]{2,1,0:T(8,128)(2,1)} %broadcast_in_dim.18), calls=%async_computation.1 | async-start | bytes 3670016 | tf_op jit(solution)/shard_map/all_to_all | solution.py:28
  9.0 17.9 %collective-permute-start = (bf16[16,3584]{1,0:T(8,128)(2,1)S(1)}, bf16[16,3584]{1,0:T(8,128)(2,1)S(1)}, u32[]{:S(2)}, u32[]{:S(2)}) collective-permute-start(bf16[16,3584]{1,0:T(8,128)(2,1)S(1)} %dynamic-slice_bitcast_fusion), channel_id=1, source_target_pairs={{0,1},{1,0},{2,3},{3,2},{4,5},{5,4},{6,7},{7,6},{8,9},{9,8},{10,11... | collective-permute-start | bytes 344072 | tf_op jit(solution)/shard_map/ppermute | solution.py:22
  26.9 1.2 copy-start.1
  29.6 8.7 %copy-start = (bf16[1,2048,448]{1,2,0:T(8,128)(2,1)S(1)}, bf16[1,2048,448]{1,2,0:T(8,128)(2,1)}, u32[]{:S(2)}) copy-start(bf16[1,2048,448]{1,2,0:T(8,128)(2,1)} %param.10) | copy-start | bytes 5505028
  29.6 34.6 %all-to-all-start = ((bf16[16,16,3584]{2,1,0:T(8,128)(2,1)}), bf16[16,16,3584]{2,1,0:T(8,128)(2,1)}, u32[]{:S(2)}, u32[]{:S(2)}) async-start(bf16[16,16,3584]{2,1,0:T(8,128)(2,1)} %broadcast_in_dim.16), calls=%async_computation | async-start | bytes 3670016 | tf_op jit(solution)/shard_map/all_to_all | solution.py:28
  38.8 1.5 copy-start.2
  40.3 1.5 copy-start.3
  41.8 8.5 %copy-start.9 = (s32[256]{0:T(256)S(1)}, s32[256]{0:T(256)}, u32[]{:S(2)}) copy-start(s32[256]{0:T(256)} %param.9) | copy-start | bytes 3076
  41.8 9.5 %copy-start.7 = (f32[256]{0:T(256)S(1)}, f32[256]{0:T(256)}, u32[]{:S(2)}) copy-start(f32[256]{0:T(256)} %param.8) | copy-start | bytes 3076
  43.0 8.2 %collective-permute-start.3 = (f32[128,256]{1,0:T(8,128)S(1)}, f32[128,256]{1,0:T(8,128)S(1)}, u32[]{:S(2)}, u32[]{:S(2)}) collective-permute-start(f32[128,256]{1,0:T(8,128)S(1)} %get-tuple-element.19), channel_id=1, source_target_pairs={{0,256},{256,0},{1,257},{257,1},{2,258},{258,2},{3,259},{259,3},{4... | collective-permute-start | bytes 393224 | tf_op jit(solution)/shard_map/ppermute | solution.py:22
  51.3 21.3 %collective-permute-start.4 = (bf16[144,256]{1,0:T(8,128)(2,1)S(1)}, bf16[144,256]{1,0:T(8,128)(2,1)S(1)}, u32[]{:S(2)}, u32[]{:S(2)}) collective-permute-start(bf16[144,256]{1,0:T(8,128)(2,1)S(1)} %pad_maximum_fusion), channel_id=1, source_target_pairs={{0,1},{1,0},{2,3},{3,2},{4,5},{5,4},{6,7},{7,6},{8,9},{9,8},{10,11... | collective-permute-start | bytes 221192 | tf_op jit(solution)/shard_map/ppermute | solution.py:22
  64.1 1.5 copy-start.4
  67.8 5.7 %collective-permute-start.1 = (f32[128,256]{1,0:T(8,128)S(1)}, f32[128,256]{1,0:T(8,128)S(1)}, u32[]{:S(2)}, u32[]{:S(2)}) collective-permute-start(f32[128,256]{1,0:T(8,128)S(1)} %get-tuple-element.17), channel_id=1, source_target_pairs={{0,256},{256,0},{1,257},{257,1},{2,258},{258,2},{3,259},{259,3},{4... | collective-permute-start | bytes 393224 | tf_op jit(solution)/shard_map/ppermute | solution.py:22
  88.3 33.1 %collective-permute-start.5 = (bf16[4,400,256]{2,1,0:T(8,128)(2,1)S(1)}, bf16[4,400,256]{2,1,0:T(8,128)(2,1)S(1)}, u32[]{:S(2)}, u32[]{:S(2)}) collective-permute-start(bf16[4,400,256]{2,1,0:T(8,128)(2,1)S(1)} %all_to_all.41.g1), channel_id=1, source_target_pairs={{0,256},{256,0},{1,257},{257,1},{2,258},{258,2},{3,259},{259,3},{4... | collective-permute-start | bytes 2457608 | tf_op jit(solution)/shard_map/ppermute | solution.py:22
  91.6 16.8 %collective-permute-start.2 = (bf16[128,256]{1,0:T(8,128)(2,1)S(1)}, bf16[128,256]{1,0:T(8,128)(2,1)S(1)}, u32[]{:S(2)}, u32[]{:S(2)}) collective-permute-start(bf16[128,256]{1,0:T(8,128)(2,1)S(1)} %get-tuple-element.30), channel_id=1, source_target_pairs={{0,1},{1,0},{2,3},{3,2},{4,5},{5,4},{6,7},{7,6},{8,9},{9,8},{10,11... | collective-permute-start | bytes 196616 | tf_op jit(solution)/shard_map/ppermute | solution.py:22
  116.4 5.0 %collective-permute-start.6 = (bf16[4,128,256]{2,1,0:T(8,128)(2,1)S(1)}, bf16[4,128,256]{2,1,0:T(8,128)(2,1)S(1)}, u32[]{:S(2)}, u32[]{:S(2)}) collective-permute-start(bf16[4,128,256]{2,1,0:T(8,128)(2,1)S(1)} %all_to_all.42.g2), channel_id=1, source_target_pairs={{0,256},{256,0},{1,257},{257,1},{2,258},{258,2},{3,259},{259,3},{4... | collective-permute-start | bytes 786440 | tf_op jit(solution)/shard_map/ppermute | solution.py:22
  124.8 1.3 copy-start.5
  126.2 41.5 %all-to-all-start.4 = ((bf16[32,16,512]{2,1,0:T(8,128)(2,1)}), bf16[32,16,512]{2,1,0:T(8,128)(2,1)S(1)}, u32[]{:S(2)}, u32[]{:S(2)}) async-start(bf16[32,16,512]{2,1,0:T(8,128)(2,1)} %bitcast.10), calls=%async_computation.4 | async-start | bytes 1048576 | tf_op jit(solution)/shard_map/all_to_all | solution.py:179
  138.4 1.6 copy-start.6
  140.0 28.0 %copy-start.8 = (f32[1,448]{1,0:T(1,128)S(1)}, f32[1,448]{1,0:T(1,128)}, u32[]{:S(2)}) copy-start(f32[1,448]{1,0:T(1,128)} %param.11) | copy-start | bytes 5380
  169.4 25.6 %all-to-all-start.5 = ((f32[16,1,272]{2,1,0:T(1,128)}), f32[16,1,272]{2,1,0:T(1,128)S(1)}, u32[]{:S(2)}, u32[]{:S(2)}) async-start(f32[16,1,272]{2,1,0:T(1,128)} %all_to_all.32), calls=%async_computation.5 | async-start | bytes 49152 | tf_op jit(solution)/shard_map/all_to_all | solution.py:210

commit v4 on v3

v4 whole, which is shorter than its diff:
```python
import jax
import jax.numpy as jnp
from jax import lax
from jax.experimental import pallas as pl
from jax.experimental.pallas import tpu as pltpu
from jax.sharding import Mesh, PartitionSpec as P

D = 3584
smooth_width = 0.1
penalty = 0.0001
tiny_term = 1e-06
LAT = ("x", "zl")
TOK = ("y", "zh")
BF = jnp.bfloat16
F32 = jnp.float32
VMEM = pl.BlockSpec(memory_space=pltpu.VMEM)
HBM = pl.BlockSpec(memory_space=pltpu.HBM)
SMEM = pl.BlockSpec(memory_space=pltpu.SMEM)
NT = (((1,), (1,)), ((), ()))


def swap(value, axis):
    return lax.ppermute(value, axis, [(0, 1), (1, 0)])


def gather(value, axes):
    size = lax.axis_size(axes)
    copies = jnp.broadcast_to(value[None], (size,) + value.shape)
    return lax.all_to_all(copies, axes, 0, 0, tiled=False)


def encode_kernel(at_ref, b0, b1, b2, b3, far_ref, enc_ref, keep_ref, send_ref, a_ref, v_ref):
    step = pl.program_id(0)
    pair_at, zh_at, y_at = at_ref[0], at_ref[1], at_ref[3]

    @pl.when(step == 0)
    def _():
        v_ref[...] = jnp.zeros_like(v_ref)

    for ref, far in ((b0, 0), (b1, 3), (b2, 1), (b3, 2)):
        row = pl.multiple_of(zh_at * 256 + ((y_at + far) % 4) * 64, 64)
        a_ref[pl.ds(row, 64), :] = ref[...]
    a_ref[pl.ds(pl.multiple_of((1 - zh_at) * 256, 256), 256), :] = far_ref[...]
    v_ref[...] += jnp.dot(a_ref[...], enc_ref[...], preferred_element_type=F32)

    @pl.when(step == pl.num_programs(0) - 1)
    def _():
        for half in range(2):
            kept = pl.multiple_of(half * 256 + pair_at * 128, 128)
            sent = pl.multiple_of(half * 256 + (1 - pair_at) * 128, 128)
            keep_ref[half * 128 : (half + 1) * 128, :] = v_ref[pl.ds(kept, 128), :]
            send_ref[half * 128 : (half + 1) * 128, :] = v_ref[pl.ds(sent, 128), :]


def decode_kernel(
    at_ref,
    g1,
    g2,
    p1,
    p2,
    dec_hbm,
    out_hbm,
    f_hbm,
    nsq_ref,
    out_ref,
    f_ref,
    dec_ref,
    part_ref,
    wide_ref,
    norm_ref,
    sems,
):
    pair_at, zh_at = at_ref[0], at_ref[1]
    parts = [
        pltpu.make_async_copy(ref.at[:, pl.ds(256, 16)], part_ref.at[k], sems.at[k])
        for k, ref in enumerate((g1, g2))
    ]
    loads = [pltpu.make_async_copy(dec_hbm, dec_ref, sems.at[2])]
    for half, own, oth in ((pair_at, g1, g2), (1 - pair_at, p1, p2)):
        row = pl.ds(pl.multiple_of(half * 256, 256), 256)
        for y in range(4):
            for ref, zh in ((own, zh_at), (oth, 1 - zh_at)):
                col = pl.ds(pl.multiple_of((2 * y + zh) * 256, 256), 256)
                loads.append(
                    pltpu.make_async_copy(
                        ref.at[y, pl.ds(0, 256)], f_ref.at[row, col], sems.at[2 + len(loads)]
                    )
                )
    for copy in parts + loads:
        copy.start()

    for copy in parts:
        copy.wait()
    nsq = jnp.zeros((8, 256), F32)
    for k in range(2):
        for y in range(4):
            rows = part_ref[k, y].astype(F32)
            nsq = nsq + (rows[0:8] + rows[8:16])
    nsq_ref[...] = nsq
    norm = jnp.sqrt(nsq) * 0.125
    high = norm.astype(BF).astype(F32)
    wide_ref[...] = jnp.zeros_like(wide_ref)
    for k in range(8):
        wide_ref[0:1, k * 256 : (k + 1) * 256] = high[k : k + 1]
        wide_ref[1:2, k * 256 : (k + 1) * 256] = (norm - high)[k : k + 1]
    norm_ref[...] = wide_ref[...].astype(BF)

    for copy in loads:
        copy.wait()
    feats_out = pltpu.make_async_copy(f_ref, f_hbm, sems.at[19])
    feats_out.start()
    copies = []
    for half in range(2):
        feats = f_ref[half * 256 : (half + 1) * 256, :]
        value = lax.dot_general(feats, dec_ref[...], NT, preferred_element_type=F32)
        sparse = lax.dot_general(feats, norm_ref[...], NT, preferred_element_type=F32)
        value, sparse = value.astype(BF), sparse.astype(BF)
        for zh in range(2):
            for yy in range(2):
                src = (zh * 2 + yy) * 64
                dst = ((half * 2 + yy) * 2 + zh) * 64
                out_ref[dst : dst + 64, 0:448] = value[src : src + 64, :]
                out_ref[dst : dst + 64, 448:512] = sparse[src : src + 64, :]
        rows = pl.ds(half * 256, 256)
        copies.append(
            pltpu.make_async_copy(out_ref.at[rows], out_hbm.at[rows], sems.at[20 + half])
        )
        copies[half].start()
    for copy in copies:
        copy.wait()
    feats_out.wait()


def numer_kernel(
    at_ref, b0, b1, b2, b3, far_ref, f_ref, dec_ref, num_ref, msq_ref, own_ref, a_ref
):
    zh_at, tok_at, y_at, lat_at = at_ref[1], at_ref[2], at_ref[3], at_ref[4]
    base = pl.multiple_of((tok_at // 2) * 896 + (tok_at % 2) * 384, 128)

    def take(ref, row, y, zh):
        window = ref[pl.ds(row, 64), pl.ds(base, 512)]
        cols = jnp.where(tok_at % 2 == 1, window[:, 64:512], window[:, 0:448])
        at = (y // 2) * 256 + zh * 128 + (y % 2) * 64
        a_ref[pl.ds(pl.multiple_of(at, 64), 64), :] = cols

    for ref, far in ((b0, 0), (b1, 3), (b2, 1), (b3, 2)):
        take(ref, 0, (y_at + far) % 4, zh_at)
    for y in range(4):
        take(far_ref, y * 64, y, 1 - zh_at)
    own_y, own_zh = lat_at // 8, (lat_at // 4) % 2
    own_at = (own_y // 2) * 256 + own_zh * 128 + (own_y % 2) * 64 + (lat_at % 4) * 16
    own_ref[...] = a_ref[pl.ds(pl.multiple_of(own_at, 16), 16), :]
    for k in range(8):
        cols = slice(k * 256, (k + 1) * 256)
        inner = jnp.dot(a_ref[...], dec_ref[:, cols], preferred_element_type=F32)
        num_ref[k : k + 1, :] = jnp.sum(
            inner * f_ref[:, cols].astype(F32), axis=0, keepdims=True
        )
    feats = f_ref[:, pl.ds(pl.multiple_of(tok_at * 256, 256), 256)].astype(F32)
    msq_ref[...] = jnp.sum(feats * feats, axis=0, keepdims=True)


def call(kernel, name, flops, outs, count, scratch, outside=0, spaces=None):
    return pl.pallas_call(
        kernel,
        out_shape=tuple(jax.ShapeDtypeStruct(shape, kind) for shape, kind in outs),
        in_specs=[SMEM] + [VMEM] * count + [HBM] * outside,
        out_specs=spaces or (VMEM,) * len(outs),
        scratch_shapes=scratch,
        compiler_params=pltpu.CompilerParams(vmem_limit_bytes=60 << 20),
        cost_estimate=pl.CostEstimate(
            flops=flops, bytes_accessed=6 << 20, transcendentals=0
        ),
        name=name,
    )


def body(activations, enc_weight, enc_bias, thresholds, dec_weight, dec_bias):
    pair_at = lax.axis_index("pair")
    x_at = lax.axis_index("x")
    zh_at = lax.axis_index("zh")
    tok_at = lax.axis_index(TOK)
    lat_at = lax.axis_index(LAT)
    act = activations[0]
    enc = enc_weight[0]
    dec = dec_weight[0]
    dec_t = dec.T
    own, width = enc.shape[1], dec.shape[1]
    tokens = 8 * act.shape[0]
    rows = tokens // lax.axis_size(LAT)
    y_at = lax.axis_index("y")
    at = jnp.stack([pair_at, zh_at, tok_at, y_at, lat_at]).astype(jnp.int32)

    quarter = swap(lax.dynamic_slice_in_dim(act, x_at * 16, 16, 0), "zh")
    blocks = [act] + [
        lax.ppermute(act, "y", [(i, (i + k) % 4) for i in range(4)]) for k in (1, 3, 2)
    ]
    copies = jnp.broadcast_to(quarter[None], (16, 16, D))
    copies, blocks[1], blocks[2] = lax.optimization_barrier((copies, blocks[1], blocks[2]))
    far = lax.all_to_all(copies, ("y", "x"), 0, 0).reshape(256, D)

    dec_wide = dec.astype(F32)
    nsq_part = jnp.sum(dec_wide * dec_wide, axis=1).reshape(8, own)

    def split(value):
        high = value.astype(BF)
        return [high, (value - high.astype(F32)).astype(BF)]

    thresh_level = thresholds.astype(F32) * 0.25

    def pick(rows, cols, at_k):
        return pl.BlockSpec((rows, cols), at_k)

    chunk = 512
    along = [pick(64, chunk, lambda k: (0, k))] * 4 + [
        pick(256, chunk, lambda k: (0, k)),
        pick(chunk, own, lambda k: (k, 0)),
    ]
    keep, send = pl.pallas_call(
        encode_kernel,
        grid=(D // chunk,),
        out_shape=(jax.ShapeDtypeStruct((256, own), F32),) * 2,
        in_specs=[SMEM] + along,
        out_specs=(pick(256, own, lambda k: (0, 0)),) * 2,
        scratch_shapes=[pltpu.VMEM((tokens, chunk), BF), pltpu.VMEM((tokens, own), F32)],
        compiler_params=pltpu.CompilerParams(vmem_limit_bytes=60 << 20),
        cost_estimate=pl.CostEstimate(
            flops=2 * tokens * D * own, bytes_accessed=6 << 20, transcendentals=0
        ),
        name="encode",
    )(at, *blocks, far, enc)
    pre = keep + swap(send, "pair") + enc_bias
    feats = (pre * jax.nn.sigmoid((pre - thresh_level) / smooth_width)).astype(BF)
    feats = jnp.concatenate([feats] + split(nsq_part), axis=0)
    over = swap(feats, "zh")
    g1 = gather(feats, "y")
    p1 = swap(g1, "pair")
    over, g1 = lax.optimization_barrier((over, g1))
    g2 = gather(over, "y")
    p2 = swap(g2, "pair")

    payload, block_feats, nsq_all = call(
        decode_kernel,
        "decode",
        2 * tokens * 8 * own * 512,
        [((tokens, 512), BF), ((tokens, 8 * own), BF), ((8, own), F32)],
        0,
        [
            pltpu.VMEM((tokens, 512), BF),
            pltpu.VMEM((tokens, 8 * own), BF),
            pltpu.VMEM((width, 8 * own), BF),
            pltpu.VMEM((2, 4, 16, own), BF),
            pltpu.VMEM((64, 8 * own), F32),
            pltpu.VMEM((64, 8 * own), BF),
            pltpu.SemaphoreType.DMA((22,)),
        ],
        5,
        (HBM, HBM, VMEM),
    )(at, g1, g2, p1, p2, dec_t)
    nsq_own = lax.dynamic_index_in_dim(nsq_all, tok_at, 0, keepdims=False)
    arrived = lax.all_to_all(payload, LAT, 0, 0, tiled=True)

    num_part, sum_sq, act_own = call(
        numer_kernel,
        "numer",
        2 * tokens * 8 * own * width,
        [((8, own), F32), ((1, own), F32), ((rows, width), BF)],
        7,
        [pltpu.VMEM((tokens, width), BF)],
    )(at, *blocks, far, block_feats, dec_t)
    mean_sq = sum_sq[0] / tokens

    total = jnp.sum(arrived.reshape(32, rows, 512).astype(F32), axis=0)
    recon_vals = total[:, :width] + dec_bias[0]
    sparse = total[:, width] + total[:, width + 1]
    residue = act_own.astype(F32) - recon_vals
    own_terms = jnp.sum(residue * residue, axis=1) / (2.0 * D) + penalty * sparse

    last = jnp.concatenate(
        [
            jnp.broadcast_to(num_part.reshape(1, 8, own), (2, 8, own)),
            jnp.broadcast_to(own_terms, (2, 8, rows)),
        ],
        axis=2,
    ).reshape(16, own + rows)
    got = lax.all_to_all(last, ("pair",) + TOK, 0, 0, tiled=True)
    token_loss = jnp.sum(got[:, own:], axis=0)
    mine = lax.dynamic_slice_in_dim(got, pair_at * 8, 8, 0)[:, :own]
    num_own = jnp.sum(mine, axis=0) / tokens
    scaling = num_own / (nsq_own * mean_sq + tiny_term)
    return (recon_vals.astype(BF)[None], token_loss, scaling[None])


def solution(mesh):
    fine = Mesh(mesh.devices.reshape(2, 4, 8, 4, 2), ("pair", "x", "zl", "y", "zh"))
    return jax.shard_map(
        body,
        mesh=fine,
        in_specs=(
            P("pair", TOK, None),
            P("pair", None, LAT + TOK),
            P(LAT + TOK),
            P(LAT + TOK),
            P("pair", LAT, TOK),
            P("pair", TOK),
        ),
        out_specs=(P("pair", LAT, TOK), P(LAT), P("pair", LAT + TOK)),
        check_vma=False,
    )
```

time: 197 us -> 209 us (1.061)
  waiting for transfers between devices: 48.1 us -> 75.8 us
  blocking collectives: 22.6 us -> 0 us
  Pallas kernels: 8.57 us -> 18.5 us
  local copies, waits for them, and re-layouts: 14.2 us -> 7.7 us
  other arithmetic: 2.76 us -> 5.05 us
    ppermute x0 -> x3, waiting for transfers between devices: none -> 24.9 us  [body(): lax.ppermute(act, 'y', [(i, (i + k) % 4) for i in range(4)])]
    all_to_all x2 -> x0, blocking collectives: 22.6 us -> none  [gather(): return lax.all_to_all(copies, axes, 0, 0, tiled=False)]
    ppermute x7 -> x5, starting transfers between devices: 61.8 us -> 41.7 us  [swap(): return lax.ppermute(value, axis, [(0, 1), (1, 0)])]
    ppermute x0 -> x3, starting transfers between devices: none -> 12.1 us  [body(): lax.ppermute(act, 'y', [(i, (i + k) % 4) for i in range(4)])]
    all_to_all x1, starting transfers between devices: 12.2 us -> 20.8 us  [body(): arrived = lax.all_to_all(payload, LAT, 0, 0, tiled=True)]
    unnamed x23 -> x26, local copies, waits for them, and re-layouts: 8.68 us -> 1.61 us
    all_to_all x0 -> x1, starting transfers between devices: none -> 6.69 us  [body(): far = lax.all_to_all(copies, ('y', 'x'), 0, 0).reshape(256, D)]
    all_to_all x2, starting transfers between devices: 13.7 us -> 7.34 us  [gather(): return lax.all_to_all(copies, axes, 0, 0, tiled=False)]
  transfers between devices with their start and end apart: 11 -> 13, of which waited for: 7 -> 8; matrix products, arithmetic and copies ran while one was open for 1% -> 1% of each run, Pallas kernels for 3% -> 3%
where the time goes in v4:
time: 209 us; the launch traced here: 208 us
  starting transfers between devices  99.7 us (48%)
  waiting for transfers between devices  75.8 us (36%)
  Pallas kernels  18.5 us (9%)
  local copies, waits for them, and re-layouts  7.7 us (4%)
  other arithmetic  5.05 us (2%)
    ppermute x5, starting transfers between devices, swap(): return lax.ppermute(value, axis, [(0, 1), (1, 0)])  41.7 us
    ppermute x3, waiting for transfers between devices, body(): lax.ppermute(act, 'y', [(i, (i + k) % 4) for i in range(4)])  24.9 us
    all_to_all x1, waiting for transfers between devices, body(): arrived = lax.all_to_all(payload, LAT, 0, 0, tiled=True)  23.9 us
    all_to_all x1, starting transfers between devices, body(): arrived = lax.all_to_all(payload, LAT, 0, 0, tiled=True)  20.8 us
    all_to_all x1, waiting for transfers between devices, body(): got = lax.all_to_all(last, ('pair',) + TOK, 0, 0, tiled=True)  14.2 us
    ppermute x3, starting transfers between devices, body(): lax.ppermute(act, 'y', [(i, (i + k) % 4) for i in range(4)])  12.1 us
    all_to_all x1, starting transfers between devices, body(): got = lax.all_to_all(last, ('pair',) + TOK, 0, 0, tiled=True)  11 us
    ppermute x5, waiting for transfers between devices, swap(): return lax.ppermute(value, axis, [(0, 1), (1, 0)])  8.79 us
  transfers between devices with their start and end apart: 13, of which 8 were waited for; matrix products, arithmetic and copies ran while one was open for 1% of the time, Pallas kernels for 3%

profile of v4, /device:TPU:1, one launch (start us, length us, event | category | flops | bytes accessed | tf_op | source)
XLA Modules:
  0.0 207.6 jit_solution(12263872127116068441)
XLA Ops:
  0.6 5.5 %collective-permute-start.2 = (bf16[64,3584]{1,0:T(8,128)(2,1)}, bf16[64,3584]{1,0:T(8,128)(2,1)S(1)}, u32[]{:S(2)}, u32[]{:S(2)}) collective-permute-start(bf16[64,3584]{1,0:T(8,128)(2,1)} %bitcast.27), channel_id=1, source_target_pairs={{0,6},{2,0},{4,2},{6,4},{1,7},{3,1},{5,3},{7,5},{8,14},{10,8},{12,... | collective-permute-start | bytes 1376264 | tf_op jit(solution)/shard_map/ppermute | solution.py:196
  6.1 1.9 collective-permute-start.1
  8.0 0.9 dynamic-slice_bitcast_fusion
  9.0 15.4 %collective-permute-start = (bf16[16,3584]{1,0:T(8,128)(2,1)S(1)}, bf16[16,3584]{1,0:T(8,128)(2,1)S(1)}, u32[]{:S(2)}, u32[]{:S(2)}) collective-permute-start(bf16[16,3584]{1,0:T(8,128)(2,1)S(1)} %dynamic-slice_bitcast_fusion), channel_id=1, source_target_pairs={{0,1},{1,0},{2,3},{3,2},{4,5},{5,4},{6,7},{7,6},{8,9},{9,8},{10,11... | collective-permute-start | bytes 344072 | tf_op jit(solution)/shard_map/ppermute | solution.py:23
  24.4 2.5 %collective-permute-done = bf16[16,3584]{1,0:T(8,128)(2,1)S(1)} collective-permute-done((bf16[16,3584]{1,0:T(8,128)(2,1)S(1)}, bf16[16,3584]{1,0:T(8,128)(2,1)S(1)}, u32[]{:S(2)}, u32[]{:S(2)}) %collective-permute-start) | collective-permute-done | bytes 114720 | tf_op jit(solution)/shard_map/ppermute | solution.py:23
  26.9 1.5 broadcast_in_dim.12
  28.4 6.7 %all-to-all-start = ((bf16[16,16,3584]{2,1,0:T(8,128)(2,1)}), bf16[16,16,3584]{2,1,0:T(8,128)(2,1)}, u32[]{:S(2)}, u32[]{:S(2)}) async-start(bf16[16,16,3584]{2,1,0:T(8,128)(2,1)} %broadcast_in_dim.12), calls=%async_computation | async-start | bytes 3670016 | tf_op jit(solution)/shard_map/all_to_all | solution.py:200
  35.1 4.7 %collective-permute-start.3 = (bf16[64,3584]{1,0:T(8,128)(2,1)S(1)}, bf16[64,3584]{1,0:T(8,128)(2,1)S(1)}, u32[]{:S(2)}, u32[]{:S(2)}) collective-permute-start(bf16[64,3584]{1,0:T(8,128)(2,1)S(1)} %bitcast.31), channel_id=1, source_target_pairs={{0,4},{2,6},{4,0},{6,2},{1,5},{3,7},{5,1},{7,3},{8,12},{10,14},{12... | collective-permute-start | bytes 1376264 | tf_op jit(solution)/shard_map/ppermute | solution.py:196
  40.9 24.9 %collective-permute-done.3.b3 = bf16[64,3584]{1,0:T(8,128)(2,1)S(1)} collective-permute-done((bf16[64,3584]{1,0:T(8,128)(2,1)S(1)}, bf16[64,3584]{1,0:T(8,128)(2,1)S(1)}, u32[]{:S(2)}, u32[]{:S(2)}) %collective-permute-start.3) | collective-permute-done | bytes 458784 | tf_op jit(solution)/shard_map/ppermute | solution.py:196
  66.5 7.0 %encode.1 = (f32[256,256]{1,0:T(8,128)}, f32[256,256]{1,0:T(8,128)}) custom-call(s32[5]{0:T(128)} %stack.23.at_ref, bf16[64,3584]{1,0:T(8,128)(2,1)} %bitcast.29, bf16[64,3584]{1,0:T(8,128)(2,1)} %copy-done.5, bf16[64,3584]{1,0:T(8,128)(2,1)} %copy-done.4, bf16[64,3584]{1,0:T(8,128)(2,1)} %copy-done.6, bf16[256,3584]{1,0:T(8,128)(2,1)} %bitcast.7.far_ref, ...), custom_call_target="tpu_custom_call" | custom-call | flops 939524096 | bytes 6291456 | tf_op jit(solution)/shard_map/encode/pallas_call | solution.py:219
  73.5 5.5 %collective-permute-start.4 = (f32[256,256]{1,0:T(8,128)}, f32[256,256]{1,0:T(8,128)S(1)}, u32[]{:S(2)}, u32[]{:S(2)}) collective-permute-start(f32[256,256]{1,0:T(8,128)} %get-tuple-element.20), channel_id=1, source_target_pairs={{0,256},{256,0},{1,257},{257,1},{2,258},{258,2},{3,259},{259,3},{4... | collective-permute-start | bytes 786440 | tf_op jit(solution)/shard_map/ppermute | solution.py:23
  79.0 1.3 collective-permute-done.4
  80.3 1.0 multiply_convert_fusion
  81.4 0.8 broadcast_in_dim.13
  82.2 3.5 %all-to-all-start.1 = ((bf16[4,272,256]{2,1,0:T(8,128)(2,1)}), bf16[4,272,256]{2,1,0:T(8,128)(2,1)S(1)}, u32[]{:S(2)}, u32[]{:S(2)}) async-start(bf16[4,272,256]{2,1,0:T(8,128)(2,1)} %broadcast_in_dim.13), calls=%async_computation.1 | async-start | bytes 1114112 | tf_op jit(solution)/shard_map/all_to_all | solution.py:29
  85.7 12.1 %collective-permute-start.5 = (bf16[272,256]{1,0:T(8,128)(2,1)S(1)}, bf16[272,256]{1,0:T(8,128)(2,1)S(1)}, u32[]{:S(2)}, u32[]{:S(2)}) collective-permute-start(bf16[272,256]{1,0:T(8,128)(2,1)S(1)} %pad_maximum_fusion), channel_id=1, source_target_pairs={{0,1},{1,0},{2,3},{3,2},{4,5},{5,4},{6,7},{7,6},{8,9},{9,8},{10,11... | collective-permute-start | bytes 417800 | tf_op jit(solution)/shard_map/ppermute | solution.py:23
  97.9 3.5 %collective-permute-done.5 = bf16[272,256]{1,0:T(8,128)(2,1)S(1)} collective-permute-done((bf16[272,256]{1,0:T(8,128)(2,1)S(1)}, bf16[272,256]{1,0:T(8,128)(2,1)S(1)}, u32[]{:S(2)}, u32[]{:S(2)}) %collective-permute-start.5) | collective-permute-done | bytes 139296 | tf_op jit(solution)/shard_map/ppermute | solution.py:23
  101.4 0.9 broadcast_in_dim.14
  102.2 3.9 %all-to-all-start.2 = ((bf16[4,272,256]{2,1,0:T(8,128)(2,1)}), bf16[4,272,256]{2,1,0:T(8,128)(2,1)S(1)}, u32[]{:S(2)}, u32[]{:S(2)}) async-start(bf16[4,272,256]{2,1,0:T(8,128)(2,1)} %broadcast_in_dim.14), calls=%async_computation.2 | async-start | bytes 1114112 | tf_op jit(solution)/shard_map/all_to_all | solution.py:29
  106.1 3.7 %collective-permute-start.6 = (bf16[4,272,256]{2,1,0:T(8,128)(2,1)S(1)}, bf16[4,272,256]{2,1,0:T(8,128)(2,1)S(1)}, u32[]{:S(2)}, u32[]{:S(2)}) collective-permute-start(bf16[4,272,256]{2,1,0:T(8,128)(2,1)S(1)} %all-to-all-done.1.g1), channel_id=1, source_target_pairs={{0,256},{256,0},{1,257},{257,1},{2,258},{258,2},{3,259},{259,3},{4... | collective-permute-start | bytes 1671176 | tf_op jit(solution)/shard_map/ppermute | solution.py:23
  109.8 4.0 %all-to-all-done.2.g2 = bf16[4,272,256]{2,1,0:T(8,128)(2,1)S(1)} async-done(((bf16[4,272,256]{2,1,0:T(8,128)(2,1)}), bf16[4,272,256]{2,1,0:T(8,128)(2,1)S(1)}, u32[]{:S(2)}, u32[]{:S(2)}) %all-to-all-start.2) | async-done | bytes 557088 | tf_op jit(solution)/shard_map/all_to_all | solution.py:29
  113.8 4.9 %collective-permute-start.7 = (bf16[4,272,256]{2,1,0:T(8,128)(2,1)S(1)}, bf16[4,272,256]{2,1,0:T(8,128)(2,1)S(1)}, u32[]{:S(2)}, u32[]{:S(2)}) collective-permute-start(bf16[4,272,256]{2,1,0:T(8,128)(2,1)S(1)} %all-to-all-done.2.g2), channel_id=1, source_target_pairs={{0,256},{256,0},{1,257},{257,1},{2,258},{258,2},{3,259},{259,3},{4... | collective-permute-start | bytes 1671176 | tf_op jit(solution)/shard_map/ppermute | solution.py:23
  118.8 1.5 collective-permute-done.7.p2
  120.4 0.8 copy-done.8
  121.2 6.1 %decode.1 = (bf16[512,512]{1,0:T(8,128)(2,1)}, bf16[512,2048]{1,0:T(8,128)(2,1)}, f32[8,256]{1,0:T(8,128)}) custom-call(s32[5]{0:T(128)} %stack.23.at_ref, bf16[4,272,256]{2,1,0:T(8,128)(2,1)} %copy-done.2, bf16[4,272,256]{2,1,0:T(8,128)(2,1)} %copy-done.3, bf16[4,272,256]{2,1,0:T(8,128)(2,1)} %copy-done.7, bf16[4,272,256]{2,1,0:T(8,128)(2,1)} %copy-done.8, ...), custom_call_target="tpu_custom_call" | custom-call | flops 1073741824 | bytes 6291456 | tf_op jit(solution)/shard_map/decode/pallas_call | solution.py:242
  127.3 20.8 %all-to-all-start.3 = ((bf16[32,16,512]{2,1,0:T(8,128)(2,1)}), bf16[32,16,512]{2,1,0:T(8,128)(2,1)S(1)}, u32[]{:S(2)}, u32[]{:S(2)}) async-start(bf16[32,16,512]{2,1,0:T(8,128)(2,1)} %bitcast.33), calls=%async_computation.3 | async-start | bytes 1048576 | tf_op jit(solution)/shard_map/all_to_all | solution.py:261
  148.1 5.4 %numer.1 = (f32[8,256]{1,0:T(8,128)}, f32[1,256]{1,0:T(1,128)}, bf16[16,448]{1,0:T(8,128)(2,1)}) custom-call(s32[5]{0:T(128)} %stack.23.at_ref, bf16[64,3584]{1,0:T(8,128)(2,1)} %bitcast.30, bf16[64,3584]{1,0:T(8,128)(2,1)} %copy-done.5, bf16[64,3584]{1,0:T(8,128)(2,1)} %copy-done.4, bf16[64,3584]{1,0:T(8,128)(2,1)} %copy-done.6, ...), custom_call_target="tpu_custom_call" | custom-call | flops 939524096 | bytes 6291456 | tf_op jit(solution)/shard_map/numer/pallas_call | solution.py:263
  153.6 23.9 %all-to-all-done.3 = bf16[32,16,512]{2,1,0:T(8,128)(2,1)S(1)} async-done(((bf16[32,16,512]{2,1,0:T(8,128)(2,1)}), bf16[32,16,512]{2,1,0:T(8,128)(2,1)S(1)}, u32[]{:S(2)}, u32[]{:S(2)}) %all-to-all-start.3) | async-done | bytes 524320 | tf_op jit(solution)/shard_map/all_to_all | solution.py:261
  177.8 1.4 multiply_reduce_fusion.1
  180.6 11.0 %all-to-all-start.4 = ((f32[16,1,272]{2,1,0:T(1,128)}), f32[16,1,272]{2,1,0:T(1,128)S(1)}, u32[]{:S(2)}, u32[]{:S(2)}) async-start(f32[16,1,272]{2,1,0:T(1,128)} %all_to_all.28), calls=%async_computation.4 | async-start | bytes 49152 | tf_op jit(solution)/shard_map/all_to_all | solution.py:286
  191.5 14.2 %all-to-all-done.4 = f32[16,1,272]{2,1,0:T(1,128)S(1)} async-done(((f32[16,1,272]{2,1,0:T(1,128)}), f32[16,1,272]{2,1,0:T(1,128)S(1)}, u32[]{:S(2)}, u32[]{:S(2)}) %all-to-all-start.4) | async-done | bytes 17440 | tf_op jit(solution)/shard_map/all_to_all | solution.py:286
  206.3 1.3 add_divide_fusion
  (47 shorter events, 4.0 us)
Async XLA Ops:
  0.6 26.2 %collective-permute-start.2 = (bf16[64,3584]{1,0:T(8,128)(2,1)}, bf16[64,3584]{1,0:T(8,128)(2,1)S(1)}, u32[]{:S(2)}, u32[]{:S(2)}) collective-permute-start(bf16[64,3584]{1,0:T(8,128)(2,1)} %bitcast.27), channel_id=1, source_target_pairs={{0,6},{2,0},{4,2},{6,4},{1,7},{3,1},{5,3},{7,5},{8,14},{10,8},{12,... | collective-permute-start | bytes 1376264 | tf_op jit(solution)/shard_map/ppermute | solution.py:196
  6.1 20.8 %collective-permute-start.1 = (bf16[64,3584]{1,0:T(8,128)(2,1)}, bf16[64,3584]{1,0:T(8,128)(2,1)S(1)}, u32[]{:S(2)}, u32[]{:S(2)}) collective-permute-start(bf16[64,3584]{1,0:T(8,128)(2,1)} %bitcast.28), channel_id=1, source_target_pairs={{0,2},{2,4},{4,6},{6,0},{1,3},{3,5},{5,7},{7,1},{8,10},{10,12},{12... | collective-permute-start | bytes 1376264 | tf_op jit(solution)/shard_map/ppermute | solution.py:196
  9.0 17.9 %collective-permute-start = (bf16[16,3584]{1,0:T(8,128)(2,1)S(1)}, bf16[16,3584]{1,0:T(8,128)(2,1)S(1)}, u32[]{:S(2)}, u32[]{:S(2)}) collective-permute-start(bf16[16,3584]{1,0:T(8,128)(2,1)S(1)} %dynamic-slice_bitcast_fusion), channel_id=1, source_target_pairs={{0,1},{1,0},{2,3},{3,2},{4,5},{5,4},{6,7},{7,6},{8,9},{9,8},{10,11... | collective-permute-start | bytes 344072 | tf_op jit(solution)/shard_map/ppermute | solution.py:23
  26.9 1.5 copy-start.4
  26.9 1.5 copy-start.5
  28.4 6.7 %copy-start.1 = (bf16[1,64,3584]{2,1,0:T(8,128)(2,1)S(1)}, bf16[1,64,3584]{2,1,0:T(8,128)(2,1)}, u32[]{:S(2)}) copy-start(bf16[1,64,3584]{2,1,0:T(8,128)(2,1)} %param.6) | copy-start | bytes 1376260
  28.4 12.1 %copy-start = (bf16[1,2048,448]{1,2,0:T(8,128)(2,1)S(1)}, bf16[1,2048,448]{1,2,0:T(8,128)(2,1)}, u32[]{:S(2)}) copy-start(bf16[1,2048,448]{1,2,0:T(8,128)(2,1)} %param.10) | copy-start | bytes 5505028
  28.4 37.3 %all-to-all-start = ((bf16[16,16,3584]{2,1,0:T(8,128)(2,1)}), bf16[16,16,3584]{2,1,0:T(8,128)(2,1)}, u32[]{:S(2)}, u32[]{:S(2)}) async-start(bf16[16,16,3584]{2,1,0:T(8,128)(2,1)} %broadcast_in_dim.12), calls=%async_computation | async-start | bytes 3670016 | tf_op jit(solution)/shard_map/all_to_all | solution.py:200
  35.1 30.6 %collective-permute-start.3 = (bf16[64,3584]{1,0:T(8,128)(2,1)S(1)}, bf16[64,3584]{1,0:T(8,128)(2,1)S(1)}, u32[]{:S(2)}, u32[]{:S(2)}) collective-permute-start(bf16[64,3584]{1,0:T(8,128)(2,1)S(1)} %bitcast.31), channel_id=1, source_target_pairs={{0,4},{2,6},{4,0},{6,2},{1,5},{3,7},{5,1},{7,3},{8,12},{10,14},{12... | collective-permute-start | bytes 1376264 | tf_op jit(solution)/shard_map/ppermute | solution.py:196
  65.8 0.8 copy-start.6
  66.5 12.4 %copy-start.11 = (s32[256]{0:T(256)S(1)}, s32[256]{0:T(256)}, u32[]{:S(2)}) copy-start(s32[256]{0:T(256)} %param.9) | copy-start | bytes 3076
  66.5 13.8 %copy-start.10 = (f32[256]{0:T(256)S(1)}, f32[256]{0:T(256)}, u32[]{:S(2)}) copy-start(f32[256]{0:T(256)} %param.8) | copy-start | bytes 3076
  73.5 6.8 %collective-permute-start.4 = (f32[256,256]{1,0:T(8,128)}, f32[256,256]{1,0:T(8,128)S(1)}, u32[]{:S(2)}, u32[]{:S(2)}) collective-permute-start(f32[256,256]{1,0:T(8,128)} %get-tuple-element.20), channel_id=1, source_target_pairs={{0,256},{256,0},{1,257},{257,1},{2,258},{258,2},{3,259},{259,3},{4... | collective-permute-start | bytes 786440 | tf_op jit(solution)/shard_map/ppermute | solution.py:23
  82.2 19.1 %all-to-all-start.1 = ((bf16[4,272,256]{2,1,0:T(8,128)(2,1)}), bf16[4,272,256]{2,1,0:T(8,128)(2,1)S(1)}, u32[]{:S(2)}, u32[]{:S(2)}) async-start(bf16[4,272,256]{2,1,0:T(8,128)(2,1)} %broadcast_in_dim.13), calls=%async_computation.1 | async-start | bytes 1114112 | tf_op jit(solution)/shard_map/all_to_all | solution.py:29
  85.7 15.6 %collective-permute-start.5 = (bf16[272,256]{1,0:T(8,128)(2,1)S(1)}, bf16[272,256]{1,0:T(8,128)(2,1)S(1)}, u32[]{:S(2)}, u32[]{:S(2)}) collective-permute-start(bf16[272,256]{1,0:T(8,128)(2,1)S(1)} %pad_maximum_fusion), channel_id=1, source_target_pairs={{0,1},{1,0},{2,3},{3,2},{4,5},{5,4},{6,7},{7,6},{8,9},{9,8},{10,11... | collective-permute-start | bytes 417800 | tf_op jit(solution)/shard_map/ppermute | solution.py:23
  101.4 19.0 %copy-start.2 = (bf16[4,272,256]{2,1,0:T(8,128)(2,1)}, bf16[4,272,256]{2,1,0:T(8,128)(2,1)S(1)}, u32[]{:S(2)}) copy-start(bf16[4,272,256]{2,1,0:T(8,128)(2,1)S(1)} %all-to-all-done.1.g1) | copy-start | bytes 1671172
  102.2 11.6 %all-to-all-start.2 = ((bf16[4,272,256]{2,1,0:T(8,128)(2,1)}), bf16[4,272,256]{2,1,0:T(8,128)(2,1)S(1)}, u32[]{:S(2)}, u32[]{:S(2)}) async-start(bf16[4,272,256]{2,1,0:T(8,128)(2,1)} %broadcast_in_dim.14), calls=%async_computation.2 | async-start | bytes 1114112 | tf_op jit(solution)/shard_map/all_to_all | solution.py:29
  106.1 12.7 %collective-permute-start.6 = (bf16[4,272,256]{2,1,0:T(8,128)(2,1)S(1)}, bf16[4,272,256]{2,1,0:T(8,128)(2,1)S(1)}, u32[]{:S(2)}, u32[]{:S(2)}) collective-permute-start(bf16[4,272,256]{2,1,0:T(8,128)(2,1)S(1)} %all-to-all-done.1.g1), channel_id=1, source_target_pairs={{0,256},{256,0},{1,257},{257,1},{2,258},{258,2},{3,259},{259,3},{4... | collective-permute-start | bytes 1671176 | tf_op jit(solution)/shard_map/ppermute | solution.py:23
  113.8 6.5 %copy-start.3 = (bf16[4,272,256]{2,1,0:T(8,128)(2,1)}, bf16[4,272,256]{2,1,0:T(8,128)(2,1)S(1)}, u32[]{:S(2)}) copy-start(bf16[4,272,256]{2,1,0:T(8,128)(2,1)S(1)} %all-to-all-done.2.g2) | copy-start | bytes 1671172
  113.8 6.5 %collective-permute-start.7 = (bf16[4,272,256]{2,1,0:T(8,128)(2,1)S(1)}, bf16[4,272,256]{2,1,0:T(8,128)(2,1)S(1)}, u32[]{:S(2)}, u32[]{:S(2)}) collective-permute-start(bf16[4,272,256]{2,1,0:T(8,128)(2,1)S(1)} %all-to-all-done.2.g2), channel_id=1, source_target_pairs={{0,256},{256,0},{1,257},{257,1},{2,258},{258,2},{3,259},{259,3},{4... | collective-permute-start | bytes 1671176 | tf_op jit(solution)/shard_map/ppermute | solution.py:23
  118.8 1.6 copy-start.7
  120.4 0.8 copy-start.8
  127.3 50.2 %all-to-all-start.3 = ((bf16[32,16,512]{2,1,0:T(8,128)(2,1)}), bf16[32,16,512]{2,1,0:T(8,128)(2,1)S(1)}, u32[]{:S(2)}, u32[]{:S(2)}) async-start(bf16[32,16,512]{2,1,0:T(8,128)(2,1)} %bitcast.33), calls=%async_computation.3 | async-start | bytes 1048576 | tf_op jit(solution)/shard_map/all_to_all | solution.py:261
  148.1 29.6 %copy-start.9 = (f32[1,448]{1,0:T(1,128)S(1)}, f32[1,448]{1,0:T(1,128)}, u32[]{:S(2)}) copy-start(f32[1,448]{1,0:T(1,128)} %param.11) | copy-start | bytes 5380
  180.6 25.2 %all-to-all-start.4 = ((f32[16,1,272]{2,1,0:T(1,128)}), f32[16,1,272]{2,1,0:T(1,128)S(1)}, u32[]{:S(2)}, u32[]{:S(2)}) async-start(f32[16,1,272]{2,1,0:T(1,128)} %all_to_all.28), calls=%async_computation.4 | async-start | bytes 49152 | tf_op jit(solution)/shard_map/all_to_all | solution.py:286

commit v5 on v3

--- a/solution.py
+++ b/solution.py
@@ -14,6 +14,7 @@
 BF = jnp.bfloat16
 F32 = jnp.float32
 VMEM = pl.BlockSpec(memory_space=pltpu.VMEM)
+ANY = pl.BlockSpec(memory_space=pl.ANY)
 SMEM = pl.BlockSpec(memory_space=pltpu.SMEM)
 NT = (((1,), (1,)), ((), ()))
 
@@ -28,18 +29,36 @@
     return lax.all_to_all(copies, axes, 0, 0, tiled=False)
 
 
-def encode_kernel(at_ref, a_ref, enc_ref, keep_ref, send_ref, cols_ref, v_ref):
-    pair_at, tok_at = at_ref[0], at_ref[2]
-    v_ref[...] = jnp.dot(a_ref[...], enc_ref[...], preferred_element_type=F32)
+def encode_kernel(at_ref, act_hbm, enc_hbm, keep_ref, send_ref, a_ref, enc_ref, v_ref, sems):
+    pair_at = at_ref[0]
+    count = a_ref.shape[0]
+    chunk = a_ref.shape[2]
+    loads = []
+    for k in range(count):
+        span = pl.ds(k * chunk, chunk)
+        loads.append(
+            (
+                pltpu.make_async_copy(act_hbm.at[:, span], a_ref.at[k], sems.at[2 * k]),
+                pltpu.make_async_copy(enc_hbm.at[span], enc_ref.at[k], sems.at[2 * k + 1]),
+            )
+        )
+    for pair in loads:
+        for copy in pair:
+            copy.start()
+    for k in range(count):
+        for copy in loads[k]:
+            copy.wait()
+        part = jnp.dot(a_ref[k], enc_ref[k], preferred_element_type=F32)
+        if k == 0:
+            v_ref[...] = part
+        else:
+            v_ref[...] += part
     keep_ref[...] = v_ref[pl.ds(pl.multiple_of(pair_at * 128, 128), 128), :]
     send_ref[...] = v_ref[pl.ds(pl.multiple_of((1 - pair_at) * 128, 128), 128), :]
-    base = (tok_at // 2) * 896 + (tok_at % 2) * 384
-    window = a_ref[:, pl.ds(pl.multiple_of(base, 128), 512)]
-    cols_ref[...] = jnp.where(tok_at % 2 == 1, window[:, 64:512], window[:, 0:448])
 
 
 def decode_kernel(
-    at_ref, g1, g2, p1, p2, dec_ref, out_ref, f_ref, nsq_ref, wide_ref, norm_ref
+    at_ref, g1, g2, p1, p2, dec_ref, out_ref, nsq_ref, f_ref, wide_ref, norm_ref
 ):
     pair_at, zh_at = at_ref[0], at_ref[1]
 
@@ -82,31 +101,70 @@
                 out_ref[dst : dst + 64, 448:512] = sparse[src : src + 64, :]
 
 
-def numer_kernel(at_ref, f_ref, near_ref, far_ref, dec_ref, num_ref, msq_ref, a_ref):
-    zh_at, tok_at = at_ref[1], at_ref[2]
-    for half in range(2):
-        near = pl.multiple_of(half * 256 + zh_at * 128, 128)
-        far = pl.multiple_of(half * 256 + (1 - zh_at) * 128, 128)
-        a_ref[pl.ds(near, 128), :] = near_ref[half * 128 : (half + 1) * 128, :]
-        a_ref[pl.ds(far, 128), :] = far_ref[half * 128 : (half + 1) * 128, :]
-    for k in range(8):
-        cols = slice(k * 256, (k + 1) * 256)
-        inner = jnp.dot(a_ref[...], dec_ref[:, cols], preferred_element_type=F32)
-        num_ref[k : k + 1, :] = jnp.sum(
-            inner * f_ref[:, cols].astype(F32), axis=0, keepdims=True
-        )
-    own = f_ref[:, pl.ds(pl.multiple_of(tok_at * 256, 256), 256)].astype(F32)
-    msq_ref[...] = jnp.sum(own * own, axis=0, keepdims=True)
-
-
-def call(kernel, name, flops, outs, count, scratch):
+def numer_kernel(
+    at_ref,
+    g1,
+    g2,
+    p1,
+    p2,
+    dec_ref,
+    near_hbm,
+    far_hbm,
+    num_ref,
+    msq_ref,
+    own_ref,
+    w_ref,
+    a_ref,
+    sems,
+):
+    pair_at, zh_at, tok_at, y_at, lat_at = [at_ref[k] for k in range(5)]
+    base = pl.multiple_of((tok_at // 2) * 896 + (tok_at % 2) * 384, 128)
+    loads = [
+        pltpu.make_async_copy(ref.at[:, pl.ds(base, 512)], w_ref.at[k], sems.at[k])
+        for k, ref in enumerate((near_hbm, far_hbm))
+    ]
+    for copy in loads:
+        copy.start()
+    for copy in loads:
+        copy.wait()
+    for k in range(2):
+        for half in range(2):
+            window = w_ref[k, half * 128 : (half + 1) * 128, :]
+            cols = jnp.where(tok_at % 2 == 1, window[:, 64:512], window[:, 0:448])
+            a_ref[half, k * 128 : (k + 1) * 128, :] = cols
+
+    for y in range(4):
+        for zh in range(2):
+            at = 2 * y + (zh_at if zh == 0 else 1 - zh_at)
+            cols = dec_ref[:, pl.ds(pl.multiple_of(at * 256, 256), 256)]
+            total = jnp.zeros((1, 256), F32)
+            for half, own, oth in ((pair_at, g1, g2), (1 - pair_at, p1, p2)):
+                inner = jnp.dot(a_ref[half], cols, preferred_element_type=F32)
+                near = own[y, 0:128, :] if zh == 0 else oth[y]
+                far = own[y, 256:384, :] if zh == 0 else own[y, 128:256, :]
+                both = inner[0:128] * near.astype(F32) + inner[128:256] * far.astype(F32)
+                total = total + jnp.sum(both, axis=0, keepdims=True)
+            num_ref[pl.ds(at, 1), :] = total
+
+    squares = jnp.zeros((128, 256), F32)
+    for own in (g1, p1):
+        for rows in (slice(0, 128), slice(256, 384)):
+            feats = own[y_at, rows, :].astype(F32)
+            squares = squares + feats * feats
+    msq_ref[...] = jnp.sum(squares, axis=0, keepdims=True)
+    own_y, own_zh = lat_at // 8, (lat_at // 4) % 2
+    row = jnp.where(own_zh == zh_at, 0, 128) + (own_y % 2) * 64 + (lat_at % 4) * 16
+    own_ref[...] = a_ref[own_y // 2, pl.ds(pl.multiple_of(row, 16), 16), :]
+
+
+def call(kernel, name, flops, outs, count, scratch, outside=0, limit=60):
     return pl.pallas_call(
         kernel,
         out_shape=tuple(jax.ShapeDtypeStruct(shape, kind) for shape, kind in outs),
-        in_specs=[SMEM] + [VMEM] * count,
+        in_specs=[SMEM] + [VMEM] * count + [ANY] * outside,
         out_specs=(VMEM,) * len(outs),
-        scratch_shapes=[pltpu.VMEM(shape, kind) for shape, kind in scratch],
-        compiler_params=pltpu.CompilerParams(vmem_limit_bytes=40 << 20),
+        scratch_shapes=scratch,
+        compiler_params=pltpu.CompilerParams(vmem_limit_bytes=limit << 20),
         cost_estimate=pl.CostEstimate(
             flops=flops, bytes_accessed=6 << 20, transcendentals=0
         ),
@@ -127,7 +185,7 @@
     own, width = enc.shape[1], dec.shape[1]
     tokens = 8 * act.shape[0]
     rows = tokens // lax.axis_size(LAT)
-    at = jnp.stack([pair_at, zh_at, tok_at]).astype(jnp.int32)
+    at = jnp.stack([pair_at, zh_at, tok_at, lax.axis_index("y"), lat_at]).astype(jnp.int32)
 
     quarter = swap(lax.dynamic_slice_in_dim(act, x_at * 16, 16, 0), "zh")
     near = gather(act, "y").reshape(256, D)
@@ -146,57 +204,72 @@
         pre = keep + swap(send, "pair") + enc_bias
         return (pre * jax.nn.sigmoid((pre - thresh_level) / smooth_width)).astype(BF)
 
-    enc_outs = [((128, own), F32), ((128, own), F32), ((256, width), BF)]
-    enc_flops = 2 * 256 * D * own
-    half_value = ((256, own), F32)
-    encode = call(encode_kernel, "encode", enc_flops, enc_outs, 2, [half_value])
-    keep, send, near_cols = encode(at, near, enc)
+    parts, chunk = 4, D // 4
+    encode = call(
+        encode_kernel,
+        "encode",
+        2 * 256 * D * own,
+        [((128, own), F32), ((128, own), F32)],
+        0,
+        [
+            pltpu.VMEM((parts, 256, chunk), BF),
+            pltpu.VMEM((parts, chunk, own), BF),
+            pltpu.VMEM((256, own), F32),
+            pltpu.SemaphoreType.DMA((2 * parts,)),
+        ],
+        2,
+    )
+    keep, send = encode(at, near, enc)
     feats_near = features(keep, send)
     over = swap(jnp.concatenate([feats_near] + split(nsq_part), axis=0), "zh")
     over_near = over[:128]
     nsq_both = nsq_part + over[128:136].astype(F32) + over[136:144].astype(F32)
 
-    keep, send, far_cols = encode(at, far, enc)
+    keep, send = encode(at, far, enc)
     feats_far = features(keep, send)
     over_far = swap(feats_far, "zh")
     g1 = gather(
         jnp.concatenate([feats_near, over_near, feats_far] + split(nsq_both), axis=0), "y"
     )
-    p1 = swap(g1, "pair")
     over_far, g1 = lax.optimization_barrier((over_far, g1))
     g2 = gather(over_far, "y")
+    p1 = swap(g1, "pair")
     p2 = swap(g2, "pair")
 
-    payload, block_feats, nsq_all = call(
+    payload, nsq_all = call(
         decode_kernel,
         "decode",
         2 * tokens * 8 * own * 512,
-        [((tokens, 512), BF), ((tokens, 8 * own), BF), ((8, own), F32)],
+        [((tokens, 512), BF), ((8, own), F32)],
         5,
-        [((64, 8 * own), F32), ((64, 8 * own), BF)],
+        [
+            pltpu.VMEM((tokens, 8 * own), BF),
+            pltpu.VMEM((64, 8 * own), F32),
+            pltpu.VMEM((64, 8 * own), BF),
+        ],
+        limit=40,
     )(at, g1, g2, p1, p2, dec_t)
     nsq_own = lax.dynamic_index_in_dim(nsq_all, tok_at, 0, keepdims=False)
     arrived = lax.all_to_all(payload, LAT, 0, 0, tiled=True)
 
-    num_part, sum_sq = call(
+    num_part, sum_sq, act_own = call(
         numer_kernel,
         "numer",
         2 * tokens * 8 * own * width,
-        [((8, own), F32), ((1, own), F32)],
-        4,
-        [((tokens, width), BF)],
-    )(at, block_feats, near_cols, far_cols, dec_t)
+        [((8, own), F32), ((1, own), F32), ((rows, width), BF)],
+        5,
+        [
+            pltpu.VMEM((2, 256, 512), BF),
+            pltpu.VMEM((2, 256, width), BF),
+            pltpu.SemaphoreType.DMA((2,)),
+        ],
+        2,
+    )(at, g1, g2, p1, p2, dec_t, near, far)
     mean_sq = sum_sq[0] / tokens
 
     total = jnp.sum(arrived.reshape(32, rows, 512).astype(F32), axis=0)
     recon_vals = total[:, :width] + dec_bias[0]
     sparse = total[:, width] + total[:, width + 1]
-    own_row = (lat_at // 8) * 64 + (lat_at % 4) * rows
-    act_own = jnp.where(
-        (lat_at // 4) % 2 == zh_at,
-        lax.dynamic_slice_in_dim(near_cols, own_row, rows, 0),
-        lax.dynamic_slice_in_dim(far_cols, own_row, rows, 0),
-    )
     residue = act_own.astype(F32) - recon_vals
     own_terms = jnp.sum(residue * residue, axis=1) / (2.0 * D) + penalty * sparse
 

time: 197 us -> 190 us (0.964)
  blocking collectives: 22.6 us -> 13.3 us
  Pallas kernels: 8.57 us -> 17 us
  local copies, waits for them, and re-layouts: 14.2 us -> 9.08 us
  other arithmetic: 2.76 us -> 5.89 us
  starting transfers between devices: 99 us -> 96.8 us
  waiting for transfers between devices: 48.1 us -> 46.1 us
    all_to_all x2 -> x1, blocking collectives: 22.6 us -> 13.3 us  [gather(): return lax.all_to_all(copies, axes, 0, 0, tiled=False)]
    unnamed x23, local copies, waits for them, and re-layouts: 8.68 us -> 1.32 us
    pallas_call x2, Pallas kernels: 3.36 us -> 8.01 us  [the longest x1 4.08 us: body(): keep, send = encode(at, near, enc)]
    pallas_call x1, Pallas kernels: 1.81 us -> 5.57 us  [body(): call(numer_kernel, 'numer', 2 * tokens * 8 * own * width, [((8, own), F32...]
    all_to_all x2 -> x3, starting transfers between devices: 13.7 us -> 17.5 us  [gather(): return lax.all_to_all(copies, axes, 0, 0, tiled=False)]
    ppermute x7, starting transfers between devices: 61.8 us -> 58.7 us  [swap(): return lax.ppermute(value, axis, [(0, 1), (1, 0)])]
    all_to_all x1, starting transfers between devices: 12.2 us -> 9.32 us  [body(): arrived = lax.all_to_all(payload, LAT, 0, 0, tiled=True)]
    all_to_all x1, waiting for transfers between devices: 25.9 us -> 23.8 us  [body(): arrived = lax.all_to_all(payload, LAT, 0, 0, tiled=True)]
  transfers between devices with their start and end apart: 11 -> 12, of which waited for: 7 -> 7; matrix products, arithmetic and copies ran while one was open for 1% -> 2% of each run, Pallas kernels for 3% -> 7%
where the time goes in v5:
time: 190 us; the launch traced here: 189 us
  starting transfers between devices  96.8 us (51%)
  waiting for transfers between devices  46.1 us (24%)
  Pallas kernels  17 us (9%)
  blocking collectives  13.3 us (7%)
  local copies, waits for them, and re-layouts  9.08 us (5%)
  other arithmetic  5.89 us (3%)
    ppermute x7, starting transfers between devices, swap(): return lax.ppermute(value, axis, [(0, 1), (1, 0)])  58.7 us
    all_to_all x1, waiting for transfers between devices, body(): arrived = lax.all_to_all(payload, LAT, 0, 0, tiled=True)  23.8 us
    all_to_all x3, starting transfers between devices, gather(): return lax.all_to_all(copies, axes, 0, 0, tiled=False)  17.5 us
    all_to_all x1, waiting for transfers between devices, body(): got = lax.all_to_all(last, ('pair',) + TOK, 0, 0, tiled=True)  14.2 us
    all_to_all x1, blocking collectives, gather(): return lax.all_to_all(copies, axes, 0, 0, tiled=False)  13.3 us
    all_to_all x1, starting transfers between devices, body(): got = lax.all_to_all(last, ('pair',) + TOK, 0, 0, tiled=True)  11.3 us
    all_to_all x1, starting transfers between devices, body(): arrived = lax.all_to_all(payload, LAT, 0, 0, tiled=True)  9.32 us
    ppermute x7, waiting for transfers between devices, swap(): return lax.ppermute(value, axis, [(0, 1), (1, 0)])  8.07 us
  transfers between devices with their start and end apart: 12, of which 7 were waited for; matrix products, arithmetic and copies ran while one was open for 2% of the time, Pallas kernels for 7%

profile of v5, /device:TPU:1, one launch (start us, length us, event | category | flops | bytes accessed | tf_op | source)
XLA Modules:
  0.0 189.0 jit_solution(16391351152050920723)
XLA Ops:
  0.6 2.4 %broadcast_in_dim.18 = bf16[4,64,3584]{2,1,0:T(8,128)(2,1)} broadcast(bf16[64,3584]{1,0:T(8,128)(2,1)} %bitcast.32), dimensions={1,2} | broadcast | bytes 2293760 | tf_op jit(solution)/shard_map/broadcast_in_dim | solution.py:28
  3.0 5.0 %all-to-all-start.1 = ((bf16[4,64,3584]{2,1,0:T(8,128)(2,1)}), bf16[4,64,3584]{2,1,0:T(8,128)(2,1)S(1)}, u32[]{:S(2)}, u32[]{:S(2)}) async-start(bf16[4,64,3584]{2,1,0:T(8,128)(2,1)} %broadcast_in_dim.18), calls=%async_computation.1 | async-start | bytes 3670016 | tf_op jit(solution)/shard_map/all_to_all | solution.py:29
  9.0 15.4 %collective-permute-start = (bf16[16,3584]{1,0:T(8,128)(2,1)S(1)}, bf16[16,3584]{1,0:T(8,128)(2,1)S(1)}, u32[]{:S(2)}, u32[]{:S(2)}) collective-permute-start(bf16[16,3584]{1,0:T(8,128)(2,1)S(1)} %dynamic-slice_bitcast_fusion), channel_id=1, source_target_pairs={{0,1},{1,0},{2,3},{3,2},{4,5},{5,4},{6,7},{7,6},{8,9},{9,8},{10,11... | collective-permute-start | bytes 344072 | tf_op jit(solution)/shard_map/ppermute | solution.py:23
  24.4 2.5 %collective-permute-done = bf16[16,3584]{1,0:T(8,128)(2,1)S(1)} collective-permute-done((bf16[16,3584]{1,0:T(8,128)(2,1)S(1)}, bf16[16,3584]{1,0:T(8,128)(2,1)S(1)}, u32[]{:S(2)}, u32[]{:S(2)}) %collective-permute-start) | collective-permute-done | bytes 114720 | tf_op jit(solution)/shard_map/ppermute | solution.py:23
  26.9 1.3 copy-done.6
  28.1 1.4 broadcast_in_dim.16
  29.6 8.7 %all-to-all-start = ((bf16[16,16,3584]{2,1,0:T(8,128)(2,1)}), bf16[16,16,3584]{2,1,0:T(8,128)(2,1)}, u32[]{:S(2)}, u32[]{:S(2)}) async-start(bf16[16,16,3584]{2,1,0:T(8,128)(2,1)} %broadcast_in_dim.16), calls=%async_computation | async-start | bytes 3670016 | tf_op jit(solution)/shard_map/all_to_all | solution.py:29
  39.4 4.1 %encode.3 = (f32[128,256]{1,0:T(8,128)}, f32[128,256]{1,0:T(8,128)}) custom-call(s32[5]{0:T(128)} %stack.23.at_ref, bf16[256,3584]{1,0:T(8,128)(2,1)} %bitcast.28, bf16[3584,256]{1,0:T(8,128)(2,1)} %bitcast.30), custom_call_target="tpu_custom_call" | custom-call | flops 469762048 | bytes 6291456 | tf_op jit(solution)/shard_map/encode/pallas_call | solution.py:222
  43.5 7.3 %collective-permute-start.3 = (f32[128,256]{1,0:T(8,128)}, f32[128,256]{1,0:T(8,128)S(1)}, u32[]{:S(2)}, u32[]{:S(2)}) collective-permute-start(f32[128,256]{1,0:T(8,128)} %get-tuple-element.17), channel_id=1, source_target_pairs={{0,256},{256,0},{1,257},{257,1},{2,258},{258,2},{3,259},{259,3},{4... | collective-permute-start | bytes 393224 | tf_op jit(solution)/shard_map/ppermute | solution.py:23
  50.8 1.2 collective-permute-done.3
  52.0 1.0 constant_dynamic-update-slice_fusion.3
  52.9 12.8 %collective-permute-start.4 = (bf16[144,256]{1,0:T(8,128)(2,1)S(1)}, bf16[144,256]{1,0:T(8,128)(2,1)S(1)}, u32[]{:S(2)}, u32[]{:S(2)}) collective-permute-start(bf16[144,256]{1,0:T(8,128)(2,1)S(1)} %pad_maximum_fusion), channel_id=1, source_target_pairs={{0,1},{1,0},{2,3},{3,2},{4,5},{5,4},{6,7},{7,6},{8,9},{9,8},{10,11... | collective-permute-start | bytes 221192 | tf_op jit(solution)/shard_map/ppermute | solution.py:23
  65.8 3.9 %encode.2 = (f32[128,256]{1,0:T(8,128)}, f32[128,256]{1,0:T(8,128)}) custom-call(s32[5]{0:T(128)} %stack.23.at_ref, bf16[256,3584]{1,0:T(8,128)(2,1)} %bitcast.6.act_hbm.far_hbm, bf16[3584,256]{1,0:T(8,128)(2,1)} %bitcast.31), custom_call_target="tpu_custom_call" | custom-call | flops 469762048 | bytes 6291456 | tf_op jit(solution)/shard_map/encode/pallas_call | solution.py:228
  69.7 3.2 %collective-permute-start.1 = (f32[128,256]{1,0:T(8,128)}, f32[128,256]{1,0:T(8,128)S(1)}, u32[]{:S(2)}, u32[]{:S(2)}) collective-permute-start(f32[128,256]{1,0:T(8,128)} %get-tuple-element.15), channel_id=1, source_target_pairs={{0,256},{256,0},{1,257},{257,1},{2,258},{258,2},{3,259},{259,3},{4... | collective-permute-start | bytes 393224 | tf_op jit(solution)/shard_map/ppermute | solution.py:23
  72.9 1.1 collective-permute-done.1
  74.0 1.0 constant_dynamic-update-slice_fusion.2
  75.0 0.9 broadcast_in_dim.19
  76.0 3.8 %all-to-all-start.2 = ((bf16[4,400,256]{2,1,0:T(8,128)(2,1)}), bf16[4,400,256]{2,1,0:T(8,128)(2,1)S(1)}, u32[]{:S(2)}, u32[]{:S(2)}) async-start(bf16[4,400,256]{2,1,0:T(8,128)(2,1)} %broadcast_in_dim.19), calls=%async_computation.2 | async-start | bytes 1638400 | tf_op jit(solution)/shard_map/all_to_all | solution.py:29
  79.7 14.1 %collective-permute-start.2 = (bf16[128,256]{1,0:T(8,128)(2,1)S(1)}, bf16[128,256]{1,0:T(8,128)(2,1)S(1)}, u32[]{:S(2)}, u32[]{:S(2)}) collective-permute-start(bf16[128,256]{1,0:T(8,128)(2,1)S(1)} %get-tuple-element.26), channel_id=1, source_target_pairs={{0,1},{1,0},{2,3},{3,2},{4,5},{5,4},{6,7},{7,6},{8,9},{9,8},{10,11... | collective-permute-start | bytes 196616 | tf_op jit(solution)/shard_map/ppermute | solution.py:23
  93.8 2.2 %collective-permute-done.2 = bf16[128,256]{1,0:T(8,128)(2,1)S(1)} collective-permute-done((bf16[128,256]{1,0:T(8,128)(2,1)S(1)}, bf16[128,256]{1,0:T(8,128)(2,1)S(1)}, u32[]{:S(2)}, u32[]{:S(2)}) %collective-permute-start.2) | collective-permute-done | bytes 65568 | tf_op jit(solution)/shard_map/ppermute | solution.py:23
  96.0 3.0 %collective-permute-start.5 = (bf16[4,400,256]{2,1,0:T(8,128)(2,1)S(1)}, bf16[4,400,256]{2,1,0:T(8,128)(2,1)S(1)}, u32[]{:S(2)}, u32[]{:S(2)}) collective-permute-start(bf16[4,400,256]{2,1,0:T(8,128)(2,1)S(1)} %all-to-all-done.2.g1), channel_id=1, source_target_pairs={{0,256},{256,0},{1,257},{257,1},{2,258},{258,2},{3,259},{259,3},{4... | collective-permute-start | bytes 2457608 | tf_op jit(solution)/shard_map/ppermute | solution.py:23
  99.0 13.3 %all_to_all.41.g2 = bf16[4,128,256]{2,1,0:T(8,128)(2,1)S(1)} all-to-all(bf16[4,128,256]{2,1,0:T(8,128)(2,1)S(1)} %broadcast_in_dim.20), channel_id=1, replica_groups=mesh['pair'=2,'x'=4,'zl'=8,'y'=4,'zh'=2] {'y'}, dimensions={0} | all-to-all | bytes 524288 | tf_op jit(solution)/shard_map/all_to_all | solution.py:29
  112.3 3.0 %collective-permute-start.6 = (bf16[4,128,256]{2,1,0:T(8,128)(2,1)S(1)}, bf16[4,128,256]{2,1,0:T(8,128)(2,1)S(1)}, u32[]{:S(2)}, u32[]{:S(2)}) collective-permute-start(bf16[4,128,256]{2,1,0:T(8,128)(2,1)S(1)} %all_to_all.41.g2), channel_id=1, source_target_pairs={{0,256},{256,0},{1,257},{257,1},{2,258},{258,2},{3,259},{259,3},{4... | collective-permute-start | bytes 786440 | tf_op jit(solution)/shard_map/ppermute | solution.py:23
  115.3 1.1 collective-permute-done.6.p2
  116.5 3.4 %decode.1 = (bf16[512,512]{1,0:T(8,128)(2,1)}, f32[8,256]{1,0:T(8,128)S(1)}) custom-call(s32[5]{0:T(128)S(1)} %copy-done.5, bf16[4,400,256]{2,1,0:T(8,128)(2,1)S(1)} %all-to-all-done.2.g1, bf16[4,128,256]{2,1,0:T(8,128)(2,1)S(1)} %all_to_all.41.g2, bf16[4,400,256]{2,1,0:T(8,128)(2,1)S(1)} %collective-permute-done.5.p1, ...), custom_call_target="tpu_custom_call" | custom-call | flops 1073741824 | bytes 6291456 | tf_op jit(solution)/shard_map/decode/pallas_call | solution.py:239
  119.9 9.3 %all-to-all-start.4 = ((bf16[32,16,512]{2,1,0:T(8,128)(2,1)}), bf16[32,16,512]{2,1,0:T(8,128)(2,1)S(1)}, u32[]{:S(2)}, u32[]{:S(2)}) async-start(bf16[32,16,512]{2,1,0:T(8,128)(2,1)} %bitcast.12), calls=%async_computation.4 | async-start | bytes 1048576 | tf_op jit(solution)/shard_map/all_to_all | solution.py:253
  129.3 5.6 %numer.1 = (f32[8,256]{1,0:T(8,128)}, f32[1,256]{1,0:T(1,128)}, bf16[16,448]{1,0:T(8,128)(2,1)}) custom-call(s32[5]{0:T(128)} %stack.23.at_ref, bf16[4,400,256]{2,1,0:T(8,128)(2,1)} %copy-done.1, bf16[4,128,256]{2,1,0:T(8,128)(2,1)} %copy-done.3, bf16[4,400,256]{2,1,0:T(8,128)(2,1)} %copy-done.2, bf16[4,128,256]{2,1,0:T(8,128)(2,1)} %copy-done.4, ...), custom_call_target="tpu_custom_call" | custom-call | flops 939524096 | bytes 6291456 | tf_op jit(solution)/shard_map/numer/pallas_call | solution.py:255
  134.8 23.8 %all-to-all-done.4 = bf16[32,16,512]{2,1,0:T(8,128)(2,1)S(1)} async-done(((bf16[32,16,512]{2,1,0:T(8,128)(2,1)}), bf16[32,16,512]{2,1,0:T(8,128)(2,1)S(1)}, u32[]{:S(2)}, u32[]{:S(2)}) %all-to-all-start.4) | async-done | bytes 524320 | tf_op jit(solution)/shard_map/all_to_all | solution.py:253
  158.9 1.4 multiply_reduce_fusion.1
  161.7 11.3 %all-to-all-start.5 = ((f32[16,1,272]{2,1,0:T(1,128)}), f32[16,1,272]{2,1,0:T(1,128)S(1)}, u32[]{:S(2)}, u32[]{:S(2)}) async-start(f32[16,1,272]{2,1,0:T(1,128)} %all_to_all.32), calls=%async_computation.5 | async-start | bytes 49152 | tf_op jit(solution)/shard_map/all_to_all | solution.py:283
  173.0 14.2 %all-to-all-done.5 = f32[16,1,272]{2,1,0:T(1,128)S(1)} async-done(((f32[16,1,272]{2,1,0:T(1,128)}), f32[16,1,272]{2,1,0:T(1,128)S(1)}, u32[]{:S(2)}, u32[]{:S(2)}) %all-to-all-start.5) | async-done | bytes 17440 | tf_op jit(solution)/shard_map/all_to_all | solution.py:283
  187.8 1.3 add_divide_fusion
  (48 shorter events, 4.3 us)
Async XLA Ops:
  3.0 23.8 %all-to-all-start.1 = ((bf16[4,64,3584]{2,1,0:T(8,128)(2,1)}), bf16[4,64,3584]{2,1,0:T(8,128)(2,1)S(1)}, u32[]{:S(2)}, u32[]{:S(2)}) async-start(bf16[4,64,3584]{2,1,0:T(8,128)(2,1)} %broadcast_in_dim.18), calls=%async_computation.1 | async-start | bytes 3670016 | tf_op jit(solution)/shard_map/all_to_all | solution.py:29
  9.0 17.9 %collective-permute-start = (bf16[16,3584]{1,0:T(8,128)(2,1)S(1)}, bf16[16,3584]{1,0:T(8,128)(2,1)S(1)}, u32[]{:S(2)}, u32[]{:S(2)}) collective-permute-start(bf16[16,3584]{1,0:T(8,128)(2,1)S(1)} %dynamic-slice_bitcast_fusion), channel_id=1, source_target_pairs={{0,1},{1,0},{2,3},{3,2},{4,5},{5,4},{6,7},{7,6},{8,9},{9,8},{10,11... | collective-permute-start | bytes 344072 | tf_op jit(solution)/shard_map/ppermute | solution.py:23
  26.9 1.3 copy-start.6
  29.6 8.7 %copy-start = (bf16[1,2048,448]{1,2,0:T(8,128)(2,1)S(1)}, bf16[1,2048,448]{1,2,0:T(8,128)(2,1)}, u32[]{:S(2)}) copy-start(bf16[1,2048,448]{1,2,0:T(8,128)(2,1)} %param.10) | copy-start | bytes 5505028
  29.6 36.2 %all-to-all-start = ((bf16[16,16,3584]{2,1,0:T(8,128)(2,1)}), bf16[16,16,3584]{2,1,0:T(8,128)(2,1)}, u32[]{:S(2)}, u32[]{:S(2)}) async-start(bf16[16,16,3584]{2,1,0:T(8,128)(2,1)} %broadcast_in_dim.16), calls=%async_computation | async-start | bytes 3670016 | tf_op jit(solution)/shard_map/all_to_all | solution.py:29
  39.4 11.4 %copy-start.9 = (s32[256]{0:T(256)S(1)}, s32[256]{0:T(256)}, u32[]{:S(2)}) copy-start(s32[256]{0:T(256)} %param.9) | copy-start | bytes 3076
  39.4 12.6 %copy-start.7 = (f32[256]{0:T(256)S(1)}, f32[256]{0:T(256)}, u32[]{:S(2)}) copy-start(f32[256]{0:T(256)} %param.8) | copy-start | bytes 3076
  43.5 8.5 %collective-permute-start.3 = (f32[128,256]{1,0:T(8,128)}, f32[128,256]{1,0:T(8,128)S(1)}, u32[]{:S(2)}, u32[]{:S(2)}) collective-permute-start(f32[128,256]{1,0:T(8,128)} %get-tuple-element.17), channel_id=1, source_target_pairs={{0,256},{256,0},{1,257},{257,1},{2,258},{258,2},{3,259},{259,3},{4... | collective-permute-start | bytes 393224 | tf_op jit(solution)/shard_map/ppermute | solution.py:23
  52.9 19.9 %collective-permute-start.4 = (bf16[144,256]{1,0:T(8,128)(2,1)S(1)}, bf16[144,256]{1,0:T(8,128)(2,1)S(1)}, u32[]{:S(2)}, u32[]{:S(2)}) collective-permute-start(bf16[144,256]{1,0:T(8,128)(2,1)S(1)} %pad_maximum_fusion), channel_id=1, source_target_pairs={{0,1},{1,0},{2,3},{3,2},{4,5},{5,4},{6,7},{7,6},{8,9},{9,8},{10,11... | collective-permute-start | bytes 221192 | tf_op jit(solution)/shard_map/ppermute | solution.py:23
  69.7 4.3 %collective-permute-start.1 = (f32[128,256]{1,0:T(8,128)}, f32[128,256]{1,0:T(8,128)S(1)}, u32[]{:S(2)}, u32[]{:S(2)}) collective-permute-start(f32[128,256]{1,0:T(8,128)} %get-tuple-element.15), channel_id=1, source_target_pairs={{0,256},{256,0},{1,257},{257,1},{2,258},{258,2},{3,259},{259,3},{4... | collective-permute-start | bytes 393224 | tf_op jit(solution)/shard_map/ppermute | solution.py:23
  75.0 41.5 %copy-start.5 = (s32[5]{0:T(128)S(1)}, s32[5]{0:T(128)}, u32[]{:S(2)}) copy-start(s32[5]{0:T(128)} %stack.23.at_ref) | copy-start | bytes 64
  76.0 20.0 %all-to-all-start.2 = ((bf16[4,400,256]{2,1,0:T(8,128)(2,1)}), bf16[4,400,256]{2,1,0:T(8,128)(2,1)S(1)}, u32[]{:S(2)}, u32[]{:S(2)}) async-start(bf16[4,400,256]{2,1,0:T(8,128)(2,1)} %broadcast_in_dim.19), calls=%async_computation.2 | async-start | bytes 1638400 | tf_op jit(solution)/shard_map/all_to_all | solution.py:29
  79.7 16.3 %collective-permute-start.2 = (bf16[128,256]{1,0:T(8,128)(2,1)S(1)}, bf16[128,256]{1,0:T(8,128)(2,1)S(1)}, u32[]{:S(2)}, u32[]{:S(2)}) collective-permute-start(bf16[128,256]{1,0:T(8,128)(2,1)S(1)} %get-tuple-element.26), channel_id=1, source_target_pairs={{0,1},{1,0},{2,3},{3,2},{4,5},{5,4},{6,7},{7,6},{8,9},{9,8},{10,11... | collective-permute-start | bytes 196616 | tf_op jit(solution)/shard_map/ppermute | solution.py:23
  96.0 23.9 %copy-start.1 = (bf16[4,400,256]{2,1,0:T(8,128)(2,1)}, bf16[4,400,256]{2,1,0:T(8,128)(2,1)S(1)}, u32[]{:S(2)}) copy-start(bf16[4,400,256]{2,1,0:T(8,128)(2,1)S(1)} %all-to-all-done.2.g1) | copy-start | bytes 2457604
  96.0 20.5 %collective-permute-start.5 = (bf16[4,400,256]{2,1,0:T(8,128)(2,1)S(1)}, bf16[4,400,256]{2,1,0:T(8,128)(2,1)S(1)}, u32[]{:S(2)}, u32[]{:S(2)}) collective-permute-start(bf16[4,400,256]{2,1,0:T(8,128)(2,1)S(1)} %all-to-all-done.2.g1), channel_id=1, source_target_pairs={{0,256},{256,0},{1,257},{257,1},{2,258},{258,2},{3,259},{259,3},{4... | collective-permute-start | bytes 2457608 | tf_op jit(solution)/shard_map/ppermute | solution.py:23
  112.3 7.6 %copy-start.3 = (bf16[4,128,256]{2,1,0:T(8,128)(2,1)}, bf16[4,128,256]{2,1,0:T(8,128)(2,1)S(1)}, u32[]{:S(2)}) copy-start(bf16[4,128,256]{2,1,0:T(8,128)(2,1)S(1)} %all_to_all.41.g2) | copy-start | bytes 786436
  112.3 4.2 %collective-permute-start.6 = (bf16[4,128,256]{2,1,0:T(8,128)(2,1)S(1)}, bf16[4,128,256]{2,1,0:T(8,128)(2,1)S(1)}, u32[]{:S(2)}, u32[]{:S(2)}) collective-permute-start(bf16[4,128,256]{2,1,0:T(8,128)(2,1)S(1)} %all_to_all.41.g2), channel_id=1, source_target_pairs={{0,256},{256,0},{1,257},{257,1},{2,258},{258,2},{3,259},{259,3},{4... | collective-permute-start | bytes 786440 | tf_op jit(solution)/shard_map/ppermute | solution.py:23
  116.5 3.4 %copy-start.4 = (bf16[4,128,256]{2,1,0:T(8,128)(2,1)}, bf16[4,128,256]{2,1,0:T(8,128)(2,1)S(1)}, u32[]{:S(2)}) copy-start(bf16[4,128,256]{2,1,0:T(8,128)(2,1)S(1)} %collective-permute-done.6.p2) | copy-start | bytes 786436
  116.5 3.4 %copy-start.2 = (bf16[4,400,256]{2,1,0:T(8,128)(2,1)}, bf16[4,400,256]{2,1,0:T(8,128)(2,1)S(1)}, u32[]{:S(2)}) copy-start(bf16[4,400,256]{2,1,0:T(8,128)(2,1)S(1)} %collective-permute-done.5.p1) | copy-start | bytes 2457604
  119.9 38.7 %all-to-all-start.4 = ((bf16[32,16,512]{2,1,0:T(8,128)(2,1)}), bf16[32,16,512]{2,1,0:T(8,128)(2,1)S(1)}, u32[]{:S(2)}, u32[]{:S(2)}) async-start(bf16[32,16,512]{2,1,0:T(8,128)(2,1)} %bitcast.12), calls=%async_computation.4 | async-start | bytes 1048576 | tf_op jit(solution)/shard_map/all_to_all | solution.py:253
  129.3 29.6 %copy-start.8 = (f32[1,448]{1,0:T(1,128)S(1)}, f32[1,448]{1,0:T(1,128)}, u32[]{:S(2)}) copy-start(f32[1,448]{1,0:T(1,128)} %param.11) | copy-start | bytes 5380
  161.7 25.5 %all-to-all-start.5 = ((f32[16,1,272]{2,1,0:T(1,128)}), f32[16,1,272]{2,1,0:T(1,128)S(1)}, u32[]{:S(2)}, u32[]{:S(2)}) async-start(f32[16,1,272]{2,1,0:T(1,128)} %all_to_all.32), calls=%async_computation.5 | async-start | bytes 49152 | tf_op jit(solution)/shard_map/all_to_all | solution.py:283

commit v6 on v5

--- a/solution.py
+++ b/solution.py
@@ -16,6 +16,7 @@
 VMEM = pl.BlockSpec(memory_space=pltpu.VMEM)
 ANY = pl.BlockSpec(memory_space=pl.ANY)
 SMEM = pl.BlockSpec(memory_space=pltpu.SMEM)
+STEPS = (0, 3, 1, 2)
 NT = (((1,), (1,)), ((), ()))
 
 
@@ -29,38 +30,10 @@
     return lax.all_to_all(copies, axes, 0, 0, tiled=False)
 
 
-def encode_kernel(at_ref, act_hbm, enc_hbm, keep_ref, send_ref, a_ref, enc_ref, v_ref, sems):
-    pair_at = at_ref[0]
-    count = a_ref.shape[0]
-    chunk = a_ref.shape[2]
-    loads = []
-    for k in range(count):
-        span = pl.ds(k * chunk, chunk)
-        loads.append(
-            (
-                pltpu.make_async_copy(act_hbm.at[:, span], a_ref.at[k], sems.at[2 * k]),
-                pltpu.make_async_copy(enc_hbm.at[span], enc_ref.at[k], sems.at[2 * k + 1]),
-            )
-        )
-    for pair in loads:
-        for copy in pair:
-            copy.start()
-    for k in range(count):
-        for copy in loads[k]:
-            copy.wait()
-        part = jnp.dot(a_ref[k], enc_ref[k], preferred_element_type=F32)
-        if k == 0:
-            v_ref[...] = part
-        else:
-            v_ref[...] += part
-    keep_ref[...] = v_ref[pl.ds(pl.multiple_of(pair_at * 128, 128), 128), :]
-    send_ref[...] = v_ref[pl.ds(pl.multiple_of((1 - pair_at) * 128, 128), 128), :]
-
-
 def decode_kernel(
     at_ref, g1, g2, p1, p2, dec_ref, out_ref, nsq_ref, f_ref, wide_ref, norm_ref
 ):
-    pair_at, zh_at = at_ref[0], at_ref[1]
+    pair_at, zh_at, y_at = at_ref[0], at_ref[1], at_ref[3]
 
     nsq = jnp.zeros((8, 256), F32)
     for y in range(4):
@@ -79,12 +52,14 @@
         near = pl.multiple_of(half * 256 + zh_at * 128, 128)
         far = pl.multiple_of(half * 256 + (1 - zh_at) * 128, 128)
         for y in range(4):
-            mine = pl.multiple_of((2 * y + zh_at) * 256, 256)
-            theirs = pl.multiple_of((2 * y + 1 - zh_at) * 256, 256)
+            ring_y = (y_at + STEPS[y]) % 4
+            mine = pl.multiple_of((2 * ring_y + zh_at) * 256, 256)
+            theirs = pl.multiple_of((2 * ring_y + 1 - zh_at) * 256, 256)
+            last = pl.multiple_of((2 * y + 1 - zh_at) * 256, 256)
             f_ref[pl.ds(near, 128), pl.ds(mine, 256)] = own[y, 0:128, :]
             f_ref[pl.ds(far, 128), pl.ds(theirs, 256)] = own[y, 128:256, :]
             f_ref[pl.ds(far, 128), pl.ds(mine, 256)] = own[y, 256:384, :]
-            f_ref[pl.ds(near, 128), pl.ds(theirs, 256)] = oth[y]
+            f_ref[pl.ds(near, 128), pl.ds(last, 256)] = oth[y]
 
     place(pair_at, g1, g2)
     place(1 - pair_at, p1, p2)
@@ -133,15 +108,16 @@
             cols = jnp.where(tok_at % 2 == 1, window[:, 64:512], window[:, 0:448])
             a_ref[half, k * 128 : (k + 1) * 128, :] = cols
 
-    for y in range(4):
+    for k in range(4):
+        y = (y_at + STEPS[k]) % 4
         for zh in range(2):
             at = 2 * y + (zh_at if zh == 0 else 1 - zh_at)
             cols = dec_ref[:, pl.ds(pl.multiple_of(at * 256, 256), 256)]
             total = jnp.zeros((1, 256), F32)
             for half, own, oth in ((pair_at, g1, g2), (1 - pair_at, p1, p2)):
                 inner = jnp.dot(a_ref[half], cols, preferred_element_type=F32)
-                near = own[y, 0:128, :] if zh == 0 else oth[y]
-                far = own[y, 256:384, :] if zh == 0 else own[y, 128:256, :]
+                near = own[k, 0:128, :] if zh == 0 else oth[y]
+                far = own[k, 256:384, :] if zh == 0 else own[k, 128:256, :]
                 both = inner[0:128] * near.astype(F32) + inner[128:256] * far.astype(F32)
                 total = total + jnp.sum(both, axis=0, keepdims=True)
             num_ref[pl.ds(at, 1), :] = total
@@ -149,12 +125,33 @@
     squares = jnp.zeros((128, 256), F32)
     for own in (g1, p1):
         for rows in (slice(0, 128), slice(256, 384)):
-            feats = own[y_at, rows, :].astype(F32)
+            feats = own[0, rows, :].astype(F32)
             squares = squares + feats * feats
     msq_ref[...] = jnp.sum(squares, axis=0, keepdims=True)
     own_y, own_zh = lat_at // 8, (lat_at // 4) % 2
     row = jnp.where(own_zh == zh_at, 0, 128) + (own_y % 2) * 64 + (lat_at % 4) * 16
     own_ref[...] = a_ref[own_y // 2, pl.ds(pl.multiple_of(row, 16), 16), :]
+
+
+def close_kernel(arrived_ref, bias_ref, act_ref, num_ref, recon_ref, last_ref):
+    total = arrived_ref[0].astype(F32)
+    for k in range(1, 32):
+        total = total + arrived_ref[k].astype(F32)
+    recon = total[:, 0:448] + bias_ref[...]
+    recon_ref[...] = recon.astype(BF)
+    residue = act_ref[...].astype(F32) - recon
+    sparse = total[:, 448:449] + total[:, 449:450]
+    terms = jnp.sum(residue * residue, axis=1, keepdims=True) / (2.0 * D) + penalty * sparse
+    row = lax.broadcasted_iota(jnp.int32, (16, 128), 0)
+    lane = lax.broadcasted_iota(jnp.int32, (16, 128), 1)
+    line = jnp.sum(jnp.where(row == lane, terms, 0.0), axis=0, keepdims=True)
+    for k in range(8):
+        for pair in range(2):
+            at = pair * 8 + k
+            last_ref[at, 0:1, :] = num_ref[k : k + 1, 0:128]
+            last_ref[at, 1:2, :] = num_ref[k : k + 1, 128:256]
+            last_ref[at, 2:3, :] = line
+            last_ref[at, 3:4, :] = line
 
 
 def call(kernel, name, flops, outs, count, scratch, outside=0, limit=60):
@@ -200,38 +197,26 @@
 
     thresh_level = thresholds.astype(F32) * 0.25
 
-    def features(keep, send):
+    def features(acts):
+        part = jnp.dot(acts, enc, preferred_element_type=F32)
+        keep = lax.dynamic_slice_in_dim(part, pair_at * 128, 128, 0)
+        send = lax.dynamic_slice_in_dim(part, (1 - pair_at) * 128, 128, 0)
         pre = keep + swap(send, "pair") + enc_bias
         return (pre * jax.nn.sigmoid((pre - thresh_level) / smooth_width)).astype(BF)
 
-    parts, chunk = 4, D // 4
-    encode = call(
-        encode_kernel,
-        "encode",
-        2 * 256 * D * own,
-        [((128, own), F32), ((128, own), F32)],
-        0,
-        [
-            pltpu.VMEM((parts, 256, chunk), BF),
-            pltpu.VMEM((parts, chunk, own), BF),
-            pltpu.VMEM((256, own), F32),
-            pltpu.SemaphoreType.DMA((2 * parts,)),
-        ],
-        2,
-    )
-    keep, send = encode(at, near, enc)
-    feats_near = features(keep, send)
+    feats_near = features(near)
     over = swap(jnp.concatenate([feats_near] + split(nsq_part), axis=0), "zh")
     over_near = over[:128]
     nsq_both = nsq_part + over[128:136].astype(F32) + over[136:144].astype(F32)
 
-    keep, send = encode(at, far, enc)
-    feats_far = features(keep, send)
-    over_far = swap(feats_far, "zh")
-    g1 = gather(
-        jnp.concatenate([feats_near, over_near, feats_far] + split(nsq_both), axis=0), "y"
-    )
-    over_far, g1 = lax.optimization_barrier((over_far, g1))
+    feats_far = features(far)
+    over_far = lax.dynamic_index_in_dim(gather(feats_far, "zh"), 1 - zh_at, 0, False)
+    packed = jnp.concatenate([feats_near, over_near, feats_far] + split(nsq_both), axis=0)
+    ring = [
+        lax.ppermute(packed, "y", [(i, (i + k) % 4) for i in range(4)]) for k in (1, 3, 2)
+    ]
+    over_far, *ring = lax.optimization_barrier((over_far, *ring))
+    g1 = jnp.stack([packed] + ring)
     g2 = gather(over_far, "y")
     p1 = swap(g1, "pair")
     p2 = swap(g2, "pair")
@@ -267,25 +252,26 @@
     )(at, g1, g2, p1, p2, dec_t, near, far)
     mean_sq = sum_sq[0] / tokens
 
-    total = jnp.sum(arrived.reshape(32, rows, 512).astype(F32), axis=0)
-    recon_vals = total[:, :width] + dec_bias[0]
-    sparse = total[:, width] + total[:, width + 1]
-    residue = act_own.astype(F32) - recon_vals
-    own_terms = jnp.sum(residue * residue, axis=1) / (2.0 * D) + penalty * sparse
-
-    last = jnp.concatenate(
-        [
-            jnp.broadcast_to(num_part.reshape(1, 8, own), (2, 8, own)),
-            jnp.broadcast_to(own_terms, (2, 8, rows)),
-        ],
-        axis=2,
-    ).reshape(16, own + rows)
+    recon, last = pl.pallas_call(
+        close_kernel,
+        out_shape=(
+            jax.ShapeDtypeStruct((rows, width), BF),
+            jax.ShapeDtypeStruct((16, 4, 128), F32),
+        ),
+        in_specs=[VMEM] * 4,
+        out_specs=(VMEM, VMEM),
+        compiler_params=pltpu.CompilerParams(vmem_limit_bytes=16 << 20),
+        cost_estimate=pl.CostEstimate(
+            flops=1 << 20, bytes_accessed=1 << 20, transcendentals=0
+        ),
+        name="close",
+    )(arrived.reshape(32, rows, 512), dec_bias, act_own, num_part)
     got = lax.all_to_all(last, ("pair",) + TOK, 0, 0, tiled=True)
-    token_loss = jnp.sum(got[:, own:], axis=0)
-    mine = lax.dynamic_slice_in_dim(got, pair_at * 8, 8, 0)[:, :own]
-    num_own = jnp.sum(mine, axis=0) / tokens
+    token_loss = jnp.sum(got[:, 2, :rows], axis=0)
+    mine = lax.dynamic_slice_in_dim(got, pair_at * 8, 8, 0)[:, :2, :]
+    num_own = jnp.sum(mine, axis=0).reshape(own) / tokens
     scaling = num_own / (nsq_own * mean_sq + tiny_term)
-    return (recon_vals.astype(BF)[None], token_loss, scaling[None])
+    return (recon[None], token_loss, scaling[None])
 
 
 def solution(mesh):

time: 190 us -> 196 us (1.032)
  starting transfers between devices: 96.8 us -> 106 us
  Pallas kernels: 17 us -> 9.53 us
  waiting for transfers between devices: 46.1 us -> 50.6 us
  matrix products: 0 us -> 4.28 us
  blocking collectives: 13.3 us -> 9.87 us
    ppermute x7 -> x6, starting transfers between devices: 58.7 us -> 47.7 us  [swap(): return lax.ppermute(value, axis, [(0, 1), (1, 0)])]
    all_to_all x3, starting transfers between devices: 17.5 us -> 28.2 us  [gather(): return lax.all_to_all(copies, axes, 0, 0, tiled=False)]
    ppermute x0 -> x3, starting transfers between devices: none -> 8.41 us  [body(): lax.ppermute(packed, 'y', [(i, (i + k) % 4) for i in range(4)])]
    pallas_call x2 -> x1, Pallas kernels: 8.01 us -> 0.85 us  [body(): pl.pallas_call(close_kernel, out_shape=(jax.ShapeDtypeStruct((rows, width...]
    dot_general x0 -> x2, matrix products: none -> 4.28 us  [features(): part = jnp.dot(acts, enc, preferred_element_type=F32)]
    all_to_all x3, waiting for transfers between devices: 0.01 us -> 3.79 us  [gather(): return lax.all_to_all(copies, axes, 0, 0, tiled=False)]
    all_to_all x1, blocking collectives: 13.3 us -> 9.87 us  [gather(): return lax.all_to_all(copies, axes, 0, 0, tiled=False)]
    ppermute x0 -> x3, waiting for transfers between devices: none -> 3.03 us  [body(): lax.ppermute(packed, 'y', [(i, (i + k) % 4) for i in range(4)])]
  transfers between devices with their start and end apart: 12 -> 14, of which waited for: 7 -> 8; matrix products, arithmetic and copies ran while one was open for 2% -> 4% of each run, Pallas kernels for 7% -> 3%
where the time goes in v6:
time: 196 us; the launch traced here: 195 us
  starting transfers between devices  106 us (54%)
  waiting for transfers between devices  50.6 us (26%)
  blocking collectives  9.87 us (5%)
  local copies, waits for them, and re-layouts  9.71 us (5%)
  Pallas kernels  9.53 us (5%)
  matrix products  4.28 us (2%)
  other arithmetic  3.95 us (2%)
    ppermute x6, starting transfers between devices, swap(): return lax.ppermute(value, axis, [(0, 1), (1, 0)])  47.7 us
    all_to_all x3, starting transfers between devices, gather(): return lax.all_to_all(copies, axes, 0, 0, tiled=False)  28.2 us
    all_to_all x1, waiting for transfers between devices, body(): arrived = lax.all_to_all(payload, LAT, 0, 0, tiled=True)  23.8 us
    all_to_all x1, waiting for transfers between devices, body(): got = lax.all_to_all(last, ('pair',) + TOK, 0, 0, tiled=True)  14.2 us
    all_to_all x1, starting transfers between devices, body(): got = lax.all_to_all(last, ('pair',) + TOK, 0, 0, tiled=True)  14.1 us
    all_to_all x1, blocking collectives, gather(): return lax.all_to_all(copies, axes, 0, 0, tiled=False)  9.87 us
    ppermute x3, starting transfers between devices, body(): lax.ppermute(packed, 'y', [(i, (i + k) % 4) for i in range(4)])  8.41 us
    all_to_all x1, starting transfers between devices, body(): arrived = lax.all_to_all(payload, LAT, 0, 0, tiled=True)  7.35 us
  transfers between devices with their start and end apart: 14, of which 8 were waited for; matrix products, arithmetic and copies ran while one was open for 4% of the time, Pallas kernels for 3%

profile of v6, /device:TPU:1, one launch (start us, length us, event | category | flops | bytes accessed | tf_op | source)
XLA Modules:
  0.0 194.6 jit_solution(12081859383737832307)
XLA Ops:
  0.6 2.5 %broadcast_in_dim.13 = bf16[4,64,3584]{2,1,0:T(8,128)(2,1)} broadcast(bf16[64,3584]{1,0:T(8,128)(2,1)} %bitcast.33), dimensions={1,2} | broadcast | bytes 2293760 | tf_op jit(solution)/shard_map/broadcast_in_dim | solution.py:29
  3.1 5.0 %all-to-all-start = ((bf16[4,64,3584]{2,1,0:T(8,128)(2,1)}), bf16[4,64,3584]{2,1,0:T(8,128)(2,1)}, u32[]{:S(2)}, u32[]{:S(2)}) async-start(bf16[4,64,3584]{2,1,0:T(8,128)(2,1)} %broadcast_in_dim.13), calls=%async_computation | async-start | bytes 3670016 | tf_op jit(solution)/shard_map/all_to_all | solution.py:30
  9.1 15.7 %collective-permute-start.2 = (bf16[16,3584]{1,0:T(8,128)(2,1)S(1)}, bf16[16,3584]{1,0:T(8,128)(2,1)S(1)}, u32[]{:S(2)}, u32[]{:S(2)}) collective-permute-start(bf16[16,3584]{1,0:T(8,128)(2,1)S(1)} %dynamic-slice_bitcast_fusion), channel_id=1, source_target_pairs={{0,1},{1,0},{2,3},{3,2},{4,5},{5,4},{6,7},{7,6},{8,9},{9,8},{10,11... | collective-permute-start | bytes 344072 | tf_op jit(solution)/shard_map/ppermute | solution.py:24
  24.7 2.5 %collective-permute-done.2 = bf16[16,3584]{1,0:T(8,128)(2,1)S(1)} collective-permute-done((bf16[16,3584]{1,0:T(8,128)(2,1)S(1)}, bf16[16,3584]{1,0:T(8,128)(2,1)S(1)}, u32[]{:S(2)}, u32[]{:S(2)}) %collective-permute-start.2) | collective-permute-done | bytes 114720 | tf_op jit(solution)/shard_map/ppermute | solution.py:24
  27.2 1.4 broadcast_in_dim.14
  28.6 8.8 %all-to-all-start.1 = ((bf16[16,16,3584]{2,1,0:T(8,128)(2,1)}), bf16[16,16,3584]{2,1,0:T(8,128)(2,1)}, u32[]{:S(2)}, u32[]{:S(2)}) async-start(bf16[16,16,3584]{2,1,0:T(8,128)(2,1)} %broadcast_in_dim.14), calls=%async_computation.1 | async-start | bytes 3670016 | tf_op jit(solution)/shard_map/all_to_all | solution.py:30
  37.5 1.9 multiply_reduce_fusion
  39.4 2.1 %fusion.2 = f32[256,256]{1,0:T(8,128)S(1)} fusion(bf16[256,3584]{1,0:T(8,128)(2,1)} %bitcast.6.near_hbm, bf16[1,3584,256]{2,1,0:T(8,128)(2,1)S(1)} %copy-done), kind=kOutput, calls=%fused_computation.3 | convolution fusion | flops 469762048 | bytes 3932160 | tf_op jit(solution)/shard_map/dot_general | solution.py:201
  41.6 3.9 %collective-permute-start = (f32[128,256]{1,0:T(8,128)S(1)}, f32[128,256]{1,0:T(8,128)S(1)}, u32[]{:S(2)}, u32[]{:S(2)}) collective-permute-start(f32[128,256]{1,0:T(8,128)S(1)} %constant_dynamic-slice_fusion.2), channel_id=1, source_target_pairs={{0,256},{256,0},{1,257},{257,1},{2,258},{258,2},{3,259},{259,3},{4... | collective-permute-start | bytes 393224 | tf_op jit(solution)/shard_map/ppermute | solution.py:24
  45.5 0.9 collective-permute-done
  46.5 15.8 %collective-permute-start.1 = (bf16[144,256]{1,0:T(8,128)(2,1)S(1)}, bf16[144,256]{1,0:T(8,128)(2,1)S(1)}, u32[]{:S(2)}, u32[]{:S(2)}) collective-permute-start(bf16[144,256]{1,0:T(8,128)(2,1)S(1)} %pad_maximum_fusion.1), channel_id=1, source_target_pairs={{0,1},{1,0},{2,3},{3,2},{4,5},{5,4},{6,7},{7,6},{8,9},{9,8},{10,11... | collective-permute-start | bytes 221192 | tf_op jit(solution)/shard_map/ppermute | solution.py:24
  62.3 2.1 %fusion = f32[256,256]{1,0:T(8,128)S(1)} fusion(bf16[256,3584]{1,0:T(8,128)(2,1)} %bitcast.10.far_hbm, bf16[1,3584,256]{2,1,0:T(8,128)(2,1)S(1)} %copy-done), kind=kOutput, calls=%fused_computation.1 | convolution fusion | flops 469762048 | bytes 3932160 | tf_op jit(solution)/shard_map/dot_general | solution.py:201
  64.5 5.3 %collective-permute-start.3 = (f32[128,256]{1,0:T(8,128)S(1)}, f32[128,256]{1,0:T(8,128)S(1)}, u32[]{:S(2)}, u32[]{:S(2)}) collective-permute-start(f32[128,256]{1,0:T(8,128)S(1)} %constant_dynamic-slice_fusion.1), channel_id=1, source_target_pairs={{0,256},{256,0},{1,257},{257,1},{2,258},{258,2},{3,259},{259,3},{4... | collective-permute-start | bytes 393224 | tf_op jit(solution)/shard_map/ppermute | solution.py:24
  69.8 0.9 collective-permute-done.3
  71.5 14.3 %all-to-all-start.2 = ((bf16[2,128,256]{2,1,0:T(8,128)(2,1)}), bf16[2,128,256]{2,1,0:T(8,128)(2,1)S(1)}, u32[]{:S(2)}, u32[]{:S(2)}) async-start(bf16[2,128,256]{2,1,0:T(8,128)(2,1)} %broadcast_in_dim.15), calls=%async_computation.2 | async-start | bytes 262144 | tf_op jit(solution)/shard_map/all_to_all | solution.py:30
  85.8 1.9 collective-permute-start.4
  87.8 4.6 %collective-permute-start.5 = (bf16[400,256]{1,0:T(8,128)(2,1)S(1)}, bf16[400,256]{1,0:T(8,128)(2,1)S(1)}, u32[]{:S(2)}, u32[]{:S(2)}) collective-permute-start(bf16[400,256]{1,0:T(8,128)(2,1)S(1)} %constant_dynamic-update-slice_fusion), channel_id=1, source_target_pairs={{0,6},{2,0},{4,2},{6,4},{1,7},{3,1},{5,3},{7,5},{8,14},{10,8},{12,... | collective-permute-start | bytes 614408 | tf_op jit(solution)/shard_map/ppermute | solution.py:216
  92.3 1.9 collective-permute-start.6
  94.3 3.8 %all-to-all-done.2 = bf16[2,128,256]{2,1,0:T(8,128)(2,1)S(1)} async-done(((bf16[2,128,256]{2,1,0:T(8,128)(2,1)}), bf16[2,128,256]{2,1,0:T(8,128)(2,1)S(1)}, u32[]{:S(2)}, u32[]{:S(2)}) %all-to-all-start.2) | async-done | bytes 131104 | tf_op jit(solution)/shard_map/all_to_all | solution.py:30
  98.1 3.0 %collective-permute-done.6 = bf16[400,256]{1,0:T(8,128)(2,1)S(1)} collective-permute-done((bf16[400,256]{1,0:T(8,128)(2,1)S(1)}, bf16[400,256]{1,0:T(8,128)(2,1)S(1)}, u32[]{:S(2)}, u32[]{:S(2)}) %collective-permute-start.6) | collective-permute-done | bytes 204832 | tf_op jit(solution)/shard_map/ppermute | solution.py:216
  101.2 4.0 %collective-permute-start.7 = (bf16[4,400,256]{2,1,0:T(8,128)(2,1)S(1)}, bf16[4,400,256]{2,1,0:T(8,128)(2,1)S(1)}, u32[]{:S(2)}, u32[]{:S(2)}) collective-permute-start(bf16[4,400,256]{2,1,0:T(8,128)(2,1)S(1)} %pad_maximum_fusion.g1), channel_id=1, source_target_pairs={{0,256},{256,0},{1,257},{257,1},{2,258},{258,2},{3,259},{259,3},{4... | collective-permute-start | bytes 2457608 | tf_op jit(solution)/shard_map/ppermute | solution.py:24
  105.3 9.9 %all_to_all.34.g2 = bf16[4,128,256]{2,1,0:T(8,128)(2,1)} all-to-all(bf16[4,128,256]{2,1,0:T(8,128)(2,1)S(1)} %broadcast_in_dim.16), channel_id=1, replica_groups=mesh['pair'=2,'x'=4,'zl'=8,'y'=4,'zh'=2] {'y'}, dimensions={0} | all-to-all | bytes 524288 | tf_op jit(solution)/shard_map/all_to_all | solution.py:30
  115.2 3.0 %collective-permute-start.8 = (bf16[4,128,256]{2,1,0:T(8,128)(2,1)}, bf16[4,128,256]{2,1,0:T(8,128)(2,1)}, u32[]{:S(2)}, u32[]{:S(2)}) collective-permute-start(bf16[4,128,256]{2,1,0:T(8,128)(2,1)} %all_to_all.34.g2), channel_id=1, source_target_pairs={{0,256},{256,0},{1,257},{257,1},{2,258},{258,2},{3,259},{259,3},{4... | collective-permute-start | bytes 786440 | tf_op jit(solution)/shard_map/ppermute | solution.py:24
  118.3 1.4 collective-permute-done.8.p2
  119.7 1.8 copy-done.1
  121.5 3.1 %decode.1 = (bf16[512,512]{1,0:T(8,128)(2,1)S(1)}, f32[8,256]{1,0:T(8,128)S(1)}) custom-call(s32[5]{0:T(128)S(1)} %stack.38.at_ref, bf16[4,400,256]{2,1,0:T(8,128)(2,1)S(1)} %pad_maximum_fusion.g1, bf16[4,128,256]{2,1,0:T(8,128)(2,1)} %all_to_all.34.g2, bf16[4,400,256]{2,1,0:T(8,128)(2,1)S(1)} %collective-permute-done.7.p1, ...), custom_call_target="tpu_custom_call" | custom-call | flops 1073741824 | bytes 6291456 | tf_op jit(solution)/shard_map/decode/pallas_call | solution.py:224
  125.4 7.4 %all-to-all-start.4 = ((bf16[32,16,512]{2,1,0:T(8,128)(2,1)}), bf16[32,16,512]{2,1,0:T(8,128)(2,1)S(1)}, u32[]{:S(2)}, u32[]{:S(2)}) async-start(bf16[32,16,512]{2,1,0:T(8,128)(2,1)} %bitcast.32), calls=%async_computation.4 | async-start | bytes 1048576 | tf_op jit(solution)/shard_map/all_to_all | solution.py:238
  132.8 5.6 %numer.1 = (f32[8,256]{1,0:T(8,128)}, f32[1,256]{1,0:T(1,128)}, bf16[16,448]{1,0:T(8,128)(2,1)}) custom-call(s32[5]{0:T(128)} %copy-done.7, bf16[4,400,256]{2,1,0:T(8,128)(2,1)} %copy-done.2, bf16[4,128,256]{2,1,0:T(8,128)(2,1)} %all_to_all.34.g2, bf16[4,400,256]{2,1,0:T(8,128)(2,1)} %copy-done.3, bf16[4,128,256]{2,1,0:T(8,128)(2,1)} %collective-permute-done.8.p2, ...), custom_call_target="tpu_custom_call" | custom-call | flops 939524096 | bytes 6291456 | tf_op jit(solution)/shard_map/numer/pallas_call | solution.py:240
  138.4 23.8 %all-to-all-done.4.arrived_ref = bf16[32,16,512]{2,1,0:T(8,128)(2,1)S(1)} async-done(((bf16[32,16,512]{2,1,0:T(8,128)(2,1)}), bf16[32,16,512]{2,1,0:T(8,128)(2,1)S(1)}, u32[]{:S(2)}, u32[]{:S(2)}) %all-to-all-start.4) | async-done | bytes 524320 | tf_op jit(solution)/shard_map/all_to_all | solution.py:238
  164.4 14.1 %all-to-all-start.5 = ((f32[16,4,128]{2,1,0:T(4,128)}), f32[16,4,128]{2,1,0:T(4,128)S(1)}, u32[]{:S(2)}, u32[]{:S(2)}) async-start(f32[16,4,128]{2,1,0:T(4,128)} %get-tuple-element.22), calls=%async_computation.5 | async-start | bytes 65536 | tf_op jit(solution)/shard_map/all_to_all | solution.py:269
  178.5 14.2 %all-to-all-done.5 = f32[16,4,128]{2,1,0:T(4,128)S(1)} async-done(((f32[16,4,128]{2,1,0:T(4,128)}), f32[16,4,128]{2,1,0:T(4,128)S(1)}, u32[]{:S(2)}, u32[]{:S(2)}) %all-to-all-start.5) | async-done | bytes 32800 | tf_op jit(solution)/shard_map/all_to_all | solution.py:269
  192.8 1.3 fusion.7
  (48 shorter events, 5.7 us)
Async XLA Ops:
  0.6 38.8 %copy-start = (bf16[1,3584,256]{2,1,0:T(8,128)(2,1)S(1)}, bf16[1,3584,256]{2,1,0:T(8,128)(2,1)}, u32[]{:S(2)}) copy-start(bf16[1,3584,256]{2,1,0:T(8,128)(2,1)} %param.7) | copy-start | bytes 5505028
  3.1 24.1 %all-to-all-start = ((bf16[4,64,3584]{2,1,0:T(8,128)(2,1)}), bf16[4,64,3584]{2,1,0:T(8,128)(2,1)}, u32[]{:S(2)}, u32[]{:S(2)}) async-start(bf16[4,64,3584]{2,1,0:T(8,128)(2,1)} %broadcast_in_dim.13), calls=%async_computation | async-start | bytes 3670016 | tf_op jit(solution)/shard_map/all_to_all | solution.py:30
  9.1 18.1 %collective-permute-start.2 = (bf16[16,3584]{1,0:T(8,128)(2,1)S(1)}, bf16[16,3584]{1,0:T(8,128)(2,1)S(1)}, u32[]{:S(2)}, u32[]{:S(2)}) collective-permute-start(bf16[16,3584]{1,0:T(8,128)(2,1)S(1)} %dynamic-slice_bitcast_fusion), channel_id=1, source_target_pairs={{0,1},{1,0},{2,3},{3,2},{4,5},{5,4},{6,7},{7,6},{8,9},{9,8},{10,11... | collective-permute-start | bytes 344072 | tf_op jit(solution)/shard_map/ppermute | solution.py:24
  28.6 33.7 %all-to-all-start.1 = ((bf16[16,16,3584]{2,1,0:T(8,128)(2,1)}), bf16[16,16,3584]{2,1,0:T(8,128)(2,1)}, u32[]{:S(2)}, u32[]{:S(2)}) async-start(bf16[16,16,3584]{2,1,0:T(8,128)(2,1)} %broadcast_in_dim.14), calls=%async_computation.1 | async-start | bytes 3670016 | tf_op jit(solution)/shard_map/all_to_all | solution.py:30
  39.4 6.1 %copy-start.10 = (s32[256]{0:T(256)S(1)}, s32[256]{0:T(256)}, u32[]{:S(2)}) copy-start(s32[256]{0:T(256)} %param.9) | copy-start | bytes 3076
  39.4 7.0 %copy-start.9 = (f32[256]{0:T(256)S(1)}, f32[256]{0:T(256)}, u32[]{:S(2)}) copy-start(f32[256]{0:T(256)} %param.8) | copy-start | bytes 3076
  41.6 4.8 %collective-permute-start = (f32[128,256]{1,0:T(8,128)S(1)}, f32[128,256]{1,0:T(8,128)S(1)}, u32[]{:S(2)}, u32[]{:S(2)}) collective-permute-start(f32[128,256]{1,0:T(8,128)S(1)} %constant_dynamic-slice_fusion.2), channel_id=1, source_target_pairs={{0,256},{256,0},{1,257},{257,1},{2,258},{258,2},{3,259},{259,3},{4... | collective-permute-start | bytes 393224 | tf_op jit(solution)/shard_map/ppermute | solution.py:24
  46.5 23.3 %collective-permute-start.1 = (bf16[144,256]{1,0:T(8,128)(2,1)S(1)}, bf16[144,256]{1,0:T(8,128)(2,1)S(1)}, u32[]{:S(2)}, u32[]{:S(2)}) collective-permute-start(bf16[144,256]{1,0:T(8,128)(2,1)S(1)} %pad_maximum_fusion.1), channel_id=1, source_target_pairs={{0,1},{1,0},{2,3},{3,2},{4,5},{5,4},{6,7},{7,6},{8,9},{9,8},{10,11... | collective-permute-start | bytes 221192 | tf_op jit(solution)/shard_map/ppermute | solution.py:24
  64.5 6.3 %collective-permute-start.3 = (f32[128,256]{1,0:T(8,128)S(1)}, f32[128,256]{1,0:T(8,128)S(1)}, u32[]{:S(2)}, u32[]{:S(2)}) collective-permute-start(f32[128,256]{1,0:T(8,128)S(1)} %constant_dynamic-slice_fusion.1), channel_id=1, source_target_pairs={{0,256},{256,0},{1,257},{257,1},{2,258},{258,2},{3,259},{259,3},{4... | collective-permute-start | bytes 393224 | tf_op jit(solution)/shard_map/ppermute | solution.py:24
  71.5 26.6 %all-to-all-start.2 = ((bf16[2,128,256]{2,1,0:T(8,128)(2,1)}), bf16[2,128,256]{2,1,0:T(8,128)(2,1)S(1)}, u32[]{:S(2)}, u32[]{:S(2)}) async-start(bf16[2,128,256]{2,1,0:T(8,128)(2,1)} %broadcast_in_dim.15), calls=%async_computation.2 | async-start | bytes 262144 | tf_op jit(solution)/shard_map/all_to_all | solution.py:30
  85.8 12.2 %collective-permute-start.4 = (bf16[400,256]{1,0:T(8,128)(2,1)S(1)}, bf16[400,256]{1,0:T(8,128)(2,1)S(1)}, u32[]{:S(2)}, u32[]{:S(2)}) collective-permute-start(bf16[400,256]{1,0:T(8,128)(2,1)S(1)} %constant_dynamic-update-slice_fusion), channel_id=1, source_target_pairs={{0,2},{2,4},{4,6},{6,0},{1,3},{3,5},{5,7},{7,1},{8,10},{10,12},{12... | collective-permute-start | bytes 614408 | tf_op jit(solution)/shard_map/ppermute | solution.py:216
  87.8 10.3 %collective-permute-start.5 = (bf16[400,256]{1,0:T(8,128)(2,1)S(1)}, bf16[400,256]{1,0:T(8,128)(2,1)S(1)}, u32[]{:S(2)}, u32[]{:S(2)}) collective-permute-start(bf16[400,256]{1,0:T(8,128)(2,1)S(1)} %constant_dynamic-update-slice_fusion), channel_id=1, source_target_pairs={{0,6},{2,0},{4,2},{6,4},{1,7},{3,1},{5,3},{7,5},{8,14},{10,8},{12,... | collective-permute-start | bytes 614408 | tf_op jit(solution)/shard_map/ppermute | solution.py:216
  92.3 8.8 %collective-permute-start.6 = (bf16[400,256]{1,0:T(8,128)(2,1)S(1)}, bf16[400,256]{1,0:T(8,128)(2,1)S(1)}, u32[]{:S(2)}, u32[]{:S(2)}) collective-permute-start(bf16[400,256]{1,0:T(8,128)(2,1)S(1)} %constant_dynamic-update-slice_fusion), channel_id=1, source_target_pairs={{0,4},{2,6},{4,0},{6,2},{1,5},{3,7},{5,1},{7,3},{8,12},{10,14},{12... | collective-permute-start | bytes 614408 | tf_op jit(solution)/shard_map/ppermute | solution.py:216
  101.2 23.4 %copy-start.2 = (bf16[4,400,256]{2,1,0:T(8,128)(2,1)}, bf16[4,400,256]{2,1,0:T(8,128)(2,1)S(1)}, u32[]{:S(2)}) copy-start(bf16[4,400,256]{2,1,0:T(8,128)(2,1)S(1)} %pad_maximum_fusion.g1) | copy-start | bytes 2457604
  101.2 18.4 %collective-permute-start.7 = (bf16[4,400,256]{2,1,0:T(8,128)(2,1)S(1)}, bf16[4,400,256]{2,1,0:T(8,128)(2,1)S(1)}, u32[]{:S(2)}, u32[]{:S(2)}) collective-permute-start(bf16[4,400,256]{2,1,0:T(8,128)(2,1)S(1)} %pad_maximum_fusion.g1), channel_id=1, source_target_pairs={{0,256},{256,0},{1,257},{257,1},{2,258},{258,2},{3,259},{259,3},{4... | collective-permute-start | bytes 2457608 | tf_op jit(solution)/shard_map/ppermute | solution.py:24
  115.2 4.5 %collective-permute-start.8 = (bf16[4,128,256]{2,1,0:T(8,128)(2,1)}, bf16[4,128,256]{2,1,0:T(8,128)(2,1)}, u32[]{:S(2)}, u32[]{:S(2)}) collective-permute-start(bf16[4,128,256]{2,1,0:T(8,128)(2,1)} %all_to_all.34.g2), channel_id=1, source_target_pairs={{0,256},{256,0},{1,257},{257,1},{2,258},{258,2},{3,259},{259,3},{4... | collective-permute-start | bytes 786440 | tf_op jit(solution)/shard_map/ppermute | solution.py:24
  118.3 6.3 %copy-start.7 = (s32[5]{0:T(128)}, s32[5]{0:T(128)S(1)}, u32[]{:S(2)}) copy-start(s32[5]{0:T(128)S(1)} %stack.38.at_ref) | copy-start | bytes 64
  119.7 4.9 %copy-start.3 = (bf16[4,400,256]{2,1,0:T(8,128)(2,1)}, bf16[4,400,256]{2,1,0:T(8,128)(2,1)S(1)}, u32[]{:S(2)}) copy-start(bf16[4,400,256]{2,1,0:T(8,128)(2,1)S(1)} %collective-permute-done.7.p1) | copy-start | bytes 2457604
  119.7 1.8 copy-start.1
  124.6 0.8 copy-start.4
  125.4 36.7 %all-to-all-start.4 = ((bf16[32,16,512]{2,1,0:T(8,128)(2,1)}), bf16[32,16,512]{2,1,0:T(8,128)(2,1)S(1)}, u32[]{:S(2)}, u32[]{:S(2)}) async-start(bf16[32,16,512]{2,1,0:T(8,128)(2,1)} %bitcast.32), calls=%async_computation.4 | async-start | bytes 1048576 | tf_op jit(solution)/shard_map/all_to_all | solution.py:238
  132.8 29.4 %copy-start.8 = (f32[1,448]{1,0:T(1,128)S(1)}, f32[1,448]{1,0:T(1,128)}, u32[]{:S(2)}) copy-start(f32[1,448]{1,0:T(1,128)} %bias_ref.1) | copy-start | bytes 5380
  162.1 0.7 copy-start.5
  162.8 0.7 copy-start.6
  164.4 28.4 %all-to-all-start.5 = ((f32[16,4,128]{2,1,0:T(4,128)}), f32[16,4,128]{2,1,0:T(4,128)S(1)}, u32[]{:S(2)}, u32[]{:S(2)}) async-start(f32[16,4,128]{2,1,0:T(4,128)} %get-tuple-element.22), calls=%async_computation.5 | async-start | bytes 65536 | tf_op jit(solution)/shard_map/all_to_all | solution.py:269

commit v7 on v5

--- a/solution.py
+++ b/solution.py
@@ -14,7 +14,7 @@
 BF = jnp.bfloat16
 F32 = jnp.float32
 VMEM = pl.BlockSpec(memory_space=pltpu.VMEM)
-ANY = pl.BlockSpec(memory_space=pl.ANY)
+HBM = pl.BlockSpec(memory_space=pltpu.HBM)
 SMEM = pl.BlockSpec(memory_space=pltpu.SMEM)
 NT = (((1,), (1,)), ((), ()))
 
@@ -157,11 +157,42 @@
     own_ref[...] = a_ref[own_y // 2, pl.ds(pl.multiple_of(row, 16), 16), :]
 
 
+def close_kernel(
+    arrived_ref, bias_ref, act_hbm, num_hbm, recon_ref, last_ref, act_ref, num_ref, sems
+):
+    loads = [
+        pltpu.make_async_copy(act_hbm, act_ref, sems.at[0]),
+        pltpu.make_async_copy(num_hbm, num_ref, sems.at[1]),
+    ]
+    for copy in loads:
+        copy.start()
+    total = arrived_ref[0].astype(F32)
+    for k in range(1, 32):
+        total = total + arrived_ref[k].astype(F32)
+    recon = total[:, 0:448] + bias_ref[...]
+    recon_ref[...] = recon.astype(BF)
+    for copy in loads:
+        copy.wait()
+    residue = act_ref[...].astype(F32) - recon
+    sparse = total[:, 448:449] + total[:, 449:450]
+    terms = jnp.sum(residue * residue, axis=1, keepdims=True) / (2.0 * D) + penalty * sparse
+    row = lax.broadcasted_iota(jnp.int32, (16, 128), 0)
+    lane = lax.broadcasted_iota(jnp.int32, (16, 128), 1)
+    line = jnp.sum(jnp.where(row == lane, terms, 0.0), axis=0, keepdims=True)
+    for k in range(8):
+        for pair in range(2):
+            at = pair * 8 + k
+            last_ref[at, 0:1, :] = num_ref[k : k + 1, 0:128]
+            last_ref[at, 1:2, :] = num_ref[k : k + 1, 128:256]
+            last_ref[at, 2:3, :] = line
+            last_ref[at, 3:4, :] = line
+
+
 def call(kernel, name, flops, outs, count, scratch, outside=0, limit=60):
     return pl.pallas_call(
         kernel,
         out_shape=tuple(jax.ShapeDtypeStruct(shape, kind) for shape, kind in outs),
-        in_specs=[SMEM] + [VMEM] * count + [ANY] * outside,
+        in_specs=[SMEM] + [VMEM] * count + [HBM] * outside,
         out_specs=(VMEM,) * len(outs),
         scratch_shapes=scratch,
         compiler_params=pltpu.CompilerParams(vmem_limit_bytes=limit << 20),
@@ -199,10 +230,6 @@
         return [high, (value - high.astype(F32)).astype(BF)]
 
     thresh_level = thresholds.astype(F32) * 0.25
-
-    def features(keep, send):
-        pre = keep + swap(send, "pair") + enc_bias
-        return (pre * jax.nn.sigmoid((pre - thresh_level) / smooth_width)).astype(BF)
 
     parts, chunk = 4, D // 4
     encode = call(
@@ -219,14 +246,22 @@
         ],
         2,
     )
-    keep, send = encode(at, near, enc)
-    feats_near = features(keep, send)
+    def features(acts, ahead):
+        if ahead:
+            keep, send = encode(at, acts, enc)
+        else:
+            part = jnp.dot(acts, enc, preferred_element_type=F32)
+            keep = lax.dynamic_slice_in_dim(part, pair_at * 128, 128, 0)
+            send = lax.dynamic_slice_in_dim(part, (1 - pair_at) * 128, 128, 0)
+        pre = keep + swap(send, "pair") + enc_bias
+        return (pre * jax.nn.sigmoid((pre - thresh_level) / smooth_width)).astype(BF)
+
+    feats_near = features(near, True)
     over = swap(jnp.concatenate([feats_near] + split(nsq_part), axis=0), "zh")
     over_near = over[:128]
     nsq_both = nsq_part + over[128:136].astype(F32) + over[136:144].astype(F32)
 
-    keep, send = encode(at, far, enc)
-    feats_far = features(keep, send)
+    feats_far = features(far, False)
     over_far = swap(feats_far, "zh")
     g1 = gather(
         jnp.concatenate([feats_near, over_near, feats_far] + split(nsq_both), axis=0), "y"
@@ -264,28 +299,35 @@
             pltpu.SemaphoreType.DMA((2,)),
         ],
         2,
+        limit=40,
     )(at, g1, g2, p1, p2, dec_t, near, far)
     mean_sq = sum_sq[0] / tokens
 
-    total = jnp.sum(arrived.reshape(32, rows, 512).astype(F32), axis=0)
-    recon_vals = total[:, :width] + dec_bias[0]
-    sparse = total[:, width] + total[:, width + 1]
-    residue = act_own.astype(F32) - recon_vals
-    own_terms = jnp.sum(residue * residue, axis=1) / (2.0 * D) + penalty * sparse
-
-    last = jnp.concatenate(
-        [
-            jnp.broadcast_to(num_part.reshape(1, 8, own), (2, 8, own)),
-            jnp.broadcast_to(own_terms, (2, 8, rows)),
+    recon, last = pl.pallas_call(
+        close_kernel,
+        out_shape=(
+            jax.ShapeDtypeStruct((rows, width), BF),
+            jax.ShapeDtypeStruct((16, 4, 128), F32),
+        ),
+        in_specs=[VMEM, VMEM, HBM, HBM],
+        out_specs=(VMEM, VMEM),
+        scratch_shapes=[
+            pltpu.VMEM((rows, width), BF),
+            pltpu.VMEM((8, own), F32),
+            pltpu.SemaphoreType.DMA((2,)),
         ],
-        axis=2,
-    ).reshape(16, own + rows)
+        compiler_params=pltpu.CompilerParams(vmem_limit_bytes=16 << 20),
+        cost_estimate=pl.CostEstimate(
+            flops=1 << 20, bytes_accessed=1 << 20, transcendentals=0
+        ),
+        name="close",
+    )(arrived.reshape(32, rows, 512), dec_bias, act_own, num_part)
     got = lax.all_to_all(last, ("pair",) + TOK, 0, 0, tiled=True)
-    token_loss = jnp.sum(got[:, own:], axis=0)
-    mine = lax.dynamic_slice_in_dim(got, pair_at * 8, 8, 0)[:, :own]
-    num_own = jnp.sum(mine, axis=0) / tokens
+    token_loss = jnp.sum(got[:, 2, :rows], axis=0)
+    mine = lax.dynamic_slice_in_dim(got, pair_at * 8, 8, 0)[:, :2, :]
+    num_own = jnp.sum(mine, axis=0).reshape(own) / tokens
     scaling = num_own / (nsq_own * mean_sq + tiny_term)
-    return (recon_vals.astype(BF)[None], token_loss, scaling[None])
+    return (recon[None], token_loss, scaling[None])
 
 
 def solution(mesh):

time: 190 us -> 186 us (0.979)
  Pallas kernels: 17 us -> 11.9 us
  other arithmetic: 5.89 us -> 2.58 us
  local copies, waits for them, and re-layouts: 9.08 us -> 11.8 us
  matrix products: 0 us -> 2.69 us
    unnamed x23 -> x25, local copies, waits for them, and re-layouts: 1.32 us -> 5.43 us
    dot_general x0 -> x1, matrix products: none -> 2.69 us  [features(): part = jnp.dot(acts, enc, preferred_element_type=F32)]
    pallas_call x1, Pallas kernels: 5.57 us -> 3.25 us  [body(): call(numer_kernel, 'numer', 2 * tokens * 8 * own * width, [((8, own), F32...]
    pallas_call x2, Pallas kernels: 8.01 us -> 6.01 us  [the longest x1 4.07 us: features(): keep, send = encode(at, acts, enc)]
  transfers between devices with their start and end apart: 12 -> 12, of which waited for: 7 -> 7; matrix products, arithmetic and copies ran while one was open for 2% -> 3% of each run, Pallas kernels for 7% -> 4%
where the time goes in v7:
time: 186 us; the launch traced here: 185 us
  starting transfers between devices  97.5 us (52%)
  waiting for transfers between devices  44.8 us (24%)
  blocking collectives  13.3 us (7%)
  Pallas kernels  11.9 us (6%)
  local copies, waits for them, and re-layouts  11.8 us (6%)
  matrix products  2.69 us (1%)
  other arithmetic  2.58 us (1%)
    ppermute x7, starting transfers between devices, swap(): return lax.ppermute(value, axis, [(0, 1), (1, 0)])  58.8 us
    all_to_all x1, waiting for transfers between devices, body(): arrived = lax.all_to_all(payload, LAT, 0, 0, tiled=True)  22.7 us
    all_to_all x3, starting transfers between devices, gather(): return lax.all_to_all(copies, axes, 0, 0, tiled=False)  17.5 us
    all_to_all x1, waiting for transfers between devices, body(): got = lax.all_to_all(last, ('pair',) + TOK, 0, 0, tiled=True)  14.2 us
    all_to_all x1, blocking collectives, gather(): return lax.all_to_all(copies, axes, 0, 0, tiled=False)  13.3 us
    all_to_all x1, starting transfers between devices, body(): got = lax.all_to_all(last, ('pair',) + TOK, 0, 0, tiled=True)  11.9 us
    all_to_all x1, starting transfers between devices, body(): arrived = lax.all_to_all(payload, LAT, 0, 0, tiled=True)  9.43 us
    ppermute x7, waiting for transfers between devices, swap(): return lax.ppermute(value, axis, [(0, 1), (1, 0)])  7.86 us
  transfers between devices with their start and end apart: 12, of which 7 were waited for; matrix products, arithmetic and copies ran while one was open for 3% of the time, Pallas kernels for 4%

profile of v7, /device:TPU:1, one launch (start us, length us, event | category | flops | bytes accessed | tf_op | source)
XLA Modules:
  0.0 185.4 jit_solution(17688808613944175990)
XLA Ops:
  0.6 2.4 %broadcast_in_dim.14 = bf16[4,64,3584]{2,1,0:T(8,128)(2,1)} broadcast(bf16[64,3584]{1,0:T(8,128)(2,1)} %bitcast.27), dimensions={1,2} | broadcast | bytes 2293760 | tf_op jit(solution)/shard_map/broadcast_in_dim | solution.py:28
  3.0 5.0 %all-to-all-start.1 = ((bf16[4,64,3584]{2,1,0:T(8,128)(2,1)}), bf16[4,64,3584]{2,1,0:T(8,128)(2,1)S(1)}, u32[]{:S(2)}, u32[]{:S(2)}) async-start(bf16[4,64,3584]{2,1,0:T(8,128)(2,1)} %broadcast_in_dim.14), calls=%async_computation.1 | async-start | bytes 3670016 | tf_op jit(solution)/shard_map/all_to_all | solution.py:29
  9.0 15.4 %collective-permute-start = (bf16[16,3584]{1,0:T(8,128)(2,1)S(1)}, bf16[16,3584]{1,0:T(8,128)(2,1)S(1)}, u32[]{:S(2)}, u32[]{:S(2)}) collective-permute-start(bf16[16,3584]{1,0:T(8,128)(2,1)S(1)} %dynamic-slice_bitcast_fusion), channel_id=1, source_target_pairs={{0,1},{1,0},{2,3},{3,2},{4,5},{5,4},{6,7},{7,6},{8,9},{9,8},{10,11... | collective-permute-start | bytes 344072 | tf_op jit(solution)/shard_map/ppermute | solution.py:23
  24.4 2.5 %collective-permute-done = bf16[16,3584]{1,0:T(8,128)(2,1)S(1)} collective-permute-done((bf16[16,3584]{1,0:T(8,128)(2,1)S(1)}, bf16[16,3584]{1,0:T(8,128)(2,1)S(1)}, u32[]{:S(2)}, u32[]{:S(2)}) %collective-permute-start) | collective-permute-done | bytes 114720 | tf_op jit(solution)/shard_map/ppermute | solution.py:23
  26.9 1.2 copy-done.1
  28.1 1.4 broadcast_in_dim.12
  29.5 8.7 %all-to-all-start = ((bf16[16,16,3584]{2,1,0:T(8,128)(2,1)}), bf16[16,16,3584]{2,1,0:T(8,128)(2,1)}, u32[]{:S(2)}, u32[]{:S(2)}) async-start(bf16[16,16,3584]{2,1,0:T(8,128)(2,1)} %broadcast_in_dim.12), calls=%async_computation | async-start | bytes 3670016 | tf_op jit(solution)/shard_map/all_to_all | solution.py:29
  39.3 4.1 %encode.1 = (f32[128,256]{1,0:T(8,128)}, f32[128,256]{1,0:T(8,128)}) custom-call(s32[5]{0:T(128)} %stack.23.at_ref, bf16[256,3584]{1,0:T(8,128)(2,1)} %bitcast.23, bf16[3584,256]{1,0:T(8,128)(2,1)} %bitcast.26), custom_call_target="tpu_custom_call" | custom-call | flops 469762048 | bytes 6291456 | tf_op jit(solution)/shard_map/encode/pallas_call | solution.py:251
  43.4 7.3 %collective-permute-start.3 = (f32[128,256]{1,0:T(8,128)}, f32[128,256]{1,0:T(8,128)S(1)}, u32[]{:S(2)}, u32[]{:S(2)}) collective-permute-start(f32[128,256]{1,0:T(8,128)} %get-tuple-element.15), channel_id=1, source_target_pairs={{0,256},{256,0},{1,257},{257,1},{2,258},{258,2},{3,259},{259,3},{4... | collective-permute-start | bytes 393224 | tf_op jit(solution)/shard_map/ppermute | solution.py:23
  50.7 1.2 collective-permute-done.3
  51.9 1.0 constant_dynamic-update-slice_fusion.3
  52.8 12.8 %collective-permute-start.4 = (bf16[144,256]{1,0:T(8,128)(2,1)S(1)}, bf16[144,256]{1,0:T(8,128)(2,1)S(1)}, u32[]{:S(2)}, u32[]{:S(2)}) collective-permute-start(bf16[144,256]{1,0:T(8,128)(2,1)S(1)} %pad_maximum_fusion), channel_id=1, source_target_pairs={{0,1},{1,0},{2,3},{3,2},{4,5},{5,4},{6,7},{7,6},{8,9},{9,8},{10,11... | collective-permute-start | bytes 221192 | tf_op jit(solution)/shard_map/ppermute | solution.py:23
  65.7 2.7 %fusion.4 = f32[256,256]{1,0:T(8,128)S(1)} fusion(bf16[256,3584]{1,0:T(8,128)(2,1)} %bitcast.6.far_hbm, bf16[1,3584,256]{2,1,0:T(8,128)(2,1)} %param.7), kind=kOutput, calls=%fused_computation.23 | convolution fusion | flops 469762048 | bytes 3932160 | tf_op jit(solution)/shard_map/dot_general | solution.py:253
  68.4 3.2 %collective-permute-start.1 = (f32[128,256]{1,0:T(8,128)S(1)}, f32[128,256]{1,0:T(8,128)S(1)}, u32[]{:S(2)}, u32[]{:S(2)}) collective-permute-start(f32[128,256]{1,0:T(8,128)S(1)} %constant_dynamic-slice_fusion.1), channel_id=1, source_target_pairs={{0,256},{256,0},{1,257},{257,1},{2,258},{258,2},{3,259},{259,3},{4... | collective-permute-start | bytes 393224 | tf_op jit(solution)/shard_map/ppermute | solution.py:23
  71.6 0.9 collective-permute-done.1
  73.6 3.7 %all-to-all-start.2 = ((bf16[4,400,256]{2,1,0:T(8,128)(2,1)}), bf16[4,400,256]{2,1,0:T(8,128)(2,1)S(1)}, u32[]{:S(2)}, u32[]{:S(2)}) async-start(bf16[4,400,256]{2,1,0:T(8,128)(2,1)} %broadcast_in_dim.15), calls=%async_computation.2 | async-start | bytes 1638400 | tf_op jit(solution)/shard_map/all_to_all | solution.py:29
  77.3 14.1 %collective-permute-start.2 = (bf16[128,256]{1,0:T(8,128)(2,1)S(1)}, bf16[128,256]{1,0:T(8,128)(2,1)S(1)}, u32[]{:S(2)}, u32[]{:S(2)}) collective-permute-start(bf16[128,256]{1,0:T(8,128)(2,1)S(1)} %get-tuple-element.26), channel_id=1, source_target_pairs={{0,1},{1,0},{2,3},{3,2},{4,5},{5,4},{6,7},{7,6},{8,9},{9,8},{10,11... | collective-permute-start | bytes 196616 | tf_op jit(solution)/shard_map/ppermute | solution.py:23
  91.4 2.2 %collective-permute-done.2 = bf16[128,256]{1,0:T(8,128)(2,1)S(1)} collective-permute-done((bf16[128,256]{1,0:T(8,128)(2,1)S(1)}, bf16[128,256]{1,0:T(8,128)(2,1)S(1)}, u32[]{:S(2)}, u32[]{:S(2)}) %collective-permute-start.2) | collective-permute-done | bytes 65568 | tf_op jit(solution)/shard_map/ppermute | solution.py:23
  93.6 3.0 %collective-permute-start.5 = (bf16[4,400,256]{2,1,0:T(8,128)(2,1)S(1)}, bf16[4,400,256]{2,1,0:T(8,128)(2,1)S(1)}, u32[]{:S(2)}, u32[]{:S(2)}) collective-permute-start(bf16[4,400,256]{2,1,0:T(8,128)(2,1)S(1)} %all-to-all-done.2.g1), channel_id=1, source_target_pairs={{0,256},{256,0},{1,257},{257,1},{2,258},{258,2},{3,259},{259,3},{4... | collective-permute-start | bytes 2457608 | tf_op jit(solution)/shard_map/ppermute | solution.py:23
  96.6 13.3 %all_to_all.34.g2 = bf16[4,128,256]{2,1,0:T(8,128)(2,1)S(1)} all-to-all(bf16[4,128,256]{2,1,0:T(8,128)(2,1)S(1)} %broadcast_in_dim.16), channel_id=1, replica_groups=mesh['pair'=2,'x'=4,'zl'=8,'y'=4,'zh'=2] {'y'}, dimensions={0} | all-to-all | bytes 524288 | tf_op jit(solution)/shard_map/all_to_all | solution.py:29
  109.9 3.0 %collective-permute-start.6 = (bf16[4,128,256]{2,1,0:T(8,128)(2,1)S(1)}, bf16[4,128,256]{2,1,0:T(8,128)(2,1)S(1)}, u32[]{:S(2)}, u32[]{:S(2)}) collective-permute-start(bf16[4,128,256]{2,1,0:T(8,128)(2,1)S(1)} %all_to_all.34.g2), channel_id=1, source_target_pairs={{0,256},{256,0},{1,257},{257,1},{2,258},{258,2},{3,259},{259,3},{4... | collective-permute-start | bytes 786440 | tf_op jit(solution)/shard_map/ppermute | solution.py:23
  112.9 1.1 collective-permute-done.6.p2
  114.1 2.6 %decode.1 = (bf16[512,512]{1,0:T(8,128)(2,1)S(1)}, f32[8,256]{1,0:T(8,128)S(1)}) custom-call(s32[5]{0:T(128)S(1)} %copy-done.8, bf16[4,400,256]{2,1,0:T(8,128)(2,1)S(1)} %all-to-all-done.2.g1, bf16[4,128,256]{2,1,0:T(8,128)(2,1)S(1)} %all_to_all.34.g2, bf16[4,400,256]{2,1,0:T(8,128)(2,1)S(1)} %collective-permute-done.5.p1, ...), custom_call_target="tpu_custom_call" | custom-call | flops 1073741824 | bytes 6291456 | tf_op jit(solution)/shard_map/decode/pallas_call | solution.py:274
  117.5 9.4 %all-to-all-start.4 = ((bf16[32,16,512]{2,1,0:T(8,128)(2,1)}), bf16[32,16,512]{2,1,0:T(8,128)(2,1)}, u32[]{:S(2)}, u32[]{:S(2)}) async-start(bf16[32,16,512]{2,1,0:T(8,128)(2,1)} %bitcast.25), calls=%async_computation.4 | async-start | bytes 1048576 | tf_op jit(solution)/shard_map/all_to_all | solution.py:288
  126.9 1.5 copy-done.2
  128.4 0.9 copy-done.4
  129.4 0.9 copy-done.6
  130.3 3.3 %numer.1 = (f32[8,256]{1,0:T(8,128)S(1)}, f32[1,256]{1,0:T(1,128)S(1)}, bf16[16,448]{1,0:T(8,128)(2,1)S(1)}) custom-call(s32[5]{0:T(128)S(1)} %copy-done.8, bf16[4,400,256]{2,1,0:T(8,128)(2,1)S(1)} %all-to-all-done.2.g1, bf16[4,128,256]{2,1,0:T(8,128)(2,1)S(1)} %copy-done.4, bf16[4,400,256]{2,1,0:T(8,128)(2,1)S(1)} %collective-permute-done.5.p1, ...), custom_call_target="tpu_custom_call" | custom-call | flops 939524096 | bytes 6291456 | tf_op jit(solution)/shard_map/numer/pallas_call | solution.py:290
  133.6 22.7 %all-to-all-done.4.arrived_ref = bf16[32,16,512]{2,1,0:T(8,128)(2,1)} async-done(((bf16[32,16,512]{2,1,0:T(8,128)(2,1)}), bf16[32,16,512]{2,1,0:T(8,128)(2,1)}, u32[]{:S(2)}, u32[]{:S(2)}) %all-to-all-start.4) | async-done | bytes 524320 | tf_op jit(solution)/shard_map/all_to_all | solution.py:288
  156.2 1.9 %close.1 = (bf16[16,448]{1,0:T(8,128)(2,1)}, f32[16,4,128]{2,1,0:T(4,128)}) custom-call(bf16[32,16,512]{2,1,0:T(8,128)(2,1)} %all-to-all-done.4.arrived_ref, f32[1,448]{1,0:T(1,128)S(1)} %copy-done.9, bf16[16,448]{1,0:T(8,128)(2,1)S(1)} %get-tuple-element.19.act_hbm, f32[8,256]{1,0:T(8,128)S(1)} %get-tuple-element.20.num_hbm), custom_call_target="tpu_custom_call" | custom-call | flops 1048576 | bytes 1048576 | tf_op jit(solution)/shard_map/close/pallas_call | solution.py:306
  158.2 11.9 %all-to-all-start.5 = ((f32[16,4,128]{2,1,0:T(4,128)}), f32[16,4,128]{2,1,0:T(4,128)S(1)}, u32[]{:S(2)}, u32[]{:S(2)}) async-start(f32[16,4,128]{2,1,0:T(4,128)} %get-tuple-element.22), calls=%async_computation.5 | async-start | bytes 65536 | tf_op jit(solution)/shard_map/all_to_all | solution.py:325
  170.0 14.2 %all-to-all-done.5 = f32[16,4,128]{2,1,0:T(4,128)S(1)} async-done(((f32[16,4,128]{2,1,0:T(4,128)}), f32[16,4,128]{2,1,0:T(4,128)S(1)}, u32[]{:S(2)}, u32[]{:S(2)}) %all-to-all-start.5) | async-done | bytes 32800 | tf_op jit(solution)/shard_map/all_to_all | solution.py:325
  (43 shorter events, 5.0 us)
Async XLA Ops:
  3.0 23.8 %all-to-all-start.1 = ((bf16[4,64,3584]{2,1,0:T(8,128)(2,1)}), bf16[4,64,3584]{2,1,0:T(8,128)(2,1)S(1)}, u32[]{:S(2)}, u32[]{:S(2)}) async-start(bf16[4,64,3584]{2,1,0:T(8,128)(2,1)} %broadcast_in_dim.14), calls=%async_computation.1 | async-start | bytes 3670016 | tf_op jit(solution)/shard_map/all_to_all | solution.py:29
  9.0 17.9 %collective-permute-start = (bf16[16,3584]{1,0:T(8,128)(2,1)S(1)}, bf16[16,3584]{1,0:T(8,128)(2,1)S(1)}, u32[]{:S(2)}, u32[]{:S(2)}) collective-permute-start(bf16[16,3584]{1,0:T(8,128)(2,1)S(1)} %dynamic-slice_bitcast_fusion), channel_id=1, source_target_pairs={{0,1},{1,0},{2,3},{3,2},{4,5},{5,4},{6,7},{7,6},{8,9},{9,8},{10,11... | collective-permute-start | bytes 344072 | tf_op jit(solution)/shard_map/ppermute | solution.py:23
  26.9 1.2 copy-start.1
  29.5 8.7 %copy-start = (bf16[1,2048,448]{1,2,0:T(8,128)(2,1)S(1)}, bf16[1,2048,448]{1,2,0:T(8,128)(2,1)}, u32[]{:S(2)}) copy-start(bf16[1,2048,448]{1,2,0:T(8,128)(2,1)} %param.10) | copy-start | bytes 5505028
  29.5 36.1 %all-to-all-start = ((bf16[16,16,3584]{2,1,0:T(8,128)(2,1)}), bf16[16,16,3584]{2,1,0:T(8,128)(2,1)}, u32[]{:S(2)}, u32[]{:S(2)}) async-start(bf16[16,16,3584]{2,1,0:T(8,128)(2,1)} %broadcast_in_dim.12), calls=%async_computation | async-start | bytes 3670016 | tf_op jit(solution)/shard_map/all_to_all | solution.py:29
  39.3 11.4 %copy-start.11 = (s32[256]{0:T(256)S(1)}, s32[256]{0:T(256)}, u32[]{:S(2)}) copy-start(s32[256]{0:T(256)} %param.9) | copy-start | bytes 3076
  39.3 12.6 %copy-start.10 = (f32[256]{0:T(256)S(1)}, f32[256]{0:T(256)}, u32[]{:S(2)}) copy-start(f32[256]{0:T(256)} %param.8) | copy-start | bytes 3076
  43.4 8.5 %collective-permute-start.3 = (f32[128,256]{1,0:T(8,128)}, f32[128,256]{1,0:T(8,128)S(1)}, u32[]{:S(2)}, u32[]{:S(2)}) collective-permute-start(f32[128,256]{1,0:T(8,128)} %get-tuple-element.15), channel_id=1, source_target_pairs={{0,256},{256,0},{1,257},{257,1},{2,258},{258,2},{3,259},{259,3},{4... | collective-permute-start | bytes 393224 | tf_op jit(solution)/shard_map/ppermute | solution.py:23
  52.8 18.7 %collective-permute-start.4 = (bf16[144,256]{1,0:T(8,128)(2,1)S(1)}, bf16[144,256]{1,0:T(8,128)(2,1)S(1)}, u32[]{:S(2)}, u32[]{:S(2)}) collective-permute-start(bf16[144,256]{1,0:T(8,128)(2,1)S(1)} %pad_maximum_fusion), channel_id=1, source_target_pairs={{0,1},{1,0},{2,3},{3,2},{4,5},{5,4},{6,7},{7,6},{8,9},{9,8},{10,11... | collective-permute-start | bytes 221192 | tf_op jit(solution)/shard_map/ppermute | solution.py:23
  68.4 4.1 %collective-permute-start.1 = (f32[128,256]{1,0:T(8,128)S(1)}, f32[128,256]{1,0:T(8,128)S(1)}, u32[]{:S(2)}, u32[]{:S(2)}) collective-permute-start(f32[128,256]{1,0:T(8,128)S(1)} %constant_dynamic-slice_fusion.1), channel_id=1, source_target_pairs={{0,256},{256,0},{1,257},{257,1},{2,258},{258,2},{3,259},{259,3},{4... | collective-permute-start | bytes 393224 | tf_op jit(solution)/shard_map/ppermute | solution.py:23
  72.6 41.5 %copy-start.8 = (s32[5]{0:T(128)S(1)}, s32[5]{0:T(128)}, u32[]{:S(2)}) copy-start(s32[5]{0:T(128)} %stack.23.at_ref) | copy-start | bytes 64
  73.6 20.0 %all-to-all-start.2 = ((bf16[4,400,256]{2,1,0:T(8,128)(2,1)}), bf16[4,400,256]{2,1,0:T(8,128)(2,1)S(1)}, u32[]{:S(2)}, u32[]{:S(2)}) async-start(bf16[4,400,256]{2,1,0:T(8,128)(2,1)} %broadcast_in_dim.15), calls=%async_computation.2 | async-start | bytes 1638400 | tf_op jit(solution)/shard_map/all_to_all | solution.py:29
  77.3 16.3 %collective-permute-start.2 = (bf16[128,256]{1,0:T(8,128)(2,1)S(1)}, bf16[128,256]{1,0:T(8,128)(2,1)S(1)}, u32[]{:S(2)}, u32[]{:S(2)}) collective-permute-start(bf16[128,256]{1,0:T(8,128)(2,1)S(1)} %get-tuple-element.26), channel_id=1, source_target_pairs={{0,1},{1,0},{2,3},{3,2},{4,5},{5,4},{6,7},{7,6},{8,9},{9,8},{10,11... | collective-permute-start | bytes 196616 | tf_op jit(solution)/shard_map/ppermute | solution.py:23
  93.6 20.5 %collective-permute-start.5 = (bf16[4,400,256]{2,1,0:T(8,128)(2,1)S(1)}, bf16[4,400,256]{2,1,0:T(8,128)(2,1)S(1)}, u32[]{:S(2)}, u32[]{:S(2)}) collective-permute-start(bf16[4,400,256]{2,1,0:T(8,128)(2,1)S(1)} %all-to-all-done.2.g1), channel_id=1, source_target_pairs={{0,256},{256,0},{1,257},{257,1},{2,258},{258,2},{3,259},{259,3},{4... | collective-permute-start | bytes 2457608 | tf_op jit(solution)/shard_map/ppermute | solution.py:23
  109.9 6.8 %copy-start.3 = (bf16[4,128,256]{2,1,0:T(8,128)(2,1)}, bf16[4,128,256]{2,1,0:T(8,128)(2,1)S(1)}, u32[]{:S(2)}) copy-start(bf16[4,128,256]{2,1,0:T(8,128)(2,1)S(1)} %all_to_all.34.g2) | copy-start | bytes 786436
  109.9 4.2 %collective-permute-start.6 = (bf16[4,128,256]{2,1,0:T(8,128)(2,1)S(1)}, bf16[4,128,256]{2,1,0:T(8,128)(2,1)S(1)}, u32[]{:S(2)}, u32[]{:S(2)}) collective-permute-start(bf16[4,128,256]{2,1,0:T(8,128)(2,1)S(1)} %all_to_all.34.g2), channel_id=1, source_target_pairs={{0,256},{256,0},{1,257},{257,1},{2,258},{258,2},{3,259},{259,3},{4... | collective-permute-start | bytes 786440 | tf_op jit(solution)/shard_map/ppermute | solution.py:23
  114.0 2.6 %copy-start.5 = (bf16[4,128,256]{2,1,0:T(8,128)(2,1)}, bf16[4,128,256]{2,1,0:T(8,128)(2,1)S(1)}, u32[]{:S(2)}) copy-start(bf16[4,128,256]{2,1,0:T(8,128)(2,1)S(1)} %collective-permute-done.6.p2) | copy-start | bytes 786436
  116.7 0.8 copy-start.7
  117.5 38.8 %all-to-all-start.4 = ((bf16[32,16,512]{2,1,0:T(8,128)(2,1)}), bf16[32,16,512]{2,1,0:T(8,128)(2,1)}, u32[]{:S(2)}, u32[]{:S(2)}) async-start(bf16[32,16,512]{2,1,0:T(8,128)(2,1)} %bitcast.25), calls=%async_computation.4 | async-start | bytes 1048576 | tf_op jit(solution)/shard_map/all_to_all | solution.py:288
  126.9 1.5 copy-start.2
  128.4 0.9 copy-start.4
  129.4 0.9 copy-start.6
  130.3 25.9 %copy-start.9 = (f32[1,448]{1,0:T(1,128)S(1)}, f32[1,448]{1,0:T(1,128)}, u32[]{:S(2)}) copy-start(f32[1,448]{1,0:T(1,128)} %bias_ref.1) | copy-start | bytes 5380
  158.2 26.1 %all-to-all-start.5 = ((f32[16,4,128]{2,1,0:T(4,128)}), f32[16,4,128]{2,1,0:T(4,128)S(1)}, u32[]{:S(2)}, u32[]{:S(2)}) async-start(f32[16,4,128]{2,1,0:T(4,128)} %get-tuple-element.22), calls=%async_computation.5 | async-start | bytes 65536 | tf_op jit(solution)/shard_map/all_to_all | solution.py:325

commit v8 on v7

v8 whole, which is shorter than its diff:
```python
import jax
import jax.numpy as jnp
from jax import lax
from jax.experimental import pallas as pl
from jax.experimental.pallas import tpu as pltpu
from jax.sharding import Mesh, PartitionSpec as P

D = 3584
smooth_width = 0.1
penalty = 0.0001
tiny_term = 1e-06
LAT = ("x", "zl")
TOK = ("y", "zh")
BF = jnp.bfloat16
F32 = jnp.float32
VMEM = pl.BlockSpec(memory_space=pltpu.VMEM)
HBM = pl.BlockSpec(memory_space=pltpu.HBM)
SMEM = pl.BlockSpec(memory_space=pltpu.SMEM)
NT = (((1,), (1,)), ((), ()))


def swap(value, axis):
    return lax.ppermute(value, axis, [(0, 1), (1, 0)])


def gather(value, axes):
    size = lax.axis_size(axes)
    copies = jnp.broadcast_to(value[None], (size,) + value.shape)
    return lax.all_to_all(copies, axes, 0, 0, tiled=False)


def encode_kernel(at_ref, act_hbm, enc_hbm, keep_ref, send_ref, a_ref, enc_ref, v_ref, sems):
    pair_at = at_ref[0]
    count = a_ref.shape[0]
    chunk = a_ref.shape[2]
    loads = []
    for k in range(count):
        span = pl.ds(k * chunk, chunk)
        loads.append(
            (
                pltpu.make_async_copy(act_hbm.at[:, span], a_ref.at[k], sems.at[2 * k]),
                pltpu.make_async_copy(enc_hbm.at[span], enc_ref.at[k], sems.at[2 * k + 1]),
            )
        )
    for pair in loads:
        for copy in pair:
            copy.start()
    for k in range(count):
        for copy in loads[k]:
            copy.wait()
        part = jnp.dot(a_ref[k], enc_ref[k], preferred_element_type=F32)
        if k == 0:
            v_ref[...] = part
        else:
            v_ref[...] += part
    for j in range(16):
        rows = slice(j * 8, (j + 1) * 8)
        kept = pl.multiple_of(j * 16 + pair_at * 8, 8)
        sent = pl.multiple_of(j * 16 + (1 - pair_at) * 8, 8)
        keep_ref[rows, :] = v_ref[pl.ds(kept, 8), :]
        send_ref[rows, :] = v_ref[pl.ds(sent, 8), :]


def decode_kernel(
    at_ref, g1, g2, dec_ref, oth_ref, out_ref, nsq_ref, f_ref, wide_ref, norm_ref
):
    zh_at = at_ref[1]

    nsq = [jnp.zeros((8, 256), F32)] * 2
    for y in range(4):
        rows = g1[y, 384:416, :].astype(F32)
        nsq[0] = nsq[0] + (rows[0:8] + rows[8:16])
        nsq[1] = nsq[1] + (rows[16:24] + rows[24:32])
    nsq_ref[...] = nsq[0]
    norm = (jnp.sqrt(nsq[0]) + jnp.sqrt(nsq[1])) * 0.125
    high = norm.astype(BF).astype(F32)
    wide_ref[...] = jnp.zeros_like(wide_ref)
    for k in range(8):
        wide_ref[0:1, k * 256 : (k + 1) * 256] = high[k : k + 1]
        wide_ref[1:2, k * 256 : (k + 1) * 256] = (norm - high)[k : k + 1]
    norm_ref[...] = wide_ref[...].astype(BF)

    for y in range(4):
        mine = pl.multiple_of((2 * y + zh_at) * 256, 256)
        theirs = pl.multiple_of((2 * y + 1 - zh_at) * 256, 256)
        f_ref[0:128, pl.ds(mine, 256)] = g1[y, 0:128, :]
        f_ref[128:256, pl.ds(theirs, 256)] = g1[y, 128:256, :]
        f_ref[128:256, pl.ds(mine, 256)] = g1[y, 256:384, :]
        f_ref[0:128, pl.ds(theirs, 256)] = g2[y]
    feats = f_ref[...]
    out = []
    for ref in (dec_ref, norm_ref, oth_ref):
        value = lax.dot_general(feats, ref[...], NT, preferred_element_type=F32)
        out.append(value.astype(BF))
    for half in range(2):
        zh = zh_at if half == 0 else 1 - zh_at
        for y in range(4):
            src = slice(half * 128 + y * 32, half * 128 + (y + 1) * 32)
            dst = pl.ds(pl.multiple_of((2 * y + zh) * 32, 32), 32)
            out_ref[dst, 0:448] = out[0][src]
            out_ref[dst, 448:512] = out[1][src]
            out_ref[dst, 512:960] = out[2][src]
            out_ref[dst, 960:1024] = jnp.zeros((32, 64), BF)


def numer_kernel(
    at_ref, g1, g2, dec_ref, oth_ref, own_ref, his_ref, num_ref, his_num_ref, msq_ref
):
    zh_at, y_at = at_ref[1], at_ref[3]
    for acts, dec, num in ((own_ref, dec_ref, num_ref), (his_ref, oth_ref, his_num_ref)):
        for y in range(4):
            for zh in range(2):
                at = 2 * y + (zh_at if zh == 0 else 1 - zh_at)
                cols = dec[:, pl.ds(pl.multiple_of(at * 256, 256), 256)]
                inner = jnp.dot(acts[...], cols, preferred_element_type=F32)
                near = g1[y, 0:128, :] if zh == 0 else g2[y]
                far = g1[y, 256:384, :] if zh == 0 else g1[y, 128:256, :]
                both = inner[0:128] * near.astype(F32) + inner[128:256] * far.astype(F32)
                num[pl.ds(at, 1), :] = jnp.sum(both, axis=0, keepdims=True)

    squares = jnp.zeros((128, 256), F32)
    for rows in (slice(0, 128), slice(256, 384)):
        feats = g1[y_at, rows, :].astype(F32)
        squares = squares + feats * feats
    msq_ref[...] = jnp.sum(squares, axis=0, keepdims=True)


def close_kernel(
    at_ref,
    arrived_ref,
    bias_ref,
    his_bias_ref,
    act_ref,
    his_act_ref,
    num_ref,
    his_num_ref,
    recon_ref,
    his_recon_ref,
    last_ref,
):
    pair_at = at_ref[0]
    total = arrived_ref[0].astype(F32)
    for k in range(1, 32):
        total = total + arrived_ref[k].astype(F32)
    terms = penalty * (total[:, 448:449] + total[:, 449:450])
    for at, bias, act, out in (
        (0, bias_ref, act_ref, recon_ref),
        (512, his_bias_ref, his_act_ref, his_recon_ref),
    ):
        recon = total[:, at : at + 448] + bias[...]
        out[...] = recon.astype(BF)
        residue = act[...].astype(F32) - recon
        terms = terms + jnp.sum(residue * residue, axis=1, keepdims=True) / (2.0 * D)
    row = lax.broadcasted_iota(jnp.int32, (8, 128), 0)
    lane = lax.broadcasted_iota(jnp.int32, (8, 128), 1)
    line = jnp.sum(jnp.where(row + pair_at * 8 == lane, terms, 0.0), axis=0, keepdims=True)
    for pair in range(2):
        num = jnp.where(pair_at == pair, num_ref[...], his_num_ref[...])
        for k in range(8):
            at = pair * 8 + k
            last_ref[at, 0:1, :] = num[k : k + 1, 0:128]
            last_ref[at, 1:2, :] = num[k : k + 1, 128:256]
            last_ref[at, 2:3, :] = line
            last_ref[at, 3:4, :] = line


def call(kernel, name, flops, outs, count, scratch, outside=0, limit=60):
    return pl.pallas_call(
        kernel,
        out_shape=tuple(jax.ShapeDtypeStruct(shape, kind) for shape, kind in outs),
        in_specs=[SMEM] + [VMEM] * count + [HBM] * outside,
        out_specs=(VMEM,) * len(outs),
        scratch_shapes=scratch,
        compiler_params=pltpu.CompilerParams(vmem_limit_bytes=limit << 20),
        cost_estimate=pl.CostEstimate(
            flops=flops, bytes_accessed=6 << 20, transcendentals=0
        ),
        name=name,
    )


def body(activations, enc_weight, enc_bias, thresholds, dec_weight, dec_bias):
    pair_at = lax.axis_index("pair")
    x_at = lax.axis_index("x")
    zh_at = lax.axis_index("zh")
    tok_at = lax.axis_index(TOK)
    lat_at = lax.axis_index(LAT)
    act = activations[0]
    enc = enc_weight[0]
    dec = dec_weight[0]
    dec_t = dec.T
    own, width = enc.shape[1], dec.shape[1]
    tokens = 8 * act.shape[0]
    rows = tokens // lax.axis_size(LAT)
    at = jnp.stack([pair_at, zh_at, tok_at, lax.axis_index("y"), lat_at]).astype(jnp.int32)

    quarter = swap(lax.dynamic_slice_in_dim(act, x_at * 16, 16, 0), "zh")
    near = gather(act, "y").reshape(256, D)
    far = gather(quarter, ("y", "x")).reshape(256, D)

    dec_wide = dec.astype(F32)
    nsq_part = jnp.sum(dec_wide * dec_wide, axis=1).reshape(8, own)

    def split(value):
        high = value.astype(BF)
        return [high, (value - high.astype(F32)).astype(BF)]

    thresh_level = thresholds.astype(F32) * 0.25

    parts, chunk = 4, D // 4
    encode = call(
        encode_kernel,
        "encode",
        2 * 256 * D * own,
        [((128, own), F32), ((128, own), F32)],
        0,
        [
            pltpu.VMEM((parts, 256, chunk), BF),
            pltpu.VMEM((parts, chunk, own), BF),
            pltpu.VMEM((256, own), F32),
            pltpu.SemaphoreType.DMA((2 * parts,)),
        ],
        2,
    )
    def halves(value):
        split_rows = value.reshape(16, 2, 8, value.shape[1])
        return [
            lax.dynamic_index_in_dim(split_rows, k, 1, False).reshape(128, value.shape[1])
            for k in (pair_at, 1 - pair_at)
        ]

    def features(acts, ahead):
        if ahead:
            keep, send = encode(at, acts, enc)
        else:
            keep, send = halves(jnp.dot(acts, enc, preferred_element_type=F32))
        pre = keep + swap(send, "pair") + enc_bias
        return (pre * jax.nn.sigmoid((pre - thresh_level) / smooth_width)).astype(BF)

    feats_near = features(near, True)
    nsq_two = [nsq_part, swap(nsq_part, "pair")]
    over = swap(
        jnp.concatenate([feats_near] + split(nsq_two[0]) + split(nsq_two[1]), axis=0), "zh"
    )
    over_near = over[:128]
    nsq_rows = []
    for k in range(2):
        rest = over[128 + 16 * k : 144 + 16 * k].astype(F32)
        nsq_rows += split(nsq_two[k] + rest[0:8] + rest[8:16])
    nsq_rows = lax.optimization_barrier(jnp.concatenate(nsq_rows, axis=0))
    dec_held, _ = lax.optimization_barrier((dec_t, feats_near))
    dec_oth = swap(dec_held, "pair")

    feats_far = features(far, False)
    over_far = swap(feats_far, "zh")
    g1 = gather(
        jnp.concatenate([feats_near, over_near, feats_far, nsq_rows], axis=0), "y"
    )
    over_far, g1 = lax.optimization_barrier((over_far, g1))
    g2 = gather(over_far, "y")

    payload, nsq_all = call(
        decode_kernel,
        "decode",
        2 * tokens * 8 * own * 512,
        [((tokens // 2, 1024), BF), ((8, own), F32)],
        4,
        [
            pltpu.VMEM((tokens // 2, 8 * own), BF),
            pltpu.VMEM((64, 8 * own), F32),
            pltpu.VMEM((64, 8 * own), BF),
        ],
        limit=40,
    )(at, g1, g2, dec_t, dec_oth)
    nsq_own = lax.dynamic_index_in_dim(nsq_all, tok_at, 0, keepdims=False)
    arrived = lax.all_to_all(payload.reshape(32, 8, 1024), LAT, 0, 0)

    cols = [
        halves(lax.dynamic_slice_in_dim(acts, tok_at * width, width, 1)) for acts in (near, far)
    ]
    own_acts = jnp.concatenate([cols[0][0], cols[1][0]], axis=0)
    bias_rows, rest = [], dec_bias
    for _ in range(3):
        bias_rows.append(rest.astype(BF))
        rest = rest - bias_rows[-1].astype(F32)
    sent = jnp.concatenate([cols[0][1], cols[1][1]] + bias_rows, axis=0)
    came = swap(sent, "pair")
    his_acts = came[:256]
    his_bias = jnp.sum(came[256:259].astype(F32), axis=0, keepdims=True)
    num_part, his_num, sum_sq = call(
        numer_kernel,
        "numer",
        2 * tokens * 8 * own * width,
        [((8, own), F32), ((8, own), F32), ((1, own), F32)],
        6,
        [],
        limit=40,
    )(at, g1, g2, dec_t, dec_oth, own_acts, his_acts)
    mean_sq = (sum_sq + swap(sum_sq, "pair"))[0] / tokens

    own_row = jnp.where((lat_at // 4) % 2 == zh_at, 0, 128)
    own_row = own_row + (lat_at // 8) * 32 + (lat_at % 4) * 8
    act_own, his_own = [
        lax.dynamic_slice_in_dim(acts, own_row, 8, 0) for acts in (own_acts, his_acts)
    ]
    recon_own, recon_his, last = call(
        close_kernel,
        "close",
        1 << 20,
        [((8, width), BF), ((8, width), BF), ((16, 4, 128), F32)],
        7,
        [],
        limit=16,
    )(at, arrived, dec_bias, his_bias, act_own, his_own, num_part, his_num)
    got = lax.all_to_all(last, ("pair",) + TOK, 0, 0, tiled=True)
    recon_came = swap(recon_his, "pair")
    recon = jnp.where(
        pair_at == 0,
        jnp.concatenate([recon_own, recon_came], axis=0),
        jnp.concatenate([recon_came, recon_own], axis=0),
    )
    token_loss = jnp.sum(got[:, 2, :rows], axis=0)
    num_own = jnp.sum(got[:, :2, :], axis=0).reshape(own) / tokens
    scaling = num_own / (nsq_own * mean_sq + tiny_term)
    return (recon[None], token_loss, scaling[None])


def solution(mesh):
    fine = Mesh(mesh.devices.reshape(2, 4, 8, 4, 2), ("pair", "x", "zl", "y", "zh"))
    return jax.shard_map(
        body,
        mesh=fine,
        in_specs=(
            P("pair", TOK, None),
            P("pair", None, LAT + TOK),
            P(LAT + TOK),
            P(LAT + TOK),
            P("pair", LAT, TOK),
            P("pair", TOK),
        ),
        out_specs=(P("pair", LAT, TOK), P(LAT), P("pair", LAT + TOK)),
        check_vma=False,
    )
```

time: 186 us -> 184 us (0.989)
  waiting for transfers between devices: 44.8 us -> 27.8 us
  starting transfers between devices: 97.5 us -> 108 us
  local copies, waits for them, and re-layouts: 11.8 us -> 16.3 us
  blocking collectives: 13.3 us -> 9.57 us
  other arithmetic: 2.58 us -> 5.67 us
    all_to_all x1, waiting for transfers between devices: 22.7 us -> 11.5 us  [body(): arrived = lax.all_to_all(payload.reshape(32, 8, 1024), LAT, 0, 0)]
    all_to_all x1, starting transfers between devices: 9.43 us -> 16.7 us  [body(): arrived = lax.all_to_all(payload.reshape(32, 8, 1024), LAT, 0, 0)]
    all_to_all x1, waiting for transfers between devices: 14.2 us -> 9.28 us  [body(): got = lax.all_to_all(last, ('pair',) + TOK, 0, 0, tiled=True)]
    ppermute x7 -> x10, starting transfers between devices: 58.8 us -> 63.2 us  [swap(): return lax.ppermute(value, axis, [(0, 1), (1, 0)])]
    concatenate x0 -> x1, local copies, waits for them, and re-layouts: none -> 3.74 us  [body(): sent = jnp.concatenate([cols[0][1], cols[1][1]] + bias_rows, axis=0)]
    all_to_all x1, blocking collectives: 13.3 us -> 9.57 us  [gather(): return lax.all_to_all(copies, axes, 0, 0, tiled=False)]
    unnamed x25 -> x14, local copies, waits for them, and re-layouts: 5.43 us -> 2.03 us
    dynamic_slice x1 -> x3, local copies, waits for them, and re-layouts: 0.02 us -> 2.26 us  [the longest x2 2.25 us: body(): lax.dynamic_slice_in_dim(acts, tok_at * width, width, 1)]
  transfers between devices with their start and end apart: 12 -> 15, of which waited for: 7 -> 7; matrix products, arithmetic and copies ran while one was open for 3% -> 10% of each run, Pallas kernels for 4% -> 4%
where the time goes in v8:
time: 184 us; the launch traced here: 183 us
  starting transfers between devices  108 us (59%)
  waiting for transfers between devices  27.8 us (15%)
  local copies, waits for them, and re-layouts  16.3 us (9%)
  Pallas kernels  11.7 us (6%)
  blocking collectives  9.57 us (5%)
  other arithmetic  5.67 us (3%)
  matrix products  2.69 us (1%)
    ppermute x10, starting transfers between devices, swap(): return lax.ppermute(value, axis, [(0, 1), (1, 0)])  63.2 us
    all_to_all x3, starting transfers between devices, gather(): return lax.all_to_all(copies, axes, 0, 0, tiled=False)  18.1 us
    all_to_all x1, starting transfers between devices, body(): arrived = lax.all_to_all(payload.reshape(32, 8, 1024), LAT, 0, 0)  16.7 us
    all_to_all x1, waiting for transfers between devices, body(): arrived = lax.all_to_all(payload.reshape(32, 8, 1024), LAT, 0, 0)  11.5 us
    all_to_all x1, starting transfers between devices, body(): got = lax.all_to_all(last, ('pair',) + TOK, 0, 0, tiled=True)  10.5 us
    all_to_all x1, blocking collectives, gather(): return lax.all_to_all(copies, axes, 0, 0, tiled=False)  9.57 us
    all_to_all x1, waiting for transfers between devices, body(): got = lax.all_to_all(last, ('pair',) + TOK, 0, 0, tiled=True)  9.28 us
    ppermute x10, waiting for transfers between devices, swap(): return lax.ppermute(value, axis, [(0, 1), (1, 0)])  6.97 us
  transfers between devices with their start and end apart: 15, of which 7 were waited for; matrix products, arithmetic and copies ran while one was open for 10% of the time, Pallas kernels for 4%

profile of v8, /device:TPU:1, one launch (start us, length us, event | category | flops | bytes accessed | tf_op | source)
XLA Modules:
  0.0 183.2 jit_solution(1315313822762426547)
XLA Ops:
  0.6 2.4 %broadcast_in_dim.14 = bf16[4,64,3584]{2,1,0:T(8,128)(2,1)} broadcast(bf16[64,3584]{1,0:T(8,128)(2,1)} %bitcast.58), dimensions={1,2} | broadcast | bytes 2293760 | tf_op jit(solution)/shard_map/broadcast_in_dim | solution.py:28
  3.1 5.0 %all-to-all-start.1 = ((bf16[4,64,3584]{2,1,0:T(8,128)(2,1)}), bf16[4,64,3584]{2,1,0:T(8,128)(2,1)S(1)}, u32[]{:S(2)}, u32[]{:S(2)}) async-start(bf16[4,64,3584]{2,1,0:T(8,128)(2,1)} %broadcast_in_dim.14), calls=%async_computation.1 | async-start | bytes 3670016 | tf_op jit(solution)/shard_map/all_to_all | solution.py:29
  9.0 15.4 %collective-permute-start = (bf16[16,3584]{1,0:T(8,128)(2,1)S(1)}, bf16[16,3584]{1,0:T(8,128)(2,1)S(1)}, u32[]{:S(2)}, u32[]{:S(2)}) collective-permute-start(bf16[16,3584]{1,0:T(8,128)(2,1)S(1)} %dynamic-slice_bitcast_fusion.5), channel_id=1, source_target_pairs={{0,1},{1,0},{2,3},{3,2},{4,5},{5,4},{6,7},{7,6},{8,9},{9,8},{10,11... | collective-permute-start | bytes 344072 | tf_op jit(solution)/shard_map/ppermute | solution.py:23
  24.4 2.5 %collective-permute-done = bf16[16,3584]{1,0:T(8,128)(2,1)S(1)} collective-permute-done((bf16[16,3584]{1,0:T(8,128)(2,1)S(1)}, bf16[16,3584]{1,0:T(8,128)(2,1)S(1)}, u32[]{:S(2)}, u32[]{:S(2)}) %collective-permute-start) | collective-permute-done | bytes 114720 | tf_op jit(solution)/shard_map/ppermute | solution.py:23
  26.9 1.2 copy-done.4
  28.1 1.4 broadcast_in_dim.12
  29.6 8.7 %all-to-all-start = ((bf16[16,16,3584]{2,1,0:T(8,128)(2,1)}), bf16[16,16,3584]{2,1,0:T(8,128)(2,1)}, u32[]{:S(2)}, u32[]{:S(2)}) async-start(bf16[16,16,3584]{2,1,0:T(8,128)(2,1)} %broadcast_in_dim.12), calls=%async_computation | async-start | bytes 3670016 | tf_op jit(solution)/shard_map/all_to_all | solution.py:29
  38.7 7.3 %collective-permute-start.4 = (f32[8,256]{1,0:T(8,128)S(1)}, f32[8,256]{1,0:T(8,128)S(1)}, u32[]{:S(2)}, u32[]{:S(2)}) collective-permute-start(f32[8,256]{1,0:T(8,128)S(1)} %reshape.128), channel_id=1, source_target_pairs={{0,256},{256,0},{1,257},{257,1},{2,258},{258,2},{3,259},{259,3},{4... | collective-permute-start | bytes 24584 | tf_op jit(solution)/shard_map/ppermute | solution.py:23
  46.6 4.1 %encode.1 = (f32[128,256]{1,0:T(8,128)}, f32[128,256]{1,0:T(8,128)}) custom-call(s32[5]{0:T(128)} %stack.23.at_ref, bf16[256,3584]{1,0:T(8,128)(2,1)} %bitcast.53, bf16[3584,256]{1,0:T(8,128)(2,1)} %bitcast.55), custom_call_target="tpu_custom_call" | custom-call | flops 469762048 | bytes 6291456 | tf_op jit(solution)/shard_map/encode/pallas_call | solution.py:234
  50.7 1.9 %collective-permute-start.3 = (f32[128,256]{1,0:T(8,128)}, f32[128,256]{1,0:T(8,128)S(1)}, u32[]{:S(2)}, u32[]{:S(2)}) collective-permute-start(f32[128,256]{1,0:T(8,128)} %get-tuple-element.17), channel_id=1, source_target_pairs={{0,256},{256,0},{1,257},{257,1},{2,258},{258,2},{3,259},{259,3},{4... | collective-permute-start | bytes 393224 | tf_op jit(solution)/shard_map/ppermute | solution.py:23
  52.7 1.5 collective-permute-done.3
  55.2 12.8 %collective-permute-start.5 = (bf16[160,256]{1,0:T(8,128)(2,1)S(1)}, bf16[160,256]{1,0:T(8,128)(2,1)S(1)}, u32[]{:S(2)}, u32[]{:S(2)}) collective-permute-start(bf16[160,256]{1,0:T(8,128)(2,1)S(1)} %constant_dynamic-update-slice_fusion), channel_id=1, source_target_pairs={{0,1},{1,0},{2,3},{3,2},{4,5},{5,4},{6,7},{7,6},{8,9},{9,8},{10,11... | collective-permute-start | bytes 245768 | tf_op jit(solution)/shard_map/ppermute | solution.py:23
  68.0 2.4 %collective-permute-start.6 = (bf16[448,2048]{1,0:T(8,128)(2,1)S(1)}, bf16[448,2048]{1,0:T(8,128)(2,1)}, u32[]{:S(2)}, u32[]{:S(2)}) collective-permute-start(bf16[448,2048]{1,0:T(8,128)(2,1)S(1)} %bitcast.47), channel_id=1, source_target_pairs={{0,256},{256,0},{1,257},{257,1},{2,258},{258,2},{3,259},{259,3},{4... | collective-permute-start | bytes 5505032 | tf_op jit(solution)/shard_map/ppermute | solution.py:23
  70.7 2.7 %fusion = f32[16,2,8,256]{3,2,1,0:T(8,128)S(1)} fusion(bf16[1,3584,256]{2,1,0:T(8,128)(2,1)} %param.7, bf16[16,16,3584]{2,1,0:T(8,128)(2,1)} %all-to-all-done), kind=kOutput, calls=%fused_computation.1 | convolution fusion | flops 469762048 | bytes 3932160 | tf_op jit(solution)/shard_map/dot_general | solution.py:236
  73.4 2.9 %collective-permute-start.1 = (f32[128,256]{1,0:T(8,128)S(1)}, f32[128,256]{1,0:T(8,128)S(1)}, u32[]{:S(2)}, u32[]{:S(2)}) collective-permute-start(f32[128,256]{1,0:T(8,128)S(1)} %dynamic-slice_bitcast_fusion.4), channel_id=1, source_target_pairs={{0,256},{256,0},{1,257},{257,1},{2,258},{258,2},{3,259},{259,3},{4... | collective-permute-start | bytes 393224 | tf_op jit(solution)/shard_map/ppermute | solution.py:23
  78.4 4.4 %all-to-all-start.2 = ((bf16[4,416,256]{2,1,0:T(8,128)(2,1)}), bf16[4,416,256]{2,1,0:T(8,128)(2,1)S(1)}, u32[]{:S(2)}, u32[]{:S(2)}) async-start(bf16[4,416,256]{2,1,0:T(8,128)(2,1)} %broadcast_in_dim.15), calls=%async_computation.2 | async-start | bytes 1703936 | tf_op jit(solution)/shard_map/all_to_all | solution.py:29
  82.8 11.9 %collective-permute-start.2 = (bf16[128,256]{1,0:T(8,128)(2,1)S(1)}, bf16[128,256]{1,0:T(8,128)(2,1)S(1)}, u32[]{:S(2)}, u32[]{:S(2)}) collective-permute-start(bf16[128,256]{1,0:T(8,128)(2,1)S(1)} %multiply_convert_fusion.1), channel_id=1, source_target_pairs={{0,1},{1,0},{2,3},{3,2},{4,5},{5,4},{6,7},{7,6},{8,9},{9,8},{10,11... | collective-permute-start | bytes 196616 | tf_op jit(solution)/shard_map/ppermute | solution.py:23
  94.7 1.8 collective-permute-done.2
  96.5 9.6 %all_to_all.30.g2 = bf16[4,128,256]{2,1,0:T(8,128)(2,1)S(1)} all-to-all(bf16[4,128,256]{2,1,0:T(8,128)(2,1)S(1)} %broadcast_in_dim.16), channel_id=1, replica_groups=mesh['pair'=2,'x'=4,'zl'=8,'y'=4,'zh'=2] {'y'}, dimensions={0} | all-to-all | bytes 524288 | tf_op jit(solution)/shard_map/all_to_all | solution.py:29
  106.1 3.1 %decode.1 = (bf16[256,1024]{1,0:T(8,128)(2,1)S(1)}, f32[8,256]{1,0:T(8,128)S(1)}) custom-call(s32[5]{0:T(128)S(1)} %copy-done.2, bf16[4,416,256]{2,1,0:T(8,128)(2,1)S(1)} %all-to-all-done.2.g1, bf16[4,128,256]{2,1,0:T(8,128)(2,1)S(1)} %all_to_all.30.g2, bf16[448,2048]{1,0:T(8,128)(2,1)S(1)} %bitcast.48, bf16[448,2048]{1,0:T(8,128)(2,1)} %collective-permute-done.6.oth_ref), custom_call_target="tpu_custom_call" | custom-call | flops 1073741824 | bytes 6291456 | tf_op jit(solution)/shard_map/decode/pallas_call | solution.py:262
  110.0 16.7 %all-to-all-start.4 = ((bf16[32,8,1024]{2,1,0:T(8,128)(2,1)}), bf16[32,8,1024]{2,1,0:T(8,128)(2,1)S(1)}, u32[]{:S(2)}, u32[]{:S(2)}) async-start(bf16[32,8,1024]{2,1,0:T(8,128)(2,1)} %bitcast.50), calls=%async_computation.4 | async-start | bytes 1048576 | tf_op jit(solution)/shard_map/all_to_all | solution.py:276
  126.7 1.1 constant_dynamic-slice_fusion.3
  127.9 1.1 constant_dynamic-slice_fusion.2
  129.8 3.7 %concatenate.42 = bf16[259,448]{1,0:T(8,128)(2,1)} concatenate(bf16[128,448]{1,0:T(8,128)(2,1)} %get-tuple-element.44, bf16[128,448]{1,0:T(8,128)(2,1)} %get-tuple-element.36, bf16[1,448]{1,0:T(2,128)(2,1)S(1)} %get-tuple-element.42, bf16[1,448]{1,0:T(2,128)(2,1)S(1)} %get-tuple-element.43, bf16[1,448]{1,0:T(2,128)(2,1)S(1)} %get-tuple-element.41), dimensions={0} | concatenate | bytes 464128 | tf_op jit(solution)/shard_map/concatenate | solution.py:286
  133.6 4.2 %collective-permute-start.7 = (bf16[259,448]{1,0:T(8,128)(2,1)}, bf16[259,448]{1,0:T(8,128)(2,1)}, u32[]{:S(2)}, u32[]{:S(2)}) collective-permute-start(bf16[259,448]{1,0:T(8,128)(2,1)} %concatenate.42), channel_id=1, source_target_pairs={{0,256},{256,0},{1,257},{257,1},{2,258},{258,2},{3,259},{259,3},{4... | collective-permute-start | bytes 696200 | tf_op jit(solution)/shard_map/ppermute | solution.py:23
  141.3 3.0 %numer.1 = (f32[8,256]{1,0:T(8,128)S(1)}, f32[8,256]{1,0:T(8,128)S(1)}, f32[1,256]{1,0:T(1,128)S(1)}) custom-call(s32[5]{0:T(128)S(1)} %copy-done.2, bf16[4,416,256]{2,1,0:T(8,128)(2,1)S(1)} %all-to-all-done.2.g1, bf16[4,128,256]{2,1,0:T(8,128)(2,1)S(1)} %all_to_all.30.g2, bf16[448,2048]{1,0:T(8,128)(2,1)S(1)} %bitcast.49, ...), custom_call_target="tpu_custom_call" | custom-call | flops 939524096 | bytes 6291456 | tf_op jit(solution)/shard_map/numer/pallas_call | solution.py:290
  144.3 11.5 %all-to-all-done.4.arrived_ref = bf16[32,8,1024]{2,1,0:T(8,128)(2,1)S(1)} async-done(((bf16[32,8,1024]{2,1,0:T(8,128)(2,1)}), bf16[32,8,1024]{2,1,0:T(8,128)(2,1)S(1)}, u32[]{:S(2)}, u32[]{:S(2)}) %all-to-all-start.4) | async-done | bytes 524320 | tf_op jit(solution)/shard_map/all_to_all | solution.py:276
  155.9 1.4 close.1
  157.3 10.5 %all-to-all-start.5 = ((f32[16,4,128]{2,1,0:T(4,128)}), f32[16,4,128]{2,1,0:T(4,128)S(1)}, u32[]{:S(2)}, u32[]{:S(2)}) async-start(f32[16,4,128]{2,1,0:T(4,128)} %get-tuple-element.26), calls=%async_computation.5 | async-start | bytes 65536 | tf_op jit(solution)/shard_map/all_to_all | solution.py:315
  167.8 2.0 %collective-permute-start.8 = (bf16[8,448]{1,0:T(8,128)(2,1)S(1)}, bf16[8,448]{1,0:T(8,128)(2,1)S(1)}, u32[]{:S(2)}, u32[]{:S(2)}) collective-permute-start(bf16[8,448]{1,0:T(8,128)(2,1)S(1)} %get-tuple-element.25), channel_id=1, source_target_pairs={{0,256},{256,0},{1,257},{257,1},{2,258},{258,2},{3,259},{259,3},{4... | collective-permute-start | bytes 21512 | tf_op jit(solution)/shard_map/ppermute | solution.py:23
  169.8 2.3 %collective-permute-start.9 = (f32[1,256]{1,0:T(1,128)S(1)}, f32[1,256]{1,0:T(1,128)S(1)}, u32[]{:S(2)}, u32[]{:S(2)}) collective-permute-start(f32[1,256]{1,0:T(1,128)S(1)} %get-tuple-element.28), channel_id=1, source_target_pairs={{0,256},{256,0},{1,257},{257,1},{2,258},{258,2},{3,259},{259,3},{4... | collective-permute-start | bytes 3080 | tf_op jit(solution)/shard_map/ppermute | solution.py:23
  172.8 9.3 %all-to-all-done.5 = f32[16,4,128]{2,1,0:T(4,128)S(1)} async-done(((f32[16,4,128]{2,1,0:T(4,128)}), f32[16,4,128]{2,1,0:T(4,128)S(1)}, u32[]{:S(2)}, u32[]{:S(2)}) %all-to-all-start.5) | async-done | bytes 32800 | tf_op jit(solution)/shard_map/all_to_all | solution.py:315
  (54 shorter events, 12.1 us)
Async XLA Ops:
  3.1 23.8 %all-to-all-start.1 = ((bf16[4,64,3584]{2,1,0:T(8,128)(2,1)}), bf16[4,64,3584]{2,1,0:T(8,128)(2,1)S(1)}, u32[]{:S(2)}, u32[]{:S(2)}) async-start(bf16[4,64,3584]{2,1,0:T(8,128)(2,1)} %broadcast_in_dim.14), calls=%async_computation.1 | async-start | bytes 3670016 | tf_op jit(solution)/shard_map/all_to_all | solution.py:29
  9.0 17.9 %collective-permute-start = (bf16[16,3584]{1,0:T(8,128)(2,1)S(1)}, bf16[16,3584]{1,0:T(8,128)(2,1)S(1)}, u32[]{:S(2)}, u32[]{:S(2)}) collective-permute-start(bf16[16,3584]{1,0:T(8,128)(2,1)S(1)} %dynamic-slice_bitcast_fusion.5), channel_id=1, source_target_pairs={{0,1},{1,0},{2,3},{3,2},{4,5},{5,4},{6,7},{7,6},{8,9},{9,8},{10,11... | collective-permute-start | bytes 344072 | tf_op jit(solution)/shard_map/ppermute | solution.py:23
  26.9 1.2 copy-start.4
  29.5 8.7 %copy-start = (bf16[1,2048,448]{1,2,0:T(8,128)(2,1)S(1)}, bf16[1,2048,448]{1,2,0:T(8,128)(2,1)}, u32[]{:S(2)}) copy-start(bf16[1,2048,448]{1,2,0:T(8,128)(2,1)} %param.10) | copy-start | bytes 5505028
  29.6 41.1 %all-to-all-start = ((bf16[16,16,3584]{2,1,0:T(8,128)(2,1)}), bf16[16,16,3584]{2,1,0:T(8,128)(2,1)}, u32[]{:S(2)}, u32[]{:S(2)}) async-start(bf16[16,16,3584]{2,1,0:T(8,128)(2,1)} %broadcast_in_dim.12), calls=%async_computation | async-start | bytes 3670016 | tf_op jit(solution)/shard_map/all_to_all | solution.py:29
  38.7 16.5 %collective-permute-start.4 = (f32[8,256]{1,0:T(8,128)S(1)}, f32[8,256]{1,0:T(8,128)S(1)}, u32[]{:S(2)}, u32[]{:S(2)}) collective-permute-start(f32[8,256]{1,0:T(8,128)S(1)} %reshape.128), channel_id=1, source_target_pairs={{0,256},{256,0},{1,257},{257,1},{2,258},{258,2},{3,259},{259,3},{4... | collective-permute-start | bytes 24584 | tf_op jit(solution)/shard_map/ppermute | solution.py:23
  46.6 6.0 %copy-start.6 = (s32[256]{0:T(256)S(1)}, s32[256]{0:T(256)}, u32[]{:S(2)}) copy-start(s32[256]{0:T(256)} %param.9) | copy-start | bytes 3076
  46.6 7.5 %copy-start.5 = (f32[256]{0:T(256)S(1)}, f32[256]{0:T(256)}, u32[]{:S(2)}) copy-start(f32[256]{0:T(256)} %param.8) | copy-start | bytes 3076
  50.7 3.5 %collective-permute-start.3 = (f32[128,256]{1,0:T(8,128)}, f32[128,256]{1,0:T(8,128)S(1)}, u32[]{:S(2)}, u32[]{:S(2)}) collective-permute-start(f32[128,256]{1,0:T(8,128)} %get-tuple-element.17), channel_id=1, source_target_pairs={{0,256},{256,0},{1,257},{257,1},{2,258},{258,2},{3,259},{259,3},{4... | collective-permute-start | bytes 393224 | tf_op jit(solution)/shard_map/ppermute | solution.py:23
  55.2 15.5 %collective-permute-start.5 = (bf16[160,256]{1,0:T(8,128)(2,1)S(1)}, bf16[160,256]{1,0:T(8,128)(2,1)S(1)}, u32[]{:S(2)}, u32[]{:S(2)}) collective-permute-start(bf16[160,256]{1,0:T(8,128)(2,1)S(1)} %constant_dynamic-update-slice_fusion), channel_id=1, source_target_pairs={{0,1},{1,0},{2,3},{3,2},{4,5},{5,4},{6,7},{7,6},{8,9},{9,8},{10,11... | collective-permute-start | bytes 245768 | tf_op jit(solution)/shard_map/ppermute | solution.py:23
  68.0 38.1 %collective-permute-start.6 = (bf16[448,2048]{1,0:T(8,128)(2,1)S(1)}, bf16[448,2048]{1,0:T(8,128)(2,1)}, u32[]{:S(2)}, u32[]{:S(2)}) collective-permute-start(bf16[448,2048]{1,0:T(8,128)(2,1)S(1)} %bitcast.47), channel_id=1, source_target_pairs={{0,256},{256,0},{1,257},{257,1},{2,258},{258,2},{3,259},{259,3},{4... | collective-permute-start | bytes 5505032 | tf_op jit(solution)/shard_map/ppermute | solution.py:23
  73.4 3.9 %collective-permute-start.1 = (f32[128,256]{1,0:T(8,128)S(1)}, f32[128,256]{1,0:T(8,128)S(1)}, u32[]{:S(2)}, u32[]{:S(2)}) collective-permute-start(f32[128,256]{1,0:T(8,128)S(1)} %dynamic-slice_bitcast_fusion.4), channel_id=1, source_target_pairs={{0,256},{256,0},{1,257},{257,1},{2,258},{258,2},{3,259},{259,3},{4... | collective-permute-start | bytes 393224 | tf_op jit(solution)/shard_map/ppermute | solution.py:23
  77.4 28.7 %copy-start.2 = (s32[5]{0:T(128)S(1)}, s32[5]{0:T(128)}, u32[]{:S(2)}) copy-start(s32[5]{0:T(128)} %stack.23.at_ref) | copy-start | bytes 64
  78.4 18.1 %all-to-all-start.2 = ((bf16[4,416,256]{2,1,0:T(8,128)(2,1)}), bf16[4,416,256]{2,1,0:T(8,128)(2,1)S(1)}, u32[]{:S(2)}, u32[]{:S(2)}) async-start(bf16[4,416,256]{2,1,0:T(8,128)(2,1)} %broadcast_in_dim.15), calls=%async_computation.2 | async-start | bytes 1703936 | tf_op jit(solution)/shard_map/all_to_all | solution.py:29
  82.8 13.7 %collective-permute-start.2 = (bf16[128,256]{1,0:T(8,128)(2,1)S(1)}, bf16[128,256]{1,0:T(8,128)(2,1)S(1)}, u32[]{:S(2)}, u32[]{:S(2)}) collective-permute-start(bf16[128,256]{1,0:T(8,128)(2,1)S(1)} %multiply_convert_fusion.1), channel_id=1, source_target_pairs={{0,1},{1,0},{2,3},{3,2},{4,5},{5,4},{6,7},{7,6},{8,9},{9,8},{10,11... | collective-permute-start | bytes 196616 | tf_op jit(solution)/shard_map/ppermute | solution.py:23
  106.1 20.7 %copy-start.3 = (f32[1,448]{1,0:T(1,128)S(1)}, f32[1,448]{1,0:T(1,128)}, u32[]{:S(2)}) copy-start(f32[1,448]{1,0:T(1,128)} %bias_ref.1) | copy-start | bytes 5380
  109.2 0.8 copy-start.1
  110.0 45.9 %all-to-all-start.4 = ((bf16[32,8,1024]{2,1,0:T(8,128)(2,1)}), bf16[32,8,1024]{2,1,0:T(8,128)(2,1)S(1)}, u32[]{:S(2)}, u32[]{:S(2)}) async-start(bf16[32,8,1024]{2,1,0:T(8,128)(2,1)} %bitcast.50), calls=%async_computation.4 | async-start | bytes 1048576 | tf_op jit(solution)/shard_map/all_to_all | solution.py:276
  133.6 6.0 %collective-permute-start.7 = (bf16[259,448]{1,0:T(8,128)(2,1)}, bf16[259,448]{1,0:T(8,128)(2,1)}, u32[]{:S(2)}, u32[]{:S(2)}) collective-permute-start(bf16[259,448]{1,0:T(8,128)(2,1)} %concatenate.42), channel_id=1, source_target_pairs={{0,256},{256,0},{1,257},{257,1},{2,258},{258,2},{3,259},{259,3},{4... | collective-permute-start | bytes 696200 | tf_op jit(solution)/shard_map/ppermute | solution.py:23
  157.3 24.8 %all-to-all-start.5 = ((f32[16,4,128]{2,1,0:T(4,128)}), f32[16,4,128]{2,1,0:T(4,128)S(1)}, u32[]{:S(2)}, u32[]{:S(2)}) async-start(f32[16,4,128]{2,1,0:T(4,128)} %get-tuple-element.26), calls=%async_computation.5 | async-start | bytes 65536 | tf_op jit(solution)/shard_map/all_to_all | solution.py:315
  167.8 4.3 %collective-permute-start.8 = (bf16[8,448]{1,0:T(8,128)(2,1)S(1)}, bf16[8,448]{1,0:T(8,128)(2,1)S(1)}, u32[]{:S(2)}, u32[]{:S(2)}) collective-permute-start(bf16[8,448]{1,0:T(8,128)(2,1)S(1)} %get-tuple-element.25), channel_id=1, source_target_pairs={{0,256},{256,0},{1,257},{257,1},{2,258},{258,2},{3,259},{259,3},{4... | collective-permute-start | bytes 21512 | tf_op jit(solution)/shard_map/ppermute | solution.py:23
  169.8 12.8 %collective-permute-start.9 = (f32[1,256]{1,0:T(1,128)S(1)}, f32[1,256]{1,0:T(1,128)S(1)}, u32[]{:S(2)}, u32[]{:S(2)}) collective-permute-start(f32[1,256]{1,0:T(1,128)S(1)} %get-tuple-element.28), channel_id=1, source_target_pairs={{0,256},{256,0},{1,257},{257,1},{2,258},{258,2},{3,259},{259,3},{4... | collective-permute-start | bytes 3080 | tf_op jit(solution)/shard_map/ppermute | solution.py:23

commit v9 on v8

--- a/solution.py
+++ b/solution.py
@@ -68,9 +68,10 @@
 
     nsq = [jnp.zeros((8, 256), F32)] * 2
     for y in range(4):
-        rows = g1[y, 384:416, :].astype(F32)
-        nsq[0] = nsq[0] + (rows[0:8] + rows[8:16])
-        nsq[1] = nsq[1] + (rows[16:24] + rows[24:32])
+        for at in (384, 416):
+            rows = g1[y, at : at + 32, :].astype(F32)
+            nsq[0] = nsq[0] + (rows[0:8] + rows[8:16])
+            nsq[1] = nsq[1] + (rows[16:24] + rows[24:32])
     nsq_ref[...] = nsq[0]
     norm = (jnp.sqrt(nsq[0]) + jnp.sqrt(nsq[1])) * 0.125
     high = norm.astype(BF).astype(F32)
@@ -195,11 +196,13 @@
     at = jnp.stack([pair_at, zh_at, tok_at, lax.axis_index("y"), lat_at]).astype(jnp.int32)
 
     quarter = swap(lax.dynamic_slice_in_dim(act, x_at * 16, 16, 0), "zh")
+    dec_wide = dec.astype(F32)
+    nsq_part = jnp.sum(dec_wide * dec_wide, axis=1).reshape(8, own)
+    nsq_two = [nsq_part, swap(nsq_part, "pair")]
+    quarter, nsq_two[0], nsq_two[1], at = lax.optimization_barrier((quarter, *nsq_two, at))
+
     near = gather(act, "y").reshape(256, D)
     far = gather(quarter, ("y", "x")).reshape(256, D)
-
-    dec_wide = dec.astype(F32)
-    nsq_part = jnp.sum(dec_wide * dec_wide, axis=1).reshape(8, own)
 
     def split(value):
         high = value.astype(BF)
@@ -229,32 +232,26 @@
             for k in (pair_at, 1 - pair_at)
         ]
 
-    def features(acts, ahead):
-        if ahead:
-            keep, send = encode(at, acts, enc)
-        else:
-            keep, send = halves(jnp.dot(acts, enc, preferred_element_type=F32))
-        pre = keep + swap(send, "pair") + enc_bias
+    def features(keep, came):
+        pre = keep + came + enc_bias
         return (pre * jax.nn.sigmoid((pre - thresh_level) / smooth_width)).astype(BF)
 
-    feats_near = features(near, True)
-    nsq_two = [nsq_part, swap(nsq_part, "pair")]
-    over = swap(
-        jnp.concatenate([feats_near] + split(nsq_two[0]) + split(nsq_two[1]), axis=0), "zh"
-    )
-    over_near = over[:128]
-    nsq_rows = []
-    for k in range(2):
-        rest = over[128 + 16 * k : 144 + 16 * k].astype(F32)
-        nsq_rows += split(nsq_two[k] + rest[0:8] + rest[8:16])
-    nsq_rows = lax.optimization_barrier(jnp.concatenate(nsq_rows, axis=0))
+    keep, send = encode(at, near, enc)
+    feats_near = features(keep, swap(send, "pair"))
+    nsq_rows = lax.optimization_barrier(
+        jnp.concatenate(split(nsq_two[0]) + split(nsq_two[1]), axis=0)
+    )
+    over = swap(jnp.concatenate([feats_near, nsq_rows], axis=0), "zh")
     dec_held, _ = lax.optimization_barrier((dec_t, feats_near))
     dec_oth = swap(dec_held, "pair")
 
-    feats_far = features(far, False)
+    part_far = jnp.dot(far, enc, preferred_element_type=F32)
+    keep, send = halves(part_far)
+    over, keep = lax.optimization_barrier((over, keep))
+    feats_far = features(keep, swap(send, "pair"))
     over_far = swap(feats_far, "zh")
     g1 = gather(
-        jnp.concatenate([feats_near, over_near, feats_far, nsq_rows], axis=0), "y"
+        jnp.concatenate([feats_near, over[:128], feats_far, nsq_rows, over[128:]], axis=0), "y"
     )
     over_far, g1 = lax.optimization_barrier((over_far, g1))
     g2 = gather(over_far, "y")
@@ -283,7 +280,8 @@
     for _ in range(3):
         bias_rows.append(rest.astype(BF))
         rest = rest - bias_rows[-1].astype(F32)
-    sent = jnp.concatenate([cols[0][1], cols[1][1]] + bias_rows, axis=0)
+    bias_rows = jnp.pad(jnp.concatenate(bias_rows, axis=0), ((0, 13), (0, 0)))
+    sent = jnp.concatenate([cols[0][1], cols[1][1], bias_rows], axis=0)
     came = swap(sent, "pair")
     his_acts = came[:256]
     his_bias = jnp.sum(came[256:259].astype(F32), axis=0, keepdims=True)

time: 184 us -> 183 us (level)
  waiting for transfers between devices: 27.8 us -> 25.1 us
  other arithmetic: 5.67 us -> 7.66 us
    unnamed x14 -> x34, local copies, waits for them, and re-layouts: 2.03 us -> 7.23 us
    all_to_all x1, starting transfers between devices: 16.7 us -> 12.1 us  [body(): arrived = lax.all_to_all(payload.reshape(32, 8, 1024), LAT, 0, 0)]
    concatenate x1, local copies, waits for them, and re-layouts: 3.74 us -> 0.01 us  [body(): jnp.concatenate([feats_near, over[:128], feats_far, nsq_rows, over[128:]]...]
    all_to_all x1, starting transfers between devices: 10.5 us -> 13.1 us  [body(): got = lax.all_to_all(last, ('pair',) + TOK, 0, 0, tiled=True)]
    ppermute x10, waiting for transfers between devices: 6.97 us -> 4.73 us  [swap(): return lax.ppermute(value, axis, [(0, 1), (1, 0)])]
  transfers between devices with their start and end apart: 15 -> 15, of which waited for: 7 -> 6; matrix products, arithmetic and copies ran while one was open for 10% -> 9% of each run, Pallas kernels for 4% -> 4%
where the time goes in v9:
time: 183 us; the launch traced here: 182 us
  starting transfers between devices  107 us (58%)
  waiting for transfers between devices  25.1 us (14%)
  local copies, waits for them, and re-layouts  17.7 us (10%)
  Pallas kernels  11.6 us (6%)
  blocking collectives  9.2 us (5%)
  other arithmetic  7.66 us (4%)
  matrix products  2.69 us (1%)
    ppermute x10, starting transfers between devices, swap(): return lax.ppermute(value, axis, [(0, 1), (1, 0)])  65 us
    all_to_all x3, starting transfers between devices, gather(): return lax.all_to_all(copies, axes, 0, 0, tiled=False)  16.8 us
    all_to_all x1, starting transfers between devices, body(): got = lax.all_to_all(last, ('pair',) + TOK, 0, 0, tiled=True)  13.1 us
    all_to_all x1, starting transfers between devices, body(): arrived = lax.all_to_all(payload.reshape(32, 8, 1024), LAT, 0, 0)  12.1 us
    all_to_all x1, waiting for transfers between devices, body(): arrived = lax.all_to_all(payload.reshape(32, 8, 1024), LAT, 0, 0)  11.1 us
    all_to_all x1, waiting for transfers between devices, body(): got = lax.all_to_all(last, ('pair',) + TOK, 0, 0, tiled=True)  9.28 us
    all_to_all x1, blocking collectives, gather(): return lax.all_to_all(copies, axes, 0, 0, tiled=False)  9.2 us
    unnamed x34, local copies, waits for them, and re-layouts  7.23 us
  transfers between devices with their start and end apart: 15, of which 6 were waited for; matrix products, arithmetic and copies ran while one was open for 9% of the time, Pallas kernels for 4%

profile of v9, /device:TPU:1, one launch (start us, length us, event | category | flops | bytes accessed | tf_op | source)
XLA Modules:
  0.0 182.1 jit_solution(2117986286170916407)
XLA Ops:
  0.6 2.4 %broadcast_in_dim.13 = bf16[4,64,3584]{2,1,0:T(8,128)(2,1)} broadcast(bf16[64,3584]{1,0:T(8,128)(2,1)} %bitcast.52), dimensions={1,2} | broadcast | bytes 2293760 | tf_op jit(solution)/shard_map/broadcast_in_dim | solution.py:28
  3.0 5.1 %all-to-all-start = ((bf16[4,64,3584]{2,1,0:T(8,128)(2,1)}), bf16[4,64,3584]{2,1,0:T(8,128)(2,1)}, u32[]{:S(2)}, u32[]{:S(2)}) async-start(bf16[4,64,3584]{2,1,0:T(8,128)(2,1)} %broadcast_in_dim.13), calls=%async_computation | async-start | bytes 3670016 | tf_op jit(solution)/shard_map/all_to_all | solution.py:29
  9.1 15.7 %collective-permute-start = (bf16[16,3584]{1,0:T(8,128)(2,1)S(1)}, bf16[16,3584]{1,0:T(8,128)(2,1)S(1)}, u32[]{:S(2)}, u32[]{:S(2)}) collective-permute-start(bf16[16,3584]{1,0:T(8,128)(2,1)S(1)} %dynamic-slice_bitcast_fusion.6), channel_id=1, source_target_pairs={{0,1},{1,0},{2,3},{3,2},{4,5},{5,4},{6,7},{7,6},{8,9},{9,8},{10,11... | collective-permute-start | bytes 344072 | tf_op jit(solution)/shard_map/ppermute | solution.py:23
  25.2 2.9 %collective-permute-start.1 = (f32[8,256]{1,0:T(8,128)S(1)}, f32[8,256]{1,0:T(8,128)S(1)}, u32[]{:S(2)}, u32[]{:S(2)}) collective-permute-start(f32[8,256]{1,0:T(8,128)S(1)} %reshape.125), channel_id=1, source_target_pairs={{0,256},{256,0},{1,257},{257,1},{2,258},{258,2},{3,259},{259,3},{4... | collective-permute-start | bytes 24584 | tf_op jit(solution)/shard_map/ppermute | solution.py:23
  28.9 1.4 broadcast_in_dim.14
  30.3 7.3 %all-to-all-start.1 = ((bf16[16,16,3584]{2,1,0:T(8,128)(2,1)}), bf16[16,16,3584]{2,1,0:T(8,128)(2,1)}, u32[]{:S(2)}, u32[]{:S(2)}) async-start(bf16[16,16,3584]{2,1,0:T(8,128)(2,1)} %broadcast_in_dim.14), calls=%async_computation.1 | async-start | bytes 3670016 | tf_op jit(solution)/shard_map/all_to_all | solution.py:29
  37.6 4.1 %encode.1 = (f32[128,256]{1,0:T(8,128)}, f32[128,256]{1,0:T(8,128)}) custom-call(s32[5]{0:T(128)} %stack.23.at_ref, bf16[256,3584]{1,0:T(8,128)(2,1)} %bitcast.8.act_hbm, bf16[3584,256]{1,0:T(8,128)(2,1)} %bitcast.49), custom_call_target="tpu_custom_call" | custom-call | flops 469762048 | bytes 6291456 | tf_op jit(solution)/shard_map/encode/pallas_call | solution.py:239
  41.7 3.9 %collective-permute-start.2 = (f32[128,256]{1,0:T(8,128)}, f32[128,256]{1,0:T(8,128)S(1)}, u32[]{:S(2)}, u32[]{:S(2)}) collective-permute-start(f32[128,256]{1,0:T(8,128)} %get-tuple-element.24), channel_id=1, source_target_pairs={{0,256},{256,0},{1,257},{257,1},{2,258},{258,2},{3,259},{259,3},{4... | collective-permute-start | bytes 393224 | tf_op jit(solution)/shard_map/ppermute | solution.py:23
  45.6 1.1 collective-permute-done.2
  47.7 15.8 %collective-permute-start.3 = (bf16[160,256]{1,0:T(8,128)(2,1)S(1)}, bf16[160,256]{1,0:T(8,128)(2,1)S(1)}, u32[]{:S(2)}, u32[]{:S(2)}) collective-permute-start(bf16[160,256]{1,0:T(8,128)(2,1)S(1)} %pad_maximum_fusion.2), channel_id=1, source_target_pairs={{0,1},{1,0},{2,3},{3,2},{4,5},{5,4},{6,7},{7,6},{8,9},{9,8},{10,11... | collective-permute-start | bytes 245768 | tf_op jit(solution)/shard_map/ppermute | solution.py:23
  63.6 2.6 %collective-permute-start.6 = (bf16[448,2048]{1,0:T(8,128)(2,1)S(1)}, bf16[448,2048]{1,0:T(8,128)(2,1)}, u32[]{:S(2)}, u32[]{:S(2)}) collective-permute-start(bf16[448,2048]{1,0:T(8,128)(2,1)S(1)} %bitcast.43), channel_id=1, source_target_pairs={{0,256},{256,0},{1,257},{257,1},{2,258},{258,2},{3,259},{259,3},{4... | collective-permute-start | bytes 5505032 | tf_op jit(solution)/shard_map/ppermute | solution.py:23
  66.2 2.7 %fusion = f32[16,2,8,256]{3,2,1,0:T(8,128)S(1)} fusion(bf16[1,3584,256]{2,1,0:T(8,128)(2,1)} %param.7, bf16[16,16,3584]{2,1,0:T(8,128)(2,1)} %all-to-all-done.1), kind=kOutput, calls=%fused_computation.1 | convolution fusion | flops 469762048 | bytes 3932160 | tf_op jit(solution)/shard_map/dot_general | solution.py:248
  68.9 1.9 %collective-permute-start.4 = (f32[128,256]{1,0:T(8,128)S(1)}, f32[128,256]{1,0:T(8,128)S(1)}, u32[]{:S(2)}, u32[]{:S(2)}) collective-permute-start(f32[128,256]{1,0:T(8,128)S(1)} %get-tuple-element.53), channel_id=1, source_target_pairs={{0,256},{256,0},{1,257},{257,1},{2,258},{258,2},{3,259},{259,3},{4... | collective-permute-start | bytes 393224 | tf_op jit(solution)/shard_map/ppermute | solution.py:23
  70.8 1.3 collective-permute-done.4
  73.2 4.4 %all-to-all-start.2 = ((bf16[4,448,256]{2,1,0:T(8,128)(2,1)}), bf16[4,448,256]{2,1,0:T(8,128)(2,1)S(1)}, u32[]{:S(2)}, u32[]{:S(2)}) async-start(bf16[4,448,256]{2,1,0:T(8,128)(2,1)} %broadcast_in_dim.15), calls=%async_computation.2 | async-start | bytes 1835008 | tf_op jit(solution)/shard_map/all_to_all | solution.py:29
  77.6 13.4 %collective-permute-start.5 = (bf16[128,256]{1,0:T(8,128)(2,1)S(1)}, bf16[128,256]{1,0:T(8,128)(2,1)S(1)}, u32[]{:S(2)}, u32[]{:S(2)}) collective-permute-start(bf16[128,256]{1,0:T(8,128)(2,1)S(1)} %get-tuple-element.42), channel_id=1, source_target_pairs={{0,1},{1,0},{2,3},{3,2},{4,5},{5,4},{6,7},{7,6},{8,9},{9,8},{10,11... | collective-permute-start | bytes 196616 | tf_op jit(solution)/shard_map/ppermute | solution.py:23
  91.0 2.2 %collective-permute-done.5 = bf16[128,256]{1,0:T(8,128)(2,1)S(1)} collective-permute-done((bf16[128,256]{1,0:T(8,128)(2,1)S(1)}, bf16[128,256]{1,0:T(8,128)(2,1)S(1)}, u32[]{:S(2)}, u32[]{:S(2)}) %collective-permute-start.5) | collective-permute-done | bytes 65568 | tf_op jit(solution)/shard_map/ppermute | solution.py:23
  93.2 9.2 %all_to_all.30.g2 = bf16[4,128,256]{2,1,0:T(8,128)(2,1)S(1)} all-to-all(bf16[4,128,256]{2,1,0:T(8,128)(2,1)S(1)} %broadcast_in_dim.16), channel_id=1, replica_groups=mesh['pair'=2,'x'=4,'zl'=8,'y'=4,'zh'=2] {'y'}, dimensions={0} | all-to-all | bytes 524288 | tf_op jit(solution)/shard_map/all_to_all | solution.py:29
  102.4 3.1 %decode.1 = (bf16[256,1024]{1,0:T(8,128)(2,1)S(1)}, f32[8,256]{1,0:T(8,128)S(1)}) custom-call(s32[5]{0:T(128)S(1)} %copy-done.2, bf16[4,448,256]{2,1,0:T(8,128)(2,1)S(1)} %all-to-all-done.2.g1, bf16[4,128,256]{2,1,0:T(8,128)(2,1)S(1)} %all_to_all.30.g2, bf16[448,2048]{1,0:T(8,128)(2,1)S(1)} %bitcast.44, bf16[448,2048]{1,0:T(8,128)(2,1)} %collective-permute-done.6.oth_ref), custom_call_target="tpu_custom_call" | custom-call | flops 1073741824 | bytes 6291456 | tf_op jit(solution)/shard_map/decode/pallas_call | solution.py:259
  106.9 12.1 %all-to-all-start.4 = ((bf16[32,8,1024]{2,1,0:T(8,128)(2,1)}), bf16[32,8,1024]{2,1,0:T(8,128)(2,1)S(1)}, u32[]{:S(2)}, u32[]{:S(2)}) async-start(bf16[32,8,1024]{2,1,0:T(8,128)(2,1)} %bitcast.46), calls=%async_computation.4 | async-start | bytes 1048576 | tf_op jit(solution)/shard_map/all_to_all | solution.py:273
  119.1 1.1 constant_dynamic-slice_fusion.3
  120.3 1.1 constant_dynamic-slice_fusion.2
  122.9 4.6 %collective-permute-start.7 = (bf16[272,448]{1,0:T(8,128)(2,1)}, bf16[272,448]{1,0:T(8,128)(2,1)}, u32[]{:S(2)}, u32[]{:S(2)}) collective-permute-start(bf16[272,448]{1,0:T(8,128)(2,1)} %pad_maximum_fusion.1), channel_id=1, source_target_pairs={{0,256},{256,0},{1,257},{257,1},{2,258},{258,2},{3,259},{259,3},{4... | collective-permute-start | bytes 731144 | tf_op jit(solution)/shard_map/ppermute | solution.py:23
  130.2 1.3 convert_reduce_fusion
  132.2 3.0 %numer.1 = (f32[8,256]{1,0:T(8,128)S(1)}, f32[8,256]{1,0:T(8,128)S(1)}, f32[1,256]{1,0:T(1,128)S(1)}) custom-call(s32[5]{0:T(128)S(1)} %copy-done.3, bf16[4,448,256]{2,1,0:T(8,128)(2,1)S(1)} %all-to-all-done.2.g1, bf16[4,128,256]{2,1,0:T(8,128)(2,1)S(1)} %all_to_all.30.g2, bf16[448,2048]{1,0:T(8,128)(2,1)S(1)} %bitcast.45, ...), custom_call_target="tpu_custom_call" | custom-call | flops 939524096 | bytes 6291456 | tf_op jit(solution)/shard_map/numer/pallas_call | solution.py:288
  137.0 11.1 %all-to-all-done.4.arrived_ref = bf16[32,8,1024]{2,1,0:T(8,128)(2,1)S(1)} async-done(((bf16[32,8,1024]{2,1,0:T(8,128)(2,1)}), bf16[32,8,1024]{2,1,0:T(8,128)(2,1)S(1)}, u32[]{:S(2)}, u32[]{:S(2)}) %all-to-all-start.4) | async-done | bytes 524320 | tf_op jit(solution)/shard_map/all_to_all | solution.py:273
  151.5 1.4 close.1
  152.9 13.1 %all-to-all-start.5 = ((f32[16,4,128]{2,1,0:T(4,128)}), f32[16,4,128]{2,1,0:T(4,128)S(1)}, u32[]{:S(2)}, u32[]{:S(2)}) async-start(f32[16,4,128]{2,1,0:T(4,128)} %get-tuple-element.38), calls=%async_computation.5 | async-start | bytes 65536 | tf_op jit(solution)/shard_map/all_to_all | solution.py:313
  166.0 2.0 %collective-permute-start.8 = (bf16[8,448]{1,0:T(8,128)(2,1)S(1)}, bf16[8,448]{1,0:T(8,128)(2,1)S(1)}, u32[]{:S(2)}, u32[]{:S(2)}) collective-permute-start(bf16[8,448]{1,0:T(8,128)(2,1)S(1)} %get-tuple-element.37), channel_id=1, source_target_pairs={{0,256},{256,0},{1,257},{257,1},{2,258},{258,2},{3,259},{259,3},{4... | collective-permute-start | bytes 21512 | tf_op jit(solution)/shard_map/ppermute | solution.py:23
  168.1 2.3 %collective-permute-start.9 = (f32[1,256]{1,0:T(1,128)}, f32[1,256]{1,0:T(1,128)S(1)}, u32[]{:S(2)}, u32[]{:S(2)}) collective-permute-start(f32[1,256]{1,0:T(1,128)} %copy-done.12), channel_id=1, source_target_pairs={{0,256},{256,0},{1,257},{257,1},{2,258},{258,2},{3,259},{259,3},{4... | collective-permute-start | bytes 3080 | tf_op jit(solution)/shard_map/ppermute | solution.py:23
  171.0 9.3 %all-to-all-done.5 = f32[16,4,128]{2,1,0:T(4,128)S(1)} async-done(((f32[16,4,128]{2,1,0:T(4,128)}), f32[16,4,128]{2,1,0:T(4,128)S(1)}, u32[]{:S(2)}, u32[]{:S(2)}) %all-to-all-start.5) | async-done | bytes 32800 | tf_op jit(solution)/shard_map/all_to_all | solution.py:313
  180.9 1.3 fusion.11
  (70 shorter events, 16.9 us)
Async XLA Ops:
  3.0 21.7 %copy-start = (bf16[1,2048,448]{1,2,0:T(8,128)(2,1)S(1)}, bf16[1,2048,448]{1,2,0:T(8,128)(2,1)}, u32[]{:S(2)}) copy-start(bf16[1,2048,448]{1,2,0:T(8,128)(2,1)} %param.10) | copy-start | bytes 5505028
  3.0 25.9 %all-to-all-start = ((bf16[4,64,3584]{2,1,0:T(8,128)(2,1)}), bf16[4,64,3584]{2,1,0:T(8,128)(2,1)}, u32[]{:S(2)}, u32[]{:S(2)}) async-start(bf16[4,64,3584]{2,1,0:T(8,128)(2,1)} %broadcast_in_dim.13), calls=%async_computation | async-start | bytes 3670016 | tf_op jit(solution)/shard_map/all_to_all | solution.py:29
  9.1 19.8 %collective-permute-start = (bf16[16,3584]{1,0:T(8,128)(2,1)S(1)}, bf16[16,3584]{1,0:T(8,128)(2,1)S(1)}, u32[]{:S(2)}, u32[]{:S(2)}) collective-permute-start(bf16[16,3584]{1,0:T(8,128)(2,1)S(1)} %dynamic-slice_bitcast_fusion.6), channel_id=1, source_target_pairs={{0,1},{1,0},{2,3},{3,2},{4,5},{5,4},{6,7},{7,6},{8,9},{9,8},{10,11... | collective-permute-start | bytes 344072 | tf_op jit(solution)/shard_map/ppermute | solution.py:23
  25.2 3.7 %collective-permute-start.1 = (f32[8,256]{1,0:T(8,128)S(1)}, f32[8,256]{1,0:T(8,128)S(1)}, u32[]{:S(2)}, u32[]{:S(2)}) collective-permute-start(f32[8,256]{1,0:T(8,128)S(1)} %reshape.125), channel_id=1, source_target_pairs={{0,256},{256,0},{1,257},{257,1},{2,258},{258,2},{3,259},{259,3},{4... | collective-permute-start | bytes 24584 | tf_op jit(solution)/shard_map/ppermute | solution.py:23
  30.3 7.3 %copy-start.15 = (s32[256]{0:T(256)S(1)}, s32[256]{0:T(256)}, u32[]{:S(2)}) copy-start(s32[256]{0:T(256)} %param.9) | copy-start | bytes 3076
  30.3 35.8 %all-to-all-start.1 = ((bf16[16,16,3584]{2,1,0:T(8,128)(2,1)}), bf16[16,16,3584]{2,1,0:T(8,128)(2,1)}, u32[]{:S(2)}, u32[]{:S(2)}) async-start(bf16[16,16,3584]{2,1,0:T(8,128)(2,1)} %broadcast_in_dim.14), calls=%async_computation.1 | async-start | bytes 3670016 | tf_op jit(solution)/shard_map/all_to_all | solution.py:29
  37.6 9.1 %copy-start.14 = (f32[256]{0:T(256)S(1)}, f32[256]{0:T(256)}, u32[]{:S(2)}) copy-start(f32[256]{0:T(256)} %param.8) | copy-start | bytes 3076
  41.7 5.0 %collective-permute-start.2 = (f32[128,256]{1,0:T(8,128)}, f32[128,256]{1,0:T(8,128)S(1)}, u32[]{:S(2)}, u32[]{:S(2)}) collective-permute-start(f32[128,256]{1,0:T(8,128)} %get-tuple-element.24), channel_id=1, source_target_pairs={{0,256},{256,0},{1,257},{257,1},{2,258},{258,2},{3,259},{259,3},{4... | collective-permute-start | bytes 393224 | tf_op jit(solution)/shard_map/ppermute | solution.py:23
  47.7 23.1 %collective-permute-start.3 = (bf16[160,256]{1,0:T(8,128)(2,1)S(1)}, bf16[160,256]{1,0:T(8,128)(2,1)S(1)}, u32[]{:S(2)}, u32[]{:S(2)}) collective-permute-start(bf16[160,256]{1,0:T(8,128)(2,1)S(1)} %pad_maximum_fusion.2), channel_id=1, source_target_pairs={{0,1},{1,0},{2,3},{3,2},{4,5},{5,4},{6,7},{7,6},{8,9},{9,8},{10,11... | collective-permute-start | bytes 245768 | tf_op jit(solution)/shard_map/ppermute | solution.py:23
  63.6 38.8 %collective-permute-start.6 = (bf16[448,2048]{1,0:T(8,128)(2,1)S(1)}, bf16[448,2048]{1,0:T(8,128)(2,1)}, u32[]{:S(2)}, u32[]{:S(2)}) collective-permute-start(bf16[448,2048]{1,0:T(8,128)(2,1)S(1)} %bitcast.43), channel_id=1, source_target_pairs={{0,256},{256,0},{1,257},{257,1},{2,258},{258,2},{3,259},{259,3},{4... | collective-permute-start | bytes 5505032 | tf_op jit(solution)/shard_map/ppermute | solution.py:23
  68.9 3.2 %collective-permute-start.4 = (f32[128,256]{1,0:T(8,128)S(1)}, f32[128,256]{1,0:T(8,128)S(1)}, u32[]{:S(2)}, u32[]{:S(2)}) collective-permute-start(f32[128,256]{1,0:T(8,128)S(1)} %get-tuple-element.53), channel_id=1, source_target_pairs={{0,256},{256,0},{1,257},{257,1},{2,258},{258,2},{3,259},{259,3},{4... | collective-permute-start | bytes 393224 | tf_op jit(solution)/shard_map/ppermute | solution.py:23
  72.2 30.2 %copy-start.2 = (s32[5]{0:T(128)S(1)}, s32[5]{0:T(128)}, u32[]{:S(2)}) copy-start(s32[5]{0:T(128)} %stack.23.at_ref) | copy-start | bytes 64
  73.2 20.0 %all-to-all-start.2 = ((bf16[4,448,256]{2,1,0:T(8,128)(2,1)}), bf16[4,448,256]{2,1,0:T(8,128)(2,1)S(1)}, u32[]{:S(2)}, u32[]{:S(2)}) async-start(bf16[4,448,256]{2,1,0:T(8,128)(2,1)} %broadcast_in_dim.15), calls=%async_computation.2 | async-start | bytes 1835008 | tf_op jit(solution)/shard_map/all_to_all | solution.py:29
  77.6 15.6 %collective-permute-start.5 = (bf16[128,256]{1,0:T(8,128)(2,1)S(1)}, bf16[128,256]{1,0:T(8,128)(2,1)S(1)}, u32[]{:S(2)}, u32[]{:S(2)}) collective-permute-start(bf16[128,256]{1,0:T(8,128)(2,1)S(1)} %get-tuple-element.42), channel_id=1, source_target_pairs={{0,1},{1,0},{2,3},{3,2},{4,5},{5,4},{6,7},{7,6},{8,9},{9,8},{10,11... | collective-permute-start | bytes 196616 | tf_op jit(solution)/shard_map/ppermute | solution.py:23
  102.4 16.7 %copy-start.10 = (f32[1,448]{1,0:T(1,128)S(1)}, f32[1,448]{1,0:T(1,128)}, u32[]{:S(2)}) copy-start(f32[1,448]{1,0:T(1,128)} %bias_ref.1) | copy-start | bytes 5380
  105.6 0.8 copy-start.1
  106.4 0.6 copy-start.13
  106.9 41.2 %all-to-all-start.4 = ((bf16[32,8,1024]{2,1,0:T(8,128)(2,1)}), bf16[32,8,1024]{2,1,0:T(8,128)(2,1)S(1)}, u32[]{:S(2)}, u32[]{:S(2)}) async-start(bf16[32,8,1024]{2,1,0:T(8,128)(2,1)} %bitcast.46), calls=%async_computation.4 | async-start | bytes 1048576 | tf_op jit(solution)/shard_map/all_to_all | solution.py:273
  122.9 6.3 %collective-permute-start.7 = (bf16[272,448]{1,0:T(8,128)(2,1)}, bf16[272,448]{1,0:T(8,128)(2,1)}, u32[]{:S(2)}, u32[]{:S(2)}) collective-permute-start(bf16[272,448]{1,0:T(8,128)(2,1)} %pad_maximum_fusion.1), channel_id=1, source_target_pairs={{0,256},{256,0},{1,257},{257,1},{2,258},{258,2},{3,259},{259,3},{4... | collective-permute-start | bytes 731144 | tf_op jit(solution)/shard_map/ppermute | solution.py:23
  131.5 0.7 copy-start.3
  135.2 0.6 copy-start.5
  135.8 0.6 copy-start.7
  136.4 0.6 copy-start.12
  148.1 0.7 copy-start.4
  148.8 0.7 copy-start.6
  149.5 0.7 copy-start.8
  150.2 0.7 copy-start.9
  150.8 0.7 copy-start.11
  152.9 27.4 %all-to-all-start.5 = ((f32[16,4,128]{2,1,0:T(4,128)}), f32[16,4,128]{2,1,0:T(4,128)S(1)}, u32[]{:S(2)}, u32[]{:S(2)}) async-start(f32[16,4,128]{2,1,0:T(4,128)} %get-tuple-element.38), calls=%async_computation.5 | async-start | bytes 65536 | tf_op jit(solution)/shard_map/all_to_all | solution.py:313
  166.0 4.3 %collective-permute-start.8 = (bf16[8,448]{1,0:T(8,128)(2,1)S(1)}, bf16[8,448]{1,0:T(8,128)(2,1)S(1)}, u32[]{:S(2)}, u32[]{:S(2)}) collective-permute-start(bf16[8,448]{1,0:T(8,128)(2,1)S(1)} %get-tuple-element.37), channel_id=1, source_target_pairs={{0,256},{256,0},{1,257},{257,1},{2,258},{258,2},{3,259},{259,3},{4... | collective-permute-start | bytes 21512 | tf_op jit(solution)/shard_map/ppermute | solution.py:23
  168.1 12.8 %collective-permute-start.9 = (f32[1,256]{1,0:T(1,128)}, f32[1,256]{1,0:T(1,128)S(1)}, u32[]{:S(2)}, u32[]{:S(2)}) collective-permute-start(f32[1,256]{1,0:T(1,128)} %copy-done.12), channel_id=1, source_target_pairs={{0,256},{256,0},{1,257},{257,1},{2,258},{258,2},{3,259},{259,3},{4... | collective-permute-start | bytes 3080 | tf_op jit(solution)/shard_map/ppermute | solution.py:23

commit v10 on v9

--- a/solution.py
+++ b/solution.py
@@ -61,18 +61,22 @@
         send_ref[rows, :] = v_ref[pl.ds(sent, 8), :]
 
 
-def decode_kernel(
-    at_ref, g1, g2, dec_ref, oth_ref, out_ref, nsq_ref, f_ref, wide_ref, norm_ref
-):
-    zh_at = at_ref[1]
-
+def norms_of(g1):
     nsq = [jnp.zeros((8, 256), F32)] * 2
     for y in range(4):
         for at in (384, 416):
             rows = g1[y, at : at + 32, :].astype(F32)
             nsq[0] = nsq[0] + (rows[0:8] + rows[8:16])
             nsq[1] = nsq[1] + (rows[16:24] + rows[24:32])
-    nsq_ref[...] = nsq[0]
+    return nsq
+
+
+def decode_kernel(
+    at_ref, g1, g2, dec_ref, oth_ref, out_ref, f_ref, wide_ref, norm_ref
+):
+    zh_at = at_ref[1]
+
+    nsq = norms_of(g1)
     norm = (jnp.sqrt(nsq[0]) + jnp.sqrt(nsq[1])) * 0.125
     high = norm.astype(BF).astype(F32)
     wide_ref[...] = jnp.zeros_like(wide_ref)
@@ -105,58 +109,69 @@
 
 
 def numer_kernel(
-    at_ref, g1, g2, dec_ref, oth_ref, own_ref, his_ref, num_ref, his_num_ref, msq_ref
+    at_ref,
+    g1,
+    g2,
+    dec_ref,
+    oth_ref,
+    own_ref,
+    his_ref,
+    bias_ref,
+    pack_ref,
+    stat_ref,
+    num_ref,
+    nsq_ref,
 ):
-    zh_at, y_at = at_ref[1], at_ref[3]
-    for acts, dec, num in ((own_ref, dec_ref, num_ref), (his_ref, oth_ref, his_num_ref)):
+    zh_at, tok_at, y_at, lat_at = [at_ref[k] for k in range(1, 5)]
+    for k, (acts, dec) in enumerate(((own_ref, dec_ref), (his_ref, oth_ref))):
+        rows = acts[0:256, :]
         for y in range(4):
             for zh in range(2):
                 at = 2 * y + (zh_at if zh == 0 else 1 - zh_at)
                 cols = dec[:, pl.ds(pl.multiple_of(at * 256, 256), 256)]
-                inner = jnp.dot(acts[...], cols, preferred_element_type=F32)
+                inner = jnp.dot(rows, cols, preferred_element_type=F32)
                 near = g1[y, 0:128, :] if zh == 0 else g2[y]
                 far = g1[y, 256:384, :] if zh == 0 else g1[y, 128:256, :]
                 both = inner[0:128] * near.astype(F32) + inner[128:256] * far.astype(F32)
-                num[pl.ds(at, 1), :] = jnp.sum(both, axis=0, keepdims=True)
+                num_ref[k, pl.ds(at, 1), :] = jnp.sum(both, axis=0, keepdims=True)
+    pack_ref[0:8, 0:256] = num_ref[0]
+    pack_ref[0:8, 256:512] = num_ref[1]
+
+    row = (lat_at // 8) * 32 + (lat_at % 4) * 8
+    row = row + jnp.where((lat_at // 4) % 2 == zh_at, 0, 128)
+    for k, acts in enumerate((own_ref, his_ref)):
+        rows = acts[pl.ds(pl.multiple_of((row // 16) * 16, 16), 16), :].astype(F32)
+        kept = jnp.where((row // 8) % 2 == 0, rows[0:8], rows[8:16])
+        pack_ref[8 + 8 * k : 16 + 8 * k, 0:448] = kept
+    pack_ref[24:25, 0:448] = bias_ref[...]
+    rows = his_ref[256:272, :].astype(F32)
+    pack_ref[25:26, 0:448] = (rows[0:1] + rows[1:2]) + rows[2:3]
 
     squares = jnp.zeros((128, 256), F32)
     for rows in (slice(0, 128), slice(256, 384)):
         feats = g1[y_at, rows, :].astype(F32)
         squares = squares + feats * feats
-    msq_ref[...] = jnp.sum(squares, axis=0, keepdims=True)
-
-
-def close_kernel(
-    at_ref,
-    arrived_ref,
-    bias_ref,
-    his_bias_ref,
-    act_ref,
-    his_act_ref,
-    num_ref,
-    his_num_ref,
-    recon_ref,
-    his_recon_ref,
-    last_ref,
-):
+    nsq_ref[...] = norms_of(g1)[0]
+    stat_ref[0:1, :] = jnp.sum(squares, axis=0, keepdims=True)
+    stat_ref[1:2, :] = nsq_ref[pl.ds(tok_at, 1), :]
+
+
+def close_kernel(at_ref, arrived_ref, pack_ref, recon_ref, his_recon_ref, last_ref):
     pair_at = at_ref[0]
     total = arrived_ref[0].astype(F32)
     for k in range(1, 32):
         total = total + arrived_ref[k].astype(F32)
     terms = penalty * (total[:, 448:449] + total[:, 449:450])
-    for at, bias, act, out in (
-        (0, bias_ref, act_ref, recon_ref),
-        (512, his_bias_ref, his_act_ref, his_recon_ref),
-    ):
-        recon = total[:, at : at + 448] + bias[...]
+    for k, out in enumerate((recon_ref, his_recon_ref)):
+        recon = total[:, 512 * k : 512 * k + 448] + pack_ref[24 + k : 25 + k, 0:448]
         out[...] = recon.astype(BF)
-        residue = act[...].astype(F32) - recon
+        residue = pack_ref[8 + 8 * k : 16 + 8 * k, 0:448] - recon
         terms = terms + jnp.sum(residue * residue, axis=1, keepdims=True) / (2.0 * D)
     row = lax.broadcasted_iota(jnp.int32, (8, 128), 0)
     lane = lax.broadcasted_iota(jnp.int32, (8, 128), 1)
     line = jnp.sum(jnp.where(row + pair_at * 8 == lane, terms, 0.0), axis=0, keepdims=True)
     for pair in range(2):
-        num = jnp.where(pair_at == pair, num_ref[...], his_num_ref[...])
+        num = jnp.where(pair_at == pair, pack_ref[0:8, 0:256], pack_ref[0:8, 256:512])
         for k in range(8):
             at = pair * 8 + k
             last_ref[at, 0:1, :] = num[k : k + 1, 0:128]
@@ -256,11 +271,11 @@
     over_far, g1 = lax.optimization_barrier((over_far, g1))
     g2 = gather(over_far, "y")
 
-    payload, nsq_all = call(
+    (payload,) = call(
         decode_kernel,
         "decode",
         2 * tokens * 8 * own * 512,
-        [((tokens // 2, 1024), BF), ((8, own), F32)],
+        [((tokens // 2, 1024), BF)],
         4,
         [
             pltpu.VMEM((tokens // 2, 8 * own), BF),
@@ -269,7 +284,6 @@
         ],
         limit=40,
     )(at, g1, g2, dec_t, dec_oth)
-    nsq_own = lax.dynamic_index_in_dim(nsq_all, tok_at, 0, keepdims=False)
     arrived = lax.all_to_all(payload.reshape(32, 8, 1024), LAT, 0, 0)
 
     cols = [
@@ -283,33 +297,27 @@
     bias_rows = jnp.pad(jnp.concatenate(bias_rows, axis=0), ((0, 13), (0, 0)))
     sent = jnp.concatenate([cols[0][1], cols[1][1], bias_rows], axis=0)
     came = swap(sent, "pair")
-    his_acts = came[:256]
-    his_bias = jnp.sum(came[256:259].astype(F32), axis=0, keepdims=True)
-    num_part, his_num, sum_sq = call(
+    pack, stats = call(
         numer_kernel,
         "numer",
         2 * tokens * 8 * own * width,
-        [((8, own), F32), ((8, own), F32), ((1, own), F32)],
-        6,
-        [],
+        [((32, 512), F32), ((2, own), F32)],
+        7,
+        [pltpu.VMEM((2, 8, own), F32), pltpu.VMEM((8, own), F32)],
         limit=40,
-    )(at, g1, g2, dec_t, dec_oth, own_acts, his_acts)
-    mean_sq = (sum_sq + swap(sum_sq, "pair"))[0] / tokens
-
-    own_row = jnp.where((lat_at // 4) % 2 == zh_at, 0, 128)
-    own_row = own_row + (lat_at // 8) * 32 + (lat_at % 4) * 8
-    act_own, his_own = [
-        lax.dynamic_slice_in_dim(acts, own_row, 8, 0) for acts in (own_acts, his_acts)
-    ]
+    )(at, g1, g2, dec_t, dec_oth, own_acts, came, dec_bias)
+    nsq_own = stats[1]
+    mean_sq = (stats[:1] + swap(stats[:1], "pair"))[0] / tokens
+
     recon_own, recon_his, last = call(
         close_kernel,
         "close",
         1 << 20,
         [((8, width), BF), ((8, width), BF), ((16, 4, 128), F32)],
-        7,
+        2,
         [],
         limit=16,
-    )(at, arrived, dec_bias, his_bias, act_own, his_own, num_part, his_num)
+    )(at, arrived, pack)
     got = lax.all_to_all(last, ("pair",) + TOK, 0, 0, tiled=True)
     recon_came = swap(recon_his, "pair")
     recon = jnp.where(

time: 183 us -> 179 us (0.978)
  waiting for transfers between devices: 25.1 us -> 32.4 us
  local copies, waits for them, and re-layouts: 17.7 us -> 11 us
  other arithmetic: 7.66 us -> 3.28 us
    all_to_all x1, waiting for transfers between devices: 11.1 us -> 17.2 us  [body(): arrived = lax.all_to_all(payload.reshape(32, 8, 1024), LAT, 0, 0)]
    unnamed x34 -> x18, local copies, waits for them, and re-layouts: 7.23 us -> 2.28 us
  transfers between devices with their start and end apart: 15 -> 15, of which waited for: 6 -> 7; matrix products, arithmetic and copies ran while one was open for 9% -> 6% of each run, Pallas kernels for 4% -> 4%
where the time goes in v10:
time: 179 us; the launch traced here: 178 us
  starting transfers between devices  107 us (60%)
  waiting for transfers between devices  32.4 us (18%)
  Pallas kernels  11.6 us (6%)
  local copies, waits for them, and re-layouts  11 us (6%)
  blocking collectives  9.2 us (5%)
  other arithmetic  3.28 us (2%)
  matrix products  2.69 us (2%)
    ppermute x10, starting transfers between devices, swap(): return lax.ppermute(value, axis, [(0, 1), (1, 0)])  65.1 us
    all_to_all x1, waiting for transfers between devices, body(): arrived = lax.all_to_all(payload.reshape(32, 8, 1024), LAT, 0, 0)  17.2 us
    all_to_all x3, starting transfers between devices, gather(): return lax.all_to_all(copies, axes, 0, 0, tiled=False)  16.8 us
    all_to_all x1, starting transfers between devices, body(): got = lax.all_to_all(last, ('pair',) + TOK, 0, 0, tiled=True)  13.2 us
    all_to_all x1, starting transfers between devices, body(): arrived = lax.all_to_all(payload.reshape(32, 8, 1024), LAT, 0, 0)  12 us
    all_to_all x1, waiting for transfers between devices, body(): got = lax.all_to_all(last, ('pair',) + TOK, 0, 0, tiled=True)  9.27 us
    all_to_all x1, blocking collectives, gather(): return lax.all_to_all(copies, axes, 0, 0, tiled=False)  9.2 us
    ppermute x10, waiting for transfers between devices, swap(): return lax.ppermute(value, axis, [(0, 1), (1, 0)])  5.9 us
  transfers between devices with their start and end apart: 15, of which 7 were waited for; matrix products, arithmetic and copies ran while one was open for 6% of the time, Pallas kernels for 4%

profile of v10, /device:TPU:1, one launch (start us, length us, event | category | flops | bytes accessed | tf_op | source)
XLA Modules:
  0.0 178.3 jit_solution(3881519775699241082)
XLA Ops:
  0.6 2.4 %broadcast_in_dim.11 = bf16[4,64,3584]{2,1,0:T(8,128)(2,1)} broadcast(bf16[64,3584]{1,0:T(8,128)(2,1)} %bitcast.50), dimensions={1,2} | broadcast | bytes 2293760 | tf_op jit(solution)/shard_map/broadcast_in_dim | solution.py:28
  3.0 5.1 %all-to-all-start = ((bf16[4,64,3584]{2,1,0:T(8,128)(2,1)}), bf16[4,64,3584]{2,1,0:T(8,128)(2,1)}, u32[]{:S(2)}, u32[]{:S(2)}) async-start(bf16[4,64,3584]{2,1,0:T(8,128)(2,1)} %broadcast_in_dim.11), calls=%async_computation | async-start | bytes 3670016 | tf_op jit(solution)/shard_map/all_to_all | solution.py:29
  9.1 15.7 %collective-permute-start = (bf16[16,3584]{1,0:T(8,128)(2,1)S(1)}, bf16[16,3584]{1,0:T(8,128)(2,1)S(1)}, u32[]{:S(2)}, u32[]{:S(2)}) collective-permute-start(bf16[16,3584]{1,0:T(8,128)(2,1)S(1)} %dynamic-slice_bitcast_fusion.6), channel_id=1, source_target_pairs={{0,1},{1,0},{2,3},{3,2},{4,5},{5,4},{6,7},{7,6},{8,9},{9,8},{10,11... | collective-permute-start | bytes 344072 | tf_op jit(solution)/shard_map/ppermute | solution.py:23
  25.2 2.9 %collective-permute-start.1 = (f32[8,256]{1,0:T(8,128)S(1)}, f32[8,256]{1,0:T(8,128)S(1)}, u32[]{:S(2)}, u32[]{:S(2)}) collective-permute-start(f32[8,256]{1,0:T(8,128)S(1)} %reshape.125), channel_id=1, source_target_pairs={{0,256},{256,0},{1,257},{257,1},{2,258},{258,2},{3,259},{259,3},{4... | collective-permute-start | bytes 24584 | tf_op jit(solution)/shard_map/ppermute | solution.py:23
  28.9 1.4 broadcast_in_dim.12
  30.3 7.3 %all-to-all-start.1 = ((bf16[16,16,3584]{2,1,0:T(8,128)(2,1)}), bf16[16,16,3584]{2,1,0:T(8,128)(2,1)}, u32[]{:S(2)}, u32[]{:S(2)}) async-start(bf16[16,16,3584]{2,1,0:T(8,128)(2,1)} %broadcast_in_dim.12), calls=%async_computation.1 | async-start | bytes 3670016 | tf_op jit(solution)/shard_map/all_to_all | solution.py:29
  37.7 4.1 %encode.1 = (f32[128,256]{1,0:T(8,128)}, f32[128,256]{1,0:T(8,128)}) custom-call(s32[5]{0:T(128)} %stack.23.at_ref, bf16[256,3584]{1,0:T(8,128)(2,1)} %bitcast.8.act_hbm, bf16[3584,256]{1,0:T(8,128)(2,1)} %bitcast.47), custom_call_target="tpu_custom_call" | custom-call | flops 469762048 | bytes 6291456 | tf_op jit(solution)/shard_map/encode/pallas_call | solution.py:254
  41.7 3.8 %collective-permute-start.2 = (f32[128,256]{1,0:T(8,128)}, f32[128,256]{1,0:T(8,128)S(1)}, u32[]{:S(2)}, u32[]{:S(2)}) collective-permute-start(f32[128,256]{1,0:T(8,128)} %get-tuple-element.21), channel_id=1, source_target_pairs={{0,256},{256,0},{1,257},{257,1},{2,258},{258,2},{3,259},{259,3},{4... | collective-permute-start | bytes 393224 | tf_op jit(solution)/shard_map/ppermute | solution.py:23
  45.6 1.1 collective-permute-done.2
  47.7 15.8 %collective-permute-start.3 = (bf16[160,256]{1,0:T(8,128)(2,1)S(1)}, bf16[160,256]{1,0:T(8,128)(2,1)S(1)}, u32[]{:S(2)}, u32[]{:S(2)}) collective-permute-start(bf16[160,256]{1,0:T(8,128)(2,1)S(1)} %pad_maximum_fusion.2), channel_id=1, source_target_pairs={{0,1},{1,0},{2,3},{3,2},{4,5},{5,4},{6,7},{7,6},{8,9},{9,8},{10,11... | collective-permute-start | bytes 245768 | tf_op jit(solution)/shard_map/ppermute | solution.py:23
  63.5 2.6 %collective-permute-start.6 = (bf16[448,2048]{1,0:T(8,128)(2,1)S(1)}, bf16[448,2048]{1,0:T(8,128)(2,1)}, u32[]{:S(2)}, u32[]{:S(2)}) collective-permute-start(bf16[448,2048]{1,0:T(8,128)(2,1)S(1)} %bitcast.42), channel_id=1, source_target_pairs={{0,256},{256,0},{1,257},{257,1},{2,258},{258,2},{3,259},{259,3},{4... | collective-permute-start | bytes 5505032 | tf_op jit(solution)/shard_map/ppermute | solution.py:23
  66.1 2.7 %fusion = f32[16,2,8,256]{3,2,1,0:T(8,128)S(1)} fusion(bf16[1,3584,256]{2,1,0:T(8,128)(2,1)} %param.7, bf16[16,16,3584]{2,1,0:T(8,128)(2,1)} %all-to-all-done.1), kind=kOutput, calls=%fused_computation.1 | convolution fusion | flops 469762048 | bytes 3932160 | tf_op jit(solution)/shard_map/dot_general | solution.py:263
  68.8 1.9 %collective-permute-start.4 = (f32[128,256]{1,0:T(8,128)S(1)}, f32[128,256]{1,0:T(8,128)S(1)}, u32[]{:S(2)}, u32[]{:S(2)}) collective-permute-start(f32[128,256]{1,0:T(8,128)S(1)} %get-tuple-element.47), channel_id=1, source_target_pairs={{0,256},{256,0},{1,257},{257,1},{2,258},{258,2},{3,259},{259,3},{4... | collective-permute-start | bytes 393224 | tf_op jit(solution)/shard_map/ppermute | solution.py:23
  70.8 1.3 collective-permute-done.4
  72.2 1.0 broadcast_in_dim.13
  73.2 4.4 %all-to-all-start.2 = ((bf16[4,448,256]{2,1,0:T(8,128)(2,1)}), bf16[4,448,256]{2,1,0:T(8,128)(2,1)S(1)}, u32[]{:S(2)}, u32[]{:S(2)}) async-start(bf16[4,448,256]{2,1,0:T(8,128)(2,1)} %broadcast_in_dim.13), calls=%async_computation.2 | async-start | bytes 1835008 | tf_op jit(solution)/shard_map/all_to_all | solution.py:29
  77.6 13.5 %collective-permute-start.5 = (bf16[128,256]{1,0:T(8,128)(2,1)S(1)}, bf16[128,256]{1,0:T(8,128)(2,1)S(1)}, u32[]{:S(2)}, u32[]{:S(2)}) collective-permute-start(bf16[128,256]{1,0:T(8,128)(2,1)S(1)} %get-tuple-element.36), channel_id=1, source_target_pairs={{0,1},{1,0},{2,3},{3,2},{4,5},{5,4},{6,7},{7,6},{8,9},{9,8},{10,11... | collective-permute-start | bytes 196616 | tf_op jit(solution)/shard_map/ppermute | solution.py:23
  91.1 2.2 %collective-permute-done.5 = bf16[128,256]{1,0:T(8,128)(2,1)S(1)} collective-permute-done((bf16[128,256]{1,0:T(8,128)(2,1)S(1)}, bf16[128,256]{1,0:T(8,128)(2,1)S(1)}, u32[]{:S(2)}, u32[]{:S(2)}) %collective-permute-start.5) | collective-permute-done | bytes 65568 | tf_op jit(solution)/shard_map/ppermute | solution.py:23
  93.3 9.2 %all_to_all.30.g2 = bf16[4,128,256]{2,1,0:T(8,128)(2,1)S(1)} all-to-all(bf16[4,128,256]{2,1,0:T(8,128)(2,1)S(1)} %broadcast_in_dim.14), channel_id=1, replica_groups=mesh['pair'=2,'x'=4,'zl'=8,'y'=4,'zh'=2] {'y'}, dimensions={0} | all-to-all | bytes 524288 | tf_op jit(solution)/shard_map/all_to_all | solution.py:29
  102.5 3.1 %decode.1 = bf16[256,1024]{1,0:T(8,128)(2,1)S(1)} custom-call(s32[5]{0:T(128)S(1)} %copy-done.4, bf16[4,448,256]{2,1,0:T(8,128)(2,1)S(1)} %all-to-all-done.2.g1, bf16[4,128,256]{2,1,0:T(8,128)(2,1)S(1)} %all_to_all.30.g2, bf16[448,2048]{1,0:T(8,128)(2,1)S(1)} %bitcast.43, bf16[448,2048]{1,0:T(8,128)(2,1)} %collective-permute-done.6.oth_ref), custom_call_target="tpu_custom_call" | custom-call | flops 1073741824 | bytes 6291456 | tf_op jit(solution)/shard_map/decode/pallas_call | solution.py:274
  106.4 12.0 %all-to-all-start.4 = ((bf16[32,8,1024]{2,1,0:T(8,128)(2,1)}), bf16[32,8,1024]{2,1,0:T(8,128)(2,1)S(1)}, u32[]{:S(2)}, u32[]{:S(2)}) async-start(bf16[32,8,1024]{2,1,0:T(8,128)(2,1)} %bitcast.45), calls=%async_computation.4 | async-start | bytes 1048576 | tf_op jit(solution)/shard_map/all_to_all | solution.py:287
  118.5 1.1 constant_dynamic-slice_fusion.1
  119.7 1.1 constant_dynamic-slice_fusion
  120.9 4.6 %collective-permute-start.7 = (bf16[272,448]{1,0:T(8,128)(2,1)S(1)}, bf16[272,448]{1,0:T(8,128)(2,1)S(1)}, u32[]{:S(2)}, u32[]{:S(2)}) collective-permute-start(bf16[272,448]{1,0:T(8,128)(2,1)S(1)} %pad_maximum_fusion), channel_id=1, source_target_pairs={{0,256},{256,0},{1,257},{257,1},{2,258},{258,2},{3,259},{259,3},{4... | collective-permute-start | bytes 731144 | tf_op jit(solution)/shard_map/ppermute | solution.py:23
  125.5 1.1 collective-permute-done.7.his_ref
  126.6 3.0 %numer.1 = (f32[32,512]{1,0:T(8,128)S(1)}, f32[2,256]{1,0:T(2,128)S(1)}) custom-call(s32[5]{0:T(128)S(1)} %copy-done.4, bf16[4,448,256]{2,1,0:T(8,128)(2,1)S(1)} %all-to-all-done.2.g1, bf16[4,128,256]{2,1,0:T(8,128)(2,1)S(1)} %all_to_all.30.g2, bf16[448,2048]{1,0:T(8,128)(2,1)S(1)} %bitcast.44, bf16[448,2048]{1,0:T(8,128)(2,1)} %collective-permute-done.6.oth_ref, ...), custom_call_target="tpu_custom_call" | custom-call | flops 939524096 | bytes 6291456 | tf_op jit(solution)/shard_map/numer/pallas_call | solution.py:300
  130.3 17.2 %all-to-all-done.4.arrived_ref = bf16[32,8,1024]{2,1,0:T(8,128)(2,1)S(1)} async-done(((bf16[32,8,1024]{2,1,0:T(8,128)(2,1)}), bf16[32,8,1024]{2,1,0:T(8,128)(2,1)S(1)}, u32[]{:S(2)}, u32[]{:S(2)}) %all-to-all-start.4) | async-done | bytes 524320 | tf_op jit(solution)/shard_map/all_to_all | solution.py:287
  148.4 1.4 close.1
  149.7 13.2 %all-to-all-start.5 = ((f32[16,4,128]{2,1,0:T(4,128)}), f32[16,4,128]{2,1,0:T(4,128)S(1)}, u32[]{:S(2)}, u32[]{:S(2)}) async-start(f32[16,4,128]{2,1,0:T(4,128)} %get-tuple-element.33), calls=%async_computation.5 | async-start | bytes 65536 | tf_op jit(solution)/shard_map/all_to_all | solution.py:321
  162.9 2.0 %collective-permute-start.8 = (bf16[8,448]{1,0:T(8,128)(2,1)S(1)}, bf16[8,448]{1,0:T(8,128)(2,1)S(1)}, u32[]{:S(2)}, u32[]{:S(2)}) collective-permute-start(bf16[8,448]{1,0:T(8,128)(2,1)S(1)} %get-tuple-element.32), channel_id=1, source_target_pairs={{0,256},{256,0},{1,257},{257,1},{2,258},{258,2},{3,259},{259,3},{4... | collective-permute-start | bytes 21512 | tf_op jit(solution)/shard_map/ppermute | solution.py:23
  164.9 2.3 %collective-permute-start.9 = (f32[1,256]{1,0:T(1,128)S(1)}, f32[1,256]{1,0:T(1,128)S(1)}, u32[]{:S(2)}, u32[]{:S(2)}) collective-permute-start(f32[1,256]{1,0:T(1,128)S(1)} %slice.24), channel_id=1, source_target_pairs={{0,256},{256,0},{1,257},{257,1},{2,258},{258,2},{3,259},{259,3},{4... | collective-permute-start | bytes 3080 | tf_op jit(solution)/shard_map/ppermute | solution.py:23
  167.9 9.3 %all-to-all-done.5 = f32[16,4,128]{2,1,0:T(4,128)S(1)} async-done(((f32[16,4,128]{2,1,0:T(4,128)}), f32[16,4,128]{2,1,0:T(4,128)S(1)}, u32[]{:S(2)}, u32[]{:S(2)}) %all-to-all-start.5) | async-done | bytes 32800 | tf_op jit(solution)/shard_map/all_to_all | solution.py:321
  (51 shorter events, 7.4 us)
Async XLA Ops:
  3.0 21.7 %copy-start = (bf16[1,2048,448]{1,2,0:T(8,128)(2,1)S(1)}, bf16[1,2048,448]{1,2,0:T(8,128)(2,1)}, u32[]{:S(2)}) copy-start(bf16[1,2048,448]{1,2,0:T(8,128)(2,1)} %param.10) | copy-start | bytes 5505028
  3.0 25.9 %all-to-all-start = ((bf16[4,64,3584]{2,1,0:T(8,128)(2,1)}), bf16[4,64,3584]{2,1,0:T(8,128)(2,1)}, u32[]{:S(2)}, u32[]{:S(2)}) async-start(bf16[4,64,3584]{2,1,0:T(8,128)(2,1)} %broadcast_in_dim.11), calls=%async_computation | async-start | bytes 3670016 | tf_op jit(solution)/shard_map/all_to_all | solution.py:29
  9.1 19.8 %collective-permute-start = (bf16[16,3584]{1,0:T(8,128)(2,1)S(1)}, bf16[16,3584]{1,0:T(8,128)(2,1)S(1)}, u32[]{:S(2)}, u32[]{:S(2)}) collective-permute-start(bf16[16,3584]{1,0:T(8,128)(2,1)S(1)} %dynamic-slice_bitcast_fusion.6), channel_id=1, source_target_pairs={{0,1},{1,0},{2,3},{3,2},{4,5},{5,4},{6,7},{7,6},{8,9},{9,8},{10,11... | collective-permute-start | bytes 344072 | tf_op jit(solution)/shard_map/ppermute | solution.py:23
  25.2 3.7 %collective-permute-start.1 = (f32[8,256]{1,0:T(8,128)S(1)}, f32[8,256]{1,0:T(8,128)S(1)}, u32[]{:S(2)}, u32[]{:S(2)}) collective-permute-start(f32[8,256]{1,0:T(8,128)S(1)} %reshape.125), channel_id=1, source_target_pairs={{0,256},{256,0},{1,257},{257,1},{2,258},{258,2},{3,259},{259,3},{4... | collective-permute-start | bytes 24584 | tf_op jit(solution)/shard_map/ppermute | solution.py:23
  30.3 7.3 %copy-start.7 = (s32[256]{0:T(256)S(1)}, s32[256]{0:T(256)}, u32[]{:S(2)}) copy-start(s32[256]{0:T(256)} %param.9) | copy-start | bytes 3076
  30.3 35.8 %all-to-all-start.1 = ((bf16[16,16,3584]{2,1,0:T(8,128)(2,1)}), bf16[16,16,3584]{2,1,0:T(8,128)(2,1)}, u32[]{:S(2)}, u32[]{:S(2)}) async-start(bf16[16,16,3584]{2,1,0:T(8,128)(2,1)} %broadcast_in_dim.12), calls=%async_computation.1 | async-start | bytes 3670016 | tf_op jit(solution)/shard_map/all_to_all | solution.py:29
  37.6 9.1 %copy-start.6 = (f32[256]{0:T(256)S(1)}, f32[256]{0:T(256)}, u32[]{:S(2)}) copy-start(f32[256]{0:T(256)} %param.8) | copy-start | bytes 3076
  41.7 5.0 %collective-permute-start.2 = (f32[128,256]{1,0:T(8,128)}, f32[128,256]{1,0:T(8,128)S(1)}, u32[]{:S(2)}, u32[]{:S(2)}) collective-permute-start(f32[128,256]{1,0:T(8,128)} %get-tuple-element.21), channel_id=1, source_target_pairs={{0,256},{256,0},{1,257},{257,1},{2,258},{258,2},{3,259},{259,3},{4... | collective-permute-start | bytes 393224 | tf_op jit(solution)/shard_map/ppermute | solution.py:23
  47.7 23.1 %collective-permute-start.3 = (bf16[160,256]{1,0:T(8,128)(2,1)S(1)}, bf16[160,256]{1,0:T(8,128)(2,1)S(1)}, u32[]{:S(2)}, u32[]{:S(2)}) collective-permute-start(bf16[160,256]{1,0:T(8,128)(2,1)S(1)} %pad_maximum_fusion.2), channel_id=1, source_target_pairs={{0,1},{1,0},{2,3},{3,2},{4,5},{5,4},{6,7},{7,6},{8,9},{9,8},{10,11... | collective-permute-start | bytes 245768 | tf_op jit(solution)/shard_map/ppermute | solution.py:23
  63.5 39.0 %collective-permute-start.6 = (bf16[448,2048]{1,0:T(8,128)(2,1)S(1)}, bf16[448,2048]{1,0:T(8,128)(2,1)}, u32[]{:S(2)}, u32[]{:S(2)}) collective-permute-start(bf16[448,2048]{1,0:T(8,128)(2,1)S(1)} %bitcast.42), channel_id=1, source_target_pairs={{0,256},{256,0},{1,257},{257,1},{2,258},{258,2},{3,259},{259,3},{4... | collective-permute-start | bytes 5505032 | tf_op jit(solution)/shard_map/ppermute | solution.py:23
  68.8 3.2 %collective-permute-start.4 = (f32[128,256]{1,0:T(8,128)S(1)}, f32[128,256]{1,0:T(8,128)S(1)}, u32[]{:S(2)}, u32[]{:S(2)}) collective-permute-start(f32[128,256]{1,0:T(8,128)S(1)} %get-tuple-element.47), channel_id=1, source_target_pairs={{0,256},{256,0},{1,257},{257,1},{2,258},{258,2},{3,259},{259,3},{4... | collective-permute-start | bytes 393224 | tf_op jit(solution)/shard_map/ppermute | solution.py:23
  72.2 30.3 %copy-start.4 = (s32[5]{0:T(128)S(1)}, s32[5]{0:T(128)}, u32[]{:S(2)}) copy-start(s32[5]{0:T(128)} %stack.23.at_ref) | copy-start | bytes 64
  73.2 20.1 %all-to-all-start.2 = ((bf16[4,448,256]{2,1,0:T(8,128)(2,1)}), bf16[4,448,256]{2,1,0:T(8,128)(2,1)S(1)}, u32[]{:S(2)}, u32[]{:S(2)}) async-start(bf16[4,448,256]{2,1,0:T(8,128)(2,1)} %broadcast_in_dim.13), calls=%async_computation.2 | async-start | bytes 1835008 | tf_op jit(solution)/shard_map/all_to_all | solution.py:29
  77.6 15.7 %collective-permute-start.5 = (bf16[128,256]{1,0:T(8,128)(2,1)S(1)}, bf16[128,256]{1,0:T(8,128)(2,1)S(1)}, u32[]{:S(2)}, u32[]{:S(2)}) collective-permute-start(bf16[128,256]{1,0:T(8,128)(2,1)S(1)} %get-tuple-element.36), channel_id=1, source_target_pairs={{0,1},{1,0},{2,3},{3,2},{4,5},{5,4},{6,7},{7,6},{8,9},{9,8},{10,11... | collective-permute-start | bytes 196616 | tf_op jit(solution)/shard_map/ppermute | solution.py:23
  102.5 16.0 %copy-start.5 = (f32[1,448]{1,0:T(1,128)S(1)}, f32[1,448]{1,0:T(1,128)}, u32[]{:S(2)}) copy-start(f32[1,448]{1,0:T(1,128)} %bias_ref.1) | copy-start | bytes 5380
  105.6 0.8 copy-start.1
  106.4 41.1 %all-to-all-start.4 = ((bf16[32,8,1024]{2,1,0:T(8,128)(2,1)}), bf16[32,8,1024]{2,1,0:T(8,128)(2,1)S(1)}, u32[]{:S(2)}, u32[]{:S(2)}) async-start(bf16[32,8,1024]{2,1,0:T(8,128)(2,1)} %bitcast.45), calls=%async_computation.4 | async-start | bytes 1048576 | tf_op jit(solution)/shard_map/all_to_all | solution.py:287
  120.9 5.7 %collective-permute-start.7 = (bf16[272,448]{1,0:T(8,128)(2,1)S(1)}, bf16[272,448]{1,0:T(8,128)(2,1)S(1)}, u32[]{:S(2)}, u32[]{:S(2)}) collective-permute-start(bf16[272,448]{1,0:T(8,128)(2,1)S(1)} %pad_maximum_fusion), channel_id=1, source_target_pairs={{0,256},{256,0},{1,257},{257,1},{2,258},{258,2},{3,259},{259,3},{4... | collective-permute-start | bytes 731144 | tf_op jit(solution)/shard_map/ppermute | solution.py:23
  129.7 0.6 copy-start.2
  147.5 0.8 copy-start.3
  149.7 27.4 %all-to-all-start.5 = ((f32[16,4,128]{2,1,0:T(4,128)}), f32[16,4,128]{2,1,0:T(4,128)S(1)}, u32[]{:S(2)}, u32[]{:S(2)}) async-start(f32[16,4,128]{2,1,0:T(4,128)} %get-tuple-element.33), calls=%async_computation.5 | async-start | bytes 65536 | tf_op jit(solution)/shard_map/all_to_all | solution.py:321
  162.9 4.3 %collective-permute-start.8 = (bf16[8,448]{1,0:T(8,128)(2,1)S(1)}, bf16[8,448]{1,0:T(8,128)(2,1)S(1)}, u32[]{:S(2)}, u32[]{:S(2)}) collective-permute-start(bf16[8,448]{1,0:T(8,128)(2,1)S(1)} %get-tuple-element.32), channel_id=1, source_target_pairs={{0,256},{256,0},{1,257},{257,1},{2,258},{258,2},{3,259},{259,3},{4... | collective-permute-start | bytes 21512 | tf_op jit(solution)/shard_map/ppermute | solution.py:23
  164.9 12.8 %collective-permute-start.9 = (f32[1,256]{1,0:T(1,128)S(1)}, f32[1,256]{1,0:T(1,128)S(1)}, u32[]{:S(2)}, u32[]{:S(2)}) collective-permute-start(f32[1,256]{1,0:T(1,128)S(1)} %slice.24), channel_id=1, source_target_pairs={{0,256},{256,0},{1,257},{257,1},{2,258},{258,2},{3,259},{259,3},{4... | collective-permute-start | bytes 3080 | tf_op jit(solution)/shard_map/ppermute | solution.py:23

commit v11 on v10

--- a/solution.py
+++ b/solution.py
@@ -71,9 +71,7 @@
     return nsq
 
 
-def decode_kernel(
-    at_ref, g1, g2, dec_ref, oth_ref, out_ref, f_ref, wide_ref, norm_ref
-):
+def decode_kernel(at_ref, g1, dec_ref, oth_ref, part_ref, norm_ref, f_ref, wide_ref):
     zh_at = at_ref[1]
 
     nsq = norms_of(g1)
@@ -91,21 +89,32 @@
         f_ref[0:128, pl.ds(mine, 256)] = g1[y, 0:128, :]
         f_ref[128:256, pl.ds(theirs, 256)] = g1[y, 128:256, :]
         f_ref[128:256, pl.ds(mine, 256)] = g1[y, 256:384, :]
-        f_ref[0:128, pl.ds(theirs, 256)] = g2[y]
+        f_ref[0:128, pl.ds(theirs, 256)] = jnp.zeros((128, 256), BF)
     feats = f_ref[...]
-    out = []
-    for ref in (dec_ref, norm_ref, oth_ref):
+    for ref, at, width in ((dec_ref, 0, 448), (norm_ref, 448, 64), (oth_ref, 512, 448)):
         value = lax.dot_general(feats, ref[...], NT, preferred_element_type=F32)
-        out.append(value.astype(BF))
-    for half in range(2):
-        zh = zh_at if half == 0 else 1 - zh_at
+        part_ref[:, at : at + width] = value
+    part_ref[:, 960:1024] = jnp.zeros((256, 64), F32)
+
+
+def finish_kernel(at_ref, g2, dec_ref, oth_ref, norm_ref, part_ref, out_ref):
+    zh_at = at_ref[1]
+    for ref, at, width in ((dec_ref, 0, 448), (norm_ref, 448, 64), (oth_ref, 512, 448)):
+        value = part_ref[0:128, at : at + width]
         for y in range(4):
-            src = slice(half * 128 + y * 32, half * 128 + (y + 1) * 32)
-            dst = pl.ds(pl.multiple_of((2 * y + zh) * 32, 32), 32)
-            out_ref[dst, 0:448] = out[0][src]
-            out_ref[dst, 448:512] = out[1][src]
-            out_ref[dst, 512:960] = out[2][src]
-            out_ref[dst, 960:1024] = jnp.zeros((32, 64), BF)
+            theirs = pl.multiple_of((2 * y + 1 - zh_at) * 256, 256)
+            cols = ref[:, pl.ds(theirs, 256)]
+            value = value + lax.dot_general(g2[y], cols, NT, preferred_element_type=F32)
+        value = value.astype(BF)
+        for y in range(4):
+            dst = pl.ds(pl.multiple_of((2 * y + zh_at) * 32, 32), 32)
+            out_ref[dst, at : at + width] = value[y * 32 : (y + 1) * 32]
+    for y in range(4):
+        dst = pl.ds(pl.multiple_of((2 * y + 1 - zh_at) * 32, 32), 32)
+        src = slice(128 + y * 32, 128 + (y + 1) * 32)
+        out_ref[dst, :] = part_ref[src, :].astype(BF)
+        near = pl.ds(pl.multiple_of((2 * y + zh_at) * 32, 32), 32)
+        out_ref[near, 960:1024] = jnp.zeros((32, 64), BF)
 
 
 def numer_kernel(
@@ -271,19 +280,24 @@
     over_far, g1 = lax.optimization_barrier((over_far, g1))
     g2 = gather(over_far, "y")
 
-    (payload,) = call(
+    partial_sums, norm_rows = call(
         decode_kernel,
         "decode",
         2 * tokens * 8 * own * 512,
+        [((tokens // 2, 1024), F32), ((64, 8 * own), BF)],
+        3,
+        [pltpu.VMEM((tokens // 2, 8 * own), BF), pltpu.VMEM((64, 8 * own), F32)],
+        limit=40,
+    )(at, g1, dec_t, dec_oth)
+    (payload,) = call(
+        finish_kernel,
+        "finish",
+        tokens * 4 * own * 512,
         [((tokens // 2, 1024), BF)],
-        4,
-        [
-            pltpu.VMEM((tokens // 2, 8 * own), BF),
-            pltpu.VMEM((64, 8 * own), F32),
-            pltpu.VMEM((64, 8 * own), BF),
-        ],
+        5,
+        [],
         limit=40,
-    )(at, g1, g2, dec_t, dec_oth)
+    )(at, g2, dec_t, dec_oth, norm_rows, partial_sums)
     arrived = lax.all_to_all(payload.reshape(32, 8, 1024), LAT, 0, 0)
 
     cols = [

time: 179 us -> 181 us (1.011)
  blocking collectives: 9.2 us -> 0 us
  starting transfers between devices: 107 us -> 112 us
  Pallas kernels: 11.6 us -> 14.7 us
  local copies, waits for them, and re-layouts: 11 us -> 13 us
    all_to_all x1 -> x0, blocking collectives: 9.2 us -> none  [gather(): return lax.all_to_all(copies, axes, 0, 0, tiled=False)]
    all_to_all x3 -> x4, starting transfers between devices: 16.8 us -> 20.7 us  [gather(): return lax.all_to_all(copies, axes, 0, 0, tiled=False)]
    pallas_call x0 -> x1, Pallas kernels: none -> 3.13 us  [body(): call(finish_kernel, 'finish', tokens * 4 * own * 512, [((tokens // 2, 102...]
    unnamed x18 -> x20, local copies, waits for them, and re-layouts: 2.28 us -> 3.69 us
  transfers between devices with their start and end apart: 15 -> 16, of which waited for: 7 -> 8; matrix products, arithmetic and copies ran while one was open for 6% -> 6% of each run, Pallas kernels for 4% -> 6%
where the time goes in v11:
time: 181 us; the launch traced here: 180 us
  starting transfers between devices  112 us (62%)
  waiting for transfers between devices  33.9 us (19%)
  Pallas kernels  14.7 us (8%)
  local copies, waits for them, and re-layouts  13 us (7%)
  other arithmetic  3.28 us (2%)
  matrix products  2.69 us (1%)
    ppermute x10, starting transfers between devices, swap(): return lax.ppermute(value, axis, [(0, 1), (1, 0)])  65 us
    all_to_all x4, starting transfers between devices, gather(): return lax.all_to_all(copies, axes, 0, 0, tiled=False)  20.7 us
    all_to_all x1, waiting for transfers between devices, body(): arrived = lax.all_to_all(payload.reshape(32, 8, 1024), LAT, 0, 0)  17.2 us
    all_to_all x1, starting transfers between devices, body(): got = lax.all_to_all(last, ('pair',) + TOK, 0, 0, tiled=True)  13.8 us
    all_to_all x1, starting transfers between devices, body(): arrived = lax.all_to_all(payload.reshape(32, 8, 1024), LAT, 0, 0)  12.1 us
    all_to_all x1, waiting for transfers between devices, body(): got = lax.all_to_all(last, ('pair',) + TOK, 0, 0, tiled=True)  9.27 us
    ppermute x10, waiting for transfers between devices, swap(): return lax.ppermute(value, axis, [(0, 1), (1, 0)])  5.96 us
    broadcast_in_dim x4, local copies, waits for them, and re-layouts, gather(): copies = jnp.broadcast_to(value[None], (size,) + value.shape)  5.53 us
  transfers between devices with their start and end apart: 16, of which 8 were waited for; matrix products, arithmetic and copies ran while one was open for 6% of the time, Pallas kernels for 6%

profile of v11, /device:TPU:1, one launch (start us, length us, event | category | flops | bytes accessed | tf_op | source)
XLA Modules:
  0.0 180.2 jit_solution(18027931149907670802)
XLA Ops:
  0.6 2.4 %broadcast_in_dim.11 = bf16[4,64,3584]{2,1,0:T(8,128)(2,1)} broadcast(bf16[64,3584]{1,0:T(8,128)(2,1)} %bitcast.50), dimensions={1,2} | broadcast | bytes 2293760 | tf_op jit(solution)/shard_map/broadcast_in_dim | solution.py:28
  3.0 5.1 %all-to-all-start = ((bf16[4,64,3584]{2,1,0:T(8,128)(2,1)}), bf16[4,64,3584]{2,1,0:T(8,128)(2,1)}, u32[]{:S(2)}, u32[]{:S(2)}) async-start(bf16[4,64,3584]{2,1,0:T(8,128)(2,1)} %broadcast_in_dim.11), calls=%async_computation | async-start | bytes 3670016 | tf_op jit(solution)/shard_map/all_to_all | solution.py:29
  9.1 15.7 %collective-permute-start = (bf16[16,3584]{1,0:T(8,128)(2,1)S(1)}, bf16[16,3584]{1,0:T(8,128)(2,1)S(1)}, u32[]{:S(2)}, u32[]{:S(2)}) collective-permute-start(bf16[16,3584]{1,0:T(8,128)(2,1)S(1)} %dynamic-slice_bitcast_fusion.6), channel_id=1, source_target_pairs={{0,1},{1,0},{2,3},{3,2},{4,5},{5,4},{6,7},{7,6},{8,9},{9,8},{10,11... | collective-permute-start | bytes 344072 | tf_op jit(solution)/shard_map/ppermute | solution.py:23
  25.1 2.9 %collective-permute-start.1 = (f32[8,256]{1,0:T(8,128)S(1)}, f32[8,256]{1,0:T(8,128)S(1)}, u32[]{:S(2)}, u32[]{:S(2)}) collective-permute-start(f32[8,256]{1,0:T(8,128)S(1)} %reshape.125), channel_id=1, source_target_pairs={{0,256},{256,0},{1,257},{257,1},{2,258},{258,2},{3,259},{259,3},{4... | collective-permute-start | bytes 24584 | tf_op jit(solution)/shard_map/ppermute | solution.py:23
  28.9 1.4 broadcast_in_dim.12
  30.3 7.3 %all-to-all-start.1 = ((bf16[16,16,3584]{2,1,0:T(8,128)(2,1)}), bf16[16,16,3584]{2,1,0:T(8,128)(2,1)}, u32[]{:S(2)}, u32[]{:S(2)}) async-start(bf16[16,16,3584]{2,1,0:T(8,128)(2,1)} %broadcast_in_dim.12), calls=%async_computation.1 | async-start | bytes 3670016 | tf_op jit(solution)/shard_map/all_to_all | solution.py:29
  37.6 4.1 %encode.1 = (f32[128,256]{1,0:T(8,128)}, f32[128,256]{1,0:T(8,128)}) custom-call(s32[5]{0:T(128)} %stack.23.at_ref, bf16[256,3584]{1,0:T(8,128)(2,1)} %bitcast.8.act_hbm, bf16[3584,256]{1,0:T(8,128)(2,1)} %bitcast.47), custom_call_target="tpu_custom_call" | custom-call | flops 469762048 | bytes 6291456 | tf_op jit(solution)/shard_map/encode/pallas_call | solution.py:263
  41.7 3.9 %collective-permute-start.2 = (f32[128,256]{1,0:T(8,128)}, f32[128,256]{1,0:T(8,128)S(1)}, u32[]{:S(2)}, u32[]{:S(2)}) collective-permute-start(f32[128,256]{1,0:T(8,128)} %get-tuple-element.23), channel_id=1, source_target_pairs={{0,256},{256,0},{1,257},{257,1},{2,258},{258,2},{3,259},{259,3},{4... | collective-permute-start | bytes 393224 | tf_op jit(solution)/shard_map/ppermute | solution.py:23
  45.6 1.1 collective-permute-done.2
  47.7 15.8 %collective-permute-start.3 = (bf16[160,256]{1,0:T(8,128)(2,1)S(1)}, bf16[160,256]{1,0:T(8,128)(2,1)S(1)}, u32[]{:S(2)}, u32[]{:S(2)}) collective-permute-start(bf16[160,256]{1,0:T(8,128)(2,1)S(1)} %pad_maximum_fusion.2), channel_id=1, source_target_pairs={{0,1},{1,0},{2,3},{3,2},{4,5},{5,4},{6,7},{7,6},{8,9},{9,8},{10,11... | collective-permute-start | bytes 245768 | tf_op jit(solution)/shard_map/ppermute | solution.py:23
  63.5 2.6 %collective-permute-start.6 = (bf16[448,2048]{1,0:T(8,128)(2,1)S(1)}, bf16[448,2048]{1,0:T(8,128)(2,1)}, u32[]{:S(2)}, u32[]{:S(2)}) collective-permute-start(bf16[448,2048]{1,0:T(8,128)(2,1)S(1)} %bitcast.42), channel_id=1, source_target_pairs={{0,256},{256,0},{1,257},{257,1},{2,258},{258,2},{3,259},{259,3},{4... | collective-permute-start | bytes 5505032 | tf_op jit(solution)/shard_map/ppermute | solution.py:23
  66.1 2.7 %fusion = f32[16,2,8,256]{3,2,1,0:T(8,128)S(1)} fusion(bf16[1,3584,256]{2,1,0:T(8,128)(2,1)} %param.7, bf16[16,16,3584]{2,1,0:T(8,128)(2,1)} %all-to-all-done.1), kind=kOutput, calls=%fused_computation.1 | convolution fusion | flops 469762048 | bytes 3932160 | tf_op jit(solution)/shard_map/dot_general | solution.py:272
  68.8 1.9 %collective-permute-start.4 = (f32[128,256]{1,0:T(8,128)S(1)}, f32[128,256]{1,0:T(8,128)S(1)}, u32[]{:S(2)}, u32[]{:S(2)}) collective-permute-start(f32[128,256]{1,0:T(8,128)S(1)} %get-tuple-element.51), channel_id=1, source_target_pairs={{0,256},{256,0},{1,257},{257,1},{2,258},{258,2},{3,259},{259,3},{4... | collective-permute-start | bytes 393224 | tf_op jit(solution)/shard_map/ppermute | solution.py:23
  70.8 1.3 collective-permute-done.4
  73.2 4.4 %all-to-all-start.2 = ((bf16[4,448,256]{2,1,0:T(8,128)(2,1)}), bf16[4,448,256]{2,1,0:T(8,128)(2,1)S(1)}, u32[]{:S(2)}, u32[]{:S(2)}) async-start(bf16[4,448,256]{2,1,0:T(8,128)(2,1)} %broadcast_in_dim.13), calls=%async_computation.2 | async-start | bytes 1835008 | tf_op jit(solution)/shard_map/all_to_all | solution.py:29
  77.6 13.4 %collective-permute-start.5 = (bf16[128,256]{1,0:T(8,128)(2,1)S(1)}, bf16[128,256]{1,0:T(8,128)(2,1)S(1)}, u32[]{:S(2)}, u32[]{:S(2)}) collective-permute-start(bf16[128,256]{1,0:T(8,128)(2,1)S(1)} %get-tuple-element.40), channel_id=1, source_target_pairs={{0,1},{1,0},{2,3},{3,2},{4,5},{5,4},{6,7},{7,6},{8,9},{9,8},{10,11... | collective-permute-start | bytes 196616 | tf_op jit(solution)/shard_map/ppermute | solution.py:23
  91.0 2.2 %collective-permute-done.5 = bf16[128,256]{1,0:T(8,128)(2,1)S(1)} collective-permute-done((bf16[128,256]{1,0:T(8,128)(2,1)S(1)}, bf16[128,256]{1,0:T(8,128)(2,1)S(1)}, u32[]{:S(2)}, u32[]{:S(2)}) %collective-permute-start.5) | collective-permute-done | bytes 65568 | tf_op jit(solution)/shard_map/ppermute | solution.py:23
  93.9 3.9 %all-to-all-start.3 = ((bf16[4,128,256]{2,1,0:T(8,128)(2,1)}), bf16[4,128,256]{2,1,0:T(8,128)(2,1)S(1)}, u32[]{:S(2)}, u32[]{:S(2)}) async-start(bf16[4,128,256]{2,1,0:T(8,128)(2,1)} %broadcast_in_dim.14), calls=%async_computation.3 | async-start | bytes 524288 | tf_op jit(solution)/shard_map/all_to_all | solution.py:29
  97.8 3.1 %decode.1 = (f32[256,1024]{1,0:T(8,128)S(1)}, bf16[64,2048]{1,0:T(8,128)(2,1)S(1)}) custom-call(s32[5]{0:T(128)S(1)} %copy-done.5, bf16[4,448,256]{2,1,0:T(8,128)(2,1)S(1)} %all-to-all-done.2.g1, bf16[448,2048]{1,0:T(8,128)(2,1)S(1)} %bitcast.43, bf16[448,2048]{1,0:T(8,128)(2,1)} %collective-permute-done.6.oth_ref), custom_call_target="tpu_custom_call" | custom-call | flops 1073741824 | bytes 6291456 | tf_op jit(solution)/shard_map/decode/pallas_call | solution.py:283
  101.9 1.4 all-to-all-done.3.g2
  103.3 1.2 copy-done.2
  104.5 3.1 %finish.1 = bf16[256,1024]{1,0:T(8,128)(2,1)} custom-call(s32[5]{0:T(128)S(1)} %copy-done.5, bf16[4,128,256]{2,1,0:T(8,128)(2,1)S(1)} %all-to-all-done.3.g2, bf16[448,2048]{1,0:T(8,128)(2,1)S(1)} %bitcast.44, bf16[448,2048]{1,0:T(8,128)(2,1)} %collective-permute-done.6.oth_ref, bf16[64,2048]{1,0:T(8,128)(2,1)S(1)} %get-tuple-element.32.norm_ref, ...), custom_call_target="tpu_custom_call" | custom-call | flops 268435456 | bytes 6291456 | tf_op jit(solution)/shard_map/finish/pallas_call | solution.py:292
  107.6 12.1 %all-to-all-start.4 = ((bf16[32,8,1024]{2,1,0:T(8,128)(2,1)}), bf16[32,8,1024]{2,1,0:T(8,128)(2,1)S(1)}, u32[]{:S(2)}, u32[]{:S(2)}) async-start(bf16[32,8,1024]{2,1,0:T(8,128)(2,1)} %bitcast.17), calls=%async_computation.4 | async-start | bytes 1048576 | tf_op jit(solution)/shard_map/all_to_all | solution.py:301
  122.2 4.6 %collective-permute-start.7 = (bf16[272,448]{1,0:T(8,128)(2,1)S(1)}, bf16[272,448]{1,0:T(8,128)(2,1)S(1)}, u32[]{:S(2)}, u32[]{:S(2)}) collective-permute-start(bf16[272,448]{1,0:T(8,128)(2,1)S(1)} %pad_maximum_fusion), channel_id=1, source_target_pairs={{0,256},{256,0},{1,257},{257,1},{2,258},{258,2},{3,259},{259,3},{4... | collective-permute-start | bytes 731144 | tf_op jit(solution)/shard_map/ppermute | solution.py:23
  126.8 1.1 collective-permute-done.7.his_ref
  127.9 3.0 %numer.1 = (f32[32,512]{1,0:T(8,128)S(1)}, f32[2,256]{1,0:T(2,128)S(1)}) custom-call(s32[5]{0:T(128)S(1)} %copy-done.5, bf16[4,448,256]{2,1,0:T(8,128)(2,1)S(1)} %all-to-all-done.2.g1, bf16[4,128,256]{2,1,0:T(8,128)(2,1)S(1)} %all-to-all-done.3.g2, bf16[448,2048]{1,0:T(8,128)(2,1)S(1)} %bitcast.45, bf16[448,2048]{1,0:T(8,128)(2,1)} %collective-permute-done.6.oth_ref, ...), custom_call_target="tpu_custom_call" | custom-call | flops 939524096 | bytes 6291456 | tf_op jit(solution)/shard_map/numer/pallas_call | solution.py:314
  131.6 17.2 %all-to-all-done.4.arrived_ref = bf16[32,8,1024]{2,1,0:T(8,128)(2,1)S(1)} async-done(((bf16[32,8,1024]{2,1,0:T(8,128)(2,1)}), bf16[32,8,1024]{2,1,0:T(8,128)(2,1)S(1)}, u32[]{:S(2)}, u32[]{:S(2)}) %all-to-all-start.4) | async-done | bytes 524320 | tf_op jit(solution)/shard_map/all_to_all | solution.py:301
  149.6 1.4 close.1
  151.0 13.8 %all-to-all-start.5 = ((f32[16,4,128]{2,1,0:T(4,128)}), f32[16,4,128]{2,1,0:T(4,128)S(1)}, u32[]{:S(2)}, u32[]{:S(2)}) async-start(f32[16,4,128]{2,1,0:T(4,128)} %get-tuple-element.37), calls=%async_computation.5 | async-start | bytes 65536 | tf_op jit(solution)/shard_map/all_to_all | solution.py:335
  164.8 2.0 %collective-permute-start.8 = (bf16[8,448]{1,0:T(8,128)(2,1)S(1)}, bf16[8,448]{1,0:T(8,128)(2,1)S(1)}, u32[]{:S(2)}, u32[]{:S(2)}) collective-permute-start(bf16[8,448]{1,0:T(8,128)(2,1)S(1)} %get-tuple-element.36), channel_id=1, source_target_pairs={{0,256},{256,0},{1,257},{257,1},{2,258},{258,2},{3,259},{259,3},{4... | collective-permute-start | bytes 21512 | tf_op jit(solution)/shard_map/ppermute | solution.py:23
  166.9 2.3 %collective-permute-start.9 = (f32[1,256]{1,0:T(1,128)S(1)}, f32[1,256]{1,0:T(1,128)S(1)}, u32[]{:S(2)}, u32[]{:S(2)}) collective-permute-start(f32[1,256]{1,0:T(1,128)S(1)} %slice.24), channel_id=1, source_target_pairs={{0,256},{256,0},{1,257},{257,1},{2,258},{258,2},{3,259},{259,3},{4... | collective-permute-start | bytes 3080 | tf_op jit(solution)/shard_map/ppermute | solution.py:23
  169.8 9.3 %all-to-all-done.5 = f32[16,4,128]{2,1,0:T(4,128)S(1)} async-done(((f32[16,4,128]{2,1,0:T(4,128)}), f32[16,4,128]{2,1,0:T(4,128)S(1)}, u32[]{:S(2)}, u32[]{:S(2)}) %all-to-all-start.5) | async-done | bytes 32800 | tf_op jit(solution)/shard_map/all_to_all | solution.py:335
  (55 shorter events, 11.5 us)
Async XLA Ops:
  3.0 21.7 %copy-start = (bf16[1,2048,448]{1,2,0:T(8,128)(2,1)S(1)}, bf16[1,2048,448]{1,2,0:T(8,128)(2,1)}, u32[]{:S(2)}) copy-start(bf16[1,2048,448]{1,2,0:T(8,128)(2,1)} %param.10) | copy-start | bytes 5505028
  3.0 25.9 %all-to-all-start = ((bf16[4,64,3584]{2,1,0:T(8,128)(2,1)}), bf16[4,64,3584]{2,1,0:T(8,128)(2,1)}, u32[]{:S(2)}, u32[]{:S(2)}) async-start(bf16[4,64,3584]{2,1,0:T(8,128)(2,1)} %broadcast_in_dim.11), calls=%async_computation | async-start | bytes 3670016 | tf_op jit(solution)/shard_map/all_to_all | solution.py:29
  9.1 19.8 %collective-permute-start = (bf16[16,3584]{1,0:T(8,128)(2,1)S(1)}, bf16[16,3584]{1,0:T(8,128)(2,1)S(1)}, u32[]{:S(2)}, u32[]{:S(2)}) collective-permute-start(bf16[16,3584]{1,0:T(8,128)(2,1)S(1)} %dynamic-slice_bitcast_fusion.6), channel_id=1, source_target_pairs={{0,1},{1,0},{2,3},{3,2},{4,5},{5,4},{6,7},{7,6},{8,9},{9,8},{10,11... | collective-permute-start | bytes 344072 | tf_op jit(solution)/shard_map/ppermute | solution.py:23
  25.1 3.7 %collective-permute-start.1 = (f32[8,256]{1,0:T(8,128)S(1)}, f32[8,256]{1,0:T(8,128)S(1)}, u32[]{:S(2)}, u32[]{:S(2)}) collective-permute-start(f32[8,256]{1,0:T(8,128)S(1)} %reshape.125), channel_id=1, source_target_pairs={{0,256},{256,0},{1,257},{257,1},{2,258},{258,2},{3,259},{259,3},{4... | collective-permute-start | bytes 24584 | tf_op jit(solution)/shard_map/ppermute | solution.py:23
  30.3 7.3 %copy-start.8 = (s32[256]{0:T(256)S(1)}, s32[256]{0:T(256)}, u32[]{:S(2)}) copy-start(s32[256]{0:T(256)} %param.9) | copy-start | bytes 3076
  30.3 35.8 %all-to-all-start.1 = ((bf16[16,16,3584]{2,1,0:T(8,128)(2,1)}), bf16[16,16,3584]{2,1,0:T(8,128)(2,1)}, u32[]{:S(2)}, u32[]{:S(2)}) async-start(bf16[16,16,3584]{2,1,0:T(8,128)(2,1)} %broadcast_in_dim.12), calls=%async_computation.1 | async-start | bytes 3670016 | tf_op jit(solution)/shard_map/all_to_all | solution.py:29
  37.6 9.1 %copy-start.7 = (f32[256]{0:T(256)S(1)}, f32[256]{0:T(256)}, u32[]{:S(2)}) copy-start(f32[256]{0:T(256)} %param.8) | copy-start | bytes 3076
  41.7 5.0 %collective-permute-start.2 = (f32[128,256]{1,0:T(8,128)}, f32[128,256]{1,0:T(8,128)S(1)}, u32[]{:S(2)}, u32[]{:S(2)}) collective-permute-start(f32[128,256]{1,0:T(8,128)} %get-tuple-element.23), channel_id=1, source_target_pairs={{0,256},{256,0},{1,257},{257,1},{2,258},{258,2},{3,259},{259,3},{4... | collective-permute-start | bytes 393224 | tf_op jit(solution)/shard_map/ppermute | solution.py:23
  47.7 23.1 %collective-permute-start.3 = (bf16[160,256]{1,0:T(8,128)(2,1)S(1)}, bf16[160,256]{1,0:T(8,128)(2,1)S(1)}, u32[]{:S(2)}, u32[]{:S(2)}) collective-permute-start(bf16[160,256]{1,0:T(8,128)(2,1)S(1)} %pad_maximum_fusion.2), channel_id=1, source_target_pairs={{0,1},{1,0},{2,3},{3,2},{4,5},{5,4},{6,7},{7,6},{8,9},{9,8},{10,11... | collective-permute-start | bytes 245768 | tf_op jit(solution)/shard_map/ppermute | solution.py:23
  63.5 34.2 %collective-permute-start.6 = (bf16[448,2048]{1,0:T(8,128)(2,1)S(1)}, bf16[448,2048]{1,0:T(8,128)(2,1)}, u32[]{:S(2)}, u32[]{:S(2)}) collective-permute-start(bf16[448,2048]{1,0:T(8,128)(2,1)S(1)} %bitcast.42), channel_id=1, source_target_pairs={{0,256},{256,0},{1,257},{257,1},{2,258},{258,2},{3,259},{259,3},{4... | collective-permute-start | bytes 5505032 | tf_op jit(solution)/shard_map/ppermute | solution.py:23
  68.8 3.2 %collective-permute-start.4 = (f32[128,256]{1,0:T(8,128)S(1)}, f32[128,256]{1,0:T(8,128)S(1)}, u32[]{:S(2)}, u32[]{:S(2)}) collective-permute-start(f32[128,256]{1,0:T(8,128)S(1)} %get-tuple-element.51), channel_id=1, source_target_pairs={{0,256},{256,0},{1,257},{257,1},{2,258},{258,2},{3,259},{259,3},{4... | collective-permute-start | bytes 393224 | tf_op jit(solution)/shard_map/ppermute | solution.py:23
  72.2 25.6 %copy-start.5 = (s32[5]{0:T(128)S(1)}, s32[5]{0:T(128)}, u32[]{:S(2)}) copy-start(s32[5]{0:T(128)} %stack.23.at_ref) | copy-start | bytes 64
  73.2 20.0 %all-to-all-start.2 = ((bf16[4,448,256]{2,1,0:T(8,128)(2,1)}), bf16[4,448,256]{2,1,0:T(8,128)(2,1)S(1)}, u32[]{:S(2)}, u32[]{:S(2)}) async-start(bf16[4,448,256]{2,1,0:T(8,128)(2,1)} %broadcast_in_dim.13), calls=%async_computation.2 | async-start | bytes 1835008 | tf_op jit(solution)/shard_map/all_to_all | solution.py:29
  77.6 15.6 %collective-permute-start.5 = (bf16[128,256]{1,0:T(8,128)(2,1)S(1)}, bf16[128,256]{1,0:T(8,128)(2,1)S(1)}, u32[]{:S(2)}, u32[]{:S(2)}) collective-permute-start(bf16[128,256]{1,0:T(8,128)(2,1)S(1)} %get-tuple-element.40), channel_id=1, source_target_pairs={{0,1},{1,0},{2,3},{3,2},{4,5},{5,4},{6,7},{7,6},{8,9},{9,8},{10,11... | collective-permute-start | bytes 196616 | tf_op jit(solution)/shard_map/ppermute | solution.py:23
  93.9 9.4 %all-to-all-start.3 = ((bf16[4,128,256]{2,1,0:T(8,128)(2,1)}), bf16[4,128,256]{2,1,0:T(8,128)(2,1)S(1)}, u32[]{:S(2)}, u32[]{:S(2)}) async-start(bf16[4,128,256]{2,1,0:T(8,128)(2,1)} %broadcast_in_dim.14), calls=%async_computation.3 | async-start | bytes 524288 | tf_op jit(solution)/shard_map/all_to_all | solution.py:29
  100.9 1.0 copy-start.1
  103.3 1.2 copy-start.2
  104.5 15.3 %copy-start.6 = (f32[1,448]{1,0:T(1,128)S(1)}, f32[1,448]{1,0:T(1,128)}, u32[]{:S(2)}) copy-start(f32[1,448]{1,0:T(1,128)} %bias_ref.1) | copy-start | bytes 5380
  107.6 41.2 %all-to-all-start.4 = ((bf16[32,8,1024]{2,1,0:T(8,128)(2,1)}), bf16[32,8,1024]{2,1,0:T(8,128)(2,1)S(1)}, u32[]{:S(2)}, u32[]{:S(2)}) async-start(bf16[32,8,1024]{2,1,0:T(8,128)(2,1)} %bitcast.17), calls=%async_computation.4 | async-start | bytes 1048576 | tf_op jit(solution)/shard_map/all_to_all | solution.py:301
  122.2 5.7 %collective-permute-start.7 = (bf16[272,448]{1,0:T(8,128)(2,1)S(1)}, bf16[272,448]{1,0:T(8,128)(2,1)S(1)}, u32[]{:S(2)}, u32[]{:S(2)}) collective-permute-start(bf16[272,448]{1,0:T(8,128)(2,1)S(1)} %pad_maximum_fusion), channel_id=1, source_target_pairs={{0,256},{256,0},{1,257},{257,1},{2,258},{258,2},{3,259},{259,3},{4... | collective-permute-start | bytes 731144 | tf_op jit(solution)/shard_map/ppermute | solution.py:23
  130.9 0.6 copy-start.3
  148.8 0.8 copy-start.4
  151.0 28.0 %all-to-all-start.5 = ((f32[16,4,128]{2,1,0:T(4,128)}), f32[16,4,128]{2,1,0:T(4,128)S(1)}, u32[]{:S(2)}, u32[]{:S(2)}) async-start(f32[16,4,128]{2,1,0:T(4,128)} %get-tuple-element.37), calls=%async_computation.5 | async-start | bytes 65536 | tf_op jit(solution)/shard_map/all_to_all | solution.py:335
  164.8 4.3 %collective-permute-start.8 = (bf16[8,448]{1,0:T(8,128)(2,1)S(1)}, bf16[8,448]{1,0:T(8,128)(2,1)S(1)}, u32[]{:S(2)}, u32[]{:S(2)}) collective-permute-start(bf16[8,448]{1,0:T(8,128)(2,1)S(1)} %get-tuple-element.36), channel_id=1, source_target_pairs={{0,256},{256,0},{1,257},{257,1},{2,258},{258,2},{3,259},{259,3},{4... | collective-permute-start | bytes 21512 | tf_op jit(solution)/shard_map/ppermute | solution.py:23
  166.9 12.8 %collective-permute-start.9 = (f32[1,256]{1,0:T(1,128)S(1)}, f32[1,256]{1,0:T(1,128)S(1)}, u32[]{:S(2)}, u32[]{:S(2)}) collective-permute-start(f32[1,256]{1,0:T(1,128)S(1)} %slice.24), channel_id=1, source_target_pairs={{0,256},{256,0},{1,257},{257,1},{2,258},{258,2},{3,259},{259,3},{4... | collective-permute-start | bytes 3080 | tf_op jit(solution)/shard_map/ppermute | solution.py:23

commit v12 on v10

--- a/solution.py
+++ b/solution.py
@@ -27,6 +27,17 @@
     size = lax.axis_size(axes)
     copies = jnp.broadcast_to(value[None], (size,) + value.shape)
     return lax.all_to_all(copies, axes, 0, 0, tiled=False)
+
+
+def copies_kernel(value_ref, out_hbm, sems):
+    copies = [
+        pltpu.make_async_copy(value_ref, out_hbm.at[k], sems.at[k])
+        for k in range(out_hbm.shape[0])
+    ]
+    for copy in copies:
+        copy.start()
+    for copy in copies:
+        copy.wait()
 
 
 def encode_kernel(at_ref, act_hbm, enc_hbm, keep_ref, send_ref, a_ref, enc_ref, v_ref, sems):
@@ -216,7 +227,19 @@
     nsq_two = [nsq_part, swap(nsq_part, "pair")]
     quarter, nsq_two[0], nsq_two[1], at = lax.optimization_barrier((quarter, *nsq_two, at))
 
-    near = gather(act, "y").reshape(256, D)
+    (copies,) = pl.pallas_call(
+        copies_kernel,
+        out_shape=(jax.ShapeDtypeStruct((4,) + act.shape, BF),),
+        in_specs=[VMEM],
+        out_specs=(HBM,),
+        scratch_shapes=[pltpu.SemaphoreType.DMA((4,))],
+        compiler_params=pltpu.CompilerParams(vmem_limit_bytes=60 << 20),
+        cost_estimate=pl.CostEstimate(
+            flops=0, bytes_accessed=2 << 20, transcendentals=0
+        ),
+        name="copies",
+    )(act)
+    near = lax.all_to_all(copies, "y", 0, 0, tiled=False).reshape(256, D)
     far = gather(quarter, ("y", "x")).reshape(256, D)
 
     def split(value):

time: 179 us -> 179 us (level)
  local copies, waits for them, and re-layouts: 11 us -> 8.63 us
  Pallas kernels: 11.6 us -> 13.9 us
    all_to_all x0 -> x1, starting transfers between devices: none -> 5.16 us  [body(): near = lax.all_to_all(copies, 'y', 0, 0, tiled=False).reshape(256, D)]
    all_to_all x3 -> x2, starting transfers between devices: 16.8 us -> 11.7 us  [gather(): return lax.all_to_all(copies, axes, 0, 0, tiled=False)]
    broadcast_in_dim x4 -> x3, local copies, waits for them, and re-layouts: 4.85 us -> 2.48 us  [gather(): copies = jnp.broadcast_to(value[None], (size,) + value.shape)]
    pallas_call x0 -> x1, Pallas kernels: none -> 2.27 us  [body(): pl.pallas_call(copies_kernel, out_shape=(jax.ShapeDtypeStruct((4,) + act....]
where the time goes in v12:
time: 179 us; the launch traced here: 178 us
  starting transfers between devices  107 us (60%)
  waiting for transfers between devices  32.4 us (18%)
  Pallas kernels  13.9 us (8%)
  blocking collectives  9.2 us (5%)
  local copies, waits for them, and re-layouts  8.63 us (5%)
  other arithmetic  3.28 us (2%)
  matrix products  2.69 us (2%)
    ppermute x10, starting transfers between devices, swap(): return lax.ppermute(value, axis, [(0, 1), (1, 0)])  65.1 us
    all_to_all x1, waiting for transfers between devices, body(): arrived = lax.all_to_all(payload.reshape(32, 8, 1024), LAT, 0, 0)  17.2 us
    all_to_all x1, starting transfers between devices, body(): got = lax.all_to_all(last, ('pair',) + TOK, 0, 0, tiled=True)  13.2 us
    all_to_all x1, starting transfers between devices, body(): arrived = lax.all_to_all(payload.reshape(32, 8, 1024), LAT, 0, 0)  12 us
    all_to_all x2, starting transfers between devices, gather(): return lax.all_to_all(copies, axes, 0, 0, tiled=False)  11.7 us
    all_to_all x1, waiting for transfers between devices, body(): got = lax.all_to_all(last, ('pair',) + TOK, 0, 0, tiled=True)  9.27 us
    all_to_all x1, blocking collectives, gather(): return lax.all_to_all(copies, axes, 0, 0, tiled=False)  9.2 us
    ppermute x10, waiting for transfers between devices, swap(): return lax.ppermute(value, axis, [(0, 1), (1, 0)])  5.9 us
  transfers between devices with their start and end apart: 15, of which 7 were waited for; matrix products, arithmetic and copies ran while one was open for 6% of the time, Pallas kernels for 4%

profile of v12, /device:TPU:1, one launch (start us, length us, event | category | flops | bytes accessed | tf_op | source)
XLA Modules:
  0.0 178.3 jit_solution(15543567061415793144)
XLA Ops:
  0.6 2.3 %copies.1 = bf16[4,64,3584]{2,1,0:T(8,128)(2,1)} custom-call(bf16[64,3584]{1,0:T(8,128)(2,1)} %bitcast.50), custom_call_target="tpu_custom_call" | custom-call | bytes 2097152 | tf_op jit(solution)/shard_map/copies/pallas_call | solution.py:230
  2.9 5.2 %all-to-all-start = ((bf16[4,64,3584]{2,1,0:T(8,128)(2,1)}), bf16[4,64,3584]{2,1,0:T(8,128)(2,1)}, u32[]{:S(2)}, u32[]{:S(2)}) async-start(bf16[4,64,3584]{2,1,0:T(8,128)(2,1)} %copies.1), calls=%async_computation | async-start | bytes 3670016 | tf_op jit(solution)/shard_map/all_to_all | solution.py:242
  9.0 15.7 %collective-permute-start = (bf16[16,3584]{1,0:T(8,128)(2,1)S(1)}, bf16[16,3584]{1,0:T(8,128)(2,1)S(1)}, u32[]{:S(2)}, u32[]{:S(2)}) collective-permute-start(bf16[16,3584]{1,0:T(8,128)(2,1)S(1)} %dynamic-slice_bitcast_fusion.6), channel_id=1, source_target_pairs={{0,1},{1,0},{2,3},{3,2},{4,5},{5,4},{6,7},{7,6},{8,9},{9,8},{10,11... | collective-permute-start | bytes 344072 | tf_op jit(solution)/shard_map/ppermute | solution.py:23
  25.1 2.9 %collective-permute-start.1 = (f32[8,256]{1,0:T(8,128)S(1)}, f32[8,256]{1,0:T(8,128)S(1)}, u32[]{:S(2)}, u32[]{:S(2)}) collective-permute-start(f32[8,256]{1,0:T(8,128)S(1)} %reshape.125), channel_id=1, source_target_pairs={{0,256},{256,0},{1,257},{257,1},{2,258},{258,2},{3,259},{259,3},{4... | collective-permute-start | bytes 24584 | tf_op jit(solution)/shard_map/ppermute | solution.py:23
  28.8 1.4 broadcast_in_dim.6
  30.2 7.3 %all-to-all-start.1 = ((bf16[16,16,3584]{2,1,0:T(8,128)(2,1)}), bf16[16,16,3584]{2,1,0:T(8,128)(2,1)}, u32[]{:S(2)}, u32[]{:S(2)}) async-start(bf16[16,16,3584]{2,1,0:T(8,128)(2,1)} %broadcast_in_dim.6), calls=%async_computation.1 | async-start | bytes 3670016 | tf_op jit(solution)/shard_map/all_to_all | solution.py:29
  37.6 4.1 %encode.1 = (f32[128,256]{1,0:T(8,128)}, f32[128,256]{1,0:T(8,128)}) custom-call(s32[5]{0:T(128)} %stack.23.at_ref, bf16[256,3584]{1,0:T(8,128)(2,1)} %bitcast.8.act_hbm, bf16[3584,256]{1,0:T(8,128)(2,1)} %bitcast.47), custom_call_target="tpu_custom_call" | custom-call | flops 469762048 | bytes 6291456 | tf_op jit(solution)/shard_map/encode/pallas_call | solution.py:277
  41.7 3.8 %collective-permute-start.2 = (f32[128,256]{1,0:T(8,128)}, f32[128,256]{1,0:T(8,128)S(1)}, u32[]{:S(2)}, u32[]{:S(2)}) collective-permute-start(f32[128,256]{1,0:T(8,128)} %get-tuple-element.21), channel_id=1, source_target_pairs={{0,256},{256,0},{1,257},{257,1},{2,258},{258,2},{3,259},{259,3},{4... | collective-permute-start | bytes 393224 | tf_op jit(solution)/shard_map/ppermute | solution.py:23
  45.5 1.1 collective-permute-done.2
  47.6 15.8 %collective-permute-start.3 = (bf16[160,256]{1,0:T(8,128)(2,1)S(1)}, bf16[160,256]{1,0:T(8,128)(2,1)S(1)}, u32[]{:S(2)}, u32[]{:S(2)}) collective-permute-start(bf16[160,256]{1,0:T(8,128)(2,1)S(1)} %pad_maximum_fusion.2), channel_id=1, source_target_pairs={{0,1},{1,0},{2,3},{3,2},{4,5},{5,4},{6,7},{7,6},{8,9},{9,8},{10,11... | collective-permute-start | bytes 245768 | tf_op jit(solution)/shard_map/ppermute | solution.py:23
  63.5 2.6 %collective-permute-start.6 = (bf16[448,2048]{1,0:T(8,128)(2,1)S(1)}, bf16[448,2048]{1,0:T(8,128)(2,1)}, u32[]{:S(2)}, u32[]{:S(2)}) collective-permute-start(bf16[448,2048]{1,0:T(8,128)(2,1)S(1)} %bitcast.42), channel_id=1, source_target_pairs={{0,256},{256,0},{1,257},{257,1},{2,258},{258,2},{3,259},{259,3},{4... | collective-permute-start | bytes 5505032 | tf_op jit(solution)/shard_map/ppermute | solution.py:23
  66.0 2.7 %fusion = f32[16,2,8,256]{3,2,1,0:T(8,128)S(1)} fusion(bf16[1,3584,256]{2,1,0:T(8,128)(2,1)} %param.7, bf16[16,16,3584]{2,1,0:T(8,128)(2,1)} %all-to-all-done.1), kind=kOutput, calls=%fused_computation.1 | convolution fusion | flops 469762048 | bytes 3932160 | tf_op jit(solution)/shard_map/dot_general | solution.py:286
  68.8 1.9 %collective-permute-start.4 = (f32[128,256]{1,0:T(8,128)S(1)}, f32[128,256]{1,0:T(8,128)S(1)}, u32[]{:S(2)}, u32[]{:S(2)}) collective-permute-start(f32[128,256]{1,0:T(8,128)S(1)} %get-tuple-element.47), channel_id=1, source_target_pairs={{0,256},{256,0},{1,257},{257,1},{2,258},{258,2},{3,259},{259,3},{4... | collective-permute-start | bytes 393224 | tf_op jit(solution)/shard_map/ppermute | solution.py:23
  70.7 1.3 collective-permute-done.4
  72.1 1.0 broadcast_in_dim.7
  73.1 4.4 %all-to-all-start.2 = ((bf16[4,448,256]{2,1,0:T(8,128)(2,1)}), bf16[4,448,256]{2,1,0:T(8,128)(2,1)S(1)}, u32[]{:S(2)}, u32[]{:S(2)}) async-start(bf16[4,448,256]{2,1,0:T(8,128)(2,1)} %broadcast_in_dim.7), calls=%async_computation.2 | async-start | bytes 1835008 | tf_op jit(solution)/shard_map/all_to_all | solution.py:29
  77.5 13.5 %collective-permute-start.5 = (bf16[128,256]{1,0:T(8,128)(2,1)S(1)}, bf16[128,256]{1,0:T(8,128)(2,1)S(1)}, u32[]{:S(2)}, u32[]{:S(2)}) collective-permute-start(bf16[128,256]{1,0:T(8,128)(2,1)S(1)} %get-tuple-element.36), channel_id=1, source_target_pairs={{0,1},{1,0},{2,3},{3,2},{4,5},{5,4},{6,7},{7,6},{8,9},{9,8},{10,11... | collective-permute-start | bytes 196616 | tf_op jit(solution)/shard_map/ppermute | solution.py:23
  91.0 2.2 %collective-permute-done.5 = bf16[128,256]{1,0:T(8,128)(2,1)S(1)} collective-permute-done((bf16[128,256]{1,0:T(8,128)(2,1)S(1)}, bf16[128,256]{1,0:T(8,128)(2,1)S(1)}, u32[]{:S(2)}, u32[]{:S(2)}) %collective-permute-start.5) | collective-permute-done | bytes 65568 | tf_op jit(solution)/shard_map/ppermute | solution.py:23
  93.2 9.2 %all_to_all.30.g2 = bf16[4,128,256]{2,1,0:T(8,128)(2,1)S(1)} all-to-all(bf16[4,128,256]{2,1,0:T(8,128)(2,1)S(1)} %broadcast_in_dim.8), channel_id=1, replica_groups=mesh['pair'=2,'x'=4,'zl'=8,'y'=4,'zh'=2] {'y'}, dimensions={0} | all-to-all | bytes 524288 | tf_op jit(solution)/shard_map/all_to_all | solution.py:29
  102.4 3.1 %decode.1 = bf16[256,1024]{1,0:T(8,128)(2,1)S(1)} custom-call(s32[5]{0:T(128)S(1)} %copy-done.4, bf16[4,448,256]{2,1,0:T(8,128)(2,1)S(1)} %all-to-all-done.2.g1, bf16[4,128,256]{2,1,0:T(8,128)(2,1)S(1)} %all_to_all.30.g2, bf16[448,2048]{1,0:T(8,128)(2,1)S(1)} %bitcast.43, bf16[448,2048]{1,0:T(8,128)(2,1)} %collective-permute-done.6.oth_ref), custom_call_target="tpu_custom_call" | custom-call | flops 1073741824 | bytes 6291456 | tf_op jit(solution)/shard_map/decode/pallas_call | solution.py:297
  106.4 12.0 %all-to-all-start.4 = ((bf16[32,8,1024]{2,1,0:T(8,128)(2,1)}), bf16[32,8,1024]{2,1,0:T(8,128)(2,1)S(1)}, u32[]{:S(2)}, u32[]{:S(2)}) async-start(bf16[32,8,1024]{2,1,0:T(8,128)(2,1)} %bitcast.45), calls=%async_computation.4 | async-start | bytes 1048576 | tf_op jit(solution)/shard_map/all_to_all | solution.py:310
  118.5 1.1 constant_dynamic-slice_fusion.1
  119.6 1.1 constant_dynamic-slice_fusion
  120.8 4.6 %collective-permute-start.7 = (bf16[272,448]{1,0:T(8,128)(2,1)S(1)}, bf16[272,448]{1,0:T(8,128)(2,1)S(1)}, u32[]{:S(2)}, u32[]{:S(2)}) collective-permute-start(bf16[272,448]{1,0:T(8,128)(2,1)S(1)} %pad_maximum_fusion), channel_id=1, source_target_pairs={{0,256},{256,0},{1,257},{257,1},{2,258},{258,2},{3,259},{259,3},{4... | collective-permute-start | bytes 731144 | tf_op jit(solution)/shard_map/ppermute | solution.py:23
  125.4 1.1 collective-permute-done.7.his_ref
  126.6 3.0 %numer.1 = (f32[32,512]{1,0:T(8,128)S(1)}, f32[2,256]{1,0:T(2,128)S(1)}) custom-call(s32[5]{0:T(128)S(1)} %copy-done.4, bf16[4,448,256]{2,1,0:T(8,128)(2,1)S(1)} %all-to-all-done.2.g1, bf16[4,128,256]{2,1,0:T(8,128)(2,1)S(1)} %all_to_all.30.g2, bf16[448,2048]{1,0:T(8,128)(2,1)S(1)} %bitcast.44, bf16[448,2048]{1,0:T(8,128)(2,1)} %collective-permute-done.6.oth_ref, ...), custom_call_target="tpu_custom_call" | custom-call | flops 939524096 | bytes 6291456 | tf_op jit(solution)/shard_map/numer/pallas_call | solution.py:323
  130.2 17.2 %all-to-all-done.4.arrived_ref = bf16[32,8,1024]{2,1,0:T(8,128)(2,1)S(1)} async-done(((bf16[32,8,1024]{2,1,0:T(8,128)(2,1)}), bf16[32,8,1024]{2,1,0:T(8,128)(2,1)S(1)}, u32[]{:S(2)}, u32[]{:S(2)}) %all-to-all-start.4) | async-done | bytes 524320 | tf_op jit(solution)/shard_map/all_to_all | solution.py:310
  148.3 1.4 close.1
  149.7 13.2 %all-to-all-start.5 = ((f32[16,4,128]{2,1,0:T(4,128)}), f32[16,4,128]{2,1,0:T(4,128)S(1)}, u32[]{:S(2)}, u32[]{:S(2)}) async-start(f32[16,4,128]{2,1,0:T(4,128)} %get-tuple-element.33), calls=%async_computation.5 | async-start | bytes 65536 | tf_op jit(solution)/shard_map/all_to_all | solution.py:344
  162.9 2.0 %collective-permute-start.8 = (bf16[8,448]{1,0:T(8,128)(2,1)S(1)}, bf16[8,448]{1,0:T(8,128)(2,1)S(1)}, u32[]{:S(2)}, u32[]{:S(2)}) collective-permute-start(bf16[8,448]{1,0:T(8,128)(2,1)S(1)} %get-tuple-element.32), channel_id=1, source_target_pairs={{0,256},{256,0},{1,257},{257,1},{2,258},{258,2},{3,259},{259,3},{4... | collective-permute-start | bytes 21512 | tf_op jit(solution)/shard_map/ppermute | solution.py:23
  164.9 2.3 %collective-permute-start.9 = (f32[1,256]{1,0:T(1,128)S(1)}, f32[1,256]{1,0:T(1,128)S(1)}, u32[]{:S(2)}, u32[]{:S(2)}) collective-permute-start(f32[1,256]{1,0:T(1,128)S(1)} %slice.24), channel_id=1, source_target_pairs={{0,256},{256,0},{1,257},{257,1},{2,258},{258,2},{3,259},{259,3},{4... | collective-permute-start | bytes 3080 | tf_op jit(solution)/shard_map/ppermute | solution.py:23
  167.8 9.3 %all-to-all-done.5 = f32[16,4,128]{2,1,0:T(4,128)S(1)} async-done(((f32[16,4,128]{2,1,0:T(4,128)}), f32[16,4,128]{2,1,0:T(4,128)S(1)}, u32[]{:S(2)}, u32[]{:S(2)}) %all-to-all-start.5) | async-done | bytes 32800 | tf_op jit(solution)/shard_map/all_to_all | solution.py:344
  (51 shorter events, 7.4 us)
Async XLA Ops:
  2.9 21.8 %copy-start = (bf16[1,2048,448]{1,2,0:T(8,128)(2,1)S(1)}, bf16[1,2048,448]{1,2,0:T(8,128)(2,1)}, u32[]{:S(2)}) copy-start(bf16[1,2048,448]{1,2,0:T(8,128)(2,1)} %param.10) | copy-start | bytes 5505028
  2.9 25.9 %all-to-all-start = ((bf16[4,64,3584]{2,1,0:T(8,128)(2,1)}), bf16[4,64,3584]{2,1,0:T(8,128)(2,1)}, u32[]{:S(2)}, u32[]{:S(2)}) async-start(bf16[4,64,3584]{2,1,0:T(8,128)(2,1)} %copies.1), calls=%async_computation | async-start | bytes 3670016 | tf_op jit(solution)/shard_map/all_to_all | solution.py:242
  9.0 19.8 %collective-permute-start = (bf16[16,3584]{1,0:T(8,128)(2,1)S(1)}, bf16[16,3584]{1,0:T(8,128)(2,1)S(1)}, u32[]{:S(2)}, u32[]{:S(2)}) collective-permute-start(bf16[16,3584]{1,0:T(8,128)(2,1)S(1)} %dynamic-slice_bitcast_fusion.6), channel_id=1, source_target_pairs={{0,1},{1,0},{2,3},{3,2},{4,5},{5,4},{6,7},{7,6},{8,9},{9,8},{10,11... | collective-permute-start | bytes 344072 | tf_op jit(solution)/shard_map/ppermute | solution.py:23
  25.1 3.7 %collective-permute-start.1 = (f32[8,256]{1,0:T(8,128)S(1)}, f32[8,256]{1,0:T(8,128)S(1)}, u32[]{:S(2)}, u32[]{:S(2)}) collective-permute-start(f32[8,256]{1,0:T(8,128)S(1)} %reshape.125), channel_id=1, source_target_pairs={{0,256},{256,0},{1,257},{257,1},{2,258},{258,2},{3,259},{259,3},{4... | collective-permute-start | bytes 24584 | tf_op jit(solution)/shard_map/ppermute | solution.py:23
  30.2 7.3 %copy-start.7 = (s32[256]{0:T(256)S(1)}, s32[256]{0:T(256)}, u32[]{:S(2)}) copy-start(s32[256]{0:T(256)} %param.9) | copy-start | bytes 3076
  30.2 35.8 %all-to-all-start.1 = ((bf16[16,16,3584]{2,1,0:T(8,128)(2,1)}), bf16[16,16,3584]{2,1,0:T(8,128)(2,1)}, u32[]{:S(2)}, u32[]{:S(2)}) async-start(bf16[16,16,3584]{2,1,0:T(8,128)(2,1)} %broadcast_in_dim.6), calls=%async_computation.1 | async-start | bytes 3670016 | tf_op jit(solution)/shard_map/all_to_all | solution.py:29
  37.6 9.1 %copy-start.6 = (f32[256]{0:T(256)S(1)}, f32[256]{0:T(256)}, u32[]{:S(2)}) copy-start(f32[256]{0:T(256)} %param.8) | copy-start | bytes 3076
  41.7 5.0 %collective-permute-start.2 = (f32[128,256]{1,0:T(8,128)}, f32[128,256]{1,0:T(8,128)S(1)}, u32[]{:S(2)}, u32[]{:S(2)}) collective-permute-start(f32[128,256]{1,0:T(8,128)} %get-tuple-element.21), channel_id=1, source_target_pairs={{0,256},{256,0},{1,257},{257,1},{2,258},{258,2},{3,259},{259,3},{4... | collective-permute-start | bytes 393224 | tf_op jit(solution)/shard_map/ppermute | solution.py:23
  47.6 23.1 %collective-permute-start.3 = (bf16[160,256]{1,0:T(8,128)(2,1)S(1)}, bf16[160,256]{1,0:T(8,128)(2,1)S(1)}, u32[]{:S(2)}, u32[]{:S(2)}) collective-permute-start(bf16[160,256]{1,0:T(8,128)(2,1)S(1)} %pad_maximum_fusion.2), channel_id=1, source_target_pairs={{0,1},{1,0},{2,3},{3,2},{4,5},{5,4},{6,7},{7,6},{8,9},{9,8},{10,11... | collective-permute-start | bytes 245768 | tf_op jit(solution)/shard_map/ppermute | solution.py:23
  63.5 39.0 %collective-permute-start.6 = (bf16[448,2048]{1,0:T(8,128)(2,1)S(1)}, bf16[448,2048]{1,0:T(8,128)(2,1)}, u32[]{:S(2)}, u32[]{:S(2)}) collective-permute-start(bf16[448,2048]{1,0:T(8,128)(2,1)S(1)} %bitcast.42), channel_id=1, source_target_pairs={{0,256},{256,0},{1,257},{257,1},{2,258},{258,2},{3,259},{259,3},{4... | collective-permute-start | bytes 5505032 | tf_op jit(solution)/shard_map/ppermute | solution.py:23
  68.8 3.2 %collective-permute-start.4 = (f32[128,256]{1,0:T(8,128)S(1)}, f32[128,256]{1,0:T(8,128)S(1)}, u32[]{:S(2)}, u32[]{:S(2)}) collective-permute-start(f32[128,256]{1,0:T(8,128)S(1)} %get-tuple-element.47), channel_id=1, source_target_pairs={{0,256},{256,0},{1,257},{257,1},{2,258},{258,2},{3,259},{259,3},{4... | collective-permute-start | bytes 393224 | tf_op jit(solution)/shard_map/ppermute | solution.py:23
  72.1 30.3 %copy-start.4 = (s32[5]{0:T(128)S(1)}, s32[5]{0:T(128)}, u32[]{:S(2)}) copy-start(s32[5]{0:T(128)} %stack.23.at_ref) | copy-start | bytes 64
  73.1 20.1 %all-to-all-start.2 = ((bf16[4,448,256]{2,1,0:T(8,128)(2,1)}), bf16[4,448,256]{2,1,0:T(8,128)(2,1)S(1)}, u32[]{:S(2)}, u32[]{:S(2)}) async-start(bf16[4,448,256]{2,1,0:T(8,128)(2,1)} %broadcast_in_dim.7), calls=%async_computation.2 | async-start | bytes 1835008 | tf_op jit(solution)/shard_map/all_to_all | solution.py:29
  77.5 15.7 %collective-permute-start.5 = (bf16[128,256]{1,0:T(8,128)(2,1)S(1)}, bf16[128,256]{1,0:T(8,128)(2,1)S(1)}, u32[]{:S(2)}, u32[]{:S(2)}) collective-permute-start(bf16[128,256]{1,0:T(8,128)(2,1)S(1)} %get-tuple-element.36), channel_id=1, source_target_pairs={{0,1},{1,0},{2,3},{3,2},{4,5},{5,4},{6,7},{7,6},{8,9},{9,8},{10,11... | collective-permute-start | bytes 196616 | tf_op jit(solution)/shard_map/ppermute | solution.py:23
  102.4 16.0 %copy-start.5 = (f32[1,448]{1,0:T(1,128)S(1)}, f32[1,448]{1,0:T(1,128)}, u32[]{:S(2)}) copy-start(f32[1,448]{1,0:T(1,128)} %bias_ref.1) | copy-start | bytes 5380
  105.6 0.8 copy-start.1
  106.4 41.1 %all-to-all-start.4 = ((bf16[32,8,1024]{2,1,0:T(8,128)(2,1)}), bf16[32,8,1024]{2,1,0:T(8,128)(2,1)S(1)}, u32[]{:S(2)}, u32[]{:S(2)}) async-start(bf16[32,8,1024]{2,1,0:T(8,128)(2,1)} %bitcast.45), calls=%async_computation.4 | async-start | bytes 1048576 | tf_op jit(solution)/shard_map/all_to_all | solution.py:310
  120.8 5.7 %collective-permute-start.7 = (bf16[272,448]{1,0:T(8,128)(2,1)S(1)}, bf16[272,448]{1,0:T(8,128)(2,1)S(1)}, u32[]{:S(2)}, u32[]{:S(2)}) collective-permute-start(bf16[272,448]{1,0:T(8,128)(2,1)S(1)} %pad_maximum_fusion), channel_id=1, source_target_pairs={{0,256},{256,0},{1,257},{257,1},{2,258},{258,2},{3,259},{259,3},{4... | collective-permute-start | bytes 731144 | tf_op jit(solution)/shard_map/ppermute | solution.py:23
  129.6 0.6 copy-start.2
  147.4 0.8 copy-start.3
  149.7 27.4 %all-to-all-start.5 = ((f32[16,4,128]{2,1,0:T(4,128)}), f32[16,4,128]{2,1,0:T(4,128)S(1)}, u32[]{:S(2)}, u32[]{:S(2)}) async-start(f32[16,4,128]{2,1,0:T(4,128)} %get-tuple-element.33), calls=%async_computation.5 | async-start | bytes 65536 | tf_op jit(solution)/shard_map/all_to_all | solution.py:344
  162.9 4.3 %collective-permute-start.8 = (bf16[8,448]{1,0:T(8,128)(2,1)S(1)}, bf16[8,448]{1,0:T(8,128)(2,1)S(1)}, u32[]{:S(2)}, u32[]{:S(2)}) collective-permute-start(bf16[8,448]{1,0:T(8,128)(2,1)S(1)} %get-tuple-element.32), channel_id=1, source_target_pairs={{0,256},{256,0},{1,257},{257,1},{2,258},{258,2},{3,259},{259,3},{4... | collective-permute-start | bytes 21512 | tf_op jit(solution)/shard_map/ppermute | solution.py:23
  164.9 12.8 %collective-permute-start.9 = (f32[1,256]{1,0:T(1,128)S(1)}, f32[1,256]{1,0:T(1,128)S(1)}, u32[]{:S(2)}, u32[]{:S(2)}) collective-permute-start(f32[1,256]{1,0:T(1,128)S(1)} %slice.24), channel_id=1, source_target_pairs={{0,256},{256,0},{1,257},{257,1},{2,258},{258,2},{3,259},{259,3},{4... | collective-permute-start | bytes 3080 | tf_op jit(solution)/shard_map/ppermute | solution.py:23

commit v13 on v12

--- a/solution.py
+++ b/solution.py
@@ -331,6 +331,7 @@
     )(at, g1, g2, dec_t, dec_oth, own_acts, came, dec_bias)
     nsq_own = stats[1]
     mean_sq = (stats[:1] + swap(stats[:1], "pair"))[0] / tokens
+    arrived, mean_sq = lax.optimization_barrier((arrived, mean_sq))
 
     recon_own, recon_his, last = call(
         close_kernel,

time: 179 us -> 179 us (level)
    all_to_all x1, waiting for transfers between devices: 17.2 us -> 14.1 us  [body(): arrived = lax.all_to_all(payload.reshape(32, 8, 1024), LAT, 0, 0)]
    ppermute x10, waiting for transfers between devices: 5.9 us -> 7.73 us  [swap(): return lax.ppermute(value, axis, [(0, 1), (1, 0)])]
  transfers between devices with their start and end apart: 15 -> 15, of which waited for: 7 -> 9; matrix products, arithmetic and copies ran while one was open for 6% -> 5% of each run, Pallas kernels for 4% -> 4%
where the time goes in v13:
time: 179 us; the launch traced here: 178 us
  starting transfers between devices  107 us (60%)
  waiting for transfers between devices  32.4 us (18%)
  Pallas kernels  13.9 us (8%)
  blocking collectives  9.2 us (5%)
  local copies, waits for them, and re-layouts  8.6 us (5%)
  other arithmetic  3.27 us (2%)
  matrix products  2.69 us (2%)
    ppermute x10, starting transfers between devices, swap(): return lax.ppermute(value, axis, [(0, 1), (1, 0)])  65.1 us
    all_to_all x1, waiting for transfers between devices, body(): arrived = lax.all_to_all(payload.reshape(32, 8, 1024), LAT, 0, 0)  14.1 us
    all_to_all x1, starting transfers between devices, body(): got = lax.all_to_all(last, ('pair',) + TOK, 0, 0, tiled=True)  13.2 us
    all_to_all x1, starting transfers between devices, body(): arrived = lax.all_to_all(payload.reshape(32, 8, 1024), LAT, 0, 0)  12.1 us
    all_to_all x2, starting transfers between devices, gather(): return lax.all_to_all(copies, axes, 0, 0, tiled=False)  11.6 us
    all_to_all x1, waiting for transfers between devices, body(): got = lax.all_to_all(last, ('pair',) + TOK, 0, 0, tiled=True)  10.6 us
    all_to_all x1, blocking collectives, gather(): return lax.all_to_all(copies, axes, 0, 0, tiled=False)  9.2 us
    ppermute x10, waiting for transfers between devices, swap(): return lax.ppermute(value, axis, [(0, 1), (1, 0)])  7.73 us
  transfers between devices with their start and end apart: 15, of which 9 were waited for; matrix products, arithmetic and copies ran while one was open for 5% of the time, Pallas kernels for 4%

profile of v13, /device:TPU:1, one launch (start us, length us, event | category | flops | bytes accessed | tf_op | source)
XLA Modules:
  0.0 178.1 jit_solution(13627689031146592839)
XLA Ops:
  0.6 2.3 %copies.1 = bf16[4,64,3584]{2,1,0:T(8,128)(2,1)} custom-call(bf16[64,3584]{1,0:T(8,128)(2,1)} %bitcast.54), custom_call_target="tpu_custom_call" | custom-call | bytes 2097152 | tf_op jit(solution)/shard_map/copies/pallas_call | solution.py:230
  2.9 5.2 %all-to-all-start = ((bf16[4,64,3584]{2,1,0:T(8,128)(2,1)}), bf16[4,64,3584]{2,1,0:T(8,128)(2,1)}, u32[]{:S(2)}, u32[]{:S(2)}) async-start(bf16[4,64,3584]{2,1,0:T(8,128)(2,1)} %copies.1), calls=%async_computation | async-start | bytes 3670016 | tf_op jit(solution)/shard_map/all_to_all | solution.py:242
  9.0 15.7 %collective-permute-start = (bf16[16,3584]{1,0:T(8,128)(2,1)S(1)}, bf16[16,3584]{1,0:T(8,128)(2,1)S(1)}, u32[]{:S(2)}, u32[]{:S(2)}) collective-permute-start(bf16[16,3584]{1,0:T(8,128)(2,1)S(1)} %dynamic-slice_bitcast_fusion.6), channel_id=1, source_target_pairs={{0,1},{1,0},{2,3},{3,2},{4,5},{5,4},{6,7},{7,6},{8,9},{9,8},{10,11... | collective-permute-start | bytes 344072 | tf_op jit(solution)/shard_map/ppermute | solution.py:23
  25.1 2.9 %collective-permute-start.1 = (f32[8,256]{1,0:T(8,128)S(1)}, f32[8,256]{1,0:T(8,128)S(1)}, u32[]{:S(2)}, u32[]{:S(2)}) collective-permute-start(f32[8,256]{1,0:T(8,128)S(1)} %reshape.117), channel_id=1, source_target_pairs={{0,256},{256,0},{1,257},{257,1},{2,258},{258,2},{3,259},{259,3},{4... | collective-permute-start | bytes 24584 | tf_op jit(solution)/shard_map/ppermute | solution.py:23
  28.8 1.4 broadcast_in_dim.8
  30.2 7.3 %all-to-all-start.1 = ((bf16[16,16,3584]{2,1,0:T(8,128)(2,1)}), bf16[16,16,3584]{2,1,0:T(8,128)(2,1)}, u32[]{:S(2)}, u32[]{:S(2)}) async-start(bf16[16,16,3584]{2,1,0:T(8,128)(2,1)} %broadcast_in_dim.8), calls=%async_computation.1 | async-start | bytes 3670016 | tf_op jit(solution)/shard_map/all_to_all | solution.py:29
  37.5 4.1 %encode.1 = (f32[128,256]{1,0:T(8,128)}, f32[128,256]{1,0:T(8,128)}) custom-call(s32[5]{0:T(128)} %stack.23.at_ref, bf16[256,3584]{1,0:T(8,128)(2,1)} %bitcast.8.act_hbm, bf16[3584,256]{1,0:T(8,128)(2,1)} %bitcast.51), custom_call_target="tpu_custom_call" | custom-call | flops 469762048 | bytes 6291456 | tf_op jit(solution)/shard_map/encode/pallas_call | solution.py:277
  41.6 3.9 %collective-permute-start.2 = (f32[128,256]{1,0:T(8,128)}, f32[128,256]{1,0:T(8,128)S(1)}, u32[]{:S(2)}, u32[]{:S(2)}) collective-permute-start(f32[128,256]{1,0:T(8,128)} %get-tuple-element.23), channel_id=1, source_target_pairs={{0,256},{256,0},{1,257},{257,1},{2,258},{258,2},{3,259},{259,3},{4... | collective-permute-start | bytes 393224 | tf_op jit(solution)/shard_map/ppermute | solution.py:23
  45.5 1.1 collective-permute-done.2
  47.6 15.8 %collective-permute-start.3 = (bf16[160,256]{1,0:T(8,128)(2,1)S(1)}, bf16[160,256]{1,0:T(8,128)(2,1)S(1)}, u32[]{:S(2)}, u32[]{:S(2)}) collective-permute-start(bf16[160,256]{1,0:T(8,128)(2,1)S(1)} %pad_maximum_fusion.2), channel_id=1, source_target_pairs={{0,1},{1,0},{2,3},{3,2},{4,5},{5,4},{6,7},{7,6},{8,9},{9,8},{10,11... | collective-permute-start | bytes 245768 | tf_op jit(solution)/shard_map/ppermute | solution.py:23
  63.5 2.6 %collective-permute-start.6 = (bf16[448,2048]{1,0:T(8,128)(2,1)S(1)}, bf16[448,2048]{1,0:T(8,128)(2,1)}, u32[]{:S(2)}, u32[]{:S(2)}) collective-permute-start(bf16[448,2048]{1,0:T(8,128)(2,1)S(1)} %bitcast.46), channel_id=1, source_target_pairs={{0,256},{256,0},{1,257},{257,1},{2,258},{258,2},{3,259},{259,3},{4... | collective-permute-start | bytes 5505032 | tf_op jit(solution)/shard_map/ppermute | solution.py:23
  66.0 2.7 %fusion = f32[16,2,8,256]{3,2,1,0:T(8,128)S(1)} fusion(bf16[1,3584,256]{2,1,0:T(8,128)(2,1)} %param.7, bf16[16,16,3584]{2,1,0:T(8,128)(2,1)} %all-to-all-done.1), kind=kOutput, calls=%fused_computation.1 | convolution fusion | flops 469762048 | bytes 3932160 | tf_op jit(solution)/shard_map/dot_general | solution.py:286
  68.8 1.9 %collective-permute-start.4 = (f32[128,256]{1,0:T(8,128)S(1)}, f32[128,256]{1,0:T(8,128)S(1)}, u32[]{:S(2)}, u32[]{:S(2)}) collective-permute-start(f32[128,256]{1,0:T(8,128)S(1)} %get-tuple-element.51), channel_id=1, source_target_pairs={{0,256},{256,0},{1,257},{257,1},{2,258},{258,2},{3,259},{259,3},{4... | collective-permute-start | bytes 393224 | tf_op jit(solution)/shard_map/ppermute | solution.py:23
  70.7 1.3 collective-permute-done.4
  73.1 4.4 %all-to-all-start.2 = ((bf16[4,448,256]{2,1,0:T(8,128)(2,1)}), bf16[4,448,256]{2,1,0:T(8,128)(2,1)S(1)}, u32[]{:S(2)}, u32[]{:S(2)}) async-start(bf16[4,448,256]{2,1,0:T(8,128)(2,1)} %broadcast_in_dim.9), calls=%async_computation.2 | async-start | bytes 1835008 | tf_op jit(solution)/shard_map/all_to_all | solution.py:29
  77.5 13.4 %collective-permute-start.5 = (bf16[128,256]{1,0:T(8,128)(2,1)S(1)}, bf16[128,256]{1,0:T(8,128)(2,1)S(1)}, u32[]{:S(2)}, u32[]{:S(2)}) collective-permute-start(bf16[128,256]{1,0:T(8,128)(2,1)S(1)} %get-tuple-element.40), channel_id=1, source_target_pairs={{0,1},{1,0},{2,3},{3,2},{4,5},{5,4},{6,7},{7,6},{8,9},{9,8},{10,11... | collective-permute-start | bytes 196616 | tf_op jit(solution)/shard_map/ppermute | solution.py:23
  90.9 2.2 %collective-permute-done.5 = bf16[128,256]{1,0:T(8,128)(2,1)S(1)} collective-permute-done((bf16[128,256]{1,0:T(8,128)(2,1)S(1)}, bf16[128,256]{1,0:T(8,128)(2,1)S(1)}, u32[]{:S(2)}, u32[]{:S(2)}) %collective-permute-start.5) | collective-permute-done | bytes 65568 | tf_op jit(solution)/shard_map/ppermute | solution.py:23
  93.1 9.2 %all_to_all.30.g2 = bf16[4,128,256]{2,1,0:T(8,128)(2,1)S(1)} all-to-all(bf16[4,128,256]{2,1,0:T(8,128)(2,1)S(1)} %broadcast_in_dim.10), channel_id=1, replica_groups=mesh['pair'=2,'x'=4,'zl'=8,'y'=4,'zh'=2] {'y'}, dimensions={0} | all-to-all | bytes 524288 | tf_op jit(solution)/shard_map/all_to_all | solution.py:29
  102.3 3.1 %decode.1 = bf16[256,1024]{1,0:T(8,128)(2,1)S(1)} custom-call(s32[5]{0:T(128)S(1)} %copy-done.4, bf16[4,448,256]{2,1,0:T(8,128)(2,1)S(1)} %all-to-all-done.2.g1, bf16[4,128,256]{2,1,0:T(8,128)(2,1)S(1)} %all_to_all.30.g2, bf16[448,2048]{1,0:T(8,128)(2,1)S(1)} %bitcast.47, bf16[448,2048]{1,0:T(8,128)(2,1)} %collective-permute-done.6.oth_ref), custom_call_target="tpu_custom_call" | custom-call | flops 1073741824 | bytes 6291456 | tf_op jit(solution)/shard_map/decode/pallas_call | solution.py:297
  106.3 12.1 %all-to-all-start.4 = ((bf16[32,8,1024]{2,1,0:T(8,128)(2,1)}), bf16[32,8,1024]{2,1,0:T(8,128)(2,1)S(1)}, u32[]{:S(2)}, u32[]{:S(2)}) async-start(bf16[32,8,1024]{2,1,0:T(8,128)(2,1)} %bitcast.49), calls=%async_computation.4 | async-start | bytes 1048576 | tf_op jit(solution)/shard_map/all_to_all | solution.py:310
  118.4 1.1 constant_dynamic-slice_fusion.1
  119.5 1.1 constant_dynamic-slice_fusion
  120.7 4.6 %collective-permute-start.7 = (bf16[272,448]{1,0:T(8,128)(2,1)S(1)}, bf16[272,448]{1,0:T(8,128)(2,1)S(1)}, u32[]{:S(2)}, u32[]{:S(2)}) collective-permute-start(bf16[272,448]{1,0:T(8,128)(2,1)S(1)} %pad_maximum_fusion), channel_id=1, source_target_pairs={{0,256},{256,0},{1,257},{257,1},{2,258},{258,2},{3,259},{259,3},{4... | collective-permute-start | bytes 731144 | tf_op jit(solution)/shard_map/ppermute | solution.py:23
  125.4 1.1 collective-permute-done.7.his_ref
  126.5 3.0 %numer.1 = (f32[32,512]{1,0:T(8,128)S(1)}, f32[2,256]{1,0:T(2,128)S(1)}) custom-call(s32[5]{0:T(128)S(1)} %copy-done.4, bf16[4,448,256]{2,1,0:T(8,128)(2,1)S(1)} %all-to-all-done.2.g1, bf16[4,128,256]{2,1,0:T(8,128)(2,1)S(1)} %all_to_all.30.g2, bf16[448,2048]{1,0:T(8,128)(2,1)S(1)} %bitcast.48, bf16[448,2048]{1,0:T(8,128)(2,1)} %collective-permute-done.6.oth_ref, ...), custom_call_target="tpu_custom_call" | custom-call | flops 939524096 | bytes 6291456 | tf_op jit(solution)/shard_map/numer/pallas_call | solution.py:323
  130.2 2.3 %collective-permute-start.8 = (f32[1,256]{1,0:T(1,128)S(1)}, f32[1,256]{1,0:T(1,128)S(1)}, u32[]{:S(2)}, u32[]{:S(2)}) collective-permute-start(f32[1,256]{1,0:T(1,128)S(1)} %slice.21), channel_id=1, source_target_pairs={{0,256},{256,0},{1,257},{257,1},{2,258},{258,2},{3,259},{259,3},{4... | collective-permute-start | bytes 3080 | tf_op jit(solution)/shard_map/ppermute | solution.py:23
  133.3 14.1 %all-to-all-done.4.arrived_ref = bf16[32,8,1024]{2,1,0:T(8,128)(2,1)S(1)} async-done(((bf16[32,8,1024]{2,1,0:T(8,128)(2,1)}), bf16[32,8,1024]{2,1,0:T(8,128)(2,1)S(1)}, u32[]{:S(2)}, u32[]{:S(2)}) %all-to-all-start.4) | async-done | bytes 524320 | tf_op jit(solution)/shard_map/all_to_all | solution.py:310
  148.2 1.4 close.1
  149.6 13.2 %all-to-all-start.5 = ((f32[16,4,128]{2,1,0:T(4,128)}), f32[16,4,128]{2,1,0:T(4,128)S(1)}, u32[]{:S(2)}, u32[]{:S(2)}) async-start(f32[16,4,128]{2,1,0:T(4,128)} %get-tuple-element.37), calls=%async_computation.5 | async-start | bytes 65536 | tf_op jit(solution)/shard_map/all_to_all | solution.py:345
  162.8 2.0 %collective-permute-start.9 = (bf16[8,448]{1,0:T(8,128)(2,1)S(1)}, bf16[8,448]{1,0:T(8,128)(2,1)S(1)}, u32[]{:S(2)}, u32[]{:S(2)}) collective-permute-start(bf16[8,448]{1,0:T(8,128)(2,1)S(1)} %get-tuple-element.36), channel_id=1, source_target_pairs={{0,256},{256,0},{1,257},{257,1},{2,258},{258,2},{3,259},{259,3},{4... | collective-permute-start | bytes 21512 | tf_op jit(solution)/shard_map/ppermute | solution.py:23
  164.8 1.0 collective-permute-done.9
  166.4 10.6 %all-to-all-done.5 = f32[16,4,128]{2,1,0:T(4,128)S(1)} async-done(((f32[16,4,128]{2,1,0:T(4,128)}), f32[16,4,128]{2,1,0:T(4,128)S(1)}, u32[]{:S(2)}, u32[]{:S(2)}) %all-to-all-start.5) | async-done | bytes 32800 | tf_op jit(solution)/shard_map/all_to_all | solution.py:345
  (51 shorter events, 9.2 us)
Async XLA Ops:
  2.9 21.7 %copy-start = (bf16[1,2048,448]{1,2,0:T(8,128)(2,1)S(1)}, bf16[1,2048,448]{1,2,0:T(8,128)(2,1)}, u32[]{:S(2)}) copy-start(bf16[1,2048,448]{1,2,0:T(8,128)(2,1)} %param.10) | copy-start | bytes 5505028
  2.9 25.9 %all-to-all-start = ((bf16[4,64,3584]{2,1,0:T(8,128)(2,1)}), bf16[4,64,3584]{2,1,0:T(8,128)(2,1)}, u32[]{:S(2)}, u32[]{:S(2)}) async-start(bf16[4,64,3584]{2,1,0:T(8,128)(2,1)} %copies.1), calls=%async_computation | async-start | bytes 3670016 | tf_op jit(solution)/shard_map/all_to_all | solution.py:242
  9.0 19.8 %collective-permute-start = (bf16[16,3584]{1,0:T(8,128)(2,1)S(1)}, bf16[16,3584]{1,0:T(8,128)(2,1)S(1)}, u32[]{:S(2)}, u32[]{:S(2)}) collective-permute-start(bf16[16,3584]{1,0:T(8,128)(2,1)S(1)} %dynamic-slice_bitcast_fusion.6), channel_id=1, source_target_pairs={{0,1},{1,0},{2,3},{3,2},{4,5},{5,4},{6,7},{7,6},{8,9},{9,8},{10,11... | collective-permute-start | bytes 344072 | tf_op jit(solution)/shard_map/ppermute | solution.py:23
  25.1 3.7 %collective-permute-start.1 = (f32[8,256]{1,0:T(8,128)S(1)}, f32[8,256]{1,0:T(8,128)S(1)}, u32[]{:S(2)}, u32[]{:S(2)}) collective-permute-start(f32[8,256]{1,0:T(8,128)S(1)} %reshape.117), channel_id=1, source_target_pairs={{0,256},{256,0},{1,257},{257,1},{2,258},{258,2},{3,259},{259,3},{4... | collective-permute-start | bytes 24584 | tf_op jit(solution)/shard_map/ppermute | solution.py:23
  30.2 7.3 %copy-start.7 = (s32[256]{0:T(256)S(1)}, s32[256]{0:T(256)}, u32[]{:S(2)}) copy-start(s32[256]{0:T(256)} %param.9) | copy-start | bytes 3076
  30.2 35.8 %all-to-all-start.1 = ((bf16[16,16,3584]{2,1,0:T(8,128)(2,1)}), bf16[16,16,3584]{2,1,0:T(8,128)(2,1)}, u32[]{:S(2)}, u32[]{:S(2)}) async-start(bf16[16,16,3584]{2,1,0:T(8,128)(2,1)} %broadcast_in_dim.8), calls=%async_computation.1 | async-start | bytes 3670016 | tf_op jit(solution)/shard_map/all_to_all | solution.py:29
  37.5 9.1 %copy-start.6 = (f32[256]{0:T(256)S(1)}, f32[256]{0:T(256)}, u32[]{:S(2)}) copy-start(f32[256]{0:T(256)} %param.8) | copy-start | bytes 3076
  41.6 5.0 %collective-permute-start.2 = (f32[128,256]{1,0:T(8,128)}, f32[128,256]{1,0:T(8,128)S(1)}, u32[]{:S(2)}, u32[]{:S(2)}) collective-permute-start(f32[128,256]{1,0:T(8,128)} %get-tuple-element.23), channel_id=1, source_target_pairs={{0,256},{256,0},{1,257},{257,1},{2,258},{258,2},{3,259},{259,3},{4... | collective-permute-start | bytes 393224 | tf_op jit(solution)/shard_map/ppermute | solution.py:23
  47.6 23.1 %collective-permute-start.3 = (bf16[160,256]{1,0:T(8,128)(2,1)S(1)}, bf16[160,256]{1,0:T(8,128)(2,1)S(1)}, u32[]{:S(2)}, u32[]{:S(2)}) collective-permute-start(bf16[160,256]{1,0:T(8,128)(2,1)S(1)} %pad_maximum_fusion.2), channel_id=1, source_target_pairs={{0,1},{1,0},{2,3},{3,2},{4,5},{5,4},{6,7},{7,6},{8,9},{9,8},{10,11... | collective-permute-start | bytes 245768 | tf_op jit(solution)/shard_map/ppermute | solution.py:23
  63.5 38.9 %collective-permute-start.6 = (bf16[448,2048]{1,0:T(8,128)(2,1)S(1)}, bf16[448,2048]{1,0:T(8,128)(2,1)}, u32[]{:S(2)}, u32[]{:S(2)}) collective-permute-start(bf16[448,2048]{1,0:T(8,128)(2,1)S(1)} %bitcast.46), channel_id=1, source_target_pairs={{0,256},{256,0},{1,257},{257,1},{2,258},{258,2},{3,259},{259,3},{4... | collective-permute-start | bytes 5505032 | tf_op jit(solution)/shard_map/ppermute | solution.py:23
  68.8 3.2 %collective-permute-start.4 = (f32[128,256]{1,0:T(8,128)S(1)}, f32[128,256]{1,0:T(8,128)S(1)}, u32[]{:S(2)}, u32[]{:S(2)}) collective-permute-start(f32[128,256]{1,0:T(8,128)S(1)} %get-tuple-element.51), channel_id=1, source_target_pairs={{0,256},{256,0},{1,257},{257,1},{2,258},{258,2},{3,259},{259,3},{4... | collective-permute-start | bytes 393224 | tf_op jit(solution)/shard_map/ppermute | solution.py:23
  72.1 30.2 %copy-start.4 = (s32[5]{0:T(128)S(1)}, s32[5]{0:T(128)}, u32[]{:S(2)}) copy-start(s32[5]{0:T(128)} %stack.23.at_ref) | copy-start | bytes 64
  73.1 20.0 %all-to-all-start.2 = ((bf16[4,448,256]{2,1,0:T(8,128)(2,1)}), bf16[4,448,256]{2,1,0:T(8,128)(2,1)S(1)}, u32[]{:S(2)}, u32[]{:S(2)}) async-start(bf16[4,448,256]{2,1,0:T(8,128)(2,1)} %broadcast_in_dim.9), calls=%async_computation.2 | async-start | bytes 1835008 | tf_op jit(solution)/shard_map/all_to_all | solution.py:29
  77.5 15.6 %collective-permute-start.5 = (bf16[128,256]{1,0:T(8,128)(2,1)S(1)}, bf16[128,256]{1,0:T(8,128)(2,1)S(1)}, u32[]{:S(2)}, u32[]{:S(2)}) collective-permute-start(bf16[128,256]{1,0:T(8,128)(2,1)S(1)} %get-tuple-element.40), channel_id=1, source_target_pairs={{0,1},{1,0},{2,3},{3,2},{4,5},{5,4},{6,7},{7,6},{8,9},{9,8},{10,11... | collective-permute-start | bytes 196616 | tf_op jit(solution)/shard_map/ppermute | solution.py:23
  102.3 16.0 %copy-start.5 = (f32[1,448]{1,0:T(1,128)S(1)}, f32[1,448]{1,0:T(1,128)}, u32[]{:S(2)}) copy-start(f32[1,448]{1,0:T(1,128)} %bias_ref.1) | copy-start | bytes 5380
  105.5 0.8 copy-start.1
  106.3 41.1 %all-to-all-start.4 = ((bf16[32,8,1024]{2,1,0:T(8,128)(2,1)}), bf16[32,8,1024]{2,1,0:T(8,128)(2,1)S(1)}, u32[]{:S(2)}, u32[]{:S(2)}) async-start(bf16[32,8,1024]{2,1,0:T(8,128)(2,1)} %bitcast.49), calls=%async_computation.4 | async-start | bytes 1048576 | tf_op jit(solution)/shard_map/all_to_all | solution.py:310
  120.7 5.8 %collective-permute-start.7 = (bf16[272,448]{1,0:T(8,128)(2,1)S(1)}, bf16[272,448]{1,0:T(8,128)(2,1)S(1)}, u32[]{:S(2)}, u32[]{:S(2)}) collective-permute-start(bf16[272,448]{1,0:T(8,128)(2,1)S(1)} %pad_maximum_fusion), channel_id=1, source_target_pairs={{0,256},{256,0},{1,257},{257,1},{2,258},{258,2},{3,259},{259,3},{4... | collective-permute-start | bytes 731144 | tf_op jit(solution)/shard_map/ppermute | solution.py:23
  129.6 0.6 copy-start.2
  130.2 3.1 %collective-permute-start.8 = (f32[1,256]{1,0:T(1,128)S(1)}, f32[1,256]{1,0:T(1,128)S(1)}, u32[]{:S(2)}, u32[]{:S(2)}) collective-permute-start(f32[1,256]{1,0:T(1,128)S(1)} %slice.21), channel_id=1, source_target_pairs={{0,256},{256,0},{1,257},{257,1},{2,258},{258,2},{3,259},{259,3},{4... | collective-permute-start | bytes 3080 | tf_op jit(solution)/shard_map/ppermute | solution.py:23
  147.3 0.8 copy-start.3
  149.6 27.4 %all-to-all-start.5 = ((f32[16,4,128]{2,1,0:T(4,128)}), f32[16,4,128]{2,1,0:T(4,128)S(1)}, u32[]{:S(2)}, u32[]{:S(2)}) async-start(f32[16,4,128]{2,1,0:T(4,128)} %get-tuple-element.37), calls=%async_computation.5 | async-start | bytes 65536 | tf_op jit(solution)/shard_map/all_to_all | solution.py:345
  162.8 3.1 %collective-permute-start.9 = (bf16[8,448]{1,0:T(8,128)(2,1)S(1)}, bf16[8,448]{1,0:T(8,128)(2,1)S(1)}, u32[]{:S(2)}, u32[]{:S(2)}) collective-permute-start(bf16[8,448]{1,0:T(8,128)(2,1)S(1)} %get-tuple-element.36), channel_id=1, source_target_pairs={{0,256},{256,0},{1,257},{257,1},{2,258},{258,2},{3,259},{259,3},{4... | collective-permute-start | bytes 21512 | tf_op jit(solution)/shard_map/ppermute | solution.py:23
